TPU v7x, 128 devices: a whole 4x4x4 slice. The times are simulated.
128 devices in a mesh: fsdp: 16 (over z_hi, x, core), context: 4 (over y), tensor: 2 (over z_lo).
Axes of the slice: x: 4, y: 4, z: 4 (z_hi: 2, z_lo: 2; z = z_hi * 2 + z_lo), core: 2. Of those that a mesh axis runs over, the one named last changes fastest.
Arguments:
- tokens: bfloat16 [32768, 1536], P(('fsdp', 'context')), may hold values from -6 to 6
- teacher: bfloat16 [32768, 1536], P(('fsdp', 'context')), may hold values from -6 to 6
- segments: int32 [16, 2048], P('fsdp'), may hold values from 0 to 66, as said below
- routes: int32 [32768, 2], P(('fsdp', 'context')), may hold values from 0 to 15, all different within a row; in each aligned block of 512 rows (0 to 511, 512 to 1023, ...) at most 96 rows name the same one
- route_weight: float32 [32768, 2], P(('fsdp', 'context')), may hold values from 2 to 16
- norm_attn: bfloat16 [1536], P(('fsdp', 'context')), may hold values from 0.5 to 1.5
- w_query: bfloat16 [1536, 1536], P(('fsdp', 'context'), 'tensor'), may hold values from -0.15625 to 0.15625
- key_weight: bfloat16 [1536, 512], P(('fsdp', 'context'), 'tensor'), may hold values from -0.15625 to 0.15625
- value_weight: bfloat16 [1536, 512], P(('fsdp', 'context'), 'tensor'), may hold values from -0.15625 to 0.15625
- w_out: bfloat16 [1536, 1536], P('tensor', ('fsdp', 'context')), may hold values from -0.625 to 0.625
- norm_ffn: bfloat16 [1536], P(('fsdp', 'context')), may hold values from 0.5 to 1.5
- w_router: bfloat16 [1536, 16], P(('fsdp', 'context')), may hold values from -0.109375 to 0.109375
- w_gate: bfloat16 [16, 1536, 1024], P('fsdp', 'context', 'tensor'), may hold values from -0.15625 to 0.15625
- w_up: bfloat16 [16, 1536, 1024], P('fsdp', 'context', 'tensor'), may hold values from -0.15625 to 0.15625
- w_down: bfloat16 [16, 1024, 1536], P('fsdp', 'tensor', 'context'), may hold values from -0.5 to 0.5
Outputs:
- output: float32 [32768, 1536], P(('fsdp', 'context'))
- loss: float32 [], replicated
- grad_tokens: float32 [32768, 1536], P(('fsdp', 'context'))
- grad_norm_attn: float32 [1536], P(('fsdp', 'context'))
- grad_query: float32 [1536, 1536], P(('fsdp', 'context'), 'tensor')
- grad_key: float32 [1536, 512], P(('fsdp', 'context'), 'tensor')
- grad_value: float32 [1536, 512], P(('fsdp', 'context'), 'tensor')
- grad_out: float32 [1536, 1536], P('tensor', ('fsdp', 'context'))
- grad_norm_ffn: float32 [1536], P(('fsdp', 'context'))
- grad_router: float32 [1536, 16], P(('fsdp', 'context'))
- grad_gate: float32 [16, 1536, 1024], P('fsdp', 'context', 'tensor')
- grad_up: float32 [16, 1536, 1024], P('fsdp', 'context', 'tensor')
- grad_down: float32 [16, 1024, 1536], P('fsdp', 'tensor', 'context')
Inputs may be any that keep to these rules, and one draw needn't show every extreme that they name: `segments`: each row is one sequence of 2048 positions: documents numbered 1, 2, 3 and so on from position 0 on, never falling, exactly 66 of them, then 512 // 8 to 256 tail pads numbered 0; one document covers positions 256 to 1536. `routes`: each row names two different experts; in each aligned block of 512 rows (the rows of one device) no expert is named by more than 96 rows, and in some blocks one is named by exactly 96.
All inputs are finite; a program needn't handle non-finite values.
Results may differ from a plain program's by a relative error of at most 0.015.
Values may be sent and summed in bfloat16 or wider, within the bound.
No kernel may reach another device: no remote copies, remote signals or barrier semaphores. Data moves between devices by JAX's collectives and lax.ppermute only.
A program may use at most 192 MiB of HBM per device.

v0:
```python
import jax
import jax.numpy as jnp
from jax import lax
from jax.sharding import PartitionSpec as P

QUERY_HEAD_COUNT = 24
KEY_VALUE_HEADS = 8
HEAD_WIDTH = 64
TOP = 2


EPSILON = 1e-06
MASKED = -1e30


def matmul(left, right):
    return jnp.dot(left, right, preferred_element_type=jnp.float32)


def matmul_t(left, right):
    return lax.dot_general(
        left, right, (((1,), (1,)), ((), ())), preferred_element_type=jnp.float32
    )


def inner_t(left, right):
    return lax.dot_general(
        left, right, (((0,), (0,)), ((), ())), preferred_element_type=jnp.float32
    )


def rms_scale(values):
    return lax.rsqrt(jnp.mean(values * values, axis=-1, keepdims=True) + EPSILON)


def norm_back(values, scale, gain_vec, upstream):
    gained = upstream * gain_vec
    grad_gain = jnp.sum(upstream * values * scale, axis=0)
    middle = jnp.mean(values * gained, axis=-1, keepdims=True)
    return (scale * gained - values * scale * scale * scale * middle, grad_gain)


def dispatch_rows(rows, owner_count, local_exp, capacity):
    feat_width = rows.shape[-1]
    moved = lax.all_to_all(
        rows.reshape(owner_count, local_exp * capacity, feat_width),
        "fsdp",
        split_axis=0,
        concat_axis=0,
        tiled=True,
    )
    return moved.reshape(owner_count, local_exp, capacity, feat_width)


def return_rows(partial_value, owner_count, local_exp, capacity):
    summed = lax.psum(partial_value, "tensor").astype(jnp.bfloat16)
    width = summed.shape[-1]
    back = lax.all_to_all(
        summed.reshape(owner_count, local_exp * capacity, width),
        "fsdp",
        split_axis=0,
        concat_axis=0,
        tiled=True,
    )
    return back.reshape(owner_count * local_exp * capacity, width)


def local(
    tokens,
    teacher,
    segments,
    routes,
    route_weight,
    norm_attn,
    w_query,
    key_weight,
    value_weight,
    w_out,
    norm_ffn,
    w_router,
    w_gate,
    w_up,
    w_down,
):
    tok_rows = tokens.shape[0]
    feat_width = tokens.shape[1]
    query_group_width = QUERY_HEAD_COUNT // KEY_VALUE_HEADS
    gathered = (
        lax.all_gather(norm_attn, ("fsdp", "context"), axis=0, tiled=True),
        lax.all_gather(w_query, ("fsdp", "context"), axis=0, tiled=True),
        lax.all_gather(key_weight, ("fsdp", "context"), axis=0, tiled=True),
        lax.all_gather(value_weight, ("fsdp", "context"), axis=0, tiled=True),
        lax.all_gather(w_out, ("fsdp", "context"), axis=1, tiled=True),
        lax.all_gather(norm_ffn, ("fsdp", "context"), axis=0, tiled=True),
        lax.all_gather(w_router, ("fsdp", "context"), axis=0, tiled=True),
    )
    gain_one = gathered[0].astype(jnp.float32)
    full_query, full_key, full_value, full_out = (
        gathered[1],
        gathered[2],
        gathered[3],
        gathered[4],
    )
    gain_two = gathered[5].astype(jnp.float32)
    full_router = gathered[6]
    resid_in = tokens.astype(jnp.float32)
    scale_one = rms_scale(resid_in)
    act_one = (resid_in * scale_one * gain_one).astype(jnp.bfloat16)
    query_row_block = matmul(act_one, full_query).astype(jnp.bfloat16)
    key_part = matmul(act_one, full_key).astype(jnp.bfloat16)
    value_part = matmul(act_one, full_value).astype(jnp.bfloat16)
    context_in = (
        lax.all_gather(key_part, "context", axis=0, tiled=True),
        lax.all_gather(value_part, "context", axis=0, tiled=True),
        lax.all_gather(w_gate, "context", axis=1, tiled=True),
        lax.all_gather(w_up, "context", axis=1, tiled=True),
        lax.all_gather(w_down, "context", axis=2, tiled=True),
    )
    key_row_block, value_row_block, gate_full, up_full, down_full = context_in
    seq_len = key_row_block.shape[0]
    kv_heads = key_part.shape[1] // HEAD_WIDTH
    head_scale = HEAD_WIDTH ** (-0.5)
    first_row = lax.axis_index("context") * tok_rows
    seg_all = segments[0]
    seg_mine = lax.dynamic_slice_in_dim(seg_all, first_row, tok_rows)
    query_pos = first_row + jnp.arange(tok_rows, dtype=jnp.int32)
    key_pos = jnp.arange(seq_len, dtype=jnp.int32)
    allowed = (seg_mine[:, None] == seg_all[None, :]) & (key_pos[None, :] <= query_pos[:, None])
    query_heads = query_row_block.reshape(
        tok_rows, kv_heads, query_group_width, HEAD_WIDTH
    ).transpose(1, 0, 2, 3)
    key_heads = key_row_block.reshape(seq_len, kv_heads, HEAD_WIDTH).transpose(1, 0, 2)
    value_heads = value_row_block.reshape(seq_len, kv_heads, HEAD_WIDTH).transpose(1, 0, 2)

    def score_block(query_one, key_one):
        raw_scores = (
            jnp.einsum("tgd,sd->gts", query_one, key_one, preferred_element_type=jnp.float32)
            * head_scale
        )
        return jnp.where(allowed[None], raw_scores, MASKED)

    def head_forward(pieces):
        query_one, key_one, value_one = pieces
        scores = score_block(query_one, key_one)
        row_max = jnp.max(scores, axis=-1, keepdims=True)
        exp_scores = jnp.exp(scores - row_max)
        row_total = jnp.sum(exp_scores, axis=-1, keepdims=True)
        weights = (exp_scores / row_total).astype(jnp.bfloat16)
        mixed_one = jnp.einsum(
            "gts,sd->tgd", weights, value_one, preferred_element_type=jnp.float32
        )
        return (mixed_one.astype(jnp.bfloat16), row_max + jnp.log(row_total))

    mixed_stack, log_total = lax.map(head_forward, (query_heads, key_heads, value_heads))
    heads_mixed_output = mixed_stack.transpose(1, 0, 2, 3).reshape(tok_rows, -1)
    attn_out = lax.psum(matmul(heads_mixed_output, full_out), "tensor")
    hidden_one = resid_in + attn_out
    scale_two = rms_scale(hidden_one)
    act_two = (hidden_one * scale_two * gain_two).astype(jnp.bfloat16)
    logits = matmul(act_two, full_router)
    router_probs = jax.nn.softmax(logits, axis=-1)
    expert_count = router_probs.shape[1]
    route_table = (
        routes[:, :, None] == jnp.arange(expert_count, dtype=jnp.int32)[None, None, :]
    ).astype(jnp.float32)
    chosen = jnp.sum(route_table * router_probs[:, None, :], axis=-1)
    gate_values = chosen * route_weight
    capacity = 3 * tok_rows * TOP // (2 * expert_count)
    route_list = routes.reshape(-1)
    onehot_table = (
        route_list[:, None] == jnp.arange(expert_count, dtype=jnp.int32)[None, :]
    ).astype(jnp.int32)
    places = jnp.sum(onehot_table * jnp.cumsum(onehot_table, axis=0), axis=-1) - 1
    slot_index = route_list * capacity + places
    source = jnp.arange(tok_rows * TOP, dtype=jnp.int32) // TOP
    owner_count = lax.axis_size("fsdp")
    local_exp = expert_count // owner_count
    send_rows = (
        jnp.zeros((expert_count * capacity, feat_width), jnp.bfloat16)
        .at[slot_index]
        .set(act_two[source])
    )
    received = dispatch_rows(send_rows, owner_count, local_exp, capacity)
    gate_proj = jnp.einsum(
        "sjcd,jdf->sjcf", received, gate_full, preferred_element_type=jnp.float32
    )
    up_proj = jnp.einsum("sjcd,jdf->sjcf", received, up_full, preferred_element_type=jnp.float32)
    inner_act = (jax.nn.silu(gate_proj) * up_proj).astype(jnp.bfloat16)
    expert_part = jnp.einsum(
        "sjcf,jfd->sjcd", inner_act, down_full, preferred_element_type=jnp.float32
    )
    returned = return_rows(expert_part, owner_count, local_exp, capacity)
    picked = returned[slot_index].reshape(tok_rows, TOP, feat_width).astype(jnp.float32)
    output = hidden_one + jnp.sum(gate_values[:, :, None] * picked, axis=1)
    valid_rows = (seg_mine != 0).astype(jnp.float32)
    difference = output - teacher.astype(jnp.float32)
    grad_output = difference * valid_rows[:, None]
    loss_parts = lax.psum(
        (jnp.sum(grad_output * difference), jnp.sum(valid_rows)), ("fsdp", "context")
    )
    loss_value = loss_parts[0] / (feat_width * loss_parts[1])
    d_picked = (
        (gate_values[:, :, None] * grad_output[:, None, :])
        .reshape(-1, feat_width)
        .astype(jnp.bfloat16)
    )
    d_gates = jnp.sum(grad_output[:, None, :] * picked, axis=-1)
    d_send = (
        jnp.zeros((expert_count * capacity, feat_width), jnp.bfloat16).at[slot_index].set(d_picked)
    )
    d_received = dispatch_rows(d_send, owner_count, local_exp, capacity)
    d_inner = jnp.einsum(
        "sjcd,jfd->sjcf", d_received, down_full, preferred_element_type=jnp.float32
    )
    grad_down_part = jnp.einsum(
        "sjcf,sjcd->jfd", inner_act, d_received, preferred_element_type=jnp.float32
    )
    sig_gate = jax.nn.sigmoid(gate_proj)
    d_gate_proj = (d_inner * up_proj * sig_gate * (1.0 + gate_proj * (1.0 - sig_gate))).astype(
        jnp.bfloat16
    )
    d_up_proj = (d_inner * gate_proj * sig_gate).astype(jnp.bfloat16)
    grad_gate_part = jnp.einsum(
        "sjcd,sjcf->jdf", received, d_gate_proj, preferred_element_type=jnp.float32
    )
    grad_up_part = jnp.einsum(
        "sjcd,sjcf->jdf", received, d_up_proj, preferred_element_type=jnp.float32
    )
    d_slots = jnp.einsum(
        "sjcf,jdf->sjcd", d_gate_proj, gate_full, preferred_element_type=jnp.float32
    )
    d_slots = d_slots + jnp.einsum(
        "sjcf,jdf->sjcd", d_up_proj, up_full, preferred_element_type=jnp.float32
    )
    d_returned = return_rows(d_slots, owner_count, local_exp, capacity)
    d_act_two = jnp.sum(
        d_returned[slot_index].reshape(tok_rows, TOP, feat_width).astype(jnp.float32), axis=1
    )
    d_router = jnp.sum(route_table * (d_gates * route_weight)[:, :, None], axis=1)
    d_logits = (
        router_probs * (d_router - jnp.sum(router_probs * d_router, axis=-1, keepdims=True))
    ).astype(jnp.bfloat16)
    grad_router_full = inner_t(act_two, d_logits)
    d_act_two = d_act_two + matmul_t(d_logits, full_router)
    d_hidden_norm, grad_gain_two = norm_back(hidden_one, scale_two, gain_two, d_act_two)
    d_hidden = grad_output + d_hidden_norm
    d_attn = d_hidden.astype(jnp.bfloat16)
    grad_out_full = inner_t(heads_mixed_output, d_attn)
    d_mixed = matmul_t(d_attn, full_out).astype(jnp.bfloat16)
    d_heads = d_mixed.reshape(tok_rows, kv_heads, query_group_width, HEAD_WIDTH).transpose(
        1, 0, 2, 3
    )

    def head_backward(pieces):
        query_one, key_one, value_one, d_one, total_one = pieces
        scores = score_block(query_one, key_one)
        weights = jnp.exp(scores - total_one)
        d_weights = jnp.einsum("tgd,sd->gts", d_one, value_one, preferred_element_type=jnp.float32)
        row_dot = jnp.sum(weights * d_weights, axis=-1, keepdims=True)
        d_scores = (weights * (d_weights - row_dot)).astype(jnp.bfloat16)
        d_query_one = (
            jnp.einsum("gts,sd->tgd", d_scores, key_one, preferred_element_type=jnp.float32)
            * head_scale
        ).astype(jnp.bfloat16)
        d_key_one = (
            jnp.einsum("gts,tgd->sd", d_scores, query_one, preferred_element_type=jnp.float32)
            * head_scale
        )
        d_value_one = jnp.einsum(
            "gts,tgd->sd", weights.astype(jnp.bfloat16), d_one, preferred_element_type=jnp.float32
        )
        return (d_query_one, d_key_one, d_value_one)

    d_query_stack, d_key_stack, d_value_stack = lax.map(
        head_backward, (query_heads, key_heads, value_heads, d_heads, log_total)
    )
    d_query = d_query_stack.transpose(1, 0, 2, 3).reshape(tok_rows, -1)
    d_keys = d_key_stack.transpose(1, 0, 2).reshape(seq_len, -1)
    d_values = d_value_stack.transpose(1, 0, 2).reshape(seq_len, -1)
    summed_ctx = (
        lax.psum_scatter(d_keys, "context", scatter_dimension=0, tiled=True),
        lax.psum_scatter(d_values, "context", scatter_dimension=0, tiled=True),
        lax.psum_scatter(grad_gate_part, "context", scatter_dimension=1, tiled=True),
        lax.psum_scatter(grad_up_part, "context", scatter_dimension=1, tiled=True),
        lax.psum_scatter(grad_down_part, "context", scatter_dimension=2, tiled=True),
    )
    d_key_mine = summed_ctx[0].astype(jnp.bfloat16)
    d_value_mine = summed_ctx[1].astype(jnp.bfloat16)
    d_act_one = (
        matmul_t(d_query, full_query)
        + matmul_t(d_key_mine, full_key)
        + matmul_t(d_value_mine, full_value)
    )
    d_act_one = lax.psum(d_act_one.astype(jnp.bfloat16), "tensor").astype(jnp.float32)
    d_norm_one, grad_gain_one = norm_back(resid_in, scale_one, gain_one, d_act_one)
    grad_tokens = d_hidden + d_norm_one
    grad_query_full = inner_t(act_one, d_query)
    grad_key_full = inner_t(act_one, d_key_mine)
    grad_value_full = inner_t(act_one, d_value_mine)
    summed = (
        lax.psum_scatter(grad_gain_one, ("fsdp", "context"), scatter_dimension=0, tiled=True),
        lax.psum_scatter(grad_query_full, ("fsdp", "context"), scatter_dimension=0, tiled=True),
        lax.psum_scatter(grad_key_full, ("fsdp", "context"), scatter_dimension=0, tiled=True),
        lax.psum_scatter(grad_value_full, ("fsdp", "context"), scatter_dimension=0, tiled=True),
        lax.psum_scatter(grad_out_full, ("fsdp", "context"), scatter_dimension=1, tiled=True),
        lax.psum_scatter(grad_gain_two, ("fsdp", "context"), scatter_dimension=0, tiled=True),
        lax.psum_scatter(grad_router_full, ("fsdp", "context"), scatter_dimension=0, tiled=True),
    )
    return (
        output,
        loss_value,
        grad_tokens,
        summed[0],
        summed[1],
        summed[2],
        summed[3],
        summed[4],
        summed[5],
        summed[6],
        summed_ctx[2],
        summed_ctx[3],
        summed_ctx[4],
    )


def solution(mesh):
    placed = (
        P(("fsdp", "context"), None),
        P(("fsdp", "context"), None),
        P("fsdp", None),
        P(("fsdp", "context"), None),
        P(("fsdp", "context"), None),
        P(("fsdp", "context")),
        P(("fsdp", "context"), "tensor"),
        P(("fsdp", "context"), "tensor"),
        P(("fsdp", "context"), "tensor"),
        P("tensor", ("fsdp", "context")),
        P(("fsdp", "context")),
        P(("fsdp", "context"), None),
        P("fsdp", "context", "tensor"),
        P("fsdp", "context", "tensor"),
        P("fsdp", "tensor", "context"),
    )
    return jax.shard_map(
        local,
        mesh=mesh,
        in_specs=placed,
        out_specs=(
            P(("fsdp", "context"), None),
            P(),
            P(("fsdp", "context"), None),
            P(("fsdp", "context")),
            P(("fsdp", "context"), "tensor"),
            P(("fsdp", "context"), "tensor"),
            P(("fsdp", "context"), "tensor"),
            P("tensor", ("fsdp", "context")),
            P(("fsdp", "context")),
            P(("fsdp", "context"), None),
            P("fsdp", "context", "tensor"),
            P("fsdp", "context", "tensor"),
            P("fsdp", "tensor", "context"),
        ),
        check_vma=False,
    )
```

profile of v0, /device:TPU:0, one launch (start us, length us, event | category | flops | bytes accessed | tf_op | source)
XLA Modules:
  0.0 3346.3 jit_solution(351653824990382263)
XLA Ops:
  12.8 172.7 %all-reduce.6 = (bf16[1536]{0:T(1024)(128)(2,1)S(1)}, bf16[1536]{0:T(1024)(128)(2,1)S(1)}) all-reduce(bf16[1536]{0:T(1024)(128)(2,1)S(1)} %dynamic-update-slice, bf16[1536]{0:T(1024)(128)(2,1)S(1)} %dynamic-update-slice.1), channel_id=1, replica_groups=mesh['fsdp'=16,'context'=4,'tensor'=2] {'fsdp','context'}, use_global_device_ids=true, to_apply=%add | all-reduce | flops 3072 | bytes 12288
  185.5 164.6 %all_gather.39 = bf16[1536,256]{1,0:T(8,128)(2,1)S(1)} all-gather(bf16[24,256]{1,0:T(8,128)(2,1)} %param.26), channel_id=1, replica_groups=mesh['fsdp'=16,'context'=4,'tensor'=2] {'fsdp','context'}, dimensions={0}, use_global_device_ids=true | all-gather | bytes 798720 | tf_op jit(solution)/shard_map/all_gather | solution.py:91
  353.8 166.8 %all_gather.37 = bf16[1536,256]{1,0:T(8,128)(2,1)S(1)} all-gather(bf16[24,256]{1,0:T(8,128)(2,1)S(1)} %copy-done.39), channel_id=1, replica_groups=mesh['fsdp'=16,'context'=4,'tensor'=2] {'fsdp','context'}, dimensions={0}, use_global_device_ids=true | all-gather | bytes 798720 | tf_op jit(solution)/shard_map/all_gather | solution.py:92
  526.7 14.3 all-gather.9.cloned.1.call-done
  543.3 70.0 %all-gather.13.cloned.1.call-done = bf16[1536,768]{1,0:T(8,128)(2,1)} async-done(((bf16[24,768]{1,0:T(8,128)(2,1)}), bf16[1536,768]{1,0:T(8,128)(2,1)}) %all-gather.13.cloned.1.call-update) | async-done | bytes 2359312 | tf_op jit(solution)/shard_map/all_gather | solution.py:90
  618.5 57.5 %while.28 = (s32[]{:T(128)}, bf16[4,512,3,64]{1,3,2,0:T(8,128)(2,1)}, f32[4,3,512,1]{2,1,3,0:T(4,128)S(1)}, bf16[4,2048,64]{1,2,0:T(8,128)(2,1)}, bf16[4,2048,64...) while((s32[]{:T(128)}, ...), condition=%wide.region_4.5_spmd.clone, body=%wide.region_1.4_spmd.clone.sunk | while | flops 846297600 | bytes 47124620 | solution.py:154
  627.2 5.6 fusion.190
  641.5 5.6 fusion.190
  655.9 5.6 fusion.190
  670.3 5.7 fusion.190
  676.0 5.9 all-gather.15.cloned.1.call-done
  681.9 5.0 fusion.137
  688.5 4.5 reduce-window.6
  693.5 82.9 %all-reduce.13.cloned.1.call-done = f32[512,1536]{1,0:T(8,128)} async-done(((f32[512,1536]{1,0:T(8,128)}), f32[512,1536]{1,0:T(8,128)}) %all-reduce.13.cloned.1.call-update) | async-done | bytes 3145744 | tf_op jit(solution)/shard_map/psum | solution.py:156
  780.7 18.7 scatter_custom_fusion
  799.3 6.8 all-to-all-start
  807.7 62.0 %all-to-all-done = bf16[16,96,1536]{2,1,0:T(8,128)(2,1)} async-done(((bf16[16,96,1536]{2,1,0:T(8,128)(2,1)}), bf16[16,96,1536]{2,1,0:T(8,128)(2,1)}, u32[]{:S(2)}, u32[]{:S(2)}) %all-to-all-start) | async-done | bytes 4718624 | tf_op jit(solution)/shard_map/all_to_all | solution.py:45
  869.6 7.1 fusion.111
  876.8 8.8 fusion.85
  885.6 8.1 convolution_bitcast_fusion.1
  893.7 217.7 %all-reduce.18 = bf16[16,1,96,1536]{3,2,0,1:T(8,128)(2,1)} all-reduce(f32[16,1,96,1536]{3,2,0,1:T(8,128)} %convolution_bitcast_fusion.1), channel_id=1, replica_groups=mesh['fsdp'=16,'context'=4,'tensor'=2] {'tensor'}, use_global_device_ids=true, to_apply=%region_14.15 | all-reduce | flops 2359296 | bytes 14155776 | tf_op jit(solution)/shard_map/psum | solution.py:56
  1111.4 7.0 all-to-all-start.1
  1118.4 211.9 %all-gather = bf16[64,24,16]{1,2,0:T(8,128)(2,1)S(1)} all-gather(bf16[1,24,16]{1,2,0:T(8,128)(2,1)S(1)} %bitcast.389), channel_id=1, replica_groups=mesh['fsdp'=16,'context'=4,'tensor'=2] {'fsdp','context'}, dimensions={0}, use_global_device_ids=true | all-gather | bytes 49920 | tf_op jit(solution)/shard_map/all_gather | solution.py:95
  1337.4 10.3 gather_fusion
  1347.7 7.7 reshape.323
  1355.4 32.0 multiply_reduce_fusion.1
  1391.2 4.7 mul.312
  1396.0 8.4 mul.313
  1404.4 10.2 scatter_custom_fusion.1
  1414.6 61.8 %all_to_all.20 = bf16[16,96,1536]{2,1,0:T(8,128)(2,1)S(1)} all-to-all(bf16[16,96,1536]{2,1,0:T(8,128)(2,1)} %bitcast.369), channel_id=1, replica_groups=mesh['fsdp'=16,'context'=4,'tensor'=2] {'fsdp'}, dimensions={0} | all-to-all | bytes 9437184 | tf_op jit(solution)/shard_map/all_to_all | solution.py:45
  1483.1 5.2 add_bitcast_fusion
  1488.3 216.9 %all-reduce.19 = bf16[16,1,96,1536]{3,2,0,1:T(8,128)(2,1)} all-reduce(f32[16,1,96,1536]{3,2,0,1:T(8,128)} %add_bitcast_fusion), channel_id=1, replica_groups=mesh['fsdp'=16,'context'=4,'tensor'=2] {'tensor'}, use_global_device_ids=true, to_apply=%region_21.22 | all-reduce | flops 2359296 | bytes 14155776 | tf_op jit(solution)/shard_map/psum | solution.py:56
  1705.2 4.9 all-to-all-start.3
  1710.1 10.0 multiply_reduce_fusion
  1722.9 50.6 %all-to-all-done.3 = bf16[16,96,1536]{2,1,0:T(8,128)(2,1)} async-done(((bf16[16,96,1536]{2,1,0:T(8,128)(2,1)}), bf16[16,96,1536]{2,1,0:T(8,128)(2,1)}, u32[]{:S(2)}, u32[]{:S(2)}) %all-to-all-start.3) | async-done | bytes 4718624 | tf_op jit(solution)/shard_map/all_to_all | solution.py:58
  1773.5 10.3 gather_fusion.1
  1783.9 7.7 reshape.324
  1791.6 11.9 reduce_sum.170
  1813.3 103.1 %while.29 = (s32[]{:T(128)}, bf16[4,512,3,64]{1,3,2,0:T(8,128)(2,1)S(1)}, f32[4,2048,64]{1,2,0:T(8,128)}, f32[4,2048,64]{1,2,0:T(8,128)}, bf16[4,2048,64]{1,2,0:...) while((s32[]{:T(128)}, ...), condition=%wide.region_29.30_spmd.clone, body=%wide.region_27.29_spmd.clone.sunk | while | flops 2063923712 | bytes 101448840 | solution.py:274
  1816.5 4.3 fusion.205
  1820.8 7.7 fusion.201
  1828.5 6.9 fusion.202
  1842.2 4.3 fusion.205
  1846.5 7.7 fusion.201
  1854.2 6.9 fusion.202
  1872.2 7.7 fusion.201
  1879.8 6.9 fusion.202
  1893.5 4.3 fusion.205
  1897.8 7.7 fusion.201
  1905.5 6.9 fusion.202
  1919.1 4.8 fusion.138
  1923.9 21.2 reduce-scatter.11.cloned.1.call-done
  1948.0 28.8 reduce-scatter.13.cloned.1.call-done
  1980.1 7.1 convolution_bitcast_fusion.2
  1988.6 6.7 convolution_bitcast_fusion.4
  1996.7 6.7 convolution_bitcast_fusion.3
  2008.9 5.5 fusion.113
  2020.5 524.0 %all-reduce.17.cloned.1.call-done = f32[1536,16]{0,1:T(8,128)} async-done(((f32[1536,16]{0,1:T(8,128)}), f32[1536,16]{0,1:T(8,128)}) %all-reduce.17.cloned.1.call-update) | async-done | bytes 98320
  2545.9 58.8 %all-reduce.15.cloned.1.call-done = bf16[512,1536]{1,0:T(8,128)(2,1)} async-done(((bf16[512,1536]{1,0:T(8,128)(2,1)}), bf16[512,1536]{1,0:T(8,128)(2,1)}) %all-reduce.15.cloned.1.call-update) | async-done | bytes 1572880 | tf_op jit(solution)/shard_map/psum | solution.py:294
  2607.4 331.4 %all-reduce.5 = (f32[]{:T(128)}, f32[]{:T(128)}, f32[1536]{0:T(1024)S(1)}, f32[1536]{0:T(1024)S(1)}) all-reduce(f32[]{:T(128)} %get-tuple-element.225, f32[]{:T(128)} %fusion.127, f32[1536]{0:T(1024)S(1)} %get-tuple-element.164, f32[1536]{0:T(1024)S(1)} %copy-done.34), channel_id=1, replica_groups=mesh['fsdp'=16,'context'=4,'tensor'=2] {'fsdp','context'}, use_global_device_ids=true, to_apply=%region_17.18 | all-reduce | flops 3074 | bytes 24592 | tf_op jit(solution)/shard_map/psum | solution.py:198
  2941.3 4.7 fusion.74
  2946.0 80.9 %reduce-scatter.17.cloned.1.call-done = f32[24,256]{1,0:T(8,128)} async-done(((f32[1536,256]{1,0:T(8,128)}), f32[24,256]{1,0:T(8,128)}) %reduce-scatter.17.cloned.1.call-update) | async-done | bytes 24592 | tf_op jit(solution)/shard_map/reduce_scatter | solution.py:303
  3026.9 155.7 %reduce-scatter.21.cloned.1.call-done = f32[768,24]{0,1:T(8,128)} async-done(((f32[768,1536]{0,1:T(8,128)}), f32[768,24]{0,1:T(8,128)}) %reduce-scatter.21.cloned.1.call-update) | async-done | bytes 73744 | tf_op jit(solution)/shard_map/reduce_scatter | solution.py:305
  3182.6 155.9 %reduce-scatter.15.cloned.1.call-done = f32[24,768]{1,0:T(8,128)} async-done(((f32[1536,768]{1,0:T(8,128)}), f32[24,768]{1,0:T(8,128)}) %reduce-scatter.15.cloned.1.call-update) | async-done | bytes 73744 | tf_op jit(solution)/shard_map/reduce_scatter | solution.py:302
  (265 shorter events, 153.7 us)
Async XLA Ops:
  7.2 517.3 %all-gather.11.cloned.1.call-start = ((), (), s32[]{:S(2)}) async-start(), calls=%async_computation.14 | async-start | bytes 1310720 | tf_op jit(solution)/shard_map/all_gather | solution.py:113
  9.0 344.7 %copy-start.39 = (bf16[24,256]{1,0:T(8,128)(2,1)S(1)}, bf16[24,256]{1,0:T(8,128)(2,1)}, u32[]{:S(2)}) copy-start(bf16[24,256]{1,0:T(8,128)(2,1)} %param.27) | copy-start | bytes 36868
  9.0 604.2 %copy-start.29 = (f32[512]{0:T(512)}, f32[512]{0:T(512)S(1)}, u32[]{:S(2)}) copy-start(f32[512]{0:T(512)S(1)} %add_rsqrt_fusion.1) | copy-start | bytes 6148
  185.4 427.9 %copy-start.24 = (f32[1536]{0:T(1024)}, f32[1536]{0:T(1024)S(1)}, u32[]{:S(2)}) copy-start(f32[1536]{0:T(1024)S(1)} %convert_element_type.117) | copy-start | bytes 18436
  185.5 336.0 %copy-start.1 = (bf16[512,1536]{1,0:T(8,128)(2,1)S(1)}, bf16[512,1536]{1,0:T(8,128)(2,1)}, u32[]{:S(2)}) copy-start(bf16[512,1536]{1,0:T(8,128)(2,1)} %param.19) | copy-start | bytes 4718596
  353.7 170.7 %copy-start.21 = (s32[1,2048]{1,0:T(1,128)S(1)}, s32[1,2048]{1,0:T(1,128)}, u32[]{:S(2)}) copy-start(s32[1,2048]{1,0:T(1,128)} %param.21) | copy-start | bytes 24580
  353.7 187.3 %all-gather.9.cloned.1.call-start = ((), (), s32[]{:S(2)}) async-start(), calls=%async_computation.13 | async-start | bytes 1310720 | tf_op jit(solution)/shard_map/all_gather | solution.py:114
  522.8 90.5 %all-gather.13.cloned.1.call-start = ((), (), s32[]{:S(2)}) async-start(), calls=%async_computation.15 | async-start | bytes 2396160 | tf_op jit(solution)/shard_map/all_gather | solution.py:90
  523.6 158.3 %all-gather.15.cloned.1.call-start = ((), (), s32[]{:S(2)}) async-start(), calls=%async_computation.16 | async-start | bytes 2396160 | tf_op jit(solution)/shard_map/all_gather | solution.py:93
  524.1 252.2 %all-reduce.13.cloned.1.call-start = ((), (), s32[]{:S(2)}) async-start(), calls=%async_computation.17 | async-start | bytes 6291456 | tf_op jit(solution)/shard_map/psum | solution.py:156
  619.4 3.9 copy-start
  633.8 3.9 copy-start
  648.2 3.9 copy-start
  662.6 3.9 copy-start
  686.9 120.7 %all-gather.17.cloned.1.call-start = ((), (), s32[]{:S(2)}) async-start(), calls=%async_computation.18 | async-start | bytes 1966080 | tf_op jit(solution)/shard_map/all_gather | solution.py:115
  693.5 637.9 %copy-start.38 = (s32[1024,1]{0,1:T(1,128)}, s32[1024,1]{0,1:T(1,128)S(1)}, u32[]{:S(2)}) copy-start(s32[1024,1]{0,1:T(1,128)S(1)} %compare_select_fusion.1) | copy-start | bytes 12292
  779.2 20.2 copy-start.31
  799.3 70.3 %all-to-all-start = ((bf16[16,96,1536]{2,1,0:T(8,128)(2,1)}), bf16[16,96,1536]{2,1,0:T(8,128)(2,1)}, u32[]{:S(2)}, u32[]{:S(2)}) async-start(bf16[16,96,1536]{2,1,0:T(8,128)(2,1)} %bitcast.368), calls=%async_computation | async-start | bytes 9437184 | tf_op jit(solution)/shard_map/all_to_all | solution.py:45
  806.1 70.6 %all-gather.19.cloned.1.call-start = ((), (), s32[]{:S(2)}) async-start(), calls=%async_computation.19 | async-start | bytes 1966080 | tf_op jit(solution)/shard_map/all_gather | solution.py:116
  806.9 78.7 %all-gather.21.cloned.1.call-start = ((), (), s32[]{:S(2)}) async-start(), calls=%async_computation.20 | async-start | bytes 1966080 | tf_op jit(solution)/shard_map/all_gather | solution.py:117
  1111.4 7.0 copy-start.40
  1111.4 226.0 %all-to-all-start.1 = ((bf16[16,96,1536]{2,1,0:T(8,128)(2,1)}), bf16[16,96,1536]{2,1,0:T(8,128)(2,1)}, u32[]{:S(2)}, u32[]{:S(2)}) async-start(bf16[16,96,1536]{2,1,0:T(8,128)(2,1)} %bitcast.366), calls=%async_computation.1 | async-start | bytes 9437184 | tf_op jit(solution)/shard_map/all_to_all | solution.py:58
  1355.4 32.0 copy-start.10
  1355.4 32.0 copy-start.35
  1389.6 1.6 copy-start.4
  1396.0 8.5 copy-start.37
  1414.6 61.8 %copy-start.43 = (bf16[1,512,1536]{2,1,0:T(8,128)(2,1)S(1)}, bf16[1,512,1536]{2,1,0:T(8,128)(2,1)}, u32[]{:S(2)}) copy-start(bf16[1,512,1536]{2,1,0:T(8,128)(2,1)} %all-gather.21.cloned.1.call-done) | copy-start | bytes 4718596
  1414.6 61.8 %copy-start.46 = (f32[16,96,512]{2,1,0:T(8,128)S(1)}, f32[16,96,512]{2,1,0:T(8,128)}, u32[]{:S(2)}) copy-start(f32[16,96,512]{2,1,0:T(8,128)} %fusion.111) | copy-start | bytes 9437188
  1414.6 61.8 %copy-start.47 = (f32[16,96,512]{2,1,0:T(8,128)S(1)}, f32[16,96,512]{2,1,0:T(8,128)}, u32[]{:S(2)}) copy-start(f32[16,96,512]{2,1,0:T(8,128)} %get-tuple-element.229) | copy-start | bytes 9437188
  1476.4 3.9 copy-start.12
  1476.4 3.9 copy-start.42
  1480.4 2.7 copy-start.44
  1480.4 2.7 copy-start.18
  1480.4 2.7 copy-start.20
  1705.2 68.4 %all-to-all-start.3 = ((bf16[16,96,1536]{2,1,0:T(8,128)(2,1)}), bf16[16,96,1536]{2,1,0:T(8,128)(2,1)}, u32[]{:S(2)}, u32[]{:S(2)}) async-start(bf16[16,96,1536]{2,1,0:T(8,128)(2,1)} %bitcast.367), calls=%async_computation.3 | async-start | bytes 9437184 | tf_op jit(solution)/shard_map/all_to_all | solution.py:58
  1710.0 235.0 %reduce-scatter.11.cloned.1.call-start = ((), (), s32[]{:S(2)}) async-start(), calls=%async_computation.21 | async-start | bytes 2621440 | tf_op jit(solution)/shard_map/reduce_scatter | solution.py:281
  1722.9 80.6 %copy-start.26 = (bf16[512,16]{0,1:T(8,128)(2,1)}, bf16[512,16]{0,1:T(8,128)(2,1)S(1)}, u32[]{:S(2)}) copy-start(bf16[512,16]{0,1:T(8,128)(2,1)S(1)} %multiply_convert_fusion.3) | copy-start | bytes 49156
  1791.6 11.9 copy-start.32
  1803.5 3.7 copy-start.7
  1803.5 3.7 copy-start.11
  1803.6 3.7 copy-start.36
  1807.3 4.3 copy-start.41
  1809.9 1.6 copy-start.3
  1811.5 1.8 copy-start.6
  1811.5 1.8 copy-start.8
  1916.4 7.5 copy-start.15
  1916.4 1.7 copy-start.5
  1916.4 1.7 copy-start.27
  1916.4 60.3 %reduce-scatter.13.cloned.1.call-start = ((), (), s32[]{:S(2)}) async-start(), calls=%async_computation.22 | async-start | bytes 2621440 | tf_op jit(solution)/shard_map/reduce_scatter | solution.py:282
  1917.0 627.5 %all-reduce.17.cloned.1.call-start = ((), (), s32[]{:S(2)}) async-start(), calls=%async_computation.31 | async-start | bytes 196608
  1919.1 685.6 %all-reduce.15.cloned.1.call-start = ((), (), s32[]{:S(2)}) async-start(), calls=%async_computation.23 | async-start | bytes 3145728 | tf_op jit(solution)/shard_map/psum | solution.py:294
  1979.8 966.1 %reduce-scatter.27.cloned.1.call-start = ((), (), s32[]{:S(2)}) async-start(), calls=%async_computation.30 | async-start | bytes 3932160 | tf_op jit(solution)/shard_map/reduce_scatter | solution.py:285
  1987.2 958.7 %reduce-scatter.23.cloned.1.call-start = ((), (), s32[]{:S(2)}) async-start(), calls=%async_computation.28 | async-start | bytes 3932160 | tf_op jit(solution)/shard_map/reduce_scatter | solution.py:283
  1995.3 950.7 %reduce-scatter.25.cloned.1.call-start = ((), (), s32[]{:S(2)}) async-start(), calls=%async_computation.29 | async-start | bytes 3932160 | tf_op jit(solution)/shard_map/reduce_scatter | solution.py:284
  2003.3 1.5 copy-start.25
  2003.3 1.5 copy-start.30
  2003.4 3.5 copy-start.23
  2003.4 942.6 %reduce-scatter.19.cloned.1.call-start = ((), (), s32[]{:S(2)}) async-start(), calls=%async_computation.26 | async-start | bytes 1597440 | tf_op jit(solution)/shard_map/reduce_scatter | solution.py:304
  2006.8 2.1 copy-start.13
  2006.8 1020.0 %reduce-scatter.17.cloned.1.call-start = ((), (), s32[]{:S(2)}) async-start(), calls=%async_computation.25 | async-start | bytes 1597440 | tf_op jit(solution)/shard_map/reduce_scatter | solution.py:303
  2008.8 1173.8 %reduce-scatter.21.cloned.1.call-start = ((), (), s32[]{:S(2)}) async-start(), calls=%async_computation.27 | async-start | bytes 4792320 | tf_op jit(solution)/shard_map/reduce_scatter | solution.py:305
  2014.4 1324.1 %reduce-scatter.15.cloned.1.call-start = ((), (), s32[]{:S(2)}) async-start(), calls=%async_computation.24 | async-start | bytes 4792320 | tf_op jit(solution)/shard_map/reduce_scatter | solution.py:302
  2019.3 588.1 %copy-start.34 = (f32[1536]{0:T(1024)S(1)}, f32[1536]{0:T(1024)}, u32[]{:S(2)}) copy-start(f32[1536]{0:T(1024)} %get-tuple-element.162) | copy-start | bytes 18436
  2604.7 336.6 %copy-start.9 = (bf16[512,1536]{1,0:T(8,128)(2,1)S(1)}, bf16[512,1536]{1,0:T(8,128)(2,1)}, u32[]{:S(2)}) copy-start(bf16[512,1536]{1,0:T(8,128)(2,1)} %all-reduce.15.cloned.1.call-done) | copy-start | bytes 4718596
  (9 other events, 9.9 us)
Sparse Core Ops, SparseCore 0:
  353.8 20.1 all-gather.10
  522.9 17.9 all-gather.8
  544.2 69.0 all-gather.12
  616.3 65.4 all-gather.14
  687.1 89.2 all-reduce.12
  778.0 27.5 all-gather.16
  808.7 28.0 all-gather.18
  838.6 26.5 all-gather.20
  1916.6 28.4 reduce-scatter.10
  1947.3 29.3 reduce-scatter.12
  1979.4 565.0 all-reduce.16
  2547.4 57.2 all-reduce.14
  2607.8 39.6 reduce-scatter.26
  2650.5 38.6 reduce-scatter.22
  2692.1 38.4 reduce-scatter.24
  2736.9 143.4 reduce-scatter.18
  2885.9 140.9 reduce-scatter.16
  3033.5 149.0 reduce-scatter.20
  3189.4 149.0 reduce-scatter.14
where the time goes:
time: 3350 us
  blocking collectives  1540 us (46%)
  waiting for transfers between devices  1310 us (39%)
  matrix products  209 us (6%)
  other arithmetic  143 us (4%)
  local copies, waits for them, and re-layouts  96.1 us (3%)
    unnamed x20, waiting for transfers between devices  527 us
    psum x2, blocking collectives, return_rows(): summed = lax.psum(partial_value, 'tensor').astype(jnp.bfloat16)  435 us
    psum x1, blocking collectives, local(): lax.psum((jnp.sum(grad_output * difference), jnp.sum(valid_rows)), ('fsdp...  331 us
    all_gather x1, blocking collectives, local(): lax.all_gather(w_router, ('fsdp', 'context'), axis=0, tiled=True)  212 us
    unnamed x1, blocking collectives  173 us
    all_gather x1, blocking collectives, local(): lax.all_gather(value_weight, ('fsdp', 'context'), axis=0, tiled=True)  167 us
    all_gather x1, blocking collectives, local(): lax.all_gather(key_weight, ('fsdp', 'context'), axis=0, tiled=True)  165 us
    reduce_scatter x1, waiting for transfers between devices, local(): lax.psum_scatter(grad_query_full, ('fsdp', 'context'), scatter_dimension=...  156 us
  transfers between devices with their start and end apart: 22, of which 13 were waited for; matrix products, arithmetic and copies ran while one was open for 6% of the time, Pallas kernels for 0%

commit v1 on v0

v1 whole, which is shorter than its diff:
```python
import jax
import jax.numpy as jnp
from jax import lax
from jax.sharding import Mesh
from jax.sharding import PartitionSpec as P

QUERY_HEAD_COUNT = 24
KEY_VALUE_HEADS = 8
HEAD_WIDTH = 64
TOP = 2
EXPERTS = 16
CAPACITY = 96

EPSILON = 1e-06
MASKED = -1e30

BF = jnp.bfloat16
F32 = jnp.float32
RING = ("h", "x", "y")


def dot(left, right, left_dim, right_dim):
    return lax.dot_general(
        left, right, (((left_dim,), (right_dim,)), ((), ())), preferred_element_type=F32
    )


def rms_scale(values):
    return lax.rsqrt(jnp.mean(values * values, axis=-1, keepdims=True) + EPSILON)


def norm_back(values, scale, gain_row, upstream):
    gained = upstream * gain_row
    grad_gain = jnp.sum(upstream * values * scale, axis=0, keepdims=True)
    middle = jnp.mean(values * gained, axis=-1, keepdims=True)
    return (scale * gained - values * scale * scale * scale * middle, grad_gain)


def swap(value, axis):
    return lax.ppermute(value, axis, [(0, 1), (1, 0)])


def tensor_sum(partial):
    mine = partial.astype(BF)
    other = swap(mine, "t")
    return mine.astype(F32) + other.astype(F32)


def gather_rows(shard):
    rows, cols = shard.shape
    mine = lax.all_to_all(
        jnp.broadcast_to(shard[None], (32, rows, cols)), RING, 0, 0, tiled=True
    ).reshape(8, 4 * rows, cols)
    other = swap(mine, "c")
    first = lax.axis_index("c") == 0
    both = jnp.stack([jnp.where(first, mine, other), jnp.where(first, other, mine)], axis=1)
    return both.reshape(64 * rows, cols)


def scatter_sum(partial):
    total_rows, cols = partial.shape
    rows = total_rows // 64
    parts = partial.reshape(8, 2, 4 * rows, cols)
    core = lax.axis_index("c")
    mine = lax.dynamic_index_in_dim(parts, core, 1, keepdims=False)
    theirs = lax.dynamic_index_in_dim(parts, 1 - core, 1, keepdims=False)
    paired = (mine.astype(F32) + swap(theirs, "c").astype(F32)).astype(BF)
    moved = lax.all_to_all(paired.reshape(32, rows, cols), RING, 0, 0, tiled=True)
    return jnp.sum(moved.astype(F32), axis=0)


def exchange_slots(rows):
    width = rows.shape[1]
    return lax.all_to_all(
        rows.reshape(EXPERTS, -1, width), ("h", "x", "c"), 0, 0, tiled=True
    ).reshape(-1, width)


def split_bf16(value):
    high = value.astype(BF)
    return high, (value - high.astype(F32)).astype(BF)


def local(
    tokens,
    teacher,
    segments,
    routes,
    route_weight,
    norm_attn,
    w_query,
    key_weight,
    value_weight,
    w_out,
    norm_ffn,
    w_router,
    w_gate,
    w_up,
    w_down,
):
    tok_rows, feat_width = tokens.shape
    group = QUERY_HEAD_COUNT // KEY_VALUE_HEADS
    q_width = w_query.shape[1]
    k_width = key_weight.shape[1]
    tix = lax.axis_index("t")
    yix = lax.axis_index("y")

    rows24 = w_query.shape[0]
    small = jnp.concatenate(
        [
            w_router,
            norm_attn[:, None],
            norm_ffn[:, None],
            jnp.zeros((rows24, 128 - EXPERTS - 2), BF),
        ],
        axis=1,
    )
    pack_one = gather_rows(jnp.concatenate([w_query, key_weight, value_weight, small], axis=1))
    full_query = pack_one[:, :q_width]
    full_kv = pack_one[:, q_width : q_width + 2 * k_width]
    full_small = pack_one[:, q_width + 2 * k_width :]
    small_rows = dot(jnp.eye(24, 128, dtype=BF), full_small, 1, 1)
    router_rows = small_rows[:EXPERTS].astype(BF)
    gain_one = small_rows[EXPERTS : EXPERTS + 1]
    gain_two = small_rows[EXPERTS + 1 : EXPERTS + 2]
    wo_shard, pack_one = lax.optimization_barrier((w_out.T, pack_one))
    full_out = gather_rows(wo_shard)

    resid_in = tokens.astype(F32)
    scale_one = rms_scale(resid_in)
    act_one = (resid_in * scale_one * gain_one).astype(BF)
    kv_mine = dot(act_one, full_kv, 1, 0).astype(BF)
    query_rows = dot(act_one, full_query, 1, 0).astype(BF)
    kv_all = lax.all_to_all(
        jnp.broadcast_to(kv_mine[None], (4,) + kv_mine.shape), "y", 0, 0, tiled=True
    ).reshape(4 * tok_rows, 2 * k_width)

    experts = jnp.stack([w_gate[0], w_up[0], w_down[0].T])
    experts_other = swap(experts, "t")
    experts_full = jnp.concatenate(
        [
            jnp.where(tix == 0, experts, experts_other),
            jnp.where(tix == 0, experts_other, experts),
        ],
        axis=2,
    )
    experts_full, kv_all = lax.optimization_barrier((experts_full, kv_all))
    gate_full = lax.all_gather(experts_full[0], "y", axis=0, tiled=True)
    up_full = lax.all_gather(experts_full[1], "y", axis=0, tiled=True)
    down_full = lax.all_gather(experts_full[2], "y", axis=0, tiled=True)

    seq_len = kv_all.shape[0]
    kv_heads = k_width // HEAD_WIDTH
    head_scale = HEAD_WIDTH ** (-0.5)
    first_row = yix * tok_rows
    seg_all = segments[0]
    seg_mine = lax.dynamic_slice_in_dim(seg_all, first_row, tok_rows)
    query_pos = first_row + jnp.arange(tok_rows, dtype=jnp.int32)
    key_pos = jnp.arange(seq_len, dtype=jnp.int32)
    allowed = (seg_mine[:, None] == seg_all[None, :]) & (key_pos[None, :] <= query_pos[:, None])
    query_heads = query_rows.reshape(tok_rows, kv_heads, group, HEAD_WIDTH).transpose(1, 0, 2, 3)
    key_heads = kv_all[:, :k_width].reshape(seq_len, kv_heads, HEAD_WIDTH).transpose(1, 0, 2)
    value_heads = kv_all[:, k_width:].reshape(seq_len, kv_heads, HEAD_WIDTH).transpose(1, 0, 2)

    def score_block(query_one, key_one):
        raw_scores = (
            jnp.einsum("tgd,sd->gts", query_one, key_one, preferred_element_type=F32) * head_scale
        )
        return jnp.where(allowed[None], raw_scores, MASKED)

    def head_forward(pieces):
        query_one, key_one, value_one = pieces
        scores = score_block(query_one, key_one)
        row_max = jnp.max(scores, axis=-1, keepdims=True)
        exp_scores = jnp.exp(scores - row_max)
        row_total = jnp.sum(exp_scores, axis=-1, keepdims=True)
        weights = (exp_scores / row_total).astype(BF)
        mixed_one = jnp.einsum("gts,sd->tgd", weights, value_one, preferred_element_type=F32)
        return (mixed_one.astype(BF), row_max + jnp.log(row_total))

    mixed_stack, log_total = lax.map(head_forward, (query_heads, key_heads, value_heads))
    mixed = mixed_stack.transpose(1, 0, 2, 3).reshape(tok_rows, -1)
    hidden = resid_in + tensor_sum(dot(mixed, full_out, 1, 1))
    scale_two = rms_scale(hidden)
    act_two = (hidden * scale_two * gain_two).astype(BF)

    logits = dot(router_rows, act_two, 1, 1)
    router = jax.nn.softmax(logits, axis=0)
    route_cols = routes.T
    weight_cols = route_weight.T
    expert_iota = lax.broadcasted_iota(jnp.int32, (EXPERTS, tok_rows), 0)
    named = [expert_iota == route_cols[k : k + 1] for k in range(TOP)]
    taken = (named[0] | named[1]).astype(BF)
    earlier = (
        lax.broadcasted_iota(jnp.int32, (tok_rows, tok_rows), 0)
        < lax.broadcasted_iota(jnp.int32, (tok_rows, tok_rows), 1)
    ).astype(BF)
    count_before = dot(taken, earlier, 1, 0)
    half = CAPACITY // 2
    slot_iota = lax.broadcasted_iota(jnp.int32, (EXPERTS * half, tok_rows), 0)
    picks = []
    gates = []
    for k in range(TOP):
        place = jnp.sum(jnp.where(named[k], count_before, 0.0), axis=0, keepdims=True)
        place = place.astype(jnp.int32) - tix * half
        slot = jnp.where((place >= 0) & (place < half), route_cols[k : k + 1] * half + place, -1)
        picks.append(slot_iota == slot)
        chosen = jnp.sum(jnp.where(named[k], router, 0.0), axis=0, keepdims=True)
        gates.append(chosen * weight_cols[k : k + 1])
    pick = (picks[0] | picks[1]).astype(BF)
    gated_pick = (
        jnp.where(picks[0], gates[0], 0.0) + jnp.where(picks[1], gates[1], 0.0)
    ).astype(BF)

    received = exchange_slots(dot(pick, act_two, 1, 0).astype(BF))
    gate_proj = dot(received, gate_full, 1, 0)
    up_proj = dot(received, up_full, 1, 0)
    inner = (jax.nn.silu(gate_proj) * up_proj).astype(BF)
    returned = exchange_slots(dot(inner, down_full, 1, 1).astype(BF))
    output = hidden + tensor_sum(dot(gated_pick, returned, 0, 0))

    valid = (seg_mine != 0).astype(F32)
    difference = output - teacher.astype(F32)
    grad_output = difference * valid[:, None]
    sse = jnp.sum(grad_output * difference)
    count = jnp.sum(valid)

    grad_output_low = grad_output.astype(BF)
    d_received = exchange_slots(dot(gated_pick, grad_output_low, 1, 0).astype(BF))
    slot_dots = dot(returned, grad_output_low, 1, 1)
    d_gates = jnp.concatenate(
        [jnp.sum(jnp.where(picks[k], slot_dots, 0.0), axis=0, keepdims=True) for k in range(TOP)]
    )
    d_gates = d_gates + swap(d_gates, "t")
    d_inner = dot(d_received, down_full, 1, 0)
    sig_gate = jax.nn.sigmoid(gate_proj)
    d_gate_proj = (d_inner * up_proj * sig_gate * (1.0 + gate_proj * (1.0 - sig_gate))).astype(BF)
    d_up_proj = (d_inner * gate_proj * sig_gate).astype(BF)
    d_slots = dot(d_gate_proj, gate_full, 1, 1) + dot(d_up_proj, up_full, 1, 1)
    d_returned = exchange_slots(d_slots.astype(BF))

    grad_experts = [
        lax.psum_scatter(part, "y", scatter_dimension=0, tiled=True)
        for part in (
            dot(received, d_gate_proj, 0, 0).astype(BF),
            dot(received, d_up_proj, 0, 0).astype(BF),
            dot(d_received, inner, 0, 0).astype(BF),
        )
    ]
    grad_stack = jnp.stack(grad_experts)
    ff_half = grad_stack.shape[2] // 2
    keep = jnp.where(tix == 0, grad_stack[:, :, :ff_half], grad_stack[:, :, ff_half:])
    give = jnp.where(tix == 0, grad_stack[:, :, ff_half:], grad_stack[:, :, :ff_half])
    grad_stack = keep.astype(F32) + swap(give, "t").astype(F32)

    d_router = jnp.where(named[0], d_gates[0:1] * weight_cols[0:1], 0.0) + jnp.where(
        named[1], d_gates[1:2] * weight_cols[1:2], 0.0
    )
    d_logits = (
        router * (d_router - jnp.sum(router * d_router, axis=0, keepdims=True))
    ).astype(BF)
    grad_router = dot(act_two, d_logits, 0, 1)
    d_act_two = tensor_sum(dot(pick, d_returned, 0, 0)) + dot(d_logits, router_rows, 0, 0)
    d_norm_two, grad_gain_two = norm_back(hidden, scale_two, gain_two, d_act_two)
    d_hidden = grad_output + d_norm_two
    d_attn = d_hidden.astype(BF)
    d_mixed = dot(d_attn, full_out, 1, 0).astype(BF)
    grad_out = dot(d_attn, mixed, 0, 0)

    sse_high, sse_low = split_bf16(jnp.full((1, feat_width), sse))
    count_high, count_low = split_bf16(jnp.full((1, feat_width), count))
    gain_high, gain_low = split_bf16(grad_gain_two)
    lines = jnp.concatenate(
        [gain_high, gain_low, sse_high, sse_low, count_high, count_low, jnp.zeros((2, feat_width), BF)]
    )
    extra = dot(lines, jnp.eye(8, 128 - EXPERTS, dtype=BF), 0, 0)
    summed_one = scatter_sum(jnp.concatenate([grad_out, grad_router, extra], axis=1).astype(BF))
    at = feat_width // 2
    own_out = summed_one[:, :at].T
    own_router = summed_one[:, at : at + EXPERTS]
    at = at + EXPERTS
    own_gain_two = summed_one[:, at] + summed_one[:, at + 1]
    loss_value = (summed_one[0, at + 2] + summed_one[0, at + 3]) / (
        feat_width * (summed_one[0, at + 4] + summed_one[0, at + 5])
    )

    d_heads = d_mixed.reshape(tok_rows, kv_heads, group, HEAD_WIDTH).transpose(1, 0, 2, 3)

    def head_backward(pieces):
        query_one, key_one, value_one, d_one, total_one = pieces
        scores = score_block(query_one, key_one)
        weights = jnp.exp(scores - total_one)
        d_weights = jnp.einsum("tgd,sd->gts", d_one, value_one, preferred_element_type=F32)
        row_dot = jnp.sum(weights * d_weights, axis=-1, keepdims=True)
        d_scores = (weights * (d_weights - row_dot)).astype(BF)
        d_query_one = (
            jnp.einsum("gts,sd->tgd", d_scores, key_one, preferred_element_type=F32) * head_scale
        ).astype(BF)
        d_key_one = (
            jnp.einsum("gts,tgd->sd", d_scores, query_one, preferred_element_type=F32) * head_scale
        )
        d_value_one = jnp.einsum(
            "gts,tgd->sd", weights.astype(BF), d_one, preferred_element_type=F32
        )
        return (d_query_one, d_key_one.astype(BF), d_value_one.astype(BF))

    d_query_stack, d_key_stack, d_value_stack = lax.map(
        head_backward, (query_heads, key_heads, value_heads, d_heads, log_total)
    )
    d_query = d_query_stack.transpose(1, 0, 2, 3).reshape(tok_rows, -1)
    d_kv = jnp.concatenate(
        [
            d_key_stack.transpose(1, 0, 2).reshape(seq_len, -1),
            d_value_stack.transpose(1, 0, 2).reshape(seq_len, -1),
        ],
        axis=1,
    )
    d_kv_parts = lax.all_to_all(d_kv.reshape(4, tok_rows, -1), "y", 0, 0, tiled=True)
    d_kv_mine = jnp.sum(d_kv_parts.astype(F32), axis=0).astype(BF)
    own_query = scatter_sum(dot(act_one, d_query, 0, 0).astype(BF))

    d_act_one = tensor_sum(dot(d_query, full_query, 1, 1) + dot(d_kv_mine, full_kv, 1, 1))
    d_norm_one, grad_gain_one = norm_back(resid_in, scale_one, gain_one, d_act_one)
    grad_tokens = d_hidden + d_norm_one
    gain_high, gain_low = split_bf16(grad_gain_one)
    lines = jnp.concatenate([gain_high, gain_low, jnp.zeros((6, feat_width), BF)])
    extra = dot(lines, jnp.eye(8, 128, dtype=BF), 0, 0)
    own_kv = scatter_sum(
        jnp.concatenate([dot(act_one, d_kv_mine, 0, 0), extra], axis=1).astype(BF)
    )
    own_gain_one = own_kv[:, 2 * k_width] + own_kv[:, 2 * k_width + 1]
    return (
        output,
        loss_value,
        grad_tokens,
        own_gain_one,
        own_query,
        own_kv[:, :k_width],
        own_kv[:, k_width : 2 * k_width],
        own_out,
        own_gain_two,
        own_router,
        grad_stack[0][None],
        grad_stack[1][None],
        grad_stack[2].T[None],
    )


def solution(mesh):
    fine = Mesh(mesh.devices.reshape(2, 4, 2, 4, 2), ("h", "x", "c", "y", "t"))
    fsdp = ("h", "x", "c")
    every = ("h", "x", "c", "y")
    return jax.shard_map(
        local,
        mesh=fine,
        in_specs=(
            P(every, None),
            P(every, None),
            P(fsdp, None),
            P(every, None),
            P(every, None),
            P(every),
            P(every, "t"),
            P(every, "t"),
            P(every, "t"),
            P("t", every),
            P(every),
            P(every, None),
            P(fsdp, "y", "t"),
            P(fsdp, "y", "t"),
            P(fsdp, "t", "y"),
        ),
        out_specs=(
            P(every, None),
            P(),
            P(every, None),
            P(every),
            P(every, "t"),
            P(every, "t"),
            P(every, "t"),
            P("t", every),
            P(every),
            P(every, None),
            P(fsdp, "y", "t"),
            P(fsdp, "y", "t"),
            P(fsdp, "t", "y"),
        ),
        check_vma=False,
    )
```

time: 3350 us -> 838 us (0.25)
  blocking collectives: 1540 us -> 118 us
  waiting for transfers between devices: 1310 us -> 272 us
  local copies, waits for them, and re-layouts: 96.1 us -> 52.9 us
  other arithmetic: 143 us -> 103 us
    psum x3 -> x0, blocking collectives: 766 us -> none  [the longest x2 435 us: return_rows(): summed = lax.psum(partial_value, 'tensor').astype(jnp.bfloat16)]
    all_gather x3 -> x0, blocking collectives: 543 us -> none  [the longest x1 212 us: local(): lax.all_gather(w_router, ('fsdp', 'context'), axis=0, tiled=True)]
    unnamed x20 -> x6, waiting for transfers between devices: 527 us -> 0.1 us
    reduce_scatter x9 -> x3, waiting for transfers between devices: 442 us -> 0.02 us  [local(): lax.psum_scatter(part, 'y', scatter_dimension=0, tiled=True)]
    unnamed x1 -> x0, blocking collectives: 173 us -> none
    ppermute x0 -> x12, waiting for transfers between devices: none -> 164 us  [swap(): return lax.ppermute(value, axis, [(0, 1), (1, 0)])]
    psum x2 -> x0, waiting for transfers between devices: 142 us -> none  [the longest x1 82.9 us: local(): attn_out = lax.psum(matmul(heads_mixed_output, full_out), 'tensor')]
    all_gather x7 -> x3, waiting for transfers between devices: 90.2 us -> 0.01 us  [the longest x1 0.01 us: local(): gate_full = lax.all_gather(experts_full[0], 'y', axis=0, tiled=True)]
  transfers between devices with their start and end apart: 22 -> 26, of which waited for: 13 -> 13; matrix products, arithmetic and copies ran while one was open for 6% -> 39% of each run, Pallas kernels for 0% -> 0%
where the time goes in v1:
time: 838 us; the launch traced here: 828 us
  waiting for transfers between devices  272 us (32%)
  matrix products  208 us (25%)
  blocking collectives  118 us (14%)
  other arithmetic  103 us (12%)
  local copies, waits for them, and re-layouts  52.9 us (6%)
  starting transfers between devices  52.6 us (6%)
  between operations  21.7 us (3%)
    ppermute x12, waiting for transfers between devices, swap(): return lax.ppermute(value, axis, [(0, 1), (1, 0)])  164 us
    dot_general x30, matrix products, dot(): lax.dot_general(left, right, (((left_dim,), (right_dim,)), ((), ())), pre...  96.4 us
    all_to_all x2, blocking collectives, exchange_slots(): lax.all_to_all(rows.reshape(EXPERTS, -1, width), ('h', 'x', 'c'), 0, 0, t...  76.3 us
    all_to_all x2, waiting for transfers between devices, exchange_slots(): lax.all_to_all(rows.reshape(EXPERTS, -1, width), ('h', 'x', 'c'), 0, 0, t...  60.1 us
    all_to_all x1, blocking collectives, gather_rows(): lax.all_to_all(jnp.broadcast_to(shard[None], (32, rows, cols)), RING, 0,...  42 us
    dot_general x4, matrix products, head_backward(): jnp.einsum('tgd,sd->gts', d_one, value_one, preferred_element_type=F32)  30.9 us
    convert_element_type x4, other arithmetic, head_backward(): d_scores = (weights * (d_weights - row_dot)).astype(BF)  27.7 us
    dot_general x8, matrix products, score_block(): jnp.einsum('tgd,sd->gts', query_one, key_one, preferred_element_type=F32)  22.8 us
  transfers between devices with their start and end apart: 26, of which 13 were waited for; matrix products, arithmetic and copies ran while one was open for 39% of the time, Pallas kernels for 0%

profile of v1, /device:TPU:0, one launch (start us, length us, event | category | flops | bytes accessed | tf_op | source)
XLA Modules:
  0.0 828.5 jit_solution(13245240734715955056)
XLA Ops:
  10.5 42.0 %all_to_all.55 = bf16[32,24,1408]{2,1,0:T(8,128)(2,1)} all-to-all(bf16[32,24,1408]{2,1,0:T(8,128)(2,1)S(1)} %broadcast_in_dim.178), channel_id=1, replica_groups=mesh['h'=2,'x'=4,'c'=2,'y'=4,'t'=2] {'h','x','y'}, dimensions={0} | all-to-all | bytes 4325376 | tf_op jit(solution)/shard_map/all_to_all | solution.py:51
  66.9 4.5 all-to-all-start.1
  71.4 11.2 %collective-permute-done = bf16[3,384,512]{2,1,0:T(8,128)(2,1)} collective-permute-done((bf16[3,384,512]{2,1,0:T(8,128)(2,1)}, bf16[3,384,512]{2,1,0:T(8,128)(2,1)}, u32[]{:S(2)}, u32[]{:S(2)}) %collective-permute-start) | collective-permute-done | bytes 1179680 | tf_op jit(solution)/shard_map/ppermute | solution.py:40
  85.8 12.5 %all-to-all-done.1 = bf16[4,512,512]{1,2,0:T(8,128)(2,1)} async-done(((bf16[4,512,512]{1,2,0:T(8,128)(2,1)}), bf16[4,512,512]{1,2,0:T(8,128)(2,1)}, u32[]{:S(2)}, u32[]{:S(2)}) %all-to-all-start.1) | async-done | bytes 2097184 | tf_op jit(solution)/shard_map/all_to_all | solution.py:134
  98.3 4.1 copy.124
  106.7 4.7 all-to-all-start.2
  115.8 14.7 %all-to-all-done.2 = bf16[32,24,768]{2,1,0:T(8,128)(2,1)} async-done(((bf16[32,24,768]{2,1,0:T(8,128)(2,1)}), bf16[32,24,768]{2,1,0:T(8,128)(2,1)}, u32[]{:S(2)}, u32[]{:S(2)}) %all-to-all-start.2) | async-done | bytes 1179680 | tf_op jit(solution)/shard_map/all_to_all | solution.py:51
  136.3 57.5 %while.28 = (s32[]{:T(128)}, bf16[4,512,3,64]{1,3,2,0:T(8,128)(2,1)}, f32[4,3,512,1]{2,1,3,0:T(4,128)S(1)}, bf16[4,2048,64]{1,2,0:T(8,128)(2,1)}, bf16[4,2048,64...) while((s32[]{:T(128)}, ...), condition=%wide.region_4.5_spmd.clone, body=%wide.region_1.4_spmd.clone.sunk | while | flops 846297600 | bytes 47124620 | solution.py:181
  137.3 3.9 fusion.216
  141.2 3.9 fusion.217
  145.0 5.7 fusion.218
  151.7 3.9 fusion.216
  155.6 3.8 fusion.217
  159.4 5.6 fusion.218
  166.0 3.9 fusion.216
  169.9 3.8 fusion.217
  173.8 5.6 fusion.218
  180.4 3.9 fusion.216
  184.3 3.9 fusion.217
  188.1 5.6 fusion.218
  199.4 35.8 %collective-permute-done.3 = bf16[512,1536]{1,0:T(8,128)(2,1)} collective-permute-done((bf16[512,1536]{1,0:T(8,128)(2,1)S(1)}, bf16[512,1536]{1,0:T(8,128)(2,1)}, u32[]{:S(2)}, u32[]{:S(2)}) %collective-permute-start.3) | collective-permute-done | bytes 1572896 | tf_op jit(solution)/shard_map/ppermute | solution.py:40
  241.5 38.8 %all_to_all.56 = bf16[16,48,1536]{2,1,0:T(8,128)(2,1)} all-to-all(bf16[16,48,1536]{2,1,0:T(8,128)(2,1)S(1)} %bitcast.392), channel_id=1, replica_groups=mesh['h'=2,'x'=4,'c'=2,'y'=4,'t'=2] {'h','x','c'}, dimensions={0} | all-to-all | bytes 4718592 | tf_op jit(solution)/shard_map/all_to_all | solution.py:74
  280.3 6.9 fusion.94
  287.2 8.4 %multiply_convert_fusion.3 = (bf16[768,1024]{1,0:T(8,128)(2,1)}, f32[768,1024]{1,0:T(8,128)}) fusion(f32[768,1024]{1,0:T(8,128)} %fusion.94, bf16[768,1536]{1,0:T(8,128)(2,1)} %bitcast.382, bf16[1,1536,1024]{2,1,0:T(8,128)(2,1)} %all-gather.9.cloned.1.call-done), kind=kOutput, calls=%fused_computation.123 | convolution fusion | flops 2420637696 | bytes 13369344 | tf_op jit(solution)/shard_map/dot_general | solution.py:23
  295.5 6.4 convolution_convert_fusion.3
  302.0 4.6 all-to-all-start.4
  306.6 32.0 %all-to-all-done.4 = bf16[16,48,1536]{2,1,0:T(8,128)(2,1)} async-done(((bf16[16,48,1536]{2,1,0:T(8,128)(2,1)}), bf16[16,48,1536]{2,1,0:T(8,128)(2,1)}, u32[]{:S(2)}, u32[]{:S(2)}) %all-to-all-start.4) | async-done | bytes 2359328 | tf_op jit(solution)/shard_map/all_to_all | solution.py:74
  343.0 35.0 %collective-permute-done.4 = bf16[512,1536]{1,0:T(8,128)(2,1)S(1)} collective-permute-done((bf16[512,1536]{1,0:T(8,128)(2,1)S(1)}, bf16[512,1536]{1,0:T(8,128)(2,1)S(1)}, u32[]{:S(2)}, u32[]{:S(2)}) %collective-permute-start.4) | collective-permute-done | bytes 1572896 | tf_op jit(solution)/shard_map/ppermute | solution.py:40
  383.0 37.5 %all_to_all.57 = bf16[16,48,1536]{2,1,0:T(8,128)(2,1)S(1)} all-to-all(bf16[16,48,1536]{2,1,0:T(8,128)(2,1)S(1)} %bitcast.391), channel_id=1, replica_groups=mesh['h'=2,'x'=4,'c'=2,'y'=4,'t'=2] {'h','x','c'}, dimensions={0} | all-to-all | bytes 4718592 | tf_op jit(solution)/shard_map/all_to_all | solution.py:74
  421.9 4.1 convolution_convert_fusion
  426.3 9.6 %multiply_convert_fusion.1 = (bf16[768,1024]{1,0:T(8,128)(2,1)}, bf16[768,1024]{1,0:T(8,128)(2,1)S(1)}) fusion(f32[768,1024]{1,0:T(8,128)} %fusion.94, f32[768,1024]{1,0:T(8,128)} %get-tuple-element.334, bf16[768,1536]{1,0:T(8,128)(2,1)} %bitcast.388, bf16[1,1536,1024]{2,1,0:T(8,128)(2,1)} %all-gather.11.cloned.1.call-done), kind=kOutput, calls=%fused_computation.119 | convolution fusion | flops 2426142720 | bytes 14942208 | tf_op jit(solution)/shard_map/dot_general | solution.py:23
  437.1 4.0 convolution_convert_fusion.2
  441.2 5.2 fusion.92
  446.4 3.9 add_convert_fusion
  450.3 4.5 all-to-all-start.6
  454.8 3.8 select_reduce_fusion.1
  458.7 28.2 %all-to-all-done.6 = bf16[16,48,1536]{2,1,0:T(8,128)(2,1)} async-done(((bf16[16,48,1536]{2,1,0:T(8,128)(2,1)}), bf16[16,48,1536]{2,1,0:T(8,128)(2,1)}, u32[]{:S(2)}, u32[]{:S(2)}) %all-to-all-start.6) | async-done | bytes 2359328 | tf_op jit(solution)/shard_map/all_to_all | solution.py:74
  486.8 4.3 convolution_convert_fusion.7
  496.5 31.1 %collective-permute-done.6 = f32[2,512]{1,0:T(2,128)S(1)} collective-permute-done((f32[2,512]{1,0:T(2,128)S(1)}, f32[2,512]{1,0:T(2,128)S(1)}, u32[]{:S(2)}, u32[]{:S(2)}) %collective-permute-start.6) | collective-permute-done | bytes 4128 | tf_op jit(solution)/shard_map/ppermute | solution.py:40
  530.3 6.4 convolution_convert_fusion.1
  536.8 3.3 multiply_reduce_fusion.1
  550.7 104.9 %while.29 = (s32[]{:T(128)}, bf16[4,512,3,64]{1,3,2,0:T(8,128)(2,1)}, bf16[4,2048,64]{1,2,0:T(8,128)(2,1)}, bf16[4,2048,64]{1,2,0:T(8,128)(2,1)}, bf16[4,2048,64...) while((s32[]{:T(128)}, ...), condition=%wide.region_22.23_spmd.clone, body=%wide.region_20.22_spmd.clone.sunk | while | flops 2064185856 | bytes 100924552 | solution.py:307
  553.5 4.2 fusion.233
  557.8 7.7 fusion.229
  565.5 7.0 fusion.230
  579.8 4.2 fusion.233
  584.0 7.7 fusion.229
  591.7 6.9 fusion.230
  606.0 4.2 fusion.233
  610.2 7.7 fusion.229
  617.9 6.9 fusion.230
  632.2 4.2 fusion.233
  636.4 7.7 fusion.229
  644.1 6.9 fusion.230
  661.7 4.6 all-to-all-start.8
  680.6 11.5 %all-to-all-done.8 = bf16[4,512,512]{1,2,0:T(8,128)(2,1)} async-done(((bf16[4,512,512]{1,2,0:T(8,128)(2,1)}), bf16[4,512,512]{1,2,0:T(8,128)(2,1)}, u32[]{:S(2)}, u32[]{:S(2)}) %all-to-all-start.8) | async-done | bytes 2097184 | tf_op jit(solution)/shard_map/all_to_all | solution.py:318
  695.0 3.6 fusion.96
  702.2 8.8 %all-to-all-start.10 = ((bf16[32,24,768]{2,1,0:T(8,128)(2,1)}), bf16[32,24,768]{2,1,0:T(8,128)(2,1)}, u32[]{:S(2)}, u32[]{:S(2)}) async-start(bf16[32,24,768]{2,1,0:T(8,128)(2,1)} %bitcast.372), calls=%async_computation.10 | async-start | bytes 2359296 | tf_op jit(solution)/shard_map/all_to_all | solution.py:68
  714.2 31.1 %collective-permute-done.8 = bf16[512,1536]{1,0:T(8,128)(2,1)} collective-permute-done((bf16[512,1536]{1,0:T(8,128)(2,1)S(1)}, bf16[512,1536]{1,0:T(8,128)(2,1)}, u32[]{:S(2)}, u32[]{:S(2)}) %collective-permute-start.8) | collective-permute-done | bytes 1572896 | tf_op jit(solution)/shard_map/ppermute | solution.py:40
  747.9 5.0 fusion.153
  754.7 8.8 %all-to-all-start.7 = ((bf16[32,24,896]{2,1,0:T(8,128)(2,1)}), bf16[32,24,896]{2,1,0:T(8,128)(2,1)}, u32[]{:S(2)}, u32[]{:S(2)}) async-start(bf16[32,24,896]{2,1,0:T(8,128)(2,1)} %bitcast.62), calls=%async_computation.7 | async-start | bytes 2752512 | tf_op jit(solution)/shard_map/all_to_all | solution.py:68
  773.1 9.8 %all-to-all-done.7 = bf16[32,24,896]{2,1,0:T(8,128)(2,1)} async-done(((bf16[32,24,896]{2,1,0:T(8,128)(2,1)}), bf16[32,24,896]{2,1,0:T(8,128)(2,1)}, u32[]{:S(2)}, u32[]{:S(2)}) %all-to-all-start.7) | async-done | bytes 1376288 | tf_op jit(solution)/shard_map/all_to_all | solution.py:68
  790.9 4.9 all-to-all-start.9
  797.2 17.4 %collective-permute-done.11 = bf16[3,384,512]{2,1,0:T(8,128)(2,1)} collective-permute-done((bf16[3,384,512]{2,1,0:T(8,128)(2,1)}, bf16[3,384,512]{2,1,0:T(8,128)(2,1)}, u32[]{:S(2)}, u32[]{:S(2)}) %collective-permute-start.11) | collective-permute-done | bytes 1179680 | tf_op jit(solution)/shard_map/ppermute | solution.py:40
  (286 shorter events, 164.7 us)
Async XLA Ops:
  10.5 42.1 %copy-start.33 = (bf16[1,512,384]{2,1,0:T(8,128)(2,1)S(1)}, bf16[1,512,384]{2,1,0:T(8,128)(2,1)}, u32[]{:S(2)}) copy-start(bf16[1,512,384]{2,1,0:T(8,128)(2,1)} %param.33) | copy-start | bytes 1179652
  10.5 42.3 %copy-start.22 = (bf16[1,384,512]{2,1,0:T(8,128)(2,1)S(1)}, bf16[1,384,512]{2,1,0:T(8,128)(2,1)}, u32[]{:S(2)}) copy-start(bf16[1,384,512]{2,1,0:T(8,128)(2,1)} %param.32) | copy-start | bytes 1179652
  10.5 42.2 %copy-start.23 = (bf16[1,384,512]{2,1,0:T(8,128)(2,1)S(1)}, bf16[1,384,512]{2,1,0:T(8,128)(2,1)}, u32[]{:S(2)}) copy-start(bf16[1,384,512]{2,1,0:T(8,128)(2,1)} %param.31) | copy-start | bytes 1179652
  52.5 2.4 copy-start.3
  52.5 4.6 collective-permute-start.1
  53.9 28.7 %collective-permute-start = (bf16[3,384,512]{2,1,0:T(8,128)(2,1)}, bf16[3,384,512]{2,1,0:T(8,128)(2,1)}, u32[]{:S(2)}, u32[]{:S(2)}) collective-permute-start(bf16[3,384,512]{2,1,0:T(8,128)(2,1)} %pad_maximum_fusion.6), channel_id=1, source_target_pairs={{0,1},{1,0},{2,3},{3,2},{4,5},{5,4},{6,7},{7,6},{8,9},{9,8},{10,11... | collective-permute-start | bytes 3538952 | tf_op jit(solution)/shard_map/ppermute | solution.py:40
  55.3 56.1 %copy-start.40 = (f32[512]{0:T(512)}, f32[512]{0:T(512)S(1)}, u32[]{:S(2)}) copy-start(f32[512]{0:T(512)S(1)} %add_rsqrt_fusion.1) | copy-start | bytes 6148
  60.2 2.0 copy-start.13
  61.3 50.2 %copy-start.35 = (f32[1536]{0:T(1024)}, f32[1536]{0:T(1024)S(1)}, u32[]{:S(2)}) copy-start(f32[1536]{0:T(1024)S(1)} %get-tuple-element.240) | copy-start | bytes 18436
  66.9 31.4 %all-to-all-start.1 = ((bf16[4,512,512]{1,2,0:T(8,128)(2,1)}), bf16[4,512,512]{1,2,0:T(8,128)(2,1)}, u32[]{:S(2)}, u32[]{:S(2)}) async-start(bf16[4,512,512]{1,2,0:T(8,128)(2,1)} %broadcast_in_dim.179), calls=%async_computation.1 | async-start | bytes 4194304 | tf_op jit(solution)/shard_map/all_to_all | solution.py:134
  71.3 209.0 %all-gather.7.cloned.1.call-start = ((), (), s32[]{:S(2)}) async-start(), calls=%async_computation.17 | async-start | bytes 3932160 | tf_op jit(solution)/shard_map/all_gather | solution.py:148
  102.4 3.1 copy-start.37
  105.5 5.9 copy-start.30
  106.7 23.9 %all-to-all-start.2 = ((bf16[32,24,768]{2,1,0:T(8,128)(2,1)}), bf16[32,24,768]{2,1,0:T(8,128)(2,1)}, u32[]{:S(2)}, u32[]{:S(2)}) async-start(bf16[32,24,768]{2,1,0:T(8,128)(2,1)} %broadcast_in_dim.180), calls=%async_computation.2 | async-start | bytes 2359296 | tf_op jit(solution)/shard_map/all_to_all | solution.py:51
  111.3 175.8 %all-gather.9.cloned.1.call-start = ((), (), s32[]{:S(2)}) async-start(), calls=%async_computation.18 | async-start | bytes 3932160 | tf_op jit(solution)/shard_map/all_gather | solution.py:149
  130.6 63.2 %collective-permute-start.2 = (bf16[8,96,768]{2,1,0:T(8,128)(2,1)}, bf16[8,96,768]{2,1,0:T(8,128)(2,1)}, u32[]{:S(2)}, u32[]{:S(2)}) collective-permute-start(bf16[8,96,768]{2,1,0:T(8,128)(2,1)} %bitcast.22), channel_id=1, source_target_pairs={{0,8},{8,0},{1,9},{9,1},{2,10},{10,2},{3,11},{11,3},{4,12},{12,4},... | collective-permute-start | bytes 3538952 | tf_op jit(solution)/shard_map/ppermute | solution.py:40
  135.1 160.4 %all-gather.11.cloned.1.call-start = ((), (), s32[]{:S(2)}) async-start(), calls=%async_computation.19 | async-start | bytes 3932160 | tf_op jit(solution)/shard_map/all_gather | solution.py:150
  137.3 3.9 copy-start
  151.7 3.9 copy-start
  166.0 3.9 copy-start
  180.4 3.9 copy-start
  195.8 2.3 copy-start.16
  196.7 2.6 copy-start.43
  198.2 37.0 %collective-permute-start.3 = (bf16[512,1536]{1,0:T(8,128)(2,1)S(1)}, bf16[512,1536]{1,0:T(8,128)(2,1)}, u32[]{:S(2)}, u32[]{:S(2)}) collective-permute-start(bf16[512,1536]{1,0:T(8,128)(2,1)S(1)} %convolution_convert_fusion.9), channel_id=1, source_target_pairs={{0,1},{1,0},{2,3},{3,2},{4,5},{5,4},{6,7},{7,6},{8,9},{9,8},{10,11... | collective-permute-start | bytes 4718600 | tf_op jit(solution)/shard_map/ppermute | solution.py:40
  199.4 39.0 %copy-start.34 = (f32[1536]{0:T(1024)S(1)}, f32[1536]{0:T(1024)}, u32[]{:S(2)}) copy-start(f32[1536]{0:T(1024)} %get-tuple-element.239) | copy-start | bytes 18436
  239.3 2.2 copy-start.7
  302.0 4.6 copy-start.42
  302.0 36.6 %all-to-all-start.4 = ((bf16[16,48,1536]{2,1,0:T(8,128)(2,1)}), bf16[16,48,1536]{2,1,0:T(8,128)(2,1)}, u32[]{:S(2)}, u32[]{:S(2)}) async-start(bf16[16,48,1536]{2,1,0:T(8,128)(2,1)} %bitcast.390), calls=%async_computation.4 | async-start | bytes 4718592 | tf_op jit(solution)/shard_map/all_to_all | solution.py:74
  306.5 460.6 %reduce-scatter.8.cloned.1.call-start = ((), (), s32[]{:S(2)}) async-start(), calls=%async_computation.16 | async-start | bytes 3932160 | tf_op jit(solution)/shard_map/reduce_scatter | solution.py:243
  338.6 39.4 %copy-start.5 = (bf16[512,1536]{1,0:T(8,128)(2,1)S(1)}, bf16[512,1536]{1,0:T(8,128)(2,1)}, u32[]{:S(2)}) copy-start(bf16[512,1536]{1,0:T(8,128)(2,1)} %param.20) | copy-start | bytes 4718596
  341.8 36.2 %collective-permute-start.4 = (bf16[512,1536]{1,0:T(8,128)(2,1)S(1)}, bf16[512,1536]{1,0:T(8,128)(2,1)S(1)}, u32[]{:S(2)}, u32[]{:S(2)}) collective-permute-start(bf16[512,1536]{1,0:T(8,128)(2,1)S(1)} %convolution_convert_fusion.8), channel_id=1, source_target_pairs={{0,1},{1,0},{2,3},{3,2},{4,5},{5,4},{6,7},{7,6},{8,9},{9,8},{10,11... | collective-permute-start | bytes 4718600 | tf_op jit(solution)/shard_map/ppermute | solution.py:40
  383.0 38.9 %copy-start.47 = (bf16[768,1024]{1,0:T(8,128)(2,1)S(1)}, bf16[768,1024]{1,0:T(8,128)(2,1)}, u32[]{:S(2)}) copy-start(bf16[768,1024]{1,0:T(8,128)(2,1)} %get-tuple-element.333) | copy-start | bytes 4718596
  426.1 341.1 %reduce-scatter.4.cloned.1.call-start = ((), (), s32[]{:S(2)}) async-start(), calls=%async_computation.14 | async-start | bytes 3932160 | tf_op jit(solution)/shard_map/reduce_scatter | solution.py:243
  426.3 10.8 %copy-start.18 = (bf16[16,48,1536]{2,1,0:T(8,128)(2,1)S(1)}, bf16[16,48,1536]{2,1,0:T(8,128)(2,1)}, u32[]{:S(2)}) copy-start(bf16[16,48,1536]{2,1,0:T(8,128)(2,1)} %all_to_all.56) | copy-start | bytes 7077892
  441.2 5.2 copy-start.44
  441.2 5.2 copy-start.46
  450.3 36.5 %all-to-all-start.6 = ((bf16[16,48,1536]{2,1,0:T(8,128)(2,1)}), bf16[16,48,1536]{2,1,0:T(8,128)(2,1)}, u32[]{:S(2)}, u32[]{:S(2)}) async-start(bf16[16,48,1536]{2,1,0:T(8,128)(2,1)} %bitcast.389), calls=%async_computation.6 | async-start | bytes 4718592 | tf_op jit(solution)/shard_map/all_to_all | solution.py:74
  454.8 312.4 %reduce-scatter.6.cloned.1.call-start = ((), (), s32[]{:S(2)}) async-start(), calls=%async_computation.15 | async-start | bytes 3932160 | tf_op jit(solution)/shard_map/reduce_scatter | solution.py:243
  491.1 45.6 %collective-permute-start.5 = (bf16[512,1536]{1,0:T(8,128)(2,1)}, bf16[512,1536]{1,0:T(8,128)(2,1)}, u32[]{:S(2)}, u32[]{:S(2)}) collective-permute-start(bf16[512,1536]{1,0:T(8,128)(2,1)} %convolution_convert_fusion.7), channel_id=1, source_target_pairs={{0,1},{1,0},{2,3},{3,2},{4,5},{5,4},{6,7},{7,6},{8,9},{9,8},{10,11... | collective-permute-start | bytes 4718600 | tf_op jit(solution)/shard_map/ppermute | solution.py:40
  491.7 35.9 %collective-permute-start.6 = (f32[2,512]{1,0:T(2,128)S(1)}, f32[2,512]{1,0:T(2,128)S(1)}, u32[]{:S(2)}, u32[]{:S(2)}) collective-permute-start(f32[2,512]{1,0:T(2,128)S(1)} %pad_maximum_fusion.7), channel_id=1, source_target_pairs={{0,1},{1,0},{2,3},{3,2},{4,5},{5,4},{6,7},{7,6},{8,9},{9,8},{10,11... | collective-permute-start | bytes 12296 | tf_op jit(solution)/shard_map/ppermute | solution.py:40
  536.7 4.6 copy-start.2
  536.8 4.6 copy-start.6
  541.3 4.6 copy-start.17
  548.2 2.5 copy-start.8
  548.2 2.5 copy-start.12
  661.6 4.7 copy-start.38
  661.6 4.7 copy-start.39
  661.7 5.1 copy-start.14
  661.7 30.5 %all-to-all-start.8 = ((bf16[4,512,512]{1,2,0:T(8,128)(2,1)}), bf16[4,512,512]{1,2,0:T(8,128)(2,1)}, u32[]{:S(2)}, u32[]{:S(2)}) async-start(bf16[4,512,512]{1,2,0:T(8,128)(2,1)} %copy.134), calls=%async_computation.8 | async-start | bytes 4194304 | tf_op jit(solution)/shard_map/all_to_all | solution.py:318
  667.7 2.6 copy-start.24
  670.8 4.2 copy-start.11
  670.8 2.6 copy-start.4
  670.8 6.7 slice-start
  672.0 39.0 %collective-permute-start.7 = (bf16[8,96,896]{2,1,0:T(8,128)(2,1)}, bf16[8,96,896]{2,1,0:T(8,128)(2,1)}, u32[]{:S(2)}, u32[]{:S(2)}) collective-permute-start(bf16[8,96,896]{2,1,0:T(8,128)(2,1)} %dynamic-slice_bitcast_fusion.1), channel_id=1, source_target_pairs={{0,8},{8,0},{1,9},{9,1},{2,10},{10,2},{3,11},{11,3},{4,12},{12,4},... | collective-permute-start | bytes 4128776 | tf_op jit(solution)/shard_map/ppermute | solution.py:40
  673.4 4.1 slice-start.1
  677.5 21.6 %collective-permute-start.10 = (bf16[8,96,768]{2,1,0:T(8,128)(2,1)}, bf16[8,96,768]{2,1,0:T(8,128)(2,1)}, u32[]{:S(2)}, u32[]{:S(2)}) collective-permute-start(bf16[8,96,768]{2,1,0:T(8,128)(2,1)} %dynamic-slice_bitcast_fusion.2), channel_id=1, source_target_pairs={{0,8},{8,0},{1,9},{9,1},{2,10},{10,2},{3,11},{11,3},{4,12},{12,4},... | collective-permute-start | bytes 3538952 | tf_op jit(solution)/shard_map/ppermute | solution.py:40
  698.5 46.8 %collective-permute-start.8 = (bf16[512,1536]{1,0:T(8,128)(2,1)S(1)}, bf16[512,1536]{1,0:T(8,128)(2,1)}, u32[]{:S(2)}, u32[]{:S(2)}) collective-permute-start(bf16[512,1536]{1,0:T(8,128)(2,1)S(1)} %fusion.96), channel_id=1, source_target_pairs={{0,1},{1,0},{2,3},{3,2},{4,5},{5,4},{6,7},{7,6},{8,9},{9,8},{10,11... | collective-permute-start | bytes 4718600 | tf_op jit(solution)/shard_map/ppermute | solution.py:40
  702.2 52.5 %all-to-all-start.10 = ((bf16[32,24,768]{2,1,0:T(8,128)(2,1)}), bf16[32,24,768]{2,1,0:T(8,128)(2,1)}, u32[]{:S(2)}, u32[]{:S(2)}) async-start(bf16[32,24,768]{2,1,0:T(8,128)(2,1)} %bitcast.372), calls=%async_computation.10 | async-start | bytes 2359296 | tf_op jit(solution)/shard_map/all_to_all | solution.py:68
  714.2 33.7 %copy-start.10 = (f32[512,1536]{1,0:T(8,128)S(1)}, f32[512,1536]{1,0:T(8,128)}, u32[]{:S(2)}) copy-start(f32[512,1536]{1,0:T(8,128)} %copy-done.9) | copy-start | bytes 9437188
  754.7 9.3 %copy-start.21 = (bf16[512,512]{0,1:T(8,128)(2,1)S(1)}, bf16[512,512]{0,1:T(8,128)(2,1)}, u32[]{:S(2)}) copy-start(bf16[512,512]{0,1:T(8,128)(2,1)} %reduce_sum.221) | copy-start | bytes 1572868
  754.7 28.1 %all-to-all-start.7 = ((bf16[32,24,896]{2,1,0:T(8,128)(2,1)}), bf16[32,24,896]{2,1,0:T(8,128)(2,1)}, u32[]{:S(2)}, u32[]{:S(2)}) async-start(bf16[32,24,896]{2,1,0:T(8,128)(2,1)} %bitcast.62), calls=%async_computation.7 | async-start | bytes 2752512 | tf_op jit(solution)/shard_map/all_to_all | solution.py:68
  767.2 21.1 %collective-permute-start.9 = (bf16[8,96,640]{2,1,0:T(8,128)(2,1)}, bf16[8,96,640]{2,1,0:T(8,128)(2,1)}, u32[]{:S(2)}, u32[]{:S(2)}) collective-permute-start(bf16[8,96,640]{2,1,0:T(8,128)(2,1)} %fusion.119), channel_id=1, source_target_pairs={{0,8},{8,0},{1,9},{9,1},{2,10},{10,2},{3,11},{11,3},{4,12},{12,4},... | collective-permute-start | bytes 2949128 | tf_op jit(solution)/shard_map/ppermute | solution.py:40
  770.4 44.2 %collective-permute-start.11 = (bf16[3,384,512]{2,1,0:T(8,128)(2,1)}, bf16[3,384,512]{2,1,0:T(8,128)(2,1)}, u32[]{:S(2)}, u32[]{:S(2)}) collective-permute-start(bf16[3,384,512]{2,1,0:T(8,128)(2,1)} %broadcast_select_fusion), channel_id=1, source_target_pairs={{0,1},{1,0},{2,3},{3,2},{4,5},{5,4},{6,7},{7,6},{8,9},{9,8},{10,11... | collective-permute-start | bytes 3538952 | tf_op jit(solution)/shard_map/ppermute | solution.py:40
  790.9 27.9 %all-to-all-start.9 = ((bf16[32,24,640]{2,1,0:T(8,128)(2,1)}), bf16[32,24,640]{2,1,0:T(8,128)(2,1)S(1)}, u32[]{:S(2)}, u32[]{:S(2)}) async-start(bf16[32,24,640]{2,1,0:T(8,128)(2,1)} %bitcast.374), calls=%async_computation.9 | async-start | bytes 1966080 | tf_op jit(solution)/shard_map/all_to_all | solution.py:68
  (15 other events, 21.9 us)
Sparse Core Ops, SparseCore 0:
  105.7 46.7 all-gather.6
  154.1 39.3 all-gather.8
  199.5 39.3 all-gather.10
  426.2 33.5 reduce-scatter.7
  462.1 37.9 reduce-scatter.3
  536.9 36.4 reduce-scatter.5

commit v2 on v1

v2 whole, which is shorter than its diff:
```python
import functools

import jax
import jax.numpy as jnp
from jax import lax
from jax.experimental import pallas as pl
from jax.experimental.pallas import tpu as pltpu
from jax.sharding import Mesh
from jax.sharding import PartitionSpec as P

QUERY_HEAD_COUNT = 24
KEY_VALUE_HEADS = 8
HEAD_WIDTH = 64
TOP = 2
EXPERTS = 16
CAPACITY = 96

EPSILON = 1e-06
MASKED = -1e30

BF = jnp.bfloat16
F32 = jnp.float32
RING = ("h", "x", "y")
GROUP = QUERY_HEAD_COUNT // KEY_VALUE_HEADS
SPAN = 512
HALF = 256


def dot(left, right, left_dim, right_dim):
    return lax.dot_general(
        left, right, (((left_dim,), (right_dim,)), ((), ())), preferred_element_type=F32
    )


def rms_scale(values):
    return lax.rsqrt(jnp.mean(values * values, axis=-1, keepdims=True) + EPSILON)


def norm_back(values, scale, gain_row, upstream):
    gained = upstream * gain_row
    grad_gain = jnp.sum(upstream * values * scale, axis=0, keepdims=True)
    middle = jnp.mean(values * gained, axis=-1, keepdims=True)
    return (scale * gained - values * scale * scale * scale * middle, grad_gain)


def swap(value, axis):
    return lax.ppermute(value, axis, [(0, 1), (1, 0)])


def both(mine, other):
    return mine.astype(F32) + other.astype(F32)


def ring_gather(shard):
    rows, cols = shard.shape
    return lax.all_to_all(jnp.broadcast_to(shard[None], (32, rows, cols)), RING, 0, 0, tiled=True)


def core_gather(mine):
    rows, cols = mine.shape[1:]
    mine = mine.reshape(8, 4 * rows, cols)
    other = swap(mine, "c")
    first = lax.axis_index("c") == 0
    pair = jnp.stack([jnp.where(first, mine, other), jnp.where(first, other, mine)], axis=1)
    return pair.reshape(64 * rows, cols)


def after(value, *earlier):
    return lax.optimization_barrier((value,) + earlier)[0]


def pair_sum(partial):
    total_rows, cols = partial.shape
    rows = total_rows // 64
    parts = partial.reshape(8, 2, 4 * rows, cols)
    core = lax.axis_index("c")
    mine = lax.dynamic_index_in_dim(parts, core, 1, keepdims=False)
    theirs = lax.dynamic_index_in_dim(parts, 1 - core, 1, keepdims=False)
    paired = (mine.astype(F32) + swap(theirs, "c").astype(F32)).astype(BF)
    return paired.reshape(32, rows, cols)


def ring_sum(paired):
    moved = lax.all_to_all(paired, RING, 0, 0, tiled=True)
    return jnp.sum(moved.astype(F32), axis=0)


def axis_parts(parts, axis, size):
    me = lax.axis_index(axis)
    mine = [lax.dynamic_index_in_dim(parts, me, 0, keepdims=False)]
    for r in range(1, size):
        block = lax.dynamic_index_in_dim(parts, (me + r) % size, 0, keepdims=False)
        mine.append(lax.ppermute(block, axis, [(i, (i + r) % size) for i in range(size)]))
    return mine


def added(parts):
    total = parts[0].astype(F32)
    for part in parts[1:]:
        total = total + part.astype(F32)
    return total


def y_parts(paired):
    rows, cols = paired.shape[1:]
    return axis_parts(paired.reshape(8, 4, rows, cols).transpose(1, 0, 2, 3), "y", 4)


def hx_sum(parts):
    by_y = added(parts).astype(BF)
    by_h = added(axis_parts(by_y.reshape(2, 4, *by_y.shape[1:]), "h", 2)).astype(BF)
    return added(axis_parts(by_h, "x", 4))


def exchange_slots(rows):
    width = rows.shape[1]
    return lax.all_to_all(
        rows.reshape(EXPERTS, -1, width), ("h", "x", "c"), 0, 0, tiled=True
    ).reshape(-1, width)


def nn(a,b):
    return lax.dot_general(a,b,(((1,),(0,)),((),())),preferred_element_type=F32)

def fold(v, op):
    return op(v.reshape(v.shape[0]//8,8,v.shape[1]),axis=0)

def write_bias(bias, seg_q, seg_k, y, half):
    width = bias.shape[2]
    for r in range(4):

        def one(r=r):
            same = seg_k[r * SPAN : (r + 1) * SPAN, :] == seg_q[...]
            if r == 0:
                key_place = lax.broadcasted_iota(jnp.int32, (SPAN, width), 0)
                query_place = lax.broadcasted_iota(jnp.int32, (SPAN, width), 1) + half * HALF
                same = same & (key_place <= query_place)
            bias[r] = jnp.where(same, 0.0, MASKED)

        pl.when(y >= r)(one)


def fwd_kernel(
    half, y_ref, q_ref, kv0, kv1, kv2, kv3, seg_q, seg_k, o_ref, lse_ref, bias, kn, vt, sc
):
    y = y_ref[0]

    @pl.when(pl.program_id(0) == 0)
    def _():
        write_bias(bias, seg_q, seg_k, y, half)

    for r, kv in enumerate((kv0, kv1, kv2, kv3)):

        def fill(r=r, kv=kv):
            kn[r] = kv[0].T
            vt[r] = kv[1]

        pl.when(y >= r)(fill)
    scale = jnp.asarray(HEAD_WIDTH**-0.5, BF)
    qs = [q_ref[h * HEAD_WIDTH : (h + 1) * HEAD_WIDTH] * scale for h in range(GROUP)]

    def scores(r, rows, tops):
        out = []
        for h in range(GROUP):
            s = nn(kn[r, rows, :], qs[h]) + bias[r, rows, :]
            sc[h, r, rows, :] = s
            out.append(jnp.maximum(tops[h], fold(s, jnp.max)))
        return tuple(out)

    own = slice(0, (half + 1) * HALF)
    low = tuple(jnp.full((8, HALF), MASKED, F32) for _ in range(GROUP))
    tops = scores(0, own, low)
    tops = lax.fori_loop(1, y + 1, lambda r, t: scores(r, slice(0, SPAN), t), tops)
    tops = [jnp.max(t, axis=0, keepdims=True) for t in tops]

    def mix(r, rows, carry):
        out = []
        for h in range(GROUP):
            total, acc = carry[h]
            p = jnp.exp(sc[h, r, rows, :] - tops[h])
            out.append((total + fold(p, jnp.sum), acc + nn(vt[r, :, rows], p.astype(BF))))
        return tuple(out)

    zero = tuple(
        (jnp.zeros((8, HALF), F32), jnp.zeros((HEAD_WIDTH, HALF), F32)) for _ in range(GROUP)
    )
    carry = mix(0, own, zero)
    carry = lax.fori_loop(1, y + 1, lambda r, c: mix(r, slice(0, SPAN), c), carry)
    for h in range(GROUP):
        total = jnp.sum(carry[h][0], axis=0, keepdims=True)
        o_ref[h * HEAD_WIDTH : (h + 1) * HEAD_WIDTH, :] = (carry[h][1] / total).astype(BF)
        lse_ref[0, h : h + 1, :] = tops[h] + jnp.log(total)


def attend(half, y, q_t, kvs, seg_q, seg_k):
    rows = GROUP * HEAD_WIDTH
    heads = q_t.shape[0] // rows
    kv_spec = pl.BlockSpec((2, HEAD_WIDTH, SPAN), lambda g: (0, g, 0))
    return pl.pallas_call(
        functools.partial(fwd_kernel, half),
        grid=(heads,),
        in_specs=[
            pl.BlockSpec(memory_space=pltpu.SMEM),
            pl.BlockSpec((rows, HALF), lambda g: (g, half)),
            kv_spec,
            kv_spec,
            kv_spec,
            kv_spec,
            pl.BlockSpec((1, HALF), lambda g: (0, half)),
            pl.BlockSpec((4 * SPAN, 1), lambda g: (0, 0)),
        ],
        out_specs=[
            pl.BlockSpec((rows, HALF), lambda g: (g, 0)),
            pl.BlockSpec((1, 8, HALF), lambda g: (g, 0, 0)),
        ],
        out_shape=[
            jax.ShapeDtypeStruct((q_t.shape[0], HALF), BF),
            jax.ShapeDtypeStruct((heads, 8, HALF), F32),
        ],
        scratch_shapes=[
            pltpu.VMEM((4, SPAN, HALF), F32),
            pltpu.VMEM((4, SPAN, HEAD_WIDTH), BF),
            pltpu.VMEM((4, HEAD_WIDTH, SPAN), BF),
            pltpu.VMEM((GROUP, 4, SPAN, HALF), F32),
        ],
        compiler_params=pltpu.CompilerParams(vmem_limit_bytes=40 << 20),
        cost_estimate=pl.CostEstimate(
            flops=14_000_000_000, bytes_accessed=6_000_000, transcendentals=6_000_000
        ),
    )(y, q_t, *kvs, seg_q, seg_k)


def bwd_kernel(y_ref, q_ref, d_ref, o_0, o_1, lse_0, lse_1, kv0, kv1, kv2, kv3, seg_q, seg_k, dq_ref, g0, g1, g2, g3, bias, kn, vn, kt, dk, dv):
    y = y_ref[0]
    @pl.when(pl.program_id(0)==0)
    def _(): write_bias(bias, seg_q, seg_k, y, 0)
    for r,kv in enumerate((kv0,kv1,kv2,kv3)):
        def fill(r=r,kv=kv):
            kn[r] = kv[0].T
            vn[r] = kv[1].T
            kt[r] = kv[0]
        pl.when(y>=r)(fill)
    dk[...] = jnp.zeros_like(dk); dv[...] = jnp.zeros_like(dv)
    scale = jnp.asarray(HEAD_WIDTH**-0.5, BF)
    for b in range(2):
        cols = slice(b*HALF,(b+1)*HALF)
        qs, qn, ds, dn, dots, lses = [],[],[],[],[],[]
        for h in range(GROUP):
            hr = slice(h*HEAD_WIDTH,(h+1)*HEAD_WIDTH)
            q = q_ref[hr, cols]*scale
            qs.append(q); qn.append(q.T)
            d = d_ref[hr, cols]
            ds.append(d); dn.append(d.T)
            dots.append(jnp.sum(d.astype(F32)*(o_0, o_1)[b][hr].astype(F32),axis=0,keepdims=True))
            lses.append((lse_0, lse_1)[b][0, h : h + 1])
        def step(r, rows, carry):
            out=[]; sum_k=None; sum_v=None
            for h in range(GROUP):
                s = nn(kn[r, rows, :], qs[h]) + bias[r, rows, cols]
                p = jnp.exp(s - lses[h])
                pv = nn(p.astype(BF), dn[h])
                dp = nn(vn[r, rows, :], ds[h])
                dsc = (p*(dp - dots[h])).astype(BF)
                pk = nn(dsc, qn[h])
                out.append(carry[h] + nn(kt[r,:,rows], dsc))
                sum_k = pk if sum_k is None else sum_k+pk
                sum_v = pv if sum_v is None else sum_v+pv
            dk[r, rows, :] += sum_k
            dv[r, rows, :] += sum_v
            return tuple(out)
        carry = step(0, slice(0,(b+1)*HALF), tuple(jnp.zeros((HEAD_WIDTH,HALF),F32) for _ in range(GROUP)))
        carry = lax.fori_loop(1, y+1, lambda r,c: step(r, slice(0,SPAN), c), carry)
        for h in range(GROUP):
            dq_ref[h*HEAD_WIDTH:(h+1)*HEAD_WIDTH, cols] = (carry[h]*HEAD_WIDTH**-0.5).astype(BF)
    for r,g in enumerate((g0,g1,g2,g3)):
        g[0] = dk[r].T.astype(BF)
        g[1] = dv[r].T.astype(BF)

def attend_back(first, count, y, q_t, d_t, outs, lses, kvs, seg_q, seg_k):
    rows = GROUP * HEAD_WIDTH
    kv_spec = pl.BlockSpec((2, HEAD_WIDTH, SPAN), lambda g: (0, first + g, 0))
    q_spec = pl.BlockSpec((rows, SPAN), lambda g: (first + g, 0))
    o_spec = pl.BlockSpec((rows, HALF), lambda g: (first + g, 0))
    lse_spec = pl.BlockSpec((1, 8, HALF), lambda g: (first + g, 0, 0))
    kv_shape = jax.ShapeDtypeStruct((2, count * HEAD_WIDTH, SPAN), BF)
    return pl.pallas_call(
        bwd_kernel,
        grid=(count,),
        in_specs=[pl.BlockSpec(memory_space=pltpu.SMEM), q_spec, q_spec]
        + [o_spec, o_spec, lse_spec, lse_spec]
        + [kv_spec] * 4
        + [pl.BlockSpec((1, SPAN), lambda g: (0, 0)), pl.BlockSpec((4 * SPAN, 1), lambda g: (0, 0))],
        out_specs=[pl.BlockSpec((rows, SPAN), lambda g: (g, 0))]
        + [pl.BlockSpec((2, HEAD_WIDTH, SPAN), lambda g: (0, g, 0))] * 4,
        out_shape=[jax.ShapeDtypeStruct((count * rows, SPAN), BF)] + [kv_shape] * 4,
        scratch_shapes=[pltpu.VMEM((4, SPAN, SPAN), F32)]
        + [pltpu.VMEM((4, SPAN, HEAD_WIDTH), BF)] * 2
        + [pltpu.VMEM((4, HEAD_WIDTH, SPAN), BF)]
        + [pltpu.VMEM((4, SPAN, HEAD_WIDTH), F32)] * 2,
        compiler_params=pltpu.CompilerParams(vmem_limit_bytes=40 << 20),
        cost_estimate=pl.CostEstimate(
            flops=28_000_000_000, bytes_accessed=6_000_000, transcendentals=6_000_000
        ),
    )(y, q_t, d_t, *outs, *lses, *kvs, seg_q, seg_k)


def split_bf16(value):
    high = value.astype(BF)
    return high, (value - high.astype(F32)).astype(BF)


def local(
    tokens,
    teacher,
    segments,
    routes,
    route_weight,
    norm_attn,
    w_query,
    key_weight,
    value_weight,
    w_out,
    norm_ffn,
    w_router,
    w_gate,
    w_up,
    w_down,
):
    tok_rows, feat_width = tokens.shape
    q_width = w_query.shape[1]
    k_width = key_weight.shape[1]
    tix = lax.axis_index("t")
    yix = lax.axis_index("y")

    small = jnp.concatenate(
        [
            w_router,
            norm_attn[:, None],
            norm_ffn[:, None],
            jnp.zeros((w_router.shape[0], 128 - EXPERTS - 2), BF),
        ],
        axis=1,
    )
    ring_kv = ring_gather(jnp.concatenate([key_weight, value_weight, small], axis=1))
    pack_kv = core_gather(ring_kv)
    ring_rest = ring_gather(jnp.concatenate([w_query, w_out.T], axis=1))
    full_kv = pack_kv[:, : 2 * k_width]
    full_small = pack_kv[:, 2 * k_width :]
    small_rows = dot(jnp.eye(24, 128, dtype=BF), full_small, 1, 1)
    router_rows = small_rows[:EXPERTS].astype(BF)
    gain_one = small_rows[EXPERTS : EXPERTS + 1]
    gain_two = small_rows[EXPERTS + 1 : EXPERTS + 2]

    resid_in = tokens.astype(F32)
    scale_one = rms_scale(resid_in)
    act_one = (resid_in * scale_one * gain_one).astype(BF)
    kv_mine = dot(full_kv, act_one, 0, 1).astype(BF).reshape(2, k_width, tok_rows)
    kvs = [kv_mine] + [
        lax.ppermute(kv_mine, "y", [(i, i + r) for i in range(4 - r)]) for r in (1, 2, 3)
    ]
    kvs[1:] = lax.optimization_barrier((*kvs[1:], ring_rest))[:3]
    pack_rest = core_gather(ring_rest)
    full_query = pack_rest[:, :q_width]
    full_out = pack_rest[:, q_width:]
    query_t = dot(full_query, act_one, 0, 1).astype(BF)

    experts = jnp.stack([w_gate[0], w_up[0], w_down[0].T])
    experts_other = after(swap(after(experts, kv_mine), "t"), kvs[1], kvs[2], kvs[3])
    experts_full = jnp.concatenate(
        [
            jnp.where(tix == 0, experts, experts_other),
            jnp.where(tix == 0, experts_other, experts),
        ],
        axis=2,
    )
    gate_full = lax.all_gather(experts_full[0], "y", axis=0, tiled=True)
    up_full = lax.all_gather(experts_full[1], "y", axis=0, tiled=True)
    down_full = lax.all_gather(experts_full[2], "y", axis=0, tiled=True)

    seg_blocks = segments[0].reshape(4, tok_rows)
    seg_mine = lax.dynamic_index_in_dim(seg_blocks, yix, 0, keepdims=False)
    seg_keys = jnp.concatenate(
        [lax.dynamic_index_in_dim(seg_blocks, (yix + 4 - r) % 4, 0, keepdims=False) for r in range(4)]
    )[:, None]
    place_y = jnp.full((1,), yix, jnp.int32)
    mixed_0, log_0 = attend(0, place_y, query_t, kvs, seg_mine[None], seg_keys)
    part_0 = dot(mixed_0, full_out, 0, 1).astype(BF)
    mixed_1, log_1 = attend(1, place_y, after(query_t, part_0), kvs, seg_mine[None], seg_keys)
    other_0 = swap(part_0, "t")
    part_1 = dot(after(mixed_1, other_0), full_out, 0, 1).astype(BF)
    other_1 = swap(part_1, "t")
    hidden = resid_in + jnp.concatenate([both(part_0, other_0), both(part_1, other_1)])
    scale_two = rms_scale(hidden)
    act_two = (hidden * scale_two * gain_two).astype(BF)

    logits = dot(router_rows, act_two, 1, 1)
    router = jax.nn.softmax(logits, axis=0)
    route_cols = routes.T
    weight_cols = route_weight.T
    expert_iota = lax.broadcasted_iota(jnp.int32, (EXPERTS, tok_rows), 0)
    named = [expert_iota == route_cols[k : k + 1] for k in range(TOP)]
    taken = (named[0] | named[1]).astype(BF)
    earlier = (
        lax.broadcasted_iota(jnp.int32, (tok_rows, tok_rows), 0)
        < lax.broadcasted_iota(jnp.int32, (tok_rows, tok_rows), 1)
    ).astype(BF)
    count_before = dot(taken, earlier, 1, 0)
    half = CAPACITY // 2
    slot_iota = lax.broadcasted_iota(jnp.int32, (EXPERTS * half, tok_rows), 0)
    picks = []
    gates = []
    for k in range(TOP):
        place = jnp.sum(jnp.where(named[k], count_before, 0.0), axis=0, keepdims=True)
        place = place.astype(jnp.int32) - tix * half
        slot = jnp.where((place >= 0) & (place < half), route_cols[k : k + 1] * half + place, -1)
        picks.append(slot_iota == slot)
        chosen = jnp.sum(jnp.where(named[k], router, 0.0), axis=0, keepdims=True)
        gates.append(chosen * weight_cols[k : k + 1])
    pick = (picks[0] | picks[1]).astype(BF)
    gated_pick = (
        jnp.where(picks[0], gates[0], 0.0) + jnp.where(picks[1], gates[1], 0.0)
    ).astype(BF)

    received = exchange_slots(dot(pick, act_two, 1, 0).astype(BF))
    gate_proj = dot(received, gate_full, 1, 0)
    up_proj = dot(received, up_full, 1, 0)
    inner = (jax.nn.silu(gate_proj) * up_proj).astype(BF)

    returned = exchange_slots(dot(inner, down_full, 1, 1).astype(BF))
    part = dot(gated_pick, returned, 0, 0).astype(BF)
    output = hidden + both(part, swap(part, "t"))
    valid = (seg_mine != 0).astype(F32)
    difference = output - teacher.astype(F32)
    grad_output = difference * valid[:, None]
    sse = jnp.sum(grad_output * difference)
    count = jnp.sum(valid)
    grad_low = grad_output.astype(BF)
    d_received = exchange_slots(dot(gated_pick, grad_low, 1, 0).astype(BF))

    slot_dots = dot(returned, grad_low, 1, 1)
    d_gates = jnp.concatenate(
        [jnp.sum(jnp.where(picks[k], slot_dots, 0.0), axis=0, keepdims=True) for k in range(TOP)]
    )
    d_gates_other = swap(d_gates, "t")
    d_received = after(d_received, d_gates_other)
    d_gates = d_gates + d_gates_other

    d_inner = dot(d_received, down_full, 1, 0)
    sig_gate = jax.nn.sigmoid(gate_proj)
    d_gate_proj = (d_inner * up_proj * sig_gate * (1.0 + gate_proj * (1.0 - sig_gate))).astype(BF)
    d_up_proj = (d_inner * gate_proj * sig_gate).astype(BF)
    d_slots = dot(d_gate_proj, gate_full, 1, 1) + dot(d_up_proj, up_full, 1, 1)
    d_returned = exchange_slots(d_slots.astype(BF))

    grad_parts = [
        dot(received, d_gate_proj, 0, 0).astype(BF),
        dot(received, d_up_proj, 0, 0).astype(BF),
        dot(d_received, inner, 0, 0).astype(BF),
    ]
    grad_experts = [
        lax.psum_scatter(part, "y", scatter_dimension=0, tiled=True) for part in grad_parts
    ]
    d_returned = after(d_returned, *grad_parts)
    grad_stack = jnp.stack(grad_experts)
    ff_half = grad_stack.shape[2] // 2
    keep = jnp.where(tix == 0, grad_stack[:, :, :ff_half], grad_stack[:, :, ff_half:])
    give = jnp.where(tix == 0, grad_stack[:, :, ff_half:], grad_stack[:, :, :ff_half])

    d_router = jnp.where(named[0], d_gates[0:1] * weight_cols[0:1], 0.0) + jnp.where(
        named[1], d_gates[1:2] * weight_cols[1:2], 0.0
    )
    d_logits = (
        router * (d_router - jnp.sum(router * d_router, axis=0, keepdims=True))
    ).astype(BF)
    grad_router = dot(act_two, d_logits, 0, 1)
    d_route = dot(d_logits, router_rows, 0, 0)
    part = dot(pick, d_returned, 0, 0).astype(BF)
    d_act_two = d_route + both(part, after(swap(part, "t"), d_route, grad_router))
    d_norm_two, grad_gain_two = norm_back(hidden, scale_two, gain_two, d_act_two)
    d_hidden = grad_output + d_norm_two
    d_attn = d_hidden.astype(BF)
    d_mixed_t = dot(full_out, d_attn, 0, 1).astype(BF)

    sse_high, sse_low = split_bf16(jnp.full((1, feat_width), sse))
    count_high, count_low = split_bf16(jnp.full((1, feat_width), count))
    gain_high, gain_low = split_bf16(grad_gain_two)
    lines = jnp.concatenate(
        [gain_high, gain_low, sse_high, sse_low, count_high, count_low, jnp.zeros((2, feat_width), BF)]
    )
    extra = dot(lines, jnp.eye(8, 128 - EXPERTS, dtype=BF), 0, 0)
    rest_small = jnp.concatenate([grad_router, extra], axis=1).astype(BF)

    saved = (d_mixed_t, (mixed_0, mixed_1), (log_0, log_1), kvs, seg_mine[None], seg_keys)

    def ring_back(parts):
        return [
            lax.ppermute(parts[r], "y", [(i, i - r) for i in range(r, 4)]) for r in (1, 2, 3)
        ]

    kv_groups = k_width // HEAD_WIDTH
    back_0 = attend_back(0, kv_groups // 2, place_y, query_t, *saved)
    others_0 = ring_back(back_0[1:])
    back_1 = attend_back(
        kv_groups // 2, kv_groups // 2, place_y, after(query_t, back_0[0]), *saved
    )
    back_1 = lax.optimization_barrier((*back_1, *others_0))[:5]
    others_1 = ring_back(back_1[1:])
    d_query_t = jnp.concatenate([back_0[0], back_1[0]])
    grad_out = dot(
        after(d_attn, d_query_t), jnp.concatenate([mixed_0, mixed_1], axis=1), 0, 1
    ).astype(BF)
    grad_query = dot(act_one, d_query_t, 0, 1).astype(BF)
    parts_one = y_parts(pair_sum(jnp.concatenate([grad_out, rest_small, grad_query], axis=1)))
    grad_stack = keep.astype(F32) + swap(after(give, d_query_t), "t").astype(F32)
    own_down = grad_stack[2].T
    d_kv_t = jnp.concatenate(
        [
            added([own, *moved])
            for own, moved in ((back_0[1], others_0), (back_1[1], others_1))
        ],
        axis=1,
    ).reshape(2 * k_width, tok_rows).astype(BF)
    d_act_part = dot(d_query_t, full_query, 0, 1) + dot(d_kv_t, full_kv, 0, 1)
    part = after(d_act_part.astype(BF), grad_stack)
    other = swap(part, "t")
    gain_high, gain_low = split_bf16(
        jnp.sum(d_act_part * resid_in * scale_one, axis=0, keepdims=True)
    )
    lines = jnp.concatenate([gain_high, gain_low, jnp.zeros((6, feat_width), BF)])
    extra = dot(lines, jnp.eye(8, 128, dtype=BF), 0, 0)
    parts_two = y_parts(
        pair_sum(jnp.concatenate([dot(act_one, d_kv_t, 0, 1), extra], axis=1).astype(BF))
    )
    summed = hx_sum(parts_one)
    own_kv = hx_sum(parts_two)
    at = feat_width // 2
    own_out = summed[:, :at].T
    own_router = summed[:, at : at + EXPERTS]
    at = at + EXPERTS
    own_gain_two = summed[:, at] + summed[:, at + 1]
    loss_value = (summed[0, at + 2] + summed[0, at + 3]) / (
        feat_width * (summed[0, at + 4] + summed[0, at + 5])
    )
    own_gain_one = own_kv[:, 2 * k_width] + own_kv[:, 2 * k_width + 1]
    own_gain_one = own_gain_one + swap(own_gain_one, "t")
    own_query = summed[:, feat_width // 2 + 128 :]
    own_down, own_out, own_kv, other = lax.optimization_barrier((own_down, own_out, own_kv, other))
    d_hidden_one, _ = norm_back(resid_in, scale_one, gain_one, both(part, other))
    grad_tokens = d_hidden + d_hidden_one
    return (
        output,
        loss_value,
        grad_tokens,
        own_gain_one,
        own_query,
        own_kv[:, :k_width],
        own_kv[:, k_width : 2 * k_width],
        own_out,
        own_gain_two,
        own_router,
        grad_stack[0][None],
        grad_stack[1][None],
        own_down[None],
    )


def solution(mesh):
    fine = Mesh(mesh.devices.reshape(2, 4, 2, 4, 2), ("h", "x", "c", "y", "t"))
    fsdp = ("h", "x", "c")
    every = ("h", "x", "c", "y")
    return jax.shard_map(
        local,
        mesh=fine,
        in_specs=(
            P(every, None),
            P(every, None),
            P(fsdp, None),
            P(every, None),
            P(every, None),
            P(every),
            P(every, "t"),
            P(every, "t"),
            P(every, "t"),
            P("t", every),
            P(every),
            P(every, None),
            P(fsdp, "y", "t"),
            P(fsdp, "y", "t"),
            P(fsdp, "t", "y"),
        ),
        out_specs=(
            P(every, None),
            P(),
            P(every, None),
            P(every),
            P(every, "t"),
            P(every, "t"),
            P(every, "t"),
            P("t", every),
            P(every),
            P(every, None),
            P(fsdp, "y", "t"),
            P(fsdp, "y", "t"),
            P(fsdp, "t", "y"),
        ),
        check_vma=False,
    )
```

time: 838 us -> 722 us (0.86)
  matrix products: 208 us -> 103 us
  blocking collectives: 118 us -> 28.1 us
  waiting for transfers between devices: 272 us -> 361 us
  other arithmetic: 103 us -> 56.6 us
  starting transfers between devices: 52.6 us -> 81.6 us
  Pallas kernels: 0 us -> 19.9 us
  local copies, waits for them, and re-layouts: 52.9 us -> 40.2 us
    dot_general x28 -> x0, matrix products: 111 us -> none  [the longest x4 30.9 us: head_backward(): jnp.einsum('tgd,sd->gts', d_one, value_one, preferred_element_type=F32)]
    ppermute x0 -> x23, waiting for transfers between devices: none -> 95.5 us  [the longest x6 46 us: ring_back(): lax.ppermute(parts[r], 'y', [(i, i - r) for i in range(r, 4)])]
    all_to_all x3 -> x1, blocking collectives: 118 us -> 28.1 us  [ring_gather(): lax.all_to_all(jnp.broadcast_to(shard[None], (32, rows, cols)), RING, 0,...]
    ppermute x0 -> x23, starting transfers between devices: none -> 40.5 us  [the longest x14 23.8 us: axis_parts(): lax.ppermute(block, axis, [(i, (i + r) % size) for i in range(size)])]
    all_to_all x2 -> x4, waiting for transfers between devices: 60.1 us -> 96.9 us  [exchange_slots(): lax.all_to_all(rows.reshape(EXPERTS, -1, width), ('h', 'x', 'c'), 0, 0, t...]
    all_to_all x6 -> x1, starting transfers between devices: 36.3 us -> 4.94 us  [ring_gather(): lax.all_to_all(jnp.broadcast_to(shard[None], (32, rows, cols)), RING, 0,...]
    all_to_all x6 -> x1, waiting for transfers between devices: 48.4 us -> 18.4 us  [ring_gather(): lax.all_to_all(jnp.broadcast_to(shard[None], (32, rows, cols)), RING, 0,...]
    convert_element_type x8 -> x9, other arithmetic: 36.9 us -> 14 us  [the longest x2 5.41 us: pair_sum(): paired = (mine.astype(F32) + swap(theirs, 'c').astype(F32)).astype(BF)]
  transfers between devices with their start and end apart: 26 -> 47, of which waited for: 13 -> 31; matrix products, arithmetic and copies ran while one was open for 39% -> 21% of each run, Pallas kernels for 0% -> 3%
where the time goes in v2:
time: 722 us; the launch traced here: 713 us
  waiting for transfers between devices  361 us (50%)
  matrix products  103 us (14%)
  starting transfers between devices  81.6 us (11%)
  other arithmetic  56.6 us (8%)
  local copies, waits for them, and re-layouts  40.2 us (6%)
  blocking collectives  28.1 us (4%)
  between operations  22.1 us (3%)
  Pallas kernels  19.9 us (3%)
    ppermute x13, waiting for transfers between devices, swap(): return lax.ppermute(value, axis, [(0, 1), (1, 0)])  145 us
    dot_general x31, matrix products, dot(): lax.dot_general(left, right, (((left_dim,), (right_dim,)), ((), ())), pre...  103 us
    all_to_all x4, waiting for transfers between devices, exchange_slots(): lax.all_to_all(rows.reshape(EXPERTS, -1, width), ('h', 'x', 'c'), 0, 0, t...  96.9 us
    ppermute x6, waiting for transfers between devices, ring_back(): lax.ppermute(parts[r], 'y', [(i, i - r) for i in range(r, 4)])  46 us
    ppermute x14, waiting for transfers between devices, axis_parts(): lax.ppermute(block, axis, [(i, (i + r) % size) for i in range(size)])  34.7 us
    all_to_all x1, blocking collectives, ring_gather(): lax.all_to_all(jnp.broadcast_to(shard[None], (32, rows, cols)), RING, 0,...  28.1 us
    all_to_all x4, starting transfers between devices, exchange_slots(): lax.all_to_all(rows.reshape(EXPERTS, -1, width), ('h', 'x', 'c'), 0, 0, t...  26.9 us
    ppermute x14, starting transfers between devices, axis_parts(): lax.ppermute(block, axis, [(i, (i + r) % size) for i in range(size)])  23.8 us
  transfers between devices with their start and end apart: 47, of which 31 were waited for; matrix products, arithmetic and copies ran while one was open for 21% of the time, Pallas kernels for 3%

profile of v2, /device:TPU:0, one launch (start us, length us, event | category | flops | bytes accessed | tf_op | source)
XLA Modules:
  0.0 712.6 jit_solution(4874012943764607215)
XLA Ops:
  10.4 28.1 %all_to_all.30 = bf16[32,24,640]{2,1,0:T(8,128)(2,1)S(1)} all-to-all(bf16[32,24,640]{2,1,0:T(8,128)(2,1)S(1)} %broadcast_in_dim.135), channel_id=1, replica_groups=mesh['h'=2,'x'=4,'c'=2,'y'=4,'t'=2] {'h','x','y'}, dimensions={0} | all-to-all | bytes 1966080 | tf_op jit(solution)/shard_map/all_to_all | solution.py:56
  40.1 4.9 all-to-all-start
  54.1 4.8 collective-permute-start.4
  60.2 2.8 collective-permute-start.2
  63.0 18.4 %all-to-all-done = bf16[32,24,1536]{2,1,0:T(8,128)(2,1)} async-done(((bf16[32,24,1536]{2,1,0:T(8,128)(2,1)}), bf16[32,24,1536]{2,1,0:T(8,128)(2,1)}, u32[]{:S(2)}, u32[]{:S(2)}) %all-to-all-start) | async-done | bytes 2359328 | tf_op jit(solution)/shard_map/all_to_all | solution.py:56
  81.4 12.5 %collective-permute-done.4.kv3 = bf16[2,256,512]{2,1,0:T(8,128)(2,1)S(1)} collective-permute-done((bf16[2,256,512]{2,1,0:T(8,128)(2,1)S(1)}, bf16[2,256,512]{2,1,0:T(8,128)(2,1)S(1)}, u32[]{:S(2)}, u32[]{:S(2)}) %collective-permute-start.4) | collective-permute-done | bytes 524320 | tf_op jit(solution)/shard_map/ppermute | solution.py:359
  96.3 2.8 collective-permute-done.7
  107.3 2.7 select_bitcast_fusion.1
  113.0 2.9 shard_map.246
  118.1 3.9 shard_map.247
  122.1 14.6 %collective-permute-done.5 = bf16[256,1536]{1,0:T(8,128)(2,1)S(1)} collective-permute-done((bf16[256,1536]{1,0:T(8,128)(2,1)S(1)}, bf16[256,1536]{1,0:T(8,128)(2,1)S(1)}, u32[]{:S(2)}, u32[]{:S(2)}) %collective-permute-start.5) | collective-permute-done | bytes 786464 | tf_op jit(solution)/shard_map/ppermute | solution.py:47
  141.8 16.5 %collective-permute-done.6 = bf16[256,1536]{1,0:T(8,128)(2,1)} collective-permute-done((bf16[256,1536]{1,0:T(8,128)(2,1)}, bf16[256,1536]{1,0:T(8,128)(2,1)}, u32[]{:S(2)}, u32[]{:S(2)}) %collective-permute-start.6) | collective-permute-done | bytes 786464 | tf_op jit(solution)/shard_map/ppermute | solution.py:47
  162.3 2.8 convolution_convert_fusion.7
  165.1 8.1 %all-to-all-start.2 = ((bf16[16,48,1536]{2,1,0:T(8,128)(2,1)}), bf16[16,48,1536]{2,1,0:T(8,128)(2,1)}, u32[]{:S(2)}, u32[]{:S(2)}) async-start(bf16[16,48,1536]{2,1,0:T(8,128)(2,1)} %bitcast.231), calls=%async_computation.2 | async-start | bytes 4718592 | tf_op jit(solution)/shard_map/all_to_all | solution.py:117
  173.3 32.1 %all-to-all-done.2 = bf16[16,48,1536]{2,1,0:T(8,128)(2,1)} async-done(((bf16[16,48,1536]{2,1,0:T(8,128)(2,1)}), bf16[16,48,1536]{2,1,0:T(8,128)(2,1)}, u32[]{:S(2)}, u32[]{:S(2)}) %all-to-all-start.2) | async-done | bytes 2359328 | tf_op jit(solution)/shard_map/all_to_all | solution.py:117
  205.3 7.0 fusion.21
  212.3 8.6 %multiply_convert_fusion.3 = (bf16[768,1024]{1,0:T(8,128)(2,1)}, f32[768,1024]{1,0:T(8,128)}) fusion(f32[768,1024]{1,0:T(8,128)} %fusion.21, bf16[768,1536]{1,0:T(8,128)(2,1)} %bitcast.33, bf16[1,1536,1024]{2,1,0:T(8,128)(2,1)} %all-gather.9.cloned.1.call-done), kind=kOutput, calls=%fused_computation.52 | convolution fusion | flops 2420637696 | bytes 13369344 | tf_op jit(solution)/shard_map/dot_general | solution.py:30
  220.9 5.4 all-gather.11.cloned.1.call-done
  226.4 6.4 convolution_convert_fusion.3
  232.8 7.5 %all-to-all-start.3 = ((bf16[16,48,1536]{2,1,0:T(8,128)(2,1)}), bf16[16,48,1536]{2,1,0:T(8,128)(2,1)}, u32[]{:S(2)}, u32[]{:S(2)}) async-start(bf16[16,48,1536]{2,1,0:T(8,128)(2,1)} %bitcast.230), calls=%async_computation.3 | async-start | bytes 4718592 | tf_op jit(solution)/shard_map/all_to_all | solution.py:117
  240.3 32.1 %all-to-all-done.3 = bf16[16,48,1536]{2,1,0:T(8,128)(2,1)} async-done(((bf16[16,48,1536]{2,1,0:T(8,128)(2,1)}), bf16[16,48,1536]{2,1,0:T(8,128)(2,1)}, u32[]{:S(2)}, u32[]{:S(2)}) %all-to-all-start.3) | async-done | bytes 2359328 | tf_op jit(solution)/shard_map/all_to_all | solution.py:117
  272.4 3.3 convolution_convert_fusion.9
  276.4 35.5 %collective-permute-done.8 = bf16[512,1536]{1,0:T(8,128)(2,1)S(1)} collective-permute-done((bf16[512,1536]{1,0:T(8,128)(2,1)S(1)}, bf16[512,1536]{1,0:T(8,128)(2,1)S(1)}, u32[]{:S(2)}, u32[]{:S(2)}) %collective-permute-start.8) | collective-permute-done | bytes 1572896 | tf_op jit(solution)/shard_map/ppermute | solution.py:47
  315.5 2.8 convolution_convert_fusion.6
  318.3 5.7 all-to-all-start.4
  324.1 3.8 select_reduce_fusion.1
  328.6 20.3 %collective-permute-done.9 = f32[2,512]{1,0:T(2,128)S(1)} collective-permute-done((f32[2,512]{1,0:T(2,128)S(1)}, f32[2,512]{1,0:T(2,128)S(1)}, u32[]{:S(2)}, u32[]{:S(2)}) %collective-permute-start.9) | collective-permute-done | bytes 4128 | tf_op jit(solution)/shard_map/ppermute | solution.py:47
  348.9 7.2 %all-to-all-done.4 = bf16[16,48,1536]{2,1,0:T(8,128)(2,1)} async-done(((bf16[16,48,1536]{2,1,0:T(8,128)(2,1)}), bf16[16,48,1536]{2,1,0:T(8,128)(2,1)}, u32[]{:S(2)}, u32[]{:S(2)}) %all-to-all-start.4) | async-done | bytes 2359328 | tf_op jit(solution)/shard_map/all_to_all | solution.py:117
  356.1 6.4 convolution_convert_fusion
  362.8 9.0 %multiply_convert_fusion.1 = (bf16[768,1024]{1,0:T(8,128)(2,1)}, bf16[768,1024]{1,0:T(8,128)(2,1)S(1)}) fusion(f32[768,1024]{1,0:T(8,128)} %fusion.21, f32[768,1024]{1,0:T(8,128)} %get-tuple-element.211, bf16[768,1536]{1,0:T(8,128)(2,1)} %bitcast.48, bf16[1,1536,1024]{2,1,0:T(8,128)(2,1)} %all-gather.11.cloned.1.call-done), kind=kOutput, calls=%fused_computation.48 | convolution fusion | flops 2426142720 | bytes 14942208 | tf_op jit(solution)/shard_map/dot_general | solution.py:30
  373.0 6.3 convolution_convert_fusion.2
  379.3 5.2 fusion.19
  384.5 4.0 add_convert_fusion
  388.5 5.6 all-to-all-start.5
  394.2 6.5 convolution_convert_fusion.1
  400.6 25.6 %all-to-all-done.5 = bf16[16,48,1536]{2,1,0:T(8,128)(2,1)} async-done(((bf16[16,48,1536]{2,1,0:T(8,128)(2,1)}), bf16[16,48,1536]{2,1,0:T(8,128)(2,1)}, u32[]{:S(2)}, u32[]{:S(2)}) %all-to-all-start.5) | async-done | bytes 2359328 | tf_op jit(solution)/shard_map/all_to_all | solution.py:117
  426.2 4.3 convolution_convert_fusion.8
  439.3 27.8 %collective-permute-done.10 = bf16[512,1536]{1,0:T(8,128)(2,1)} collective-permute-done((bf16[512,1536]{1,0:T(8,128)(2,1)}, bf16[512,1536]{1,0:T(8,128)(2,1)}, u32[]{:S(2)}, u32[]{:S(2)}) %collective-permute-start.10) | collective-permute-done | bytes 1572896 | tf_op jit(solution)/shard_map/ppermute | solution.py:47
  467.1 5.1 multiply_reduce_fusion
  472.3 5.0 fusion.103
  479.5 6.7 shard_map.248
  487.2 6.4 shard_map.249
  498.7 13.9 %collective-permute-done.11 = bf16[2,128,512]{2,1,0:T(8,128)(2,1)S(1)} collective-permute-done((bf16[2,128,512]{2,1,0:T(8,128)(2,1)}, bf16[2,128,512]{2,1,0:T(8,128)(2,1)S(1)}, u32[]{:S(2)}, u32[]{:S(2)}) %collective-permute-start.11) | collective-permute-done | bytes 262176 | tf_op jit(solution)/shard_map/ppermute | solution.py:497
  512.6 13.7 %collective-permute-done.12 = bf16[2,128,512]{2,1,0:T(8,128)(2,1)S(1)} collective-permute-done((bf16[2,128,512]{2,1,0:T(8,128)(2,1)}, bf16[2,128,512]{2,1,0:T(8,128)(2,1)S(1)}, u32[]{:S(2)}, u32[]{:S(2)}) %collective-permute-start.12) | collective-permute-done | bytes 262176 | tf_op jit(solution)/shard_map/ppermute | solution.py:497
  526.4 15.5 %collective-permute-done.13 = bf16[2,128,512]{2,1,0:T(8,128)(2,1)S(1)} collective-permute-done((bf16[2,128,512]{2,1,0:T(8,128)(2,1)}, bf16[2,128,512]{2,1,0:T(8,128)(2,1)S(1)}, u32[]{:S(2)}, u32[]{:S(2)}) %collective-permute-start.13) | collective-permute-done | bytes 262176 | tf_op jit(solution)/shard_map/ppermute | solution.py:497
  542.8 3.1 convolution_convert_fusion.4
  551.4 3.0 pad_maximum_fusion
  554.3 7.7 %copy.81 = bf16[1536,1664]{1,0:T(8,128)(2,1)} copy(bf16[1536,1664]{0,1:T(8,128)(2,1)} %pad_maximum_fusion) | data formatting | bytes 10223616 | tf_op jit(solution)/shard_map/concatenate | solution.py:513
  562.2 2.9 collective-permute-done.24
  567.1 5.5 fusion.104
  572.7 2.7 copy.82
  579.4 3.4 dynamic-slice_bitcast_fusion
  587.9 4.0 collective-permute-start.29
  593.3 4.7 collective-permute-done.27
  598.0 4.6 collective-permute-done.29
  607.5 4.5 collective-permute-done.30
  617.7 4.0 fusion
  627.8 3.1 collective-permute-done.33
  633.0 4.0 collective-permute-done.32
  639.8 12.0 %collective-permute-done.35 = f32[24]{0:T(128)S(1)} collective-permute-done((f32[24]{0:T(128)S(1)}, f32[24]{0:T(128)S(1)}, u32[]{:S(2)}, u32[]{:S(2)}) %collective-permute-start.35) | collective-permute-done | bytes 128 | tf_op jit(solution)/shard_map/ppermute | solution.py:47
  658.2 8.2 %collective-permute-done.18 = bf16[4,24,1664]{2,1,0:T(8,128)(2,1)S(1)} collective-permute-done((bf16[4,24,1664]{2,1,0:T(8,128)(2,1)S(1)}, bf16[4,24,1664]{2,1,0:T(8,128)(2,1)S(1)}, u32[]{:S(2)}, u32[]{:S(2)}) %collective-permute-start.18) | collective-permute-done | bytes 319520 | tf_op jit(solution)/shard_map/ppermute | solution.py:93
  672.5 3.2 collective-permute-done.20
  681.1 12.9 %collective-permute-done.34 = bf16[512,1536]{1,0:T(8,128)(2,1)} collective-permute-done((bf16[512,1536]{1,0:T(8,128)(2,1)S(1)}, bf16[512,1536]{1,0:T(8,128)(2,1)}, u32[]{:S(2)}, u32[]{:S(2)}) %collective-permute-start.34) | collective-permute-done | bytes 1572896 | tf_op jit(solution)/shard_map/ppermute | solution.py:47
  699.1 5.3 fusion.7
  (323 shorter events, 121.3 us)
Async XLA Ops:
  7.2 31.3 %copy-start.59 = (bf16[768,24]{0,1:T(8,128)(2,1)S(1)}, bf16[768,24]{0,1:T(8,128)(2,1)}, u32[]{:S(2)}) copy-start(bf16[768,24]{0,1:T(8,128)(2,1)} %param.24) | copy-start | bytes 110596
  7.2 31.3 %copy-start.60 = (bf16[24,768]{1,0:T(8,128)(2,1)S(1)}, bf16[24,768]{1,0:T(8,128)(2,1)}, u32[]{:S(2)}) copy-start(bf16[24,768]{1,0:T(8,128)(2,1)} %param.21) | copy-start | bytes 110596
  38.5 10.6 %collective-permute-start.1 = (bf16[8,96,640]{2,1,0:T(8,128)(2,1)S(1)}, bf16[8,96,640]{2,1,0:T(8,128)(2,1)}, u32[]{:S(2)}, u32[]{:S(2)}) collective-permute-start(bf16[8,96,640]{2,1,0:T(8,128)(2,1)S(1)} %bitcast.217), channel_id=1, source_target_pairs={{0,8},{8,0},{1,9},{9,1},{2,10},{10,2},{3,11},{11,3},{4,12},{12,4},... | collective-permute-start | bytes 2949128 | tf_op jit(solution)/shard_map/ppermute | solution.py:47
  40.1 41.3 %all-to-all-start = ((bf16[32,24,1536]{2,1,0:T(8,128)(2,1)}), bf16[32,24,1536]{2,1,0:T(8,128)(2,1)}, u32[]{:S(2)}, u32[]{:S(2)}) async-start(bf16[32,24,1536]{2,1,0:T(8,128)(2,1)} %broadcast_in_dim.131), calls=%async_computation | async-start | bytes 4718592 | tf_op jit(solution)/shard_map/all_to_all | solution.py:56
  45.1 128.2 %all-gather.7.cloned.1.call-start = ((), (), s32[]{:S(2)}) async-start(), calls=%async_computation.12 | async-start | bytes 3932160 | tf_op jit(solution)/shard_map/all_gather | solution.py:376
  49.1 61.4 %copy-start.66 = (f32[512]{0:T(512)}, f32[512]{0:T(512)S(1)}, u32[]{:S(2)}) copy-start(f32[512]{0:T(512)S(1)} %add_rsqrt_fusion.1) | copy-start | bytes 6148
  51.8 47.3 %copy-start.41 = (bf16[1,512,384]{1,2,0:T(8,128)(2,1)S(1)}, bf16[1,512,384]{1,2,0:T(8,128)(2,1)}, u32[]{:S(2)}) copy-start(bf16[1,512,384]{1,2,0:T(8,128)(2,1)} %copy-done.40) | copy-start | bytes 1179652
  53.0 46.1 %collective-permute-start.7 = (bf16[3,384,512]{2,1,0:T(8,128)(2,1)}, bf16[3,384,512]{2,1,0:T(8,128)(2,1)}, u32[]{:S(2)}, u32[]{:S(2)}) collective-permute-start(bf16[3,384,512]{2,1,0:T(8,128)(2,1)} %pad_maximum_fusion.4), channel_id=1, source_target_pairs={{0,1},{1,0},{2,3},{3,2},{4,5},{5,4},{6,7},{7,6},{8,9},{9,8},{10,11... | collective-permute-start | bytes 3538952 | tf_op jit(solution)/shard_map/ppermute | solution.py:47
  54.1 39.9 %collective-permute-start.4 = (bf16[2,256,512]{2,1,0:T(8,128)(2,1)S(1)}, bf16[2,256,512]{2,1,0:T(8,128)(2,1)S(1)}, u32[]{:S(2)}, u32[]{:S(2)}) collective-permute-start(bf16[2,256,512]{2,1,0:T(8,128)(2,1)S(1)} %bitcast.194), channel_id=1, source_target_pairs={{0,6},{1,7},{8,14},{9,15},{16,22},{17,23},{24,30},{25,31},{32,38},... | collective-permute-start | bytes 1572872 | tf_op jit(solution)/shard_map/ppermute | solution.py:359
  58.9 35.1 %collective-permute-start.3 = (bf16[2,256,512]{2,1,0:T(8,128)(2,1)S(1)}, bf16[2,256,512]{2,1,0:T(8,128)(2,1)S(1)}, u32[]{:S(2)}, u32[]{:S(2)}) collective-permute-start(bf16[2,256,512]{2,1,0:T(8,128)(2,1)S(1)} %bitcast.195), channel_id=1, source_target_pairs={{0,4},{2,6},{1,5},{3,7},{8,12},{10,14},{9,13},{11,15},{16,20},{18,... | collective-permute-start | bytes 1572872 | tf_op jit(solution)/shard_map/ppermute | solution.py:359
  60.2 36.1 %collective-permute-start.2 = (bf16[2,256,512]{2,1,0:T(8,128)(2,1)S(1)}, bf16[2,256,512]{2,1,0:T(8,128)(2,1)S(1)}, u32[]{:S(2)}, u32[]{:S(2)}) collective-permute-start(bf16[2,256,512]{2,1,0:T(8,128)(2,1)S(1)} %bitcast.196), channel_id=1, source_target_pairs={{0,2},{2,4},{4,6},{1,3},{3,5},{5,7},{8,10},{10,12},{12,14},{9,11},... | collective-permute-start | bytes 1572872 | tf_op jit(solution)/shard_map/ppermute | solution.py:359
  96.2 383.2 %copy-start = (bf16[2,256,512]{2,1,0:T(8,128)(2,1)}, bf16[2,256,512]{2,1,0:T(8,128)(2,1)S(1)}, u32[]{:S(2)}) copy-start(bf16[2,256,512]{2,1,0:T(8,128)(2,1)S(1)} %collective-permute-done.2.kv1) | copy-start | bytes 1572868
  102.3 110.0 %all-gather.9.cloned.1.call-start = ((), (), s32[]{:S(2)}) async-start(), calls=%async_computation.13 | async-start | bytes 3932160 | tf_op jit(solution)/shard_map/all_gather | solution.py:377
  102.4 5.0 collective-permute-start
  104.8 121.6 %all-gather.11.cloned.1.call-start = ((), (), s32[]{:S(2)}) async-start(), calls=%async_computation.14 | async-start | bytes 3932160 | tf_op jit(solution)/shard_map/all_gather | solution.py:378
  110.5 26.2 %copy-start.38 = (bf16[8,2,96,1536]{3,2,1,0:T(8,128)(2,1)}, bf16[8,2,96,1536]{3,2,1,0:T(8,128)(2,1)S(1)}, u32[]{:S(2)}) copy-start(bf16[8,2,96,1536]{3,2,1,0:T(8,128)(2,1)S(1)} %pad_maximum_fusion.1) | copy-start | bytes 14155780
  116.8 19.9 %collective-permute-start.5 = (bf16[256,1536]{1,0:T(8,128)(2,1)S(1)}, bf16[256,1536]{1,0:T(8,128)(2,1)S(1)}, u32[]{:S(2)}, u32[]{:S(2)}) collective-permute-start(bf16[256,1536]{1,0:T(8,128)(2,1)S(1)} %convolution_convert_fusion.11), channel_id=1, source_target_pairs={{0,1},{1,0},{2,3},{3,2},{4,5},{5,4},{6,7},{7,6},{8,9},{9,8},{10,11... | collective-permute-start | bytes 2359304 | tf_op jit(solution)/shard_map/ppermute | solution.py:47
  122.0 18.1 %copy-start.65 = (s32[512,2]{0,1:T(2,128)S(1)}, s32[512,2]{0,1:T(2,128)}, u32[]{:S(2)}) copy-start(s32[512,2]{0,1:T(2,128)} %param.18) | copy-start | bytes 12292
  139.1 19.2 %collective-permute-start.6 = (bf16[256,1536]{1,0:T(8,128)(2,1)}, bf16[256,1536]{1,0:T(8,128)(2,1)}, u32[]{:S(2)}, u32[]{:S(2)}) collective-permute-start(bf16[256,1536]{1,0:T(8,128)(2,1)} %convolution_convert_fusion.10), channel_id=1, source_target_pairs={{0,1},{1,0},{2,3},{3,2},{4,5},{5,4},{6,7},{7,6},{8,9},{9,8},{10,11... | collective-permute-start | bytes 2359304 | tf_op jit(solution)/shard_map/ppermute | solution.py:47
  141.7 18.1 %copy-start.28 = (bf16[512,1536]{1,0:T(8,128)(2,1)S(1)}, bf16[512,1536]{1,0:T(8,128)(2,1)}, u32[]{:S(2)}) copy-start(bf16[512,1536]{1,0:T(8,128)(2,1)} %param.15) | copy-start | bytes 4718596
  165.1 40.2 %all-to-all-start.2 = ((bf16[16,48,1536]{2,1,0:T(8,128)(2,1)}), bf16[16,48,1536]{2,1,0:T(8,128)(2,1)}, u32[]{:S(2)}, u32[]{:S(2)}) async-start(bf16[16,48,1536]{2,1,0:T(8,128)(2,1)} %bitcast.231), calls=%async_computation.2 | async-start | bytes 4718592 | tf_op jit(solution)/shard_map/all_to_all | solution.py:117
  232.8 39.6 %all-to-all-start.3 = ((bf16[16,48,1536]{2,1,0:T(8,128)(2,1)}), bf16[16,48,1536]{2,1,0:T(8,128)(2,1)}, u32[]{:S(2)}, u32[]{:S(2)}) async-start(bf16[16,48,1536]{2,1,0:T(8,128)(2,1)} %bitcast.230), calls=%async_computation.3 | async-start | bytes 4718592 | tf_op jit(solution)/shard_map/all_to_all | solution.py:117
  272.4 39.5 %copy-start.21 = (f32[512,1536]{1,0:T(8,128)S(1)}, f32[512,1536]{1,0:T(8,128)}, u32[]{:S(2)}) copy-start(f32[512,1536]{1,0:T(8,128)} %copy-done.20) | copy-start | bytes 9437188
  272.4 39.5 %copy-start.32 = (bf16[512,1536]{1,0:T(8,128)(2,1)S(1)}, bf16[512,1536]{1,0:T(8,128)(2,1)}, u32[]{:S(2)}) copy-start(bf16[512,1536]{1,0:T(8,128)(2,1)} %param.16) | copy-start | bytes 4718596
  275.7 36.2 %collective-permute-start.8 = (bf16[512,1536]{1,0:T(8,128)(2,1)S(1)}, bf16[512,1536]{1,0:T(8,128)(2,1)S(1)}, u32[]{:S(2)}, u32[]{:S(2)}) collective-permute-start(bf16[512,1536]{1,0:T(8,128)(2,1)S(1)} %convolution_convert_fusion.9), channel_id=1, source_target_pairs={{0,1},{1,0},{2,3},{3,2},{4,5},{5,4},{6,7},{7,6},{8,9},{9,8},{10,11... | collective-permute-start | bytes 4718600 | tf_op jit(solution)/shard_map/ppermute | solution.py:47
  318.3 37.8 %all-to-all-start.4 = ((bf16[16,48,1536]{2,1,0:T(8,128)(2,1)}), bf16[16,48,1536]{2,1,0:T(8,128)(2,1)}, u32[]{:S(2)}, u32[]{:S(2)}) async-start(bf16[16,48,1536]{2,1,0:T(8,128)(2,1)} %bitcast.228), calls=%async_computation.4 | async-start | bytes 4718592 | tf_op jit(solution)/shard_map/all_to_all | solution.py:117
  324.0 291.8 %reduce-scatter.8.cloned.1.call-start = ((), (), s32[]{:S(2)}) async-start(), calls=%async_computation.11 | async-start | bytes 3932160 | tf_op jit(solution)/shard_map/reduce_scatter | solution.py:461
  327.9 21.0 %collective-permute-start.9 = (f32[2,512]{1,0:T(2,128)S(1)}, f32[2,512]{1,0:T(2,128)S(1)}, u32[]{:S(2)}, u32[]{:S(2)}) collective-permute-start(f32[2,512]{1,0:T(2,128)S(1)} %pad_maximum_fusion.7), channel_id=1, source_target_pairs={{0,1},{1,0},{2,3},{3,2},{4,5},{5,4},{6,7},{7,6},{8,9},{9,8},{10,11... | collective-permute-start | bytes 12296 | tf_op jit(solution)/shard_map/ppermute | solution.py:47
  362.6 253.2 %reduce-scatter.4.cloned.1.call-start = ((), (), s32[]{:S(2)}) async-start(), calls=%async_computation.9 | async-start | bytes 3932160 | tf_op jit(solution)/shard_map/reduce_scatter | solution.py:461
  388.5 37.7 %all-to-all-start.5 = ((bf16[16,48,1536]{2,1,0:T(8,128)(2,1)}), bf16[16,48,1536]{2,1,0:T(8,128)(2,1)}, u32[]{:S(2)}, u32[]{:S(2)}) async-start(bf16[16,48,1536]{2,1,0:T(8,128)(2,1)} %bitcast.229), calls=%async_computation.5 | async-start | bytes 4718592 | tf_op jit(solution)/shard_map/all_to_all | solution.py:117
  394.1 221.7 %reduce-scatter.6.cloned.1.call-start = ((), (), s32[]{:S(2)}) async-start(), calls=%async_computation.10 | async-start | bytes 3932160 | tf_op jit(solution)/shard_map/reduce_scatter | solution.py:461
  430.5 36.6 %collective-permute-start.10 = (bf16[512,1536]{1,0:T(8,128)(2,1)}, bf16[512,1536]{1,0:T(8,128)(2,1)}, u32[]{:S(2)}, u32[]{:S(2)}) collective-permute-start(bf16[512,1536]{1,0:T(8,128)(2,1)} %convolution_convert_fusion.8), channel_id=1, source_target_pairs={{0,1},{1,0},{2,3},{3,2},{4,5},{5,4},{6,7},{7,6},{8,9},{9,8},{10,11... | collective-permute-start | bytes 4718600 | tf_op jit(solution)/shard_map/ppermute | solution.py:47
  439.3 33.0 %copy-start.22 = (f32[512,1536]{1,0:T(8,128)S(1)}, f32[512,1536]{1,0:T(8,128)}, u32[]{:S(2)}) copy-start(f32[512,1536]{1,0:T(8,128)} %copy-done.20) | copy-start | bytes 9437188
  439.3 33.0 %copy-start.24 = (f32[512,1536]{1,0:T(8,128)S(1)}, f32[512,1536]{1,0:T(8,128)}, u32[]{:S(2)}) copy-start(f32[512,1536]{1,0:T(8,128)} %copy-done.23) | copy-start | bytes 9437188
  439.3 33.0 %copy-start.25 = (f32[512,1536]{1,0:T(8,128)S(1)}, f32[512,1536]{1,0:T(8,128)}, u32[]{:S(2)}) copy-start(f32[512,1536]{1,0:T(8,128)} %fusion.84) | copy-start | bytes 9437188
  487.2 55.5 %copy-start.57 = (f32[1536]{0:T(1024)S(1)}, f32[1536]{0:T(1024)}, u32[]{:S(2)}) copy-start(f32[1536]{0:T(1024)} %copy-done.55) | copy-start | bytes 18436
  487.2 55.5 %copy-start.67 = (f32[512]{0:T(512)S(1)}, f32[512]{0:T(512)}, u32[]{:S(2)}) copy-start(f32[512]{0:T(512)} %copy-done.66) | copy-start | bytes 6148
  493.6 19.0 %collective-permute-start.11 = (bf16[2,128,512]{2,1,0:T(8,128)(2,1)}, bf16[2,128,512]{2,1,0:T(8,128)(2,1)S(1)}, u32[]{:S(2)}, u32[]{:S(2)}) collective-permute-start(bf16[2,128,512]{2,1,0:T(8,128)(2,1)} %get-tuple-element.71), channel_id=1, source_target_pairs={{2,0},{4,2},{6,4},{3,1},{5,3},{7,5},{10,8},{12,10},{14,12},{11,9},... | collective-permute-start | bytes 786440 | tf_op jit(solution)/shard_map/ppermute | solution.py:497
  494.9 31.4 %collective-permute-start.12 = (bf16[2,128,512]{2,1,0:T(8,128)(2,1)}, bf16[2,128,512]{2,1,0:T(8,128)(2,1)S(1)}, u32[]{:S(2)}, u32[]{:S(2)}) collective-permute-start(bf16[2,128,512]{2,1,0:T(8,128)(2,1)} %get-tuple-element.72), channel_id=1, source_target_pairs={{4,0},{6,2},{5,1},{7,3},{12,8},{14,10},{13,9},{15,11},{20,16},{22,... | collective-permute-start | bytes 786440 | tf_op jit(solution)/shard_map/ppermute | solution.py:497
  496.2 45.6 %collective-permute-start.13 = (bf16[2,128,512]{2,1,0:T(8,128)(2,1)}, bf16[2,128,512]{2,1,0:T(8,128)(2,1)S(1)}, u32[]{:S(2)}, u32[]{:S(2)}) collective-permute-start(bf16[2,128,512]{2,1,0:T(8,128)(2,1)} %get-tuple-element.73), channel_id=1, source_target_pairs={{6,0},{7,1},{14,8},{15,9},{22,16},{23,17},{30,24},{31,25},{38,32},... | collective-permute-start | bytes 786440 | tf_op jit(solution)/shard_map/ppermute | solution.py:497
  545.9 16.3 %collective-permute-start.22 = (bf16[2,128,512]{2,1,0:T(8,128)(2,1)S(1)}, bf16[2,128,512]{2,1,0:T(8,128)(2,1)S(1)}, u32[]{:S(2)}, u32[]{:S(2)}) collective-permute-start(bf16[2,128,512]{2,1,0:T(8,128)(2,1)S(1)} %copy-done.7), channel_id=1, source_target_pairs={{2,0},{4,2},{6,4},{3,1},{5,3},{7,5},{10,8},{12,10},{14,12},{11,9},... | collective-permute-start | bytes 786440 | tf_op jit(solution)/shard_map/ppermute | solution.py:497
  547.3 14.9 %collective-permute-start.23 = (bf16[2,128,512]{2,1,0:T(8,128)(2,1)S(1)}, bf16[2,128,512]{2,1,0:T(8,128)(2,1)S(1)}, u32[]{:S(2)}, u32[]{:S(2)}) collective-permute-start(bf16[2,128,512]{2,1,0:T(8,128)(2,1)S(1)} %copy-done.5), channel_id=1, source_target_pairs={{4,0},{6,2},{5,1},{7,3},{12,8},{14,10},{13,9},{15,11},{20,16},{22,... | collective-permute-start | bytes 786440 | tf_op jit(solution)/shard_map/ppermute | solution.py:497
  548.6 16.5 %collective-permute-start.24 = (bf16[2,128,512]{2,1,0:T(8,128)(2,1)S(1)}, bf16[2,128,512]{2,1,0:T(8,128)(2,1)S(1)}, u32[]{:S(2)}, u32[]{:S(2)}) collective-permute-start(bf16[2,128,512]{2,1,0:T(8,128)(2,1)S(1)} %copy-done.3), channel_id=1, source_target_pairs={{6,0},{7,1},{14,8},{15,9},{22,16},{23,17},{30,24},{31,25},{38,32},... | collective-permute-start | bytes 786440 | tf_op jit(solution)/shard_map/ppermute | solution.py:497
  579.4 3.9 collective-permute-start.26
  582.7 34.9 %collective-permute-start.14 = (bf16[8,96,1664]{2,1,0:T(8,128)(2,1)}, bf16[8,96,1664]{2,1,0:T(8,128)(2,1)}, u32[]{:S(2)}, u32[]{:S(2)}) collective-permute-start(bf16[8,96,1664]{2,1,0:T(8,128)(2,1)} %dynamic-slice_bitcast_fusion), channel_id=1, source_target_pairs={{0,8},{8,0},{1,9},{9,1},{2,10},{10,2},{3,11},{11,3},{4,12},{12,4},... | collective-permute-start | bytes 7667720 | tf_op jit(solution)/shard_map/ppermute | solution.py:47
  585.7 12.2 %collective-permute-start.27 = (bf16[8,24,640]{2,1,0:T(8,128)(2,1)S(1)}, bf16[8,24,640]{2,1,0:T(8,128)(2,1)S(1)}, u32[]{:S(2)}, u32[]{:S(2)}) collective-permute-start(bf16[8,24,640]{2,1,0:T(8,128)(2,1)S(1)} %get-tuple-element.179), channel_id=1, source_target_pairs={{0,2},{2,4},{4,6},{6,0},{1,3},{3,5},{5,7},{7,1},{8,10},{10,12},{12... | collective-permute-start | bytes 737288 | tf_op jit(solution)/shard_map/ppermute | solution.py:93
  587.9 14.7 %collective-permute-start.29 = (bf16[8,24,640]{2,1,0:T(8,128)(2,1)S(1)}, bf16[8,24,640]{2,1,0:T(8,128)(2,1)S(1)}, u32[]{:S(2)}, u32[]{:S(2)}) collective-permute-start(bf16[8,24,640]{2,1,0:T(8,128)(2,1)S(1)} %get-tuple-element.180), channel_id=1, source_target_pairs={{0,6},{2,0},{4,2},{6,4},{1,7},{3,1},{5,3},{7,5},{8,14},{10,8},{12,... | collective-permute-start | bytes 737288 | tf_op jit(solution)/shard_map/ppermute | solution.py:93
  591.9 12.5 %collective-permute-start.28 = (bf16[8,24,640]{2,1,0:T(8,128)(2,1)S(1)}, bf16[8,24,640]{2,1,0:T(8,128)(2,1)S(1)}, u32[]{:S(2)}, u32[]{:S(2)}) collective-permute-start(bf16[8,24,640]{2,1,0:T(8,128)(2,1)S(1)} %get-tuple-element.181), channel_id=1, source_target_pairs={{0,4},{2,6},{4,0},{6,2},{1,5},{3,7},{5,1},{7,3},{8,12},{10,14},{12... | collective-permute-start | bytes 737288 | tf_op jit(solution)/shard_map/ppermute | solution.py:93
  605.5 6.5 collective-permute-start.30
  613.3 13.6 %collective-permute-start.31 = (bf16[24,640]{1,0:T(8,128)(2,1)}, bf16[24,640]{1,0:T(8,128)(2,1)S(1)}, u32[]{:S(2)}, u32[]{:S(2)}) collective-permute-start(bf16[24,640]{1,0:T(8,128)(2,1)} %get-tuple-element.191), channel_id=1, source_target_pairs={{0,16},{16,32},{32,48},{48,0},{1,17},{17,33},{33,49},{49,1},{2,18}... | collective-permute-start | bytes 92168 | tf_op jit(solution)/shard_map/ppermute | solution.py:93
  621.8 30.4 %collective-permute-start.15 = (bf16[8,24,1664]{2,1,0:T(8,128)(2,1)S(1)}, bf16[8,24,1664]{2,1,0:T(8,128)(2,1)}, u32[]{:S(2)}, u32[]{:S(2)}) collective-permute-start(bf16[8,24,1664]{2,1,0:T(8,128)(2,1)S(1)} %get-tuple-element.165), channel_id=1, source_target_pairs={{0,2},{2,4},{4,6},{6,0},{1,3},{3,5},{5,7},{7,1},{8,10},{10,12},{12... | collective-permute-start | bytes 1916936 | tf_op jit(solution)/shard_map/ppermute | solution.py:93
  623.1 29.2 %collective-permute-start.17 = (bf16[8,24,1664]{2,1,0:T(8,128)(2,1)S(1)}, bf16[8,24,1664]{2,1,0:T(8,128)(2,1)}, u32[]{:S(2)}, u32[]{:S(2)}) collective-permute-start(bf16[8,24,1664]{2,1,0:T(8,128)(2,1)S(1)} %get-tuple-element.166), channel_id=1, source_target_pairs={{0,6},{2,0},{4,2},{6,4},{1,7},{3,1},{5,3},{7,5},{8,14},{10,8},{12,... | collective-permute-start | bytes 1916936 | tf_op jit(solution)/shard_map/ppermute | solution.py:93
  625.1 27.1 %collective-permute-start.16 = (bf16[8,24,1664]{2,1,0:T(8,128)(2,1)S(1)}, bf16[8,24,1664]{2,1,0:T(8,128)(2,1)}, u32[]{:S(2)}, u32[]{:S(2)}) collective-permute-start(bf16[8,24,1664]{2,1,0:T(8,128)(2,1)S(1)} %get-tuple-element.167), channel_id=1, source_target_pairs={{0,4},{2,6},{4,0},{6,2},{1,5},{3,7},{5,1},{7,3},{8,12},{10,14},{12... | collective-permute-start | bytes 1916936 | tf_op jit(solution)/shard_map/ppermute | solution.py:93
  626.4 29.9 %collective-permute-start.25 = (bf16[3,384,512]{2,1,0:T(8,128)(2,1)}, bf16[3,384,512]{2,1,0:T(8,128)(2,1)}, u32[]{:S(2)}, u32[]{:S(2)}) collective-permute-start(bf16[3,384,512]{2,1,0:T(8,128)(2,1)} %broadcast_select_fusion), channel_id=1, source_target_pairs={{0,1},{1,0},{2,3},{3,2},{4,5},{5,4},{6,7},{7,6},{8,9},{9,8},{10,11... | collective-permute-start | bytes 3538952 | tf_op jit(solution)/shard_map/ppermute | solution.py:47
  627.0 4.0 collective-permute-start.33
  631.5 5.5 collective-permute-start.32
  633.0 23.3 %copy-start.31 = (bf16[3,384,1024]{2,1,0:T(8,128)(2,1)S(1)}, bf16[3,384,1024]{2,1,0:T(8,128)(2,1)}, u32[]{:S(2)}) copy-start(bf16[3,384,1024]{2,1,0:T(8,128)(2,1)} %copy-done.30) | copy-start | bytes 7077892
  638.0 13.7 %collective-permute-start.35 = (f32[24]{0:T(128)S(1)}, f32[24]{0:T(128)S(1)}, u32[]{:S(2)}, u32[]{:S(2)}) collective-permute-start(f32[24]{0:T(128)S(1)} %fusion.88), channel_id=1, source_target_pairs={{0,1},{1,0},{2,3},{3,2},{4,5},{5,4},{6,7},{7,6},{8,9},{9,8},{10,11... | collective-permute-start | bytes 296 | tf_op jit(solution)/shard_map/ppermute | solution.py:47
  654.3 12.1 %collective-permute-start.18 = (bf16[4,24,1664]{2,1,0:T(8,128)(2,1)S(1)}, bf16[4,24,1664]{2,1,0:T(8,128)(2,1)S(1)}, u32[]{:S(2)}, u32[]{:S(2)}) collective-permute-start(bf16[4,24,1664]{2,1,0:T(8,128)(2,1)S(1)} %dynamic-slice_bitcast_fusion.4), channel_id=1, source_target_pairs={{0,64},{64,0},{1,65},{65,1},{2,66},{66,2},{3,67},{67,3},{4,68},{68... | collective-permute-start | bytes 958472 | tf_op jit(solution)/shard_map/ppermute | solution.py:93
  658.1 35.9 %collective-permute-start.34 = (bf16[512,1536]{1,0:T(8,128)(2,1)S(1)}, bf16[512,1536]{1,0:T(8,128)(2,1)}, u32[]{:S(2)}, u32[]{:S(2)}) collective-permute-start(bf16[512,1536]{1,0:T(8,128)(2,1)S(1)} %copy-done.37), channel_id=1, source_target_pairs={{0,1},{1,0},{2,3},{3,2},{4,5},{5,4},{6,7},{7,6},{8,9},{9,8},{10,11... | collective-permute-start | bytes 4718600 | tf_op jit(solution)/shard_map/ppermute | solution.py:47
  666.5 5.7 collective-permute-start.19
  668.1 4.4 collective-permute-start.21
  669.8 24.8 %copy-start.58 = (f32[1536]{0:T(1024)S(1)}, f32[1536]{0:T(1024)}, u32[]{:S(2)}) copy-start(f32[1536]{0:T(1024)} %copy-done.55) | copy-start | bytes 18436
  669.8 5.9 collective-permute-start.20
  (59 other events, 223.2 us)
Sparse Core Ops, SparseCore 0:
  102.4 41.0 all-gather.6
  145.2 39.7 all-gather.8
  186.6 39.7 all-gather.10
  362.7 40.5 reduce-scatter.7
  405.6 37.9 reduce-scatter.3
  445.8 37.9 reduce-scatter.5

commit v3 on v2

--- a/solution.py
+++ b/solution.py
@@ -51,38 +51,28 @@
     return mine.astype(F32) + other.astype(F32)
 
 
-def ring_gather(shard):
-    rows, cols = shard.shape
-    return lax.all_to_all(jnp.broadcast_to(shard[None], (32, rows, cols)), RING, 0, 0, tiled=True)
+def gather_hy(shard):
+    wide = jnp.broadcast_to(shard[None], (8, *shard.shape))
+    return lax.all_to_all(wide, ("h", "y"), 0, 0, tiled=True)
+
+
+def gather_x(shards):
+    wide = jnp.broadcast_to(shards[None], (4, *shards.shape))
+    return lax.all_to_all(wide, "x", 0, 0, tiled=True)
 
 
 def core_gather(mine):
-    rows, cols = mine.shape[1:]
-    mine = mine.reshape(8, 4 * rows, cols)
+    rows, cols = mine.shape[2:]
+    mine = mine.reshape(4, 2, 4 * rows, cols)
     other = swap(mine, "c")
+    mine, other = mine.transpose(1, 0, 2, 3), other.transpose(1, 0, 2, 3)
     first = lax.axis_index("c") == 0
-    pair = jnp.stack([jnp.where(first, mine, other), jnp.where(first, other, mine)], axis=1)
+    pair = jnp.stack([jnp.where(first, mine, other), jnp.where(first, other, mine)], axis=2)
     return pair.reshape(64 * rows, cols)
 
 
 def after(value, *earlier):
     return lax.optimization_barrier((value,) + earlier)[0]
-
-
-def pair_sum(partial):
-    total_rows, cols = partial.shape
-    rows = total_rows // 64
-    parts = partial.reshape(8, 2, 4 * rows, cols)
-    core = lax.axis_index("c")
-    mine = lax.dynamic_index_in_dim(parts, core, 1, keepdims=False)
-    theirs = lax.dynamic_index_in_dim(parts, 1 - core, 1, keepdims=False)
-    paired = (mine.astype(F32) + swap(theirs, "c").astype(F32)).astype(BF)
-    return paired.reshape(32, rows, cols)
-
-
-def ring_sum(paired):
-    moved = lax.all_to_all(paired, RING, 0, 0, tiled=True)
-    return jnp.sum(moved.astype(F32), axis=0)
 
 
 def axis_parts(parts, axis, size):
@@ -99,17 +89,6 @@
     for part in parts[1:]:
         total = total + part.astype(F32)
     return total
-
-
-def y_parts(paired):
-    rows, cols = paired.shape[1:]
-    return axis_parts(paired.reshape(8, 4, rows, cols).transpose(1, 0, 2, 3), "y", 4)
-
-
-def hx_sum(parts):
-    by_y = added(parts).astype(BF)
-    by_h = added(axis_parts(by_y.reshape(2, 4, *by_y.shape[1:]), "h", 2)).astype(BF)
-    return added(axis_parts(by_h, "x", 4))
 
 
 def exchange_slots(rows):
@@ -297,16 +276,215 @@
         + [pltpu.VMEM((4, SPAN, HEAD_WIDTH), BF)] * 2
         + [pltpu.VMEM((4, HEAD_WIDTH, SPAN), BF)]
         + [pltpu.VMEM((4, SPAN, HEAD_WIDTH), F32)] * 2,
+        compiler_params=pltpu.CompilerParams(vmem_limit_bytes=60 << 20),
+        cost_estimate=pl.CostEstimate(
+            flops=150_000_000_000, bytes_accessed=6_000_000, transcendentals=6_000_000
+        ),
+    )(y, q_t, d_t, *outs, *lses, *kvs, seg_q, seg_k)
+
+
+def flat(ref):
+    return ref[...].reshape(ref.shape[0] * ref.shape[2], ref.shape[3])
+
+
+def experts_kernel(x_ref, gate_ref, up_ref, down_ref, g_ref, u_ref, inner_ref, out_ref, acc):
+    step = pl.program_id(0)
+    down_t = flat(down_ref).T
+
+    @pl.when(step == 0)
+    def _():
+        acc[...] = jnp.zeros_like(acc)
+
+    x = x_ref[...]
+    g_ref[...] = nn(x, flat(gate_ref))
+    u_ref[...] = nn(x, flat(up_ref))
+    for m in range(x_ref.shape[0] // HALF):
+        rows = slice(m * HALF, (m + 1) * HALF)
+        gate = g_ref[rows]
+        inner_ref[rows] = (gate * jax.nn.sigmoid(gate) * u_ref[rows]).astype(BF)
+    for n in range(acc.shape[1] // SPAN):
+        cols = slice(n * SPAN, (n + 1) * SPAN)
+        acc[:, cols] += nn(inner_ref[...], down_t[:, cols])
+
+    @pl.when(step == pl.num_programs(0) - 1)
+    def _():
+        out_ref[...] = acc[...].astype(BF)
+
+
+def experts_back_kernel(
+    d_ref, g_ref, u_ref, gate_ref, up_ref, down_ref, dg_ref, du_ref, out_ref, acc, inner
+):
+    step = pl.program_id(0)
+    gate_t = flat(gate_ref).T
+    up_t = flat(up_ref).T
+
+    @pl.when(step == 0)
+    def _():
+        acc[...] = jnp.zeros_like(acc)
+
+    inner[...] = nn(d_ref[...], flat(down_ref))
+    for m in range(d_ref.shape[0] // HALF):
+        rows = slice(m * HALF, (m + 1) * HALF)
+        d_inner = inner[rows]
+        gate = g_ref[rows]
+        sig = jax.nn.sigmoid(gate)
+        dg_ref[rows] = (d_inner * u_ref[rows] * sig * (1.0 + gate * (1.0 - sig))).astype(BF)
+        du_ref[rows] = (d_inner * gate * sig).astype(BF)
+    for n in range(acc.shape[1] // SPAN):
+        cols = slice(n * SPAN, (n + 1) * SPAN)
+        acc[:, cols] += nn(dg_ref[...], gate_t[:, cols]) + nn(du_ref[...], up_t[:, cols])
+
+    @pl.when(step == pl.num_programs(0) - 1)
+    def _():
+        out_ref[...] = acc[...].astype(BF)
+
+
+def expert_grads_kernel(x_ref, d_ref, dg_ref, du_ref, inner_ref, out_ref, x_t, d_t):
+    @pl.when(pl.program_id(0) == 0)
+    def _():
+        x_t[...] = x_ref[...].T
+        d_t[...] = d_ref[...].T
+
+    depth = out_ref.shape[2]
+    for i, (left, right) in enumerate(((x_t, dg_ref), (x_t, du_ref), (d_t, inner_ref))):
+        for y in range(4):
+            out_ref[y, i] = nn(left[y * depth : (y + 1) * depth], right[...]).astype(BF)
+
+
+def expert_specs(rows, width, hidden):
+    whole = pl.BlockSpec((rows, width), lambda b: (0, 0))
+    weights = [
+        pl.BlockSpec((4, 1, width // 4, HALF), functools.partial(lambda i, b: (0, i, 0, b), i))
+        for i in range(3)
+    ]
+    column = pl.BlockSpec((rows, HALF), lambda b: (0, b))
+    return dict(
+        grid=(hidden // HALF,),
+        scratch_shapes=[pltpu.VMEM((rows, width), F32)],
+        compiler_params=pltpu.CompilerParams(vmem_limit_bytes=60 << 20),
+        cost_estimate=pl.CostEstimate(
+            flops=6 * rows * width * hidden, bytes_accessed=20_000_000, transcendentals=rows * hidden
+        ),
+    ), whole, weights, column
+
+
+def run_experts(x, experts_full):
+    rows, width = x.shape
+    hidden = experts_full.shape[3]
+    common, whole, weights, column = expert_specs(rows, width, hidden)
+    wide = jax.ShapeDtypeStruct((rows, hidden), F32)
+    return pl.pallas_call(
+        experts_kernel,
+        in_specs=[whole] + weights,
+        out_specs=[column, column, column, whole],
+        out_shape=[
+            wide,
+            wide,
+            jax.ShapeDtypeStruct((rows, hidden), BF),
+            jax.ShapeDtypeStruct((rows, width), BF),
+        ],
+        **common,
+    )(x, experts_full, experts_full, experts_full)
+
+
+def run_experts_back(d, gate, up, experts_full):
+    rows, width = d.shape
+    hidden = experts_full.shape[3]
+    common, whole, weights, column = expert_specs(rows, width, hidden)
+    low = jax.ShapeDtypeStruct((rows, hidden), BF)
+    common["scratch_shapes"] = common["scratch_shapes"] + [pltpu.VMEM((rows, HALF), F32)]
+    return pl.pallas_call(
+        experts_back_kernel,
+        in_specs=[whole, column, column] + weights,
+        out_specs=[column, column, whole],
+        out_shape=[low, low, jax.ShapeDtypeStruct((rows, width), BF)],
+        **common,
+    )(d, gate, up, experts_full, experts_full, experts_full)
+
+
+def expert_grads(x, d, d_gate, d_up, inner):
+    rows, width = x.shape
+    hidden = inner.shape[1]
+    common, whole, _, column = expert_specs(rows, width, hidden)
+    common["scratch_shapes"] = [pltpu.VMEM((width, rows), BF)] * 2
+    return pl.pallas_call(
+        expert_grads_kernel,
+        in_specs=[whole, whole, column, column, column],
+        out_specs=pl.BlockSpec((4, 3, width // 4, HALF), lambda b: (0, 0, 0, b)),
+        out_shape=jax.ShapeDtypeStruct((4, 3, width // 4, hidden), BF),
+        **common,
+    )(x, d, d_gate, d_up, inner)
+
+
+def grads_kernel(plan, first_axis, core_ref, *refs):
+    ins, (own_ref, other_ref, pack) = refs[:-3], refs[-3:]
+    at = 0
+    turned = {}
+    for terms in plan:
+        total = None
+        for left, right, first in terms:
+            if left is None:
+                high = ins[right][...].astype(BF).astype(F32)
+                rest = ins[right][...] - high
+                total = jnp.zeros((384, 128), F32) if total is None else total
+                pack[:, at : at + 128] = total
+                pack[:, at + 16 : at + 24] = high.T
+                pack[:, at + 24 : at + 32] = rest.T
+                total = None
+                at = at + 128
+                continue
+            if left not in turned:
+                turned[left] = ins[left][...].T
+            width = ins[right].shape[1]
+            rows = turned[left][:, first : first + width]
+            piece = dot(rows, ins[right][...], 1, 1)
+            total = piece if total is None else total + piece
+        if total is not None:
+            pack[:, at : at + total.shape[1]] = total
+            at = at + total.shape[1]
+    for core in range(2):
+
+        @pl.when(core_ref[0] == core)
+        def _(core=core):
+            for j in range(2):
+                for y in range(4):
+                    for ref, c in ((own_ref, core), (other_ref, 1 - core)):
+                        row = (2 * j + c) * 96 + y * 24
+                        value = pack[row : row + 24, :].astype(BF)
+                        if first_axis == "x":
+                            ref[j, y, 0] = value
+                        else:
+                            ref[y, j, 0] = value
+
+
+def pack_grads(plan, first_axis, arrays, wide, cols):
+    specs = []
+    for i, value in enumerate(arrays):
+        if i in wide:
+            specs.append(pl.BlockSpec((value.shape[0], 384), lambda b: (0, b)))
+        else:
+            specs.append(pl.BlockSpec(value.shape, lambda b: (0, 0)))
+    out = jax.ShapeDtypeStruct((4, 4, 2, 24, cols), BF)
+    if first_axis == "x":
+        out_spec = pl.BlockSpec((2, 4, 1, 24, cols), lambda b: (b % 2, 0, b // 2, 0, 0))
+    else:
+        out_spec = pl.BlockSpec((4, 2, 1, 24, cols), lambda b: (0, b % 2, b // 2, 0, 0))
+    return pl.pallas_call(
+        functools.partial(grads_kernel, plan, first_axis),
+        grid=(arrays[wide[0]].shape[1] // 384,),
+        in_specs=[pl.BlockSpec(memory_space=pltpu.SMEM)] + specs,
+        out_specs=[out_spec, out_spec],
+        out_shape=[out, out],
+        scratch_shapes=[pltpu.VMEM((384, cols), F32)],
         compiler_params=pltpu.CompilerParams(vmem_limit_bytes=40 << 20),
         cost_estimate=pl.CostEstimate(
-            flops=28_000_000_000, bytes_accessed=6_000_000, transcendentals=6_000_000
+            flops=20_000_000_000, bytes_accessed=12_000_000, transcendentals=0
         ),
-    )(y, q_t, d_t, *outs, *lses, *kvs, seg_q, seg_k)
-
-
-def split_bf16(value):
-    high = value.astype(BF)
-    return high, (value - high.astype(F32)).astype(BF)
+    )(jnp.full((1,), lax.axis_index("c"), jnp.int32), *arrays)
+
+
+def paired(own, theirs):
+    return (own.astype(F32) + swap(theirs, "c").astype(F32)).astype(BF)
 
 
 def local(
@@ -341,11 +519,12 @@
         ],
         axis=1,
     )
-    ring_kv = ring_gather(jnp.concatenate([key_weight, value_weight, small], axis=1))
-    pack_kv = core_gather(ring_kv)
-    ring_rest = ring_gather(jnp.concatenate([w_query, w_out.T], axis=1))
-    full_kv = pack_kv[:, : 2 * k_width]
-    full_small = pack_kv[:, 2 * k_width :]
+    by_hy = gather_hy(jnp.concatenate([key_weight, value_weight, small, w_query, w_out.T], axis=1))
+    kv_cols = 2 * k_width + 128
+    pack = core_gather(gather_x(by_hy[:, :, :kv_cols]))
+    full_kv = pack[:, : 2 * k_width]
+    full_small = pack[:, 2 * k_width :]
+    ring_rest = gather_x(by_hy[:, :, kv_cols:])
     small_rows = dot(jnp.eye(24, 128, dtype=BF), full_small, 1, 1)
     router_rows = small_rows[:EXPERTS].astype(BF)
     gain_one = small_rows[EXPERTS : EXPERTS + 1]
@@ -359,23 +538,18 @@
         lax.ppermute(kv_mine, "y", [(i, i + r) for i in range(4 - r)]) for r in (1, 2, 3)
     ]
     kvs[1:] = lax.optimization_barrier((*kvs[1:], ring_rest))[:3]
-    pack_rest = core_gather(ring_rest)
-    full_query = pack_rest[:, :q_width]
-    full_out = pack_rest[:, q_width:]
+    rest = core_gather(ring_rest)
+    full_query = rest[:, :q_width]
+    full_out = rest[:, q_width:]
     query_t = dot(full_query, act_one, 0, 1).astype(BF)
 
-    experts = jnp.stack([w_gate[0], w_up[0], w_down[0].T])
-    experts_other = after(swap(after(experts, kv_mine), "t"), kvs[1], kvs[2], kvs[3])
-    experts_full = jnp.concatenate(
-        [
-            jnp.where(tix == 0, experts, experts_other),
-            jnp.where(tix == 0, experts_other, experts),
-        ],
-        axis=2,
-    )
-    gate_full = lax.all_gather(experts_full[0], "y", axis=0, tiled=True)
-    up_full = lax.all_gather(experts_full[1], "y", axis=0, tiled=True)
-    down_full = lax.all_gather(experts_full[2], "y", axis=0, tiled=True)
+    late_gate, late_up, late_down = lax.optimization_barrier(
+        (w_gate[0], w_up[0], w_down[0], kv_mine)
+    )[:3]
+    experts = jnp.stack([late_gate, late_up, late_down.T])
+    experts_other = after(swap(experts, "t"), kvs[1], kvs[2], kvs[3])
+    experts_full = jnp.concatenate([experts, experts_other], axis=2)
+    experts_full = lax.all_gather(experts_full, "y", axis=0)
 
     seg_blocks = segments[0].reshape(4, tok_rows)
     seg_mine = lax.dynamic_index_in_dim(seg_blocks, yix, 0, keepdims=False)
@@ -422,11 +596,8 @@
     ).astype(BF)
 
     received = exchange_slots(dot(pick, act_two, 1, 0).astype(BF))
-    gate_proj = dot(received, gate_full, 1, 0)
-    up_proj = dot(received, up_full, 1, 0)
-    inner = (jax.nn.silu(gate_proj) * up_proj).astype(BF)
-
-    returned = exchange_slots(dot(inner, down_full, 1, 1).astype(BF))
+    gate_proj, up_proj, inner, slots_out = run_experts(received, experts_full)
+    returned = exchange_slots(slots_out)
     part = dot(gated_pick, returned, 0, 0).astype(BF)
     output = hidden + both(part, swap(part, "t"))
     valid = (seg_mine != 0).astype(F32)
@@ -445,26 +616,18 @@
     d_received = after(d_received, d_gates_other)
     d_gates = d_gates + d_gates_other
 
-    d_inner = dot(d_received, down_full, 1, 0)
-    sig_gate = jax.nn.sigmoid(gate_proj)
-    d_gate_proj = (d_inner * up_proj * sig_gate * (1.0 + gate_proj * (1.0 - sig_gate))).astype(BF)
-    d_up_proj = (d_inner * gate_proj * sig_gate).astype(BF)
-    d_slots = dot(d_gate_proj, gate_full, 1, 1) + dot(d_up_proj, up_full, 1, 1)
-    d_returned = exchange_slots(d_slots.astype(BF))
-
-    grad_parts = [
-        dot(received, d_gate_proj, 0, 0).astype(BF),
-        dot(received, d_up_proj, 0, 0).astype(BF),
-        dot(d_received, inner, 0, 0).astype(BF),
-    ]
-    grad_experts = [
-        lax.psum_scatter(part, "y", scatter_dimension=0, tiled=True) for part in grad_parts
-    ]
-    d_returned = after(d_returned, *grad_parts)
-    grad_stack = jnp.stack(grad_experts)
-    ff_half = grad_stack.shape[2] // 2
-    keep = jnp.where(tix == 0, grad_stack[:, :, :ff_half], grad_stack[:, :, ff_half:])
-    give = jnp.where(tix == 0, grad_stack[:, :, ff_half:], grad_stack[:, :, :ff_half])
+    d_gate_proj, d_up_proj, d_slots = run_experts_back(
+        d_received, gate_proj, up_proj, experts_full
+    )
+    d_returned = exchange_slots(d_slots)
+    received, d_received = after(received, d_slots), after(d_received, d_slots)
+
+    grad_parts = expert_grads(received, d_received, d_gate_proj, d_up_proj, inner)
+    grad_experts = lax.psum_scatter(grad_parts, "y", scatter_dimension=0)
+    d_returned = after(d_returned, grad_parts)
+    ff_half = w_gate.shape[2]
+    keep = grad_experts[:, :, :ff_half]
+    give = grad_experts[:, :, ff_half:]
 
     d_router = jnp.where(named[0], d_gates[0:1] * weight_cols[0:1], 0.0) + jnp.where(
         named[1], d_gates[1:2] * weight_cols[1:2], 0.0
@@ -472,79 +635,107 @@
     d_logits = (
         router * (d_router - jnp.sum(router * d_router, axis=0, keepdims=True))
     ).astype(BF)
-    grad_router = dot(act_two, d_logits, 0, 1)
     d_route = dot(d_logits, router_rows, 0, 0)
     part = dot(pick, d_returned, 0, 0).astype(BF)
-    d_act_two = d_route + both(part, after(swap(part, "t"), d_route, grad_router))
+    d_act_two = d_route + both(part, after(swap(part, "t"), d_route))
     d_norm_two, grad_gain_two = norm_back(hidden, scale_two, gain_two, d_act_two)
     d_hidden = grad_output + d_norm_two
     d_attn = d_hidden.astype(BF)
     d_mixed_t = dot(full_out, d_attn, 0, 1).astype(BF)
 
-    sse_high, sse_low = split_bf16(jnp.full((1, feat_width), sse))
-    count_high, count_low = split_bf16(jnp.full((1, feat_width), count))
-    gain_high, gain_low = split_bf16(grad_gain_two)
-    lines = jnp.concatenate(
-        [gain_high, gain_low, sse_high, sse_low, count_high, count_low, jnp.zeros((2, feat_width), BF)]
-    )
-    extra = dot(lines, jnp.eye(8, 128 - EXPERTS, dtype=BF), 0, 0)
-    rest_small = jnp.concatenate([grad_router, extra], axis=1).astype(BF)
-
-    saved = (d_mixed_t, (mixed_0, mixed_1), (log_0, log_1), kvs, seg_mine[None], seg_keys)
+    saved = ((mixed_0, mixed_1), (log_0, log_1), kvs, seg_mine[None], seg_keys)
+    half_groups = k_width // HEAD_WIDTH // 2
+    back_0 = attend_back(0, half_groups, place_y, query_t, d_mixed_t, *saved)
 
     def ring_back(parts):
         return [
             lax.ppermute(parts[r], "y", [(i, i - r) for i in range(r, 4)]) for r in (1, 2, 3)
         ]
 
-    kv_groups = k_width // HEAD_WIDTH
-    back_0 = attend_back(0, kv_groups // 2, place_y, query_t, *saved)
+    *back_0, d_mixed_t, give = lax.optimization_barrier((*back_0, d_mixed_t, give))
+    back_1 = attend_back(half_groups, half_groups, place_y, query_t, d_mixed_t, *saved)
     others_0 = ring_back(back_0[1:])
-    back_1 = attend_back(
-        kv_groups // 2, kv_groups // 2, place_y, after(query_t, back_0[0]), *saved
-    )
-    back_1 = lax.optimization_barrier((*back_1, *others_0))[:5]
+    given = swap(give, "t")
+    *back_1, o1, o2, o3, given, d_attn_late, gain_late, d_logits_late, back_0[0] = (
+        lax.optimization_barrier(
+            (*back_1, *others_0, given, d_attn, grad_gain_two, d_logits, back_0[0])
+        )
+    )
+    others_0 = [o1, o2, o3]
+
     others_1 = ring_back(back_1[1:])
-    d_query_t = jnp.concatenate([back_0[0], back_1[0]])
-    grad_out = dot(
-        after(d_attn, d_query_t), jnp.concatenate([mixed_0, mixed_1], axis=1), 0, 1
-    ).astype(BF)
-    grad_query = dot(act_one, d_query_t, 0, 1).astype(BF)
-    parts_one = y_parts(pair_sum(jnp.concatenate([grad_out, rest_small, grad_query], axis=1)))
-    grad_stack = keep.astype(F32) + swap(after(give, d_query_t), "t").astype(F32)
+    lines = jnp.concatenate(
+        [
+            gain_late,
+            jnp.full((1, feat_width), sse),
+            jnp.full((1, feat_width), count),
+            jnp.zeros((5, feat_width), F32),
+        ]
+    )
+    logits_pad = jnp.concatenate(
+        [d_logits_late, jnp.zeros((128 - EXPERTS, tok_rows), BF)]
+    )
+    own_one, theirs_one = pack_grads(
+        (
+            ((0, 4, 0), (0, 5, HALF)),
+            ((2, 6, 0), (None, 3, 0)),
+            ((1, 7, 0),),
+            ((1, 8, 0),),
+        ),
+        "x",
+        (d_attn_late, act_one, act_two, lines, mixed_0, mixed_1, logits_pad, back_0[0], back_1[0]),
+        (0, 1, 2, 3),
+        feat_width // 2 + 128 + q_width,
+    )
+    d_act_query = dot(jnp.concatenate([back_0[0], back_1[0]]), full_query, 0, 1)
+    o1, o2, o3, own_one, theirs_one, d_act_query = lax.optimization_barrier(
+        (*others_1, own_one, theirs_one, d_act_query)
+    )
+
+    d_kv_t = jnp.concatenate(
+        [added([back_0[1], *others_0]), added([back_1[1], o1, o2, o3])], axis=1
+    ).reshape(2 * k_width, tok_rows).astype(BF)
+    d_act_part = d_act_query + dot(d_kv_t, full_kv, 0, 1)
+    part = d_act_part.astype(BF)
+    pair_one = paired(own_one, theirs_one)
+    lines = jnp.concatenate(
+        [
+            jnp.sum(d_act_part * resid_in * scale_one, axis=0, keepdims=True),
+            jnp.zeros((7, feat_width), F32),
+        ]
+    )
+    own_two, theirs_two = pack_grads(
+        (((0, 2, 0),), ((None, 1, 0),)), "y", (act_one, lines, d_kv_t), (0, 1), 2 * k_width + 128
+    )
+    part, pair_one, own_two, theirs_two = lax.optimization_barrier(
+        (part, pair_one, own_two, theirs_two)
+    )
+    other = swap(part, "t")
+    parts_one = axis_parts(pair_one, "x", 4)
+    ring_two = lax.all_to_all(paired(own_two, theirs_two), "y", 0, 0, tiled=True)
+    grad_stack = keep.astype(F32) + given.astype(F32)
     own_down = grad_stack[2].T
-    d_kv_t = jnp.concatenate(
-        [
-            added([own, *moved])
-            for own, moved in ((back_0[1], others_0), (back_1[1], others_1))
-        ],
-        axis=1,
-    ).reshape(2 * k_width, tok_rows).astype(BF)
-    d_act_part = dot(d_query_t, full_query, 0, 1) + dot(d_kv_t, full_kv, 0, 1)
-    part = after(d_act_part.astype(BF), grad_stack)
-    other = swap(part, "t")
-    gain_high, gain_low = split_bf16(
-        jnp.sum(d_act_part * resid_in * scale_one, axis=0, keepdims=True)
-    )
-    lines = jnp.concatenate([gain_high, gain_low, jnp.zeros((6, feat_width), BF)])
-    extra = dot(lines, jnp.eye(8, 128, dtype=BF), 0, 0)
-    parts_two = y_parts(
-        pair_sum(jnp.concatenate([dot(act_one, d_kv_t, 0, 1), extra], axis=1).astype(BF))
-    )
-    summed = hx_sum(parts_one)
-    own_kv = hx_sum(parts_two)
+    *parts_one, ring_two, own_down, other = lax.optimization_barrier(
+        (*parts_one, ring_two, own_down, other)
+    )
+    by_x = added(parts_one).astype(BF)
+    by_xy = added(axis_parts(by_x, "y", 4)).astype(BF)
+    by_xy, other = lax.optimization_barrier((by_xy, other))
+    summed = added(axis_parts(by_xy, "h", 2))
+    by_y = jnp.sum(ring_two.astype(F32), axis=0).astype(BF)
+    ring_two = lax.all_to_all(by_y.reshape(8, *by_y.shape[2:]), ("x", "h"), 0, 0, tiled=True)
+    own_kv = jnp.sum(ring_two.astype(F32), axis=0)
+    own_query = summed[:, feat_width // 2 + 128 :]
     at = feat_width // 2
     own_out = summed[:, :at].T
     own_router = summed[:, at : at + EXPERTS]
     at = at + EXPERTS
-    own_gain_two = summed[:, at] + summed[:, at + 1]
-    loss_value = (summed[0, at + 2] + summed[0, at + 3]) / (
-        feat_width * (summed[0, at + 4] + summed[0, at + 5])
-    )
-    own_gain_one = own_kv[:, 2 * k_width] + own_kv[:, 2 * k_width + 1]
+    own_gain_two = summed[:, at] + summed[:, at + 8]
+    loss_value = (summed[0, at + 1] + summed[0, at + 9]) / (
+        feat_width * (summed[0, at + 2] + summed[0, at + 10])
+    )
+    own_gain_one = own_kv[:, 2 * k_width + EXPERTS] + own_kv[:, 2 * k_width + EXPERTS + 8]
     own_gain_one = own_gain_one + swap(own_gain_one, "t")
-    own_query = summed[:, feat_width // 2 + 128 :]
-    own_down, own_out, own_kv, other = lax.optimization_barrier((own_down, own_out, own_kv, other))
     d_hidden_one, _ = norm_back(resid_in, scale_one, gain_one, both(part, other))
     grad_tokens = d_hidden + d_hidden_one
     return (

time: 722 us -> 631 us (0.87)
  waiting for transfers between devices: 361 us -> 274 us
  matrix products: 103 us -> 23.1 us
  Pallas kernels: 19.9 us -> 78.4 us
  blocking collectives: 28.1 us -> 76.8 us
  starting transfers between devices: 81.6 us -> 69.4 us
  other arithmetic: 56.6 us -> 44.9 us
    dot_general x31 -> x16, matrix products: 103 us -> 23.1 us  [dot(): lax.dot_general(left, right, (((left_dim,), (right_dim,)), ((), ())), pre...]
    pallas_call x0 -> x5, Pallas kernels: none -> 52.7 us  [the longest x1 17.1 us: run_experts_back(): pl.pallas_call(experts_back_kernel, in_specs=[whole, column, column] + we...]
    all_to_all x1 -> x3, blocking collectives: 28.1 us -> 76.8 us  [the longest x1 36.8 us: exchange_slots(): lax.all_to_all(rows.reshape(EXPERTS, -1, width), ('h', 'x', 'c'), 0, 0, t...]
    all_to_all x4 -> x3, waiting for transfers between devices: 96.9 us -> 57.5 us  [exchange_slots(): lax.all_to_all(rows.reshape(EXPERTS, -1, width), ('h', 'x', 'c'), 0, 0, t...]
    ppermute x6, waiting for transfers between devices: 46 us -> 7.32 us  [ring_back(): lax.ppermute(parts[r], 'y', [(i, i - r) for i in range(r, 4)])]
    reduce_scatter x3 -> x1, waiting for transfers between devices: 0.01 us -> 27.1 us  [local(): grad_experts = lax.psum_scatter(grad_parts, 'y', scatter_dimension=0)]
    all_to_all x4 -> x3, starting transfers between devices: 26.9 us -> 15.1 us  [exchange_slots(): lax.all_to_all(rows.reshape(EXPERTS, -1, width), ('h', 'x', 'c'), 0, 0, t...]
    ppermute x14 -> x7, starting transfers between devices: 23.8 us -> 13.3 us  [axis_parts(): lax.ppermute(block, axis, [(i, (i + r) % size) for i in range(size)])]
  transfers between devices with their start and end apart: 47 -> 37, of which waited for: 31 -> 21; matrix products, arithmetic and copies ran while one was open for 21% -> 11% of each run, Pallas kernels for 3% -> 8%
where the time goes in v3:
time: 631 us; the launch traced here: 622 us
  waiting for transfers between devices  274 us (43%)
  Pallas kernels  78.4 us (12%)
  blocking collectives  76.8 us (12%)
  starting transfers between devices  69.4 us (11%)
  other arithmetic  44.9 us (7%)
  local copies, waits for them, and re-layouts  36 us (6%)
  matrix products  23.1 us (4%)
  between operations  19.3 us (3%)
    ppermute x13, waiting for transfers between devices, swap(): return lax.ppermute(value, axis, [(0, 1), (1, 0)])  136 us
    all_to_all x3, waiting for transfers between devices, exchange_slots(): lax.all_to_all(rows.reshape(EXPERTS, -1, width), ('h', 'x', 'c'), 0, 0, t...  57.5 us
    all_to_all x1, blocking collectives, exchange_slots(): lax.all_to_all(rows.reshape(EXPERTS, -1, width), ('h', 'x', 'c'), 0, 0, t...  36.8 us
    reduce_scatter x1, waiting for transfers between devices, local(): grad_experts = lax.psum_scatter(grad_parts, 'y', scatter_dimension=0)  27.1 us
    ppermute x7, waiting for transfers between devices, axis_parts(): lax.ppermute(block, axis, [(i, (i + r) % size) for i in range(size)])  26.5 us
    dot_general x16, matrix products, dot(): lax.dot_general(left, right, (((left_dim,), (right_dim,)), ((), ())), pre...  23.1 us
    all_to_all x1, blocking collectives, gather_hy(): return lax.all_to_all(wide, ('h', 'y'), 0, 0, tiled=True)  23 us
    pallas_call x1, Pallas kernels, run_experts_back(): pl.pallas_call(experts_back_kernel, in_specs=[whole, column, column] + we...  17.1 us
  transfers between devices with their start and end apart: 37, of which 21 were waited for; matrix products, arithmetic and copies ran while one was open for 11% of the time, Pallas kernels for 8%

profile of v3, /device:TPU:0, one launch (start us, length us, event | category | flops | bytes accessed | tf_op | source)
XLA Modules:
  0.0 621.8 jit_solution(14919821268276344188)
XLA Ops:
  10.4 23.0 %all_to_all.45 = bf16[8,24,2176]{2,1,0:T(8,128)(2,1)} all-to-all(bf16[8,24,2176]{2,1,0:T(8,128)(2,1)S(1)} %broadcast_in_dim.143), channel_id=1, replica_groups=mesh['h'=2,'x'=4,'c'=2,'y'=4,'t'=2] {'h','y'}, dimensions={0} | all-to-all | bytes 1671168 | tf_op jit(solution)/shard_map/all_to_all | solution.py:56
  34.6 17.0 %all_to_all.46 = bf16[4,8,24,640]{3,2,1,0:T(8,128)(2,1)S(1)} all-to-all(bf16[4,8,24,640]{3,2,1,0:T(8,128)(2,1)S(1)} %broadcast_in_dim.145), channel_id=1, replica_groups=mesh['h'=2,'x'=4,'c'=2,'y'=4,'t'=2] {'x'}, dimensions={0} | all-to-all | bytes 1966080 | tf_op jit(solution)/shard_map/all_to_all | solution.py:61
  52.2 1.9 slice.137
  54.2 2.7 broadcast_in_dim.144
  56.8 4.5 all-to-all-start.1
  68.6 3.1 collective-permute-start.4
  73.1 3.5 collective-permute-start.2
  76.6 14.9 %all-to-all-done.1 = bf16[4,8,24,1536]{3,2,1,0:T(8,128)(2,1)} async-done(((bf16[4,8,24,1536]{3,2,1,0:T(8,128)(2,1)}), bf16[4,8,24,1536]{3,2,1,0:T(8,128)(2,1)}, u32[]{:S(2)}, u32[]{:S(2)}) %all-to-all-start.1) | async-done | bytes 2359328 | tf_op jit(solution)/shard_map/all_to_all | solution.py:61
  91.5 3.0 collective-permute-done.4.kv3
  96.3 3.2 pad_maximum_fusion.1
  102.0 2.5 collective-permute-done
  104.5 2.7 select_bitcast_fusion.1
  110.1 4.2 shard_map.246
  116.4 4.8 shard_map.247
  121.8 13.2 %collective-permute-done.5 = bf16[256,1536]{1,0:T(8,128)(2,1)S(1)} collective-permute-done((bf16[256,1536]{1,0:T(8,128)(2,1)S(1)}, bf16[256,1536]{1,0:T(8,128)(2,1)S(1)}, u32[]{:S(2)}, u32[]{:S(2)}) %collective-permute-start.5) | collective-permute-done | bytes 786464 | tf_op jit(solution)/shard_map/ppermute | solution.py:47
  138.3 16.6 %collective-permute-done.6 = bf16[256,1536]{1,0:T(8,128)(2,1)} collective-permute-done((bf16[256,1536]{1,0:T(8,128)(2,1)S(1)}, bf16[256,1536]{1,0:T(8,128)(2,1)}, u32[]{:S(2)}, u32[]{:S(2)}) %collective-permute-start.6) | collective-permute-done | bytes 786464 | tf_op jit(solution)/shard_map/ppermute | solution.py:47
  160.7 36.8 %all_to_all.47 = bf16[16,48,1536]{2,1,0:T(8,128)(2,1)} all-to-all(bf16[16,48,1536]{2,1,0:T(8,128)(2,1)S(1)} %bitcast.157), channel_id=1, replica_groups=mesh['h'=2,'x'=4,'c'=2,'y'=4,'t'=2] {'h','x','c'}, dimensions={0} | all-to-all | bytes 4718592 | tf_op jit(solution)/shard_map/all_to_all | solution.py:96
  197.5 13.7 %shard_map.248 = (f32[768,1024]{1,0:T(8,128)}, f32[768,1024]{1,0:T(8,128)}, bf16[768,1024]{1,0:T(8,128)(2,1)}, bf16[768,1536]{1,0:T(8,128)(2,1)}) custom-call(bf16[768,1536]{1,0:T(8,128)(2,1)} %bitcast.135, bf16[4,3,384,1024]{3,2,1,0:T(8,128)(2,1)} %bitcast.129, bf16[4,3,384,1024]{3,2,1,0:T(8,128)(2,1)} %bitcast.130, bf16[4,3,384,1024]{3,2,1,0:T(8,128)(2,1)} %bitcast.131), custom_call_target="tpu_custom_call" | custom-call | flops 7247757312 | bytes 20000000 | tf_op jit(solution)/shard_map/pallas_call | solution.py:376
  211.2 3.7 all-to-all-start.4
  215.0 32.0 %all-to-all-done.4 = bf16[16,48,1536]{2,1,0:T(8,128)(2,1)S(1)} async-done(((bf16[16,48,1536]{2,1,0:T(8,128)(2,1)}), bf16[16,48,1536]{2,1,0:T(8,128)(2,1)S(1)}, u32[]{:S(2)}, u32[]{:S(2)}) %all-to-all-start.4) | async-done | bytes 2359328 | tf_op jit(solution)/shard_map/all_to_all | solution.py:96
  249.4 35.6 %collective-permute-done.8 = bf16[512,1536]{1,0:T(8,128)(2,1)S(1)} collective-permute-done((bf16[512,1536]{1,0:T(8,128)(2,1)S(1)}, bf16[512,1536]{1,0:T(8,128)(2,1)S(1)}, u32[]{:S(2)}, u32[]{:S(2)}) %collective-permute-start.8) | collective-permute-done | bytes 1572896 | tf_op jit(solution)/shard_map/ppermute | solution.py:47
  285.0 2.0 fusion.7
  287.4 2.9 convolution_convert_fusion
  290.3 5.8 all-to-all-start.5
  296.1 3.8 select_reduce_fusion.1
  300.4 20.3 %collective-permute-done.9 = f32[2,512]{1,0:T(2,128)S(1)} collective-permute-done((f32[2,512]{1,0:T(2,128)S(1)}, f32[2,512]{1,0:T(2,128)S(1)}, u32[]{:S(2)}, u32[]{:S(2)}) %collective-permute-start.9) | collective-permute-done | bytes 4128 | tf_op jit(solution)/shard_map/ppermute | solution.py:47
  320.8 7.4 %all-to-all-done.5 = bf16[16,48,1536]{2,1,0:T(8,128)(2,1)} async-done(((bf16[16,48,1536]{2,1,0:T(8,128)(2,1)}), bf16[16,48,1536]{2,1,0:T(8,128)(2,1)}, u32[]{:S(2)}, u32[]{:S(2)}) %all-to-all-start.5) | async-done | bytes 2359328 | tf_op jit(solution)/shard_map/all_to_all | solution.py:96
  328.2 17.1 %shard_map.249 = (bf16[768,1024]{1,0:T(8,128)(2,1)}, bf16[768,1024]{1,0:T(8,128)(2,1)}, bf16[768,1536]{1,0:T(8,128)(2,1)}) custom-call(bf16[768,1536]{1,0:T(8,128)(2,1)} %bitcast.52.d_ref, f32[768,1024]{1,0:T(8,128)} %get-tuple-element.104.g_ref, f32[768,1024]{1,0:T(8,128)} %get-tuple-element.105.u_ref, bf16[4,3,384,1024]{3,2,1,0:T(8,128)(2,1)} %bitcast.132, ...), custom_call_target="tpu_custom_call" | custom-call | flops 7247757312 | bytes 20000000 | tf_op jit(solution)/shard_map/pallas_call | solution.py:396
  345.2 5.6 all-to-all-start.6
  350.9 13.9 %shard_map.250 = bf16[4,3,384,1024]{3,2,1,0:T(8,128)(2,1)} custom-call(bf16[768,1536]{1,0:T(8,128)(2,1)} %bitcast.136, bf16[768,1536]{1,0:T(8,128)(2,1)} %bitcast.52.d_ref, bf16[768,1024]{1,0:T(8,128)(2,1)} %get-tuple-element.109.dg_ref, bf16[768,1024]{1,0:T(8,128)(2,1)} %get-tuple-element.110.du_ref, bf16[768,1024]{1,0:T(8,128)(2,1)} %get-tuple-element.111.inner_ref), custom_call_target="tpu_custom_call" | custom-call | flops 7247757312 | bytes 20000000 | tf_op jit(solution)/shard_map/pallas_call | solution.py:410
  364.9 18.1 %all-to-all-done.6 = bf16[16,48,1536]{2,1,0:T(8,128)(2,1)} async-done(((bf16[16,48,1536]{2,1,0:T(8,128)(2,1)}), bf16[16,48,1536]{2,1,0:T(8,128)(2,1)}, u32[]{:S(2)}, u32[]{:S(2)}) %all-to-all-start.6) | async-done | bytes 2359328 | tf_op jit(solution)/shard_map/all_to_all | solution.py:96
  382.9 3.1 convolution_convert_fusion.2
  391.3 31.1 %collective-permute-done.10 = bf16[512,1536]{1,0:T(8,128)(2,1)S(1)} collective-permute-done((bf16[512,1536]{1,0:T(8,128)(2,1)S(1)}, bf16[512,1536]{1,0:T(8,128)(2,1)S(1)}, u32[]{:S(2)}, u32[]{:S(2)}) %collective-permute-start.10) | collective-permute-done | bytes 1572896 | tf_op jit(solution)/shard_map/ppermute | solution.py:47
  424.2 3.3 fusion.64
  427.6 2.3 fusion.21.d_ref
  429.9 8.3 %shard_map.251 = (bf16[384,512]{1,0:T(8,128)(2,1)}, bf16[2,128,512]{2,1,0:T(8,128)(2,1)}, bf16[2,128,512]{2,1,0:T(8,128)(2,1)}, bf16[2,128,512]{2,1,0:T(8,128)(2,1)}, bf16[2,128,512]{2,1,0:T(8,128)(2,1)}) custom-call(s32[1]{0:T(128)} %bitcast.y_ref, bf16[768,512]{1,0:T(8,128)(2,1)} %copy-done.20, bf16[768,512]{1,0:T(8,128)(2,1)} %fusion.21.d_ref, ...), custom_call_target="tpu_custom_call" | custom-call | flops 149999992832 | bytes 6000000 | tf_op jit(solution)/shard_map/pallas_call | solution.py:265
  438.3 27.1 %reduce-scatter.2.cloned.1.call-done = bf16[1,3,384,1024]{3,2,1,0:T(8,128)(2,1)} async-done(((bf16[4,3,384,1024]{3,2,1,0:T(8,128)(2,1)}), bf16[1,3,384,1024]{3,2,1,0:T(8,128)(2,1)}) %reduce-scatter.2.cloned.1.call-update) | async-done | bytes 2359312 | tf_op jit(solution)/shard_map/reduce_scatter | solution.py:626
  465.3 2.4 slice.152
  471.7 1.9 collective-permute-start.14
  473.6 8.4 %shard_map.252 = (bf16[384,512]{1,0:T(8,128)(2,1)}, bf16[2,128,512]{2,1,0:T(8,128)(2,1)}, bf16[2,128,512]{2,1,0:T(8,128)(2,1)}, bf16[2,128,512]{2,1,0:T(8,128)(2,1)}, bf16[2,128,512]{2,1,0:T(8,128)(2,1)}) custom-call(s32[1]{0:T(128)} %bitcast.y_ref, bf16[768,512]{1,0:T(8,128)(2,1)} %copy-done.20, bf16[768,512]{1,0:T(8,128)(2,1)} %fusion.21.d_ref, ...), custom_call_target="tpu_custom_call" | custom-call | flops 149999992832 | bytes 6000000 | tf_op jit(solution)/shard_map/pallas_call | solution.py:265
  482.0 4.5 collective-permute-done.13
  486.5 13.5 %collective-permute-done.14 = bf16[3,384,512]{2,1,0:T(8,128)(2,1)} collective-permute-done((bf16[3,384,512]{2,1,0:T(8,128)(2,1)}, bf16[3,384,512]{2,1,0:T(8,128)(2,1)}, u32[]{:S(2)}, u32[]{:S(2)}) %collective-permute-start.14) | collective-permute-done | bytes 1179680 | tf_op jit(solution)/shard_map/ppermute | solution.py:47
  507.5 5.6 shard_map.253
  516.0 2.8 collective-permute-done.17
  520.7 1.8 fusion.10
  522.6 2.4 shard_map.254
  525.0 2.1 add_convert_fusion
  527.6 1.5 collective-permute-start.23
  529.9 2.5 add_convert_fusion.1
  532.4 5.3 all-to-all-start.7
  537.7 2.8 dynamic-slice_bitcast_fusion
  540.6 2.7 collective-permute-start.21
  545.0 1.7 convert_add_fusion.1
  548.0 22.8 %collective-permute-done.21 = bf16[4,2,24,1664]{3,2,1,0:T(8,128)(2,1)S(1)} collective-permute-done((bf16[4,2,24,1664]{3,2,1,0:T(8,128)(2,1)S(1)}, bf16[4,2,24,1664]{3,2,1,0:T(8,128)(2,1)S(1)}, u32[]{:S(2)}, u32[]{:S(2)}) %collective-permute-start.21) | collective-permute-done | bytes 639008 | tf_op jit(solution)/shard_map/ppermute | solution.py:83
  570.9 3.7 collective-permute-done.19
  575.4 2.0 add_convert_fusion.4
  579.0 1.7 collective-permute-start.24
  580.8 1.5 collective-permute-start.26
  582.3 2.0 collective-permute-start.25
  585.2 4.9 all-to-all-start.8
  592.5 2.8 fusion.11
  595.4 3.6 collective-permute-start.27
  599.0 4.8 fusion.6
  605.4 2.3 collective-permute-done.28
  (264 shorter events, 73.7 us)
Async XLA Ops:
  10.4 41.2 %copy-start.49 = (bf16[1,512,384]{2,1,0:T(8,128)(2,1)S(1)}, bf16[1,512,384]{2,1,0:T(8,128)(2,1)}, u32[]{:S(2)}) copy-start(bf16[1,512,384]{2,1,0:T(8,128)(2,1)} %param.29) | copy-start | bytes 1179652
  33.5 18.4 %copy-start.26 = (bf16[512,1536]{1,0:T(8,128)(2,1)S(1)}, bf16[512,1536]{1,0:T(8,128)(2,1)}, u32[]{:S(2)}) copy-start(bf16[512,1536]{1,0:T(8,128)(2,1)} %param.15) | copy-start | bytes 4718596
  51.6 9.8 %collective-permute-start.1 = (bf16[4,2,96,640]{3,2,1,0:T(8,128)(2,1)S(1)}, bf16[4,2,96,640]{3,2,1,0:T(8,128)(2,1)}, u32[]{:S(2)}, u32[]{:S(2)}) collective-permute-start(bf16[4,2,96,640]{3,2,1,0:T(8,128)(2,1)S(1)} %bitcast.147), channel_id=1, source_target_pairs={{0,8},{8,0},{1,9},{9,1},{2,10},{10,2},{3,11},{11,3},{4,12},{12,4},... | collective-permute-start | bytes 2949128 | tf_op jit(solution)/shard_map/ppermute | solution.py:47
  52.2 12.1 %copy-start.56 = (f32[512]{0:T(512)}, f32[512]{0:T(512)S(1)}, u32[]{:S(2)}) copy-start(f32[512]{0:T(512)S(1)} %add_rsqrt_fusion.1) | copy-start | bytes 6148
  56.8 34.7 %all-to-all-start.1 = ((bf16[4,8,24,1536]{3,2,1,0:T(8,128)(2,1)}), bf16[4,8,24,1536]{3,2,1,0:T(8,128)(2,1)}, u32[]{:S(2)}, u32[]{:S(2)}) async-start(bf16[4,8,24,1536]{3,2,1,0:T(8,128)(2,1)} %broadcast_in_dim.144), calls=%async_computation.1 | async-start | bytes 4718592 | tf_op jit(solution)/shard_map/all_to_all | solution.py:61
  61.3 136.2 %all-gather.3.cloned.1.call-start = ((), (), s32[]{:S(2)}) async-start(), calls=%async_computation.11 | async-start | bytes 11796480 | tf_op jit(solution)/shard_map/all_gather | solution.py:552
  64.8 43.3 %copy-start.4 = (bf16[512,1536]{1,0:T(8,128)(2,1)}, bf16[512,1536]{1,0:T(8,128)(2,1)S(1)}, u32[]{:S(2)}) copy-start(bf16[512,1536]{1,0:T(8,128)(2,1)S(1)} %fusion.2.refs_1_.refs_0_) | copy-start | bytes 4718596
  65.9 50.6 %copy-start.9 = (bf16[512,512]{1,0:T(8,128)(2,1)}, bf16[512,512]{1,0:T(8,128)(2,1)S(1)}, u32[]{:S(2)}) copy-start(bf16[512,512]{1,0:T(8,128)(2,1)S(1)} %fusion.31) | copy-start | bytes 1572868
  67.6 28.7 %collective-permute-start.7 = (bf16[3,384,512]{2,1,0:T(8,128)(2,1)}, bf16[3,384,512]{2,1,0:T(8,128)(2,1)}, u32[]{:S(2)}, u32[]{:S(2)}) collective-permute-start(bf16[3,384,512]{2,1,0:T(8,128)(2,1)} %pad_maximum_fusion.3), channel_id=1, source_target_pairs={{0,1},{1,0},{2,3},{3,2},{4,5},{5,4},{6,7},{7,6},{8,9},{9,8},{10,11... | collective-permute-start | bytes 3538952 | tf_op jit(solution)/shard_map/ppermute | solution.py:47
  68.6 25.9 %collective-permute-start.4 = (bf16[2,256,512]{2,1,0:T(8,128)(2,1)S(1)}, bf16[2,256,512]{2,1,0:T(8,128)(2,1)S(1)}, u32[]{:S(2)}, u32[]{:S(2)}) collective-permute-start(bf16[2,256,512]{2,1,0:T(8,128)(2,1)S(1)} %bitcast.122), channel_id=1, source_target_pairs={{0,6},{1,7},{8,14},{9,15},{16,22},{17,23},{24,30},{25,31},{32,38},... | collective-permute-start | bytes 1572872 | tf_op jit(solution)/shard_map/ppermute | solution.py:538
  71.7 22.8 %collective-permute-start.3 = (bf16[2,256,512]{2,1,0:T(8,128)(2,1)S(1)}, bf16[2,256,512]{2,1,0:T(8,128)(2,1)S(1)}, u32[]{:S(2)}, u32[]{:S(2)}) collective-permute-start(bf16[2,256,512]{2,1,0:T(8,128)(2,1)S(1)} %bitcast.123), channel_id=1, source_target_pairs={{0,4},{2,6},{1,5},{3,7},{8,12},{10,14},{9,13},{11,15},{16,20},{18,... | collective-permute-start | bytes 1572872 | tf_op jit(solution)/shard_map/ppermute | solution.py:538
  73.1 22.8 %collective-permute-start.2 = (bf16[2,256,512]{2,1,0:T(8,128)(2,1)S(1)}, bf16[2,256,512]{2,1,0:T(8,128)(2,1)}, u32[]{:S(2)}, u32[]{:S(2)}) collective-permute-start(bf16[2,256,512]{2,1,0:T(8,128)(2,1)S(1)} %bitcast.124), channel_id=1, source_target_pairs={{0,2},{2,4},{4,6},{1,3},{3,5},{5,7},{8,10},{10,12},{12,14},{9,11},... | collective-permute-start | bytes 1572872 | tf_op jit(solution)/shard_map/ppermute | solution.py:538
  99.5 5.0 collective-permute-start
  101.3 15.1 %copy-start.7 = (s32[2048,1]{1,0:T(8,128)}, s32[2048,1]{1,0:T(8,128)S(1)}, u32[]{:S(2)}) copy-start(s32[2048,1]{1,0:T(8,128)S(1)} %copy.82.seg_k) | copy-start | bytes 24580
  102.0 147.4 %copy-start.8 = (s32[1,512]{1,0:T(1,128)}, s32[1,512]{1,0:T(1,128)S(1)}, u32[]{:S(2)}) copy-start(s32[1,512]{1,0:T(1,128)S(1)} %get-tuple-element.249.seg_q) | copy-start | bytes 6148
  108.0 27.0 %copy-start.35 = (bf16[2,4,2,96,1536]{4,3,2,1,0:T(8,128)(2,1)}, bf16[2,4,2,96,1536]{4,3,2,1,0:T(8,128)(2,1)S(1)}, u32[]{:S(2)}) copy-start(bf16[2,4,2,96,1536]{4,3,2,1,0:T(8,128)(2,1)S(1)} %copy.80) | copy-start | bytes 14155780
  115.2 19.9 %collective-permute-start.5 = (bf16[256,1536]{1,0:T(8,128)(2,1)S(1)}, bf16[256,1536]{1,0:T(8,128)(2,1)S(1)}, u32[]{:S(2)}, u32[]{:S(2)}) collective-permute-start(bf16[256,1536]{1,0:T(8,128)(2,1)S(1)} %convolution_convert_fusion.5), channel_id=1, source_target_pairs={{0,1},{1,0},{2,3},{3,2},{4,5},{5,4},{6,7},{7,6},{8,9},{9,8},{10,11... | collective-permute-start | bytes 2359304 | tf_op jit(solution)/shard_map/ppermute | solution.py:47
  121.8 16.5 %copy-start.16 = (bf16[768,256]{1,0:T(8,128)(2,1)}, bf16[768,256]{1,0:T(8,128)(2,1)S(1)}, u32[]{:S(2)}) copy-start(bf16[768,256]{1,0:T(8,128)(2,1)S(1)} %get-tuple-element.97.o_1.refs_5_) | copy-start | bytes 1179652
  121.8 15.1 %copy-start.60 = (s32[512,2]{0,1:T(2,128)S(1)}, s32[512,2]{0,1:T(2,128)}, u32[]{:S(2)}) copy-start(s32[512,2]{0,1:T(2,128)} %param.18) | copy-start | bytes 12292
  135.9 19.0 %collective-permute-start.6 = (bf16[256,1536]{1,0:T(8,128)(2,1)S(1)}, bf16[256,1536]{1,0:T(8,128)(2,1)}, u32[]{:S(2)}, u32[]{:S(2)}) collective-permute-start(bf16[256,1536]{1,0:T(8,128)(2,1)S(1)} %convolution_convert_fusion.4), channel_id=1, source_target_pairs={{0,1},{1,0},{2,3},{3,2},{4,5},{5,4},{6,7},{7,6},{8,9},{9,8},{10,11... | collective-permute-start | bytes 2359304 | tf_op jit(solution)/shard_map/ppermute | solution.py:47
  138.3 18.0 %copy-start.27 = (bf16[512,1536]{1,0:T(8,128)(2,1)S(1)}, bf16[512,1536]{1,0:T(8,128)(2,1)}, u32[]{:S(2)}) copy-start(bf16[512,1536]{1,0:T(8,128)(2,1)} %param.15) | copy-start | bytes 4718596
  211.2 35.7 %all-to-all-start.4 = ((bf16[16,48,1536]{2,1,0:T(8,128)(2,1)}), bf16[16,48,1536]{2,1,0:T(8,128)(2,1)S(1)}, u32[]{:S(2)}, u32[]{:S(2)}) async-start(bf16[16,48,1536]{2,1,0:T(8,128)(2,1)} %bitcast.156), calls=%async_computation.4 | async-start | bytes 4718592 | tf_op jit(solution)/shard_map/all_to_all | solution.py:96
  246.9 38.1 %copy-start.24 = (f32[512,1536]{1,0:T(8,128)S(1)}, f32[512,1536]{1,0:T(8,128)}, u32[]{:S(2)}) copy-start(f32[512,1536]{1,0:T(8,128)} %copy-done.23) | copy-start | bytes 9437188
  246.9 38.1 %copy-start.30 = (bf16[512,1536]{1,0:T(8,128)(2,1)S(1)}, bf16[512,1536]{1,0:T(8,128)(2,1)}, u32[]{:S(2)}) copy-start(bf16[512,1536]{1,0:T(8,128)(2,1)} %param.16) | copy-start | bytes 4718596
  248.4 36.6 %collective-permute-start.8 = (bf16[512,1536]{1,0:T(8,128)(2,1)S(1)}, bf16[512,1536]{1,0:T(8,128)(2,1)S(1)}, u32[]{:S(2)}, u32[]{:S(2)}) collective-permute-start(bf16[512,1536]{1,0:T(8,128)(2,1)S(1)} %convolution_convert_fusion.3), channel_id=1, source_target_pairs={{0,1},{1,0},{2,3},{3,2},{4,5},{5,4},{6,7},{7,6},{8,9},{9,8},{10,11... | collective-permute-start | bytes 4718600 | tf_op jit(solution)/shard_map/ppermute | solution.py:47
  287.0 137.3 %copy-start.29 = (f32[512,1536]{1,0:T(8,128)}, f32[512,1536]{1,0:T(8,128)S(1)}, u32[]{:S(2)}) copy-start(f32[512,1536]{1,0:T(8,128)S(1)} %get-tuple-element.247) | copy-start | bytes 9437188
  290.3 37.9 %all-to-all-start.5 = ((bf16[16,48,1536]{2,1,0:T(8,128)(2,1)}), bf16[16,48,1536]{2,1,0:T(8,128)(2,1)}, u32[]{:S(2)}, u32[]{:S(2)}) async-start(bf16[16,48,1536]{2,1,0:T(8,128)(2,1)} %bitcast.155), calls=%async_computation.5 | async-start | bytes 4718592 | tf_op jit(solution)/shard_map/all_to_all | solution.py:96
  299.9 20.9 %collective-permute-start.9 = (f32[2,512]{1,0:T(2,128)S(1)}, f32[2,512]{1,0:T(2,128)S(1)}, u32[]{:S(2)}, u32[]{:S(2)}) collective-permute-start(f32[2,512]{1,0:T(2,128)S(1)} %pad_maximum_fusion.5), channel_id=1, source_target_pairs={{0,1},{1,0},{2,3},{3,2},{4,5},{5,4},{6,7},{7,6},{8,9},{9,8},{10,11... | collective-permute-start | bytes 12296 | tf_op jit(solution)/shard_map/ppermute | solution.py:47
  345.2 37.7 %all-to-all-start.6 = ((bf16[16,48,1536]{2,1,0:T(8,128)(2,1)}), bf16[16,48,1536]{2,1,0:T(8,128)(2,1)}, u32[]{:S(2)}, u32[]{:S(2)}) async-start(bf16[16,48,1536]{2,1,0:T(8,128)(2,1)} %bitcast.154), calls=%async_computation.6 | async-start | bytes 4718592 | tf_op jit(solution)/shard_map/all_to_all | solution.py:96
  350.9 114.5 %reduce-scatter.2.cloned.1.call-start = ((), (), s32[]{:S(2)}) async-start(), calls=%async_computation.10 | async-start | bytes 11796480 | tf_op jit(solution)/shard_map/reduce_scatter | solution.py:626
  386.1 36.4 %copy-start.25 = (f32[512,1536]{1,0:T(8,128)S(1)}, f32[512,1536]{1,0:T(8,128)}, u32[]{:S(2)}) copy-start(f32[512,1536]{1,0:T(8,128)} %copy-done.23) | copy-start | bytes 9437188
  386.1 36.3 %collective-permute-start.10 = (bf16[512,1536]{1,0:T(8,128)(2,1)S(1)}, bf16[512,1536]{1,0:T(8,128)(2,1)S(1)}, u32[]{:S(2)}, u32[]{:S(2)}) collective-permute-start(bf16[512,1536]{1,0:T(8,128)(2,1)S(1)} %convolution_convert_fusion.2), channel_id=1, source_target_pairs={{0,1},{1,0},{2,3},{3,2},{4,5},{5,4},{6,7},{7,6},{8,9},{9,8},{10,11... | collective-permute-start | bytes 4718600 | tf_op jit(solution)/shard_map/ppermute | solution.py:47
  391.3 33.0 %copy-start.31 = (bf16[512,1536]{1,0:T(8,128)(2,1)S(1)}, bf16[512,1536]{1,0:T(8,128)(2,1)}, u32[]{:S(2)}) copy-start(bf16[512,1536]{1,0:T(8,128)(2,1)} %param.16) | copy-start | bytes 4718596
  467.8 14.2 %collective-permute-start.11 = (bf16[2,128,512]{2,1,0:T(8,128)(2,1)}, bf16[2,128,512]{2,1,0:T(8,128)(2,1)}, u32[]{:S(2)}, u32[]{:S(2)}) collective-permute-start(bf16[2,128,512]{2,1,0:T(8,128)(2,1)} %get-tuple-element.127), channel_id=1, source_target_pairs={{2,0},{4,2},{6,4},{3,1},{5,3},{7,5},{10,8},{12,10},{14,12},{11,9},... | collective-permute-start | bytes 786440 | tf_op jit(solution)/shard_map/ppermute | solution.py:652
  469.1 12.9 %collective-permute-start.12 = (bf16[2,128,512]{2,1,0:T(8,128)(2,1)}, bf16[2,128,512]{2,1,0:T(8,128)(2,1)}, u32[]{:S(2)}, u32[]{:S(2)}) collective-permute-start(bf16[2,128,512]{2,1,0:T(8,128)(2,1)} %get-tuple-element.128), channel_id=1, source_target_pairs={{4,0},{6,2},{5,1},{7,3},{12,8},{14,10},{13,9},{15,11},{20,16},{22,... | collective-permute-start | bytes 786440 | tf_op jit(solution)/shard_map/ppermute | solution.py:652
  470.4 16.2 %collective-permute-start.13 = (bf16[2,128,512]{2,1,0:T(8,128)(2,1)}, bf16[2,128,512]{2,1,0:T(8,128)(2,1)}, u32[]{:S(2)}, u32[]{:S(2)}) collective-permute-start(bf16[2,128,512]{2,1,0:T(8,128)(2,1)} %get-tuple-element.129), channel_id=1, source_target_pairs={{6,0},{7,1},{14,8},{15,9},{22,16},{23,17},{30,24},{31,25},{38,32},... | collective-permute-start | bytes 786440 | tf_op jit(solution)/shard_map/ppermute | solution.py:652
  471.7 28.4 %collective-permute-start.14 = (bf16[3,384,512]{2,1,0:T(8,128)(2,1)}, bf16[3,384,512]{2,1,0:T(8,128)(2,1)}, u32[]{:S(2)}, u32[]{:S(2)}) collective-permute-start(bf16[3,384,512]{2,1,0:T(8,128)(2,1)} %slice.152), channel_id=1, source_target_pairs={{0,1},{1,0},{2,3},{3,2},{4,5},{5,4},{6,7},{7,6},{8,9},{9,8},{10,11... | collective-permute-start | bytes 3538952 | tf_op jit(solution)/shard_map/ppermute | solution.py:47
  473.5 26.5 %copy-start.53 = (bf16[16,512]{1,0:T(8,128)(2,1)S(1)}, bf16[16,512]{1,0:T(8,128)(2,1)}, u32[]{:S(2)}) copy-start(bf16[16,512]{1,0:T(8,128)(2,1)} %copy-done.52) | copy-start | bytes 49156
  473.5 30.5 %copy-start.58 = (f32[1,1536]{1,0:T(1,128)S(1)}, f32[1,1536]{1,0:T(1,128)}, u32[]{:S(2)}) copy-start(f32[1,1536]{1,0:T(1,128)} %broadcast_in_dim.162) | copy-start | bytes 18436
  473.5 30.5 %copy-start.62 = (f32[8]{0:T(128)S(1)}, f32[8]{0:T(128)}, u32[]{:S(2)}) copy-start(f32[8]{0:T(128)} %pad.9.clone) | copy-start | bytes 100
  473.5 30.5 %copy-start.63 = (f32[8]{0:T(128)S(1)}, f32[8]{0:T(128)}, u32[]{:S(2)}) copy-start(f32[8]{0:T(128)} %pad.8.clone) | copy-start | bytes 100
  473.5 30.5 %copy-start.64 = (f32[8]{0:T(128)S(1)}, f32[8]{0:T(128)}, u32[]{:S(2)}) copy-start(f32[8]{0:T(128)} %pad.7.clone) | copy-start | bytes 100
  473.5 30.6 %copy-start.1 = (bf16[512,1536]{1,0:T(8,128)(2,1)S(1)}, bf16[512,1536]{1,0:T(8,128)(2,1)}, u32[]{:S(2)}) copy-start(bf16[512,1536]{1,0:T(8,128)(2,1)} %copy-done) | copy-start | bytes 4718596
  473.6 30.6 %copy-start.3 = (bf16[512,1536]{1,0:T(8,128)(2,1)S(1)}, bf16[512,1536]{1,0:T(8,128)(2,1)}, u32[]{:S(2)}) copy-start(bf16[512,1536]{1,0:T(8,128)(2,1)} %copy-done.2) | copy-start | bytes 4718596
  473.6 30.6 %copy-start.15 = (bf16[768,256]{1,0:T(8,128)(2,1)S(1)}, bf16[768,256]{1,0:T(8,128)(2,1)}, u32[]{:S(2)}) copy-start(bf16[768,256]{1,0:T(8,128)(2,1)} %copy-done.14) | copy-start | bytes 1179652
  473.6 30.6 %copy-start.17 = (bf16[768,256]{1,0:T(8,128)(2,1)S(1)}, bf16[768,256]{1,0:T(8,128)(2,1)}, u32[]{:S(2)}) copy-start(bf16[768,256]{1,0:T(8,128)(2,1)} %copy-done.16) | copy-start | bytes 1179652
  500.1 15.9 %collective-permute-start.15 = (bf16[2,128,512]{2,1,0:T(8,128)(2,1)}, bf16[2,128,512]{2,1,0:T(8,128)(2,1)S(1)}, u32[]{:S(2)}, u32[]{:S(2)}) collective-permute-start(bf16[2,128,512]{2,1,0:T(8,128)(2,1)} %get-tuple-element.132), channel_id=1, source_target_pairs={{2,0},{4,2},{6,4},{3,1},{5,3},{7,5},{10,8},{12,10},{14,12},{11,9},... | collective-permute-start | bytes 786440 | tf_op jit(solution)/shard_map/ppermute | solution.py:652
  501.4 14.7 %collective-permute-start.16 = (bf16[2,128,512]{2,1,0:T(8,128)(2,1)}, bf16[2,128,512]{2,1,0:T(8,128)(2,1)S(1)}, u32[]{:S(2)}, u32[]{:S(2)}) collective-permute-start(bf16[2,128,512]{2,1,0:T(8,128)(2,1)} %get-tuple-element.133), channel_id=1, source_target_pairs={{4,0},{6,2},{5,1},{7,3},{12,8},{14,10},{13,9},{15,11},{20,16},{22,... | collective-permute-start | bytes 786440 | tf_op jit(solution)/shard_map/ppermute | solution.py:652
  502.7 16.2 %collective-permute-start.17 = (bf16[2,128,512]{2,1,0:T(8,128)(2,1)}, bf16[2,128,512]{2,1,0:T(8,128)(2,1)S(1)}, u32[]{:S(2)}, u32[]{:S(2)}) collective-permute-start(bf16[2,128,512]{2,1,0:T(8,128)(2,1)} %get-tuple-element.134), channel_id=1, source_target_pairs={{6,0},{7,1},{14,8},{15,9},{22,16},{23,17},{30,24},{31,25},{38,32},... | collective-permute-start | bytes 786440 | tf_op jit(solution)/shard_map/ppermute | solution.py:652
  518.8 6.2 collective-permute-start.18
  527.1 2.8 collective-permute-start.22
  527.6 47.8 %collective-permute-start.23 = (bf16[512,1536]{1,0:T(8,128)(2,1)}, bf16[512,1536]{1,0:T(8,128)(2,1)}, u32[]{:S(2)}, u32[]{:S(2)}) collective-permute-start(bf16[512,1536]{1,0:T(8,128)(2,1)} %get-tuple-element.159), channel_id=1, source_target_pairs={{0,1},{1,0},{2,3},{3,2},{4,5},{5,4},{6,7},{7,6},{8,9},{9,8},{10,11... | collective-permute-start | bytes 4718600 | tf_op jit(solution)/shard_map/ppermute | solution.py:47
  532.4 43.0 %all-to-all-start.7 = ((bf16[4,4,2,24,640]{4,3,2,1,0:T(8,128)(2,1)}), bf16[4,4,2,24,640]{4,3,2,1,0:T(8,128)(2,1)S(1)}, u32[]{:S(2)}, u32[]{:S(2)}) async-start(bf16[4,4,2,24,640]{4,3,2,1,0:T(8,128)(2,1)} %add_convert_fusion.1), calls=%async_computation.8 | async-start | bytes 1966080 | tf_op jit(solution)/shard_map/all_to_all | solution.py:715
  537.7 7.2 %copy-start.39 = (bf16[1,3,384,1024]{3,2,1,0:T(8,128)(2,1)S(1)}, bf16[1,3,384,1024]{3,2,1,0:T(8,128)(2,1)}, u32[]{:S(2)}) copy-start(bf16[1,3,384,1024]{3,2,1,0:T(8,128)(2,1)} %reduce-scatter.2.cloned.1.call-done) | copy-start | bytes 7077892
  540.6 30.3 %collective-permute-start.21 = (bf16[4,2,24,1664]{3,2,1,0:T(8,128)(2,1)S(1)}, bf16[4,2,24,1664]{3,2,1,0:T(8,128)(2,1)S(1)}, u32[]{:S(2)}, u32[]{:S(2)}) collective-permute-start(bf16[4,2,24,1664]{3,2,1,0:T(8,128)(2,1)S(1)} %get-tuple-element.258), channel_id=1, source_target_pairs={{0,48},{16,0},{32,16},{48,32},{1,49},{17,1},{33,17},{49,33},{2,50}... | collective-permute-start | bytes 1916936 | tf_op jit(solution)/shard_map/ppermute | solution.py:83
  543.2 27.6 %collective-permute-start.20 = (bf16[4,2,24,1664]{3,2,1,0:T(8,128)(2,1)S(1)}, bf16[4,2,24,1664]{3,2,1,0:T(8,128)(2,1)S(1)}, u32[]{:S(2)}, u32[]{:S(2)}) collective-permute-start(bf16[4,2,24,1664]{3,2,1,0:T(8,128)(2,1)S(1)} %get-tuple-element.259), channel_id=1, source_target_pairs={{0,32},{16,48},{32,0},{48,16},{1,33},{17,49},{33,1},{49,17},{2,34}... | collective-permute-start | bytes 1916936 | tf_op jit(solution)/shard_map/ppermute | solution.py:83
  544.1 30.5 %collective-permute-start.19 = (bf16[4,2,24,1664]{3,2,1,0:T(8,128)(2,1)S(1)}, bf16[4,2,24,1664]{3,2,1,0:T(8,128)(2,1)S(1)}, u32[]{:S(2)}, u32[]{:S(2)}) collective-permute-start(bf16[4,2,24,1664]{3,2,1,0:T(8,128)(2,1)S(1)} %get-tuple-element.260), channel_id=1, source_target_pairs={{0,16},{16,32},{32,48},{48,0},{1,17},{17,33},{33,49},{49,1},{2,18}... | collective-permute-start | bytes 1916936 | tf_op jit(solution)/shard_map/ppermute | solution.py:83
  578.2 14.3 %copy-start.55 = (f32[1536]{0:T(1024)S(1)}, f32[1536]{0:T(1024)}, u32[]{:S(2)}) copy-start(f32[1536]{0:T(1024)} %copy-done.54) | copy-start | bytes 18436
  579.0 12.2 %collective-permute-start.24 = (bf16[2,24,1664]{2,1,0:T(8,128)(2,1)}, bf16[2,24,1664]{2,1,0:T(8,128)(2,1)}, u32[]{:S(2)}, u32[]{:S(2)}) collective-permute-start(bf16[2,24,1664]{2,1,0:T(8,128)(2,1)} %get-tuple-element.267), channel_id=1, source_target_pairs={{0,2},{2,4},{4,6},{6,0},{1,3},{3,5},{5,7},{7,1},{8,10},{10,12},{12... | collective-permute-start | bytes 479240 | tf_op jit(solution)/shard_map/ppermute | solution.py:83
  580.8 10.5 %collective-permute-start.26 = (bf16[2,24,1664]{2,1,0:T(8,128)(2,1)}, bf16[2,24,1664]{2,1,0:T(8,128)(2,1)}, u32[]{:S(2)}, u32[]{:S(2)}) collective-permute-start(bf16[2,24,1664]{2,1,0:T(8,128)(2,1)} %get-tuple-element.268), channel_id=1, source_target_pairs={{0,6},{2,0},{4,2},{6,4},{1,7},{3,1},{5,3},{7,5},{8,14},{10,8},{12,... | collective-permute-start | bytes 479240 | tf_op jit(solution)/shard_map/ppermute | solution.py:83
  582.3 9.0 %collective-permute-start.25 = (bf16[2,24,1664]{2,1,0:T(8,128)(2,1)S(1)}, bf16[2,24,1664]{2,1,0:T(8,128)(2,1)}, u32[]{:S(2)}, u32[]{:S(2)}) collective-permute-start(bf16[2,24,1664]{2,1,0:T(8,128)(2,1)S(1)} %get-tuple-element.269), channel_id=1, source_target_pairs={{0,4},{2,6},{4,0},{6,2},{1,5},{3,7},{5,1},{7,3},{8,12},{10,14},{12... | collective-permute-start | bytes 479240 | tf_op jit(solution)/shard_map/ppermute | solution.py:83
  585.2 18.7 %all-to-all-start.8 = ((bf16[8,24,640]{2,1,0:T(8,128)(2,1)}), bf16[8,24,640]{2,1,0:T(8,128)(2,1)S(1)}, u32[]{:S(2)}, u32[]{:S(2)}) async-start(bf16[8,24,640]{2,1,0:T(8,128)(2,1)} %bitcast.160), calls=%async_computation.9 | async-start | bytes 491520 | tf_op jit(solution)/shard_map/all_to_all | solution.py:726
  595.4 12.8 %collective-permute-start.27 = (bf16[24,1664]{1,0:T(8,128)(2,1)S(1)}, bf16[24,1664]{1,0:T(8,128)(2,1)S(1)}, u32[]{:S(2)}, u32[]{:S(2)}) collective-permute-start(bf16[24,1664]{1,0:T(8,128)(2,1)S(1)} %dynamic-slice_bitcast_fusion.7), channel_id=1, source_target_pairs={{0,64},{64,0},{1,65},{65,1},{2,66},{66,2},{3,67},{67,3},{4,68},{68... | collective-permute-start | bytes 239624 | tf_op jit(solution)/shard_map/ppermute | solution.py:83
  604.1 3.6 collective-permute-start.28
  (40 other events, 110.6 us)
Sparse Core Ops, SparseCore 0:
  99.6 92.5 all-gather.2
  365.0 100.3 reduce-scatter.1

commit v4 on v3

--- a/solution.py
+++ b/solution.py
@@ -4,6 +4,7 @@
 import jax.numpy as jnp
 from jax import lax
 from jax.experimental import pallas as pl
+from jax.experimental.layout import Layout, with_layout_constraint
 from jax.experimental.pallas import tpu as pltpu
 from jax.sharding import Mesh
 from jax.sharding import PartitionSpec as P
@@ -153,21 +154,24 @@
     tops = [jnp.max(t, axis=0, keepdims=True) for t in tops]
 
     def mix(r, rows, carry):
-        out = []
+        totals, acc = carry
+        out, weights = [], []
         for h in range(GROUP):
-            total, acc = carry[h]
             p = jnp.exp(sc[h, r, rows, :] - tops[h])
-            out.append((total + fold(p, jnp.sum), acc + nn(vt[r, :, rows], p.astype(BF))))
-        return tuple(out)
-
-    zero = tuple(
-        (jnp.zeros((8, HALF), F32), jnp.zeros((HEAD_WIDTH, HALF), F32)) for _ in range(GROUP)
+            out.append(totals[h] + fold(p, jnp.sum))
+            weights.append(p.astype(BF))
+        return tuple(out), acc + nn(vt[r, :, rows], jnp.concatenate(weights, 1))
+
+    zero = (
+        tuple(jnp.zeros((8, HALF), F32) for _ in range(GROUP)),
+        jnp.zeros((HEAD_WIDTH, GROUP * HALF), F32),
     )
     carry = mix(0, own, zero)
-    carry = lax.fori_loop(1, y + 1, lambda r, c: mix(r, slice(0, SPAN), c), carry)
+    totals, acc = lax.fori_loop(1, y + 1, lambda r, c: mix(r, slice(0, SPAN), c), carry)
     for h in range(GROUP):
-        total = jnp.sum(carry[h][0], axis=0, keepdims=True)
-        o_ref[h * HEAD_WIDTH : (h + 1) * HEAD_WIDTH, :] = (carry[h][1] / total).astype(BF)
+        total = jnp.sum(totals[h], axis=0, keepdims=True)
+        mixed = acc[:, h * HALF : (h + 1) * HALF] / total
+        o_ref[h * HEAD_WIDTH : (h + 1) * HEAD_WIDTH, :] = mixed.astype(BF)
         lse_ref[0, h : h + 1, :] = tops[h] + jnp.log(total)
 
 
@@ -209,7 +213,7 @@
     )(y, q_t, *kvs, seg_q, seg_k)
 
 
-def bwd_kernel(y_ref, q_ref, d_ref, o_0, o_1, lse_0, lse_1, kv0, kv1, kv2, kv3, seg_q, seg_k, dq_ref, g0, g1, g2, g3, bias, kn, vn, kt, dk, dv):
+def bwd_kernel(y_ref, q_ref, d_ref, o_0, o_1, lse_0, lse_1, kv0, kv1, kv2, kv3, seg_q, seg_k, dq_ref, g0, g1, g2, g3, bias, kn, vn, kt, dvk):
     y = y_ref[0]
     @pl.when(pl.program_id(0)==0)
     def _(): write_bias(bias, seg_q, seg_k, y, 0)
@@ -219,7 +223,7 @@
             vn[r] = kv[1].T
             kt[r] = kv[0]
         pl.when(y>=r)(fill)
-    dk[...] = jnp.zeros_like(dk); dv[...] = jnp.zeros_like(dv)
+    dvk[...] = jnp.zeros_like(dvk)
     scale = jnp.asarray(HEAD_WIDTH**-0.5, BF)
     for b in range(2):
         cols = slice(b*HALF,(b+1)*HALF)
@@ -232,28 +236,33 @@
             ds.append(d); dn.append(d.T)
             dots.append(jnp.sum(d.astype(F32)*(o_0, o_1)[b][hr].astype(F32),axis=0,keepdims=True))
             lses.append((lse_0, lse_1)[b][0, h : h + 1])
+        right = []
+        for h in range(GROUP):
+            none = jnp.zeros_like(dn[h])
+            right += [jnp.concatenate([dn[h], none], 1), jnp.concatenate([none, qn[h]], 1)]
+        right = jnp.concatenate(right, 0)
+
         def step(r, rows, carry):
-            out=[]; sum_k=None; sum_v=None
+            left = []
             for h in range(GROUP):
                 s = nn(kn[r, rows, :], qs[h]) + bias[r, rows, cols]
                 p = jnp.exp(s - lses[h])
-                pv = nn(p.astype(BF), dn[h])
                 dp = nn(vn[r, rows, :], ds[h])
-                dsc = (p*(dp - dots[h])).astype(BF)
-                pk = nn(dsc, qn[h])
-                out.append(carry[h] + nn(kt[r,:,rows], dsc))
-                sum_k = pk if sum_k is None else sum_k+pk
-                sum_v = pv if sum_v is None else sum_v+pv
-            dk[r, rows, :] += sum_k
-            dv[r, rows, :] += sum_v
-            return tuple(out)
-        carry = step(0, slice(0,(b+1)*HALF), tuple(jnp.zeros((HEAD_WIDTH,HALF),F32) for _ in range(GROUP)))
+                dsc = (p * (dp - dots[h])).astype(BF)
+                left += [p.astype(BF), dsc]
+            dvk[r, rows, :] += nn(jnp.concatenate(left, 1), right)
+            return carry + nn(kt[r, :, rows], jnp.concatenate(left[1::2], 1))
+
+        carry = step(0, slice(0, (b + 1) * HALF), jnp.zeros((HEAD_WIDTH, GROUP * HALF), F32))
         carry = lax.fori_loop(1, y+1, lambda r,c: step(r, slice(0,SPAN), c), carry)
         for h in range(GROUP):
-            dq_ref[h*HEAD_WIDTH:(h+1)*HEAD_WIDTH, cols] = (carry[h]*HEAD_WIDTH**-0.5).astype(BF)
+            dq_ref[h*HEAD_WIDTH:(h+1)*HEAD_WIDTH, cols] = (
+                carry[:, h * HALF : (h + 1) * HALF] * HEAD_WIDTH**-0.5
+            ).astype(BF)
     for r,g in enumerate((g0,g1,g2,g3)):
-        g[0] = dk[r].T.astype(BF)
-        g[1] = dv[r].T.astype(BF)
+        turned = dvk[r].T.astype(BF)
+        g[0] = turned[HEAD_WIDTH:]
+        g[1] = turned[:HEAD_WIDTH]
 
 def attend_back(first, count, y, q_t, d_t, outs, lses, kvs, seg_q, seg_k):
     rows = GROUP * HEAD_WIDTH
@@ -275,7 +284,7 @@
         scratch_shapes=[pltpu.VMEM((4, SPAN, SPAN), F32)]
         + [pltpu.VMEM((4, SPAN, HEAD_WIDTH), BF)] * 2
         + [pltpu.VMEM((4, HEAD_WIDTH, SPAN), BF)]
-        + [pltpu.VMEM((4, SPAN, HEAD_WIDTH), F32)] * 2,
+        + [pltpu.VMEM((4, SPAN, 2 * HEAD_WIDTH), F32)],
         compiler_params=pltpu.CompilerParams(vmem_limit_bytes=60 << 20),
         cost_estimate=pl.CostEstimate(
             flops=150_000_000_000, bytes_accessed=6_000_000, transcendentals=6_000_000
@@ -284,7 +293,7 @@
 
 
 def flat(ref):
-    return ref[...].reshape(ref.shape[0] * ref.shape[2], ref.shape[3])
+    return ref[...].reshape(ref.shape[0] * ref.shape[3], ref.shape[4])
 
 
 def experts_kernel(x_ref, gate_ref, up_ref, down_ref, g_ref, u_ref, inner_ref, out_ref, acc):
@@ -345,16 +354,19 @@
         x_t[...] = x_ref[...].T
         d_t[...] = d_ref[...].T
 
-    depth = out_ref.shape[2]
+    depth = out_ref.shape[3]
     for i, (left, right) in enumerate(((x_t, dg_ref), (x_t, du_ref), (d_t, inner_ref))):
         for y in range(4):
-            out_ref[y, i] = nn(left[y * depth : (y + 1) * depth], right[...]).astype(BF)
+            out_ref[y, 0, i] = nn(left[y * depth : (y + 1) * depth], right[...]).astype(BF)
 
 
 def expert_specs(rows, width, hidden):
     whole = pl.BlockSpec((rows, width), lambda b: (0, 0))
     weights = [
-        pl.BlockSpec((4, 1, width // 4, HALF), functools.partial(lambda i, b: (0, i, 0, b), i))
+        pl.BlockSpec(
+            (4, 1, 1, width // 4, HALF),
+            functools.partial(lambda i, b: (0, b // 2, i, 0, b % 2), i),
+        )
         for i in range(3)
     ]
     column = pl.BlockSpec((rows, HALF), lambda b: (0, b))
@@ -370,7 +382,7 @@
 
 def run_experts(x, experts_full):
     rows, width = x.shape
-    hidden = experts_full.shape[3]
+    hidden = 2 * experts_full.shape[4]
     common, whole, weights, column = expert_specs(rows, width, hidden)
     wide = jax.ShapeDtypeStruct((rows, hidden), F32)
     return pl.pallas_call(
@@ -389,7 +401,7 @@
 
 def run_experts_back(d, gate, up, experts_full):
     rows, width = d.shape
-    hidden = experts_full.shape[3]
+    hidden = 2 * experts_full.shape[4]
     common, whole, weights, column = expert_specs(rows, width, hidden)
     low = jax.ShapeDtypeStruct((rows, hidden), BF)
     common["scratch_shapes"] = common["scratch_shapes"] + [pltpu.VMEM((rows, HALF), F32)]
@@ -410,8 +422,8 @@
     return pl.pallas_call(
         expert_grads_kernel,
         in_specs=[whole, whole, column, column, column],
-        out_specs=pl.BlockSpec((4, 3, width // 4, HALF), lambda b: (0, 0, 0, b)),
-        out_shape=jax.ShapeDtypeStruct((4, 3, width // 4, hidden), BF),
+        out_specs=pl.BlockSpec((4, 1, 3, width // 4, HALF), lambda b: (0, b // 2, 0, 0, b % 2)),
+        out_shape=jax.ShapeDtypeStruct((4, 2, 3, width // 4, hidden // 2), BF),
         **common,
     )(x, d, d_gate, d_up, inner)
 
@@ -457,7 +469,7 @@
                             ref[y, j, 0] = value
 
 
-def pack_grads(plan, first_axis, arrays, wide, cols):
+def pack_grads(plan, first_axis, arrays, wide, cols, flops):
     specs = []
     for i, value in enumerate(arrays):
         if i in wide:
@@ -476,15 +488,32 @@
         out_specs=[out_spec, out_spec],
         out_shape=[out, out],
         scratch_shapes=[pltpu.VMEM((384, cols), F32)],
-        compiler_params=pltpu.CompilerParams(vmem_limit_bytes=40 << 20),
+        compiler_params=pltpu.CompilerParams(
+            vmem_limit_bytes=(60 if len(arrays) > 4 else 40) << 20
+        ),
         cost_estimate=pl.CostEstimate(
-            flops=20_000_000_000, bytes_accessed=12_000_000, transcendentals=0
+            flops=flops, bytes_accessed=flops // 2000, transcendentals=0
         ),
     )(jnp.full((1,), lax.axis_index("c"), jnp.int32), *arrays)
 
 
-def paired(own, theirs):
-    return (own.astype(F32) + swap(theirs, "c").astype(F32)).astype(BF)
+def pair_blocks(own, theirs, axis):
+    received = swap(theirs, "c")
+    me = lax.axis_index(axis)
+    blocks = []
+    for r in range(4):
+        mine, other = (
+            lax.dynamic_index_in_dim(part, (me + r) % 4, 0, keepdims=False)
+            for part in (own, received)
+        )
+        blocks.append(both(mine, other).astype(BF))
+    return blocks
+
+
+def send_blocks(blocks, axis):
+    return blocks[:1] + [
+        lax.ppermute(blocks[r], axis, [(i, (i + r) % 4) for i in range(4)]) for r in range(1, 4)
+    ]
 
 
 def local(
@@ -519,12 +548,24 @@
         ],
         axis=1,
     )
-    by_hy = gather_hy(jnp.concatenate([key_weight, value_weight, small, w_query, w_out.T], axis=1))
+    experts = jnp.stack([w_gate[0], w_up[0], w_down[0].T])
+    by_hy, experts = lax.optimization_barrier(
+        (
+            gather_hy(
+                jnp.concatenate([key_weight, value_weight, small, w_query, w_out.T], axis=1)
+            ),
+            experts,
+        )
+    )
     kv_cols = 2 * k_width + 128
-    pack = core_gather(gather_x(by_hy[:, :, :kv_cols]))
+    wide_rest = by_hy[:, :, kv_cols:]
+    wide_rest = jnp.broadcast_to(wide_rest[None], (4, *wide_rest.shape))
+    ring_kv, wide_rest = lax.optimization_barrier((gather_x(by_hy[:, :, :kv_cols]), wide_rest))
+    experts_other = swap(experts, "t")
+    ring_rest = lax.all_to_all(wide_rest, "x", 0, 0, tiled=True)
+    pack = core_gather(ring_kv)
     full_kv = pack[:, : 2 * k_width]
     full_small = pack[:, 2 * k_width :]
-    ring_rest = gather_x(by_hy[:, :, kv_cols:])
     small_rows = dot(jnp.eye(24, 128, dtype=BF), full_small, 1, 1)
     router_rows = small_rows[:EXPERTS].astype(BF)
     gain_one = small_rows[EXPERTS : EXPERTS + 1]
@@ -537,18 +578,16 @@
     kvs = [kv_mine] + [
         lax.ppermute(kv_mine, "y", [(i, i + r) for i in range(4 - r)]) for r in (1, 2, 3)
     ]
-    kvs[1:] = lax.optimization_barrier((*kvs[1:], ring_rest))[:3]
+    experts_other, ring_rest = lax.optimization_barrier((experts_other, ring_rest))
+    experts_full = jnp.stack([experts, experts_other])
+    *kvs[1:], ring_rest, experts_full = lax.optimization_barrier(
+        (*kvs[1:], ring_rest, experts_full)
+    )
     rest = core_gather(ring_rest)
     full_query = rest[:, :q_width]
     full_out = rest[:, q_width:]
     query_t = dot(full_query, act_one, 0, 1).astype(BF)
 
-    late_gate, late_up, late_down = lax.optimization_barrier(
-        (w_gate[0], w_up[0], w_down[0], kv_mine)
-    )[:3]
-    experts = jnp.stack([late_gate, late_up, late_down.T])
-    experts_other = after(swap(experts, "t"), kvs[1], kvs[2], kvs[3])
-    experts_full = jnp.concatenate([experts, experts_other], axis=2)
     experts_full = lax.all_gather(experts_full, "y", axis=0)
 
     seg_blocks = segments[0].reshape(4, tok_rows)
@@ -595,10 +634,12 @@
         jnp.where(picks[0], gates[0], 0.0) + jnp.where(picks[1], gates[1], 0.0)
     ).astype(BF)
 
-    received = exchange_slots(dot(pick, act_two, 1, 0).astype(BF))
+    received, pick_t, gated_pick_t = lax.optimization_barrier(
+        (exchange_slots(dot(pick, act_two, 1, 0).astype(BF)), pick.T, gated_pick.T)
+    )
     gate_proj, up_proj, inner, slots_out = run_experts(received, experts_full)
     returned = exchange_slots(slots_out)
-    part = dot(gated_pick, returned, 0, 0).astype(BF)
+    part = dot(gated_pick_t, returned, 1, 0).astype(BF)
     output = hidden + both(part, swap(part, "t"))
     valid = (seg_mine != 0).astype(F32)
     difference = output - teacher.astype(F32)
@@ -625,9 +666,7 @@
     grad_parts = expert_grads(received, d_received, d_gate_proj, d_up_proj, inner)
     grad_experts = lax.psum_scatter(grad_parts, "y", scatter_dimension=0)
     d_returned = after(d_returned, grad_parts)
-    ff_half = w_gate.shape[2]
-    keep = grad_experts[:, :, :ff_half]
-    give = grad_experts[:, :, ff_half:]
+    keep, give = grad_experts[0], grad_experts[1]
 
     d_router = jnp.where(named[0], d_gates[0:1] * weight_cols[0:1], 0.0) + jnp.where(
         named[1], d_gates[1:2] * weight_cols[1:2], 0.0
@@ -636,7 +675,7 @@
         router * (d_router - jnp.sum(router * d_router, axis=0, keepdims=True))
     ).astype(BF)
     d_route = dot(d_logits, router_rows, 0, 0)
-    part = dot(pick, d_returned, 0, 0).astype(BF)
+    part = dot(pick_t, d_returned, 1, 0).astype(BF)
     d_act_two = d_route + both(part, after(swap(part, "t"), d_route))
     d_norm_two, grad_gain_two = norm_back(hidden, scale_two, gain_two, d_act_two)
     d_hidden = grad_output + d_norm_two
@@ -655,15 +694,16 @@
     *back_0, d_mixed_t, give = lax.optimization_barrier((*back_0, d_mixed_t, give))
     back_1 = attend_back(half_groups, half_groups, place_y, query_t, d_mixed_t, *saved)
     others_0 = ring_back(back_0[1:])
-    given = swap(give, "t")
-    *back_1, o1, o2, o3, given, d_attn_late, gain_late, d_logits_late, back_0[0] = (
+    given_0 = swap(give[:2], "t")
+    *back_1, o1, o2, o3, given_0, give, d_attn_late, gain_late, d_logits_late, back_0[0] = (
         lax.optimization_barrier(
-            (*back_1, *others_0, given, d_attn, grad_gain_two, d_logits, back_0[0])
+            (*back_1, *others_0, given_0, give[2], d_attn, grad_gain_two, d_logits, back_0[0])
         )
     )
     others_0 = [o1, o2, o3]
 
     others_1 = ring_back(back_1[1:])
+    given_1 = swap(give, "t")
     lines = jnp.concatenate(
         [
             gain_late,
@@ -686,10 +726,11 @@
         (d_attn_late, act_one, act_two, lines, mixed_0, mixed_1, logits_pad, back_0[0], back_1[0]),
         (0, 1, 2, 3),
         feat_width // 2 + 128 + q_width,
+        20_000_000_000,
     )
     d_act_query = dot(jnp.concatenate([back_0[0], back_1[0]]), full_query, 0, 1)
-    o1, o2, o3, own_one, theirs_one, d_act_query = lax.optimization_barrier(
-        (*others_1, own_one, theirs_one, d_act_query)
+    o1, o2, o3, given_1, own_one, theirs_one, d_act_query = lax.optimization_barrier(
+        (*others_1, given_1, own_one, theirs_one, d_act_query)
     )
 
     d_kv_t = jnp.concatenate(
@@ -697,35 +738,40 @@
     ).reshape(2 * k_width, tok_rows).astype(BF)
     d_act_part = d_act_query + dot(d_kv_t, full_kv, 0, 1)
     part = d_act_part.astype(BF)
-    pair_one = paired(own_one, theirs_one)
+    blocks_one = pair_blocks(own_one, theirs_one, "x")
+    gain_row = jnp.sum(d_act_part * resid_in * scale_one, axis=0, keepdims=True)
     lines = jnp.concatenate(
-        [
-            jnp.sum(d_act_part * resid_in * scale_one, axis=0, keepdims=True),
-            jnp.zeros((7, feat_width), F32),
-        ]
+        [gain_row, jnp.zeros((7, feat_width), F32)]
     )
     own_two, theirs_two = pack_grads(
-        (((0, 2, 0),), ((None, 1, 0),)), "y", (act_one, lines, d_kv_t), (0, 1), 2 * k_width + 128
-    )
-    part, pair_one, own_two, theirs_two = lax.optimization_barrier(
-        (part, pair_one, own_two, theirs_two)
+        (((0, 2, 0),), ((None, 1, 0),)),
+        "y",
+        (act_one, lines, d_kv_t),
+        (0, 1),
+        2 * k_width + 128,
+        2_000_000_000,
+    )
+    part, own_two, theirs_two, *blocks_one = lax.optimization_barrier(
+        (part, own_two, theirs_two, *blocks_one)
     )
     other = swap(part, "t")
-    parts_one = axis_parts(pair_one, "x", 4)
-    ring_two = lax.all_to_all(paired(own_two, theirs_two), "y", 0, 0, tiled=True)
-    grad_stack = keep.astype(F32) + given.astype(F32)
-    own_down = grad_stack[2].T
+    parts_one = send_blocks(blocks_one, "x")
+    paired_two = both(own_two, swap(theirs_two, "c")).astype(BF)
+    ring_two = lax.all_to_all(paired_two, "y", 0, 0, tiled=True)
+    grad_wide = keep[:2].astype(F32) + given_0.astype(F32)
+    own_down = with_layout_constraint(both(keep[2], given_1).T, Layout(major_to_minor=(0, 1)))
     *parts_one, ring_two, own_down, other = lax.optimization_barrier(
         (*parts_one, ring_two, own_down, other)
     )
     by_x = added(parts_one).astype(BF)
-    by_xy = added(axis_parts(by_x, "y", 4)).astype(BF)
+    by_y = jnp.sum(ring_two.astype(F32), axis=0).astype(BF)
+    by_xy = jnp.concatenate(
+        [added(axis_parts(by_x, "y", 4)), added(axis_parts(by_y, "x", 4))], axis=2
+    ).astype(BF)
     by_xy, other = lax.optimization_barrier((by_xy, other))
     summed = added(axis_parts(by_xy, "h", 2))
-    by_y = jnp.sum(ring_two.astype(F32), axis=0).astype(BF)
-    ring_two = lax.all_to_all(by_y.reshape(8, *by_y.shape[2:]), ("x", "h"), 0, 0, tiled=True)
-    own_kv = jnp.sum(ring_two.astype(F32), axis=0)
-    own_query = summed[:, feat_width // 2 + 128 :]
+    own_kv = summed[:, by_x.shape[3] :]
+    own_query = summed[:, feat_width // 2 + 128 : by_x.shape[3]]
     at = feat_width // 2
     own_out = summed[:, :at].T
     own_router = summed[:, at : at + EXPERTS]
@@ -735,9 +781,9 @@
         feat_width * (summed[0, at + 2] + summed[0, at + 10])
     )
     own_gain_one = own_kv[:, 2 * k_width + EXPERTS] + own_kv[:, 2 * k_width + EXPERTS + 8]
-    own_gain_one = own_gain_one + swap(own_gain_one, "t")
     d_hidden_one, _ = norm_back(resid_in, scale_one, gain_one, both(part, other))
     grad_tokens = d_hidden + d_hidden_one
+    own_gain_one = own_gain_one + swap(own_gain_one, "t")
     return (
         output,
         loss_value,
@@ -749,8 +795,8 @@
         own_out,
         own_gain_two,
         own_router,
-        grad_stack[0][None],
-        grad_stack[1][None],
+        grad_wide[0][None],
+        grad_wide[1][None],
         own_down[None],
     )
 

time: 631 us -> 634 us (level)
  blocking collectives: 76.8 us -> 37.5 us
  starting transfers between devices: 69.4 us -> 92 us
  local copies, waits for them, and re-layouts: 36 us -> 44 us
    all_to_all x2 -> x0, blocking collectives: 40 us -> none  [the longest x1 23 us: gather_hy(): return lax.all_to_all(wide, ('h', 'y'), 0, 0, tiled=True)]
    ppermute x7, waiting for transfers between devices: 26.5 us -> 6.16 us  [axis_parts(): lax.ppermute(block, axis, [(i, (i + r) % size) for i in range(size)])]
    all_to_all x2 -> x3, waiting for transfers between devices: 0.01 us -> 20.3 us  [the longest x1 13.6 us: gather_hy(): return lax.all_to_all(wide, ('h', 'y'), 0, 0, tiled=True)]
    all_to_all x3, waiting for transfers between devices: 57.5 us -> 42.5 us  [exchange_slots(): lax.all_to_all(rows.reshape(EXPERTS, -1, width), ('h', 'x', 'c'), 0, 0, t...]
    all_to_all x2 -> x3, starting transfers between devices: 10.2 us -> 24.2 us  [the longest x1 11.8 us: local(): ring_two = lax.all_to_all(paired_two, 'y', 0, 0, tiled=True)]
    pallas_call x0 -> x1, local copies, waits for them, and re-layouts: none -> 12.7 us  [expert_grads(): pl.pallas_call(expert_grads_kernel, in_specs=[whole, whole, column, colum...]
    reduce_scatter x1, waiting for transfers between devices: 27.1 us -> 38 us  [local(): grad_experts = lax.psum_scatter(grad_parts, 'y', scatter_dimension=0)]
    ppermute x13 -> x14, waiting for transfers between devices: 136 us -> 143 us  [swap(): return lax.ppermute(value, axis, [(0, 1), (1, 0)])]
  transfers between devices with their start and end apart: 37 -> 42, of which waited for: 21 -> 22; matrix products, arithmetic and copies ran while one was open for 11% -> 15% of each run, Pallas kernels for 8% -> 8%
where the time goes in v4:
time: 634 us; the launch traced here: 624 us
  waiting for transfers between devices  273 us (43%)
  starting transfers between devices  92 us (15%)
  Pallas kernels  78.5 us (12%)
  other arithmetic  50.8 us (8%)
  local copies, waits for them, and re-layouts  44 us (7%)
  blocking collectives  37.5 us (6%)
  matrix products  28.7 us (5%)
  between operations  19.4 us (3%)
    ppermute x14, waiting for transfers between devices, swap(): return lax.ppermute(value, axis, [(0, 1), (1, 0)])  143 us
    all_to_all x3, waiting for transfers between devices, exchange_slots(): lax.all_to_all(rows.reshape(EXPERTS, -1, width), ('h', 'x', 'c'), 0, 0, t...  42.5 us
    reduce_scatter x1, waiting for transfers between devices, local(): grad_experts = lax.psum_scatter(grad_parts, 'y', scatter_dimension=0)  38 us
    all_to_all x1, blocking collectives, exchange_slots(): lax.all_to_all(rows.reshape(EXPERTS, -1, width), ('h', 'x', 'c'), 0, 0, t...  37.5 us
    dot_general x16, matrix products, dot(): lax.dot_general(left, right, (((left_dim,), (right_dim,)), ((), ())), pre...  28.7 us
    ppermute x7, starting transfers between devices, axis_parts(): lax.ppermute(block, axis, [(i, (i + r) % size) for i in range(size)])  19.5 us
    pallas_call x1, Pallas kernels, run_experts_back(): pl.pallas_call(experts_back_kernel, in_specs=[whole, column, column] + we...  17.2 us
    pallas_call x2, Pallas kernels, attend_back(): pl.pallas_call(bwd_kernel, grid=(count,), in_specs=[pl.BlockSpec(memory_s...  14.2 us
  transfers between devices with their start and end apart: 42, of which 22 were waited for; matrix products, arithmetic and copies ran while one was open for 15% of the time, Pallas kernels for 8%

profile of v4, /device:TPU:0, one launch (start us, length us, event | category | flops | bytes accessed | tf_op | source)
XLA Modules:
  0.0 623.7 jit_solution(6633359849290431706)
XLA Ops:
  11.4 7.9 %all-to-all-start = ((bf16[8,24,2176]{2,1,0:T(8,128)(2,1)}), bf16[8,24,2176]{2,1,0:T(8,128)(2,1)S(1)}, u32[]{:S(2)}, u32[]{:S(2)}) async-start(bf16[8,24,2176]{2,1,0:T(8,128)(2,1)} %broadcast_in_dim.149), calls=%async_computation | async-start | bytes 1671168 | tf_op jit(solution)/shard_map/all_to_all | solution.py:57
  20.7 13.6 %all-to-all-done = bf16[8,24,2176]{2,1,0:T(8,128)(2,1)S(1)} async-done(((bf16[8,24,2176]{2,1,0:T(8,128)(2,1)}), bf16[8,24,2176]{2,1,0:T(8,128)(2,1)S(1)}, u32[]{:S(2)}, u32[]{:S(2)}) %all-to-all-start) | async-done | bytes 835616 | tf_op jit(solution)/shard_map/all_to_all | solution.py:57
  35.5 4.3 all-to-all-start.1
  41.0 13.0 %all-to-all-done.1 = bf16[4,8,24,640]{3,2,1,0:T(8,128)(2,1)S(1)} async-done(((bf16[4,8,24,640]{3,2,1,0:T(8,128)(2,1)}), bf16[4,8,24,640]{3,2,1,0:T(8,128)(2,1)S(1)}, u32[]{:S(2)}, u32[]{:S(2)}) %all-to-all-start.1) | async-done | bytes 983072 | tf_op jit(solution)/shard_map/all_to_all | solution.py:62
  57.1 4.5 all-to-all-start.2
  66.7 2.4 collective-permute-start.2
  69.1 2.1 collective-permute-start.1
  71.2 13.6 %collective-permute-done.4 = bf16[3,384,512]{2,1,0:T(8,128)(2,1)} collective-permute-done((bf16[3,384,512]{2,1,0:T(8,128)(2,1)}, bf16[3,384,512]{2,1,0:T(8,128)(2,1)}, u32[]{:S(2)}, u32[]{:S(2)}) %collective-permute-start.4) | collective-permute-done | bytes 1179680 | tf_op jit(solution)/shard_map/ppermute | solution.py:48
  84.8 6.7 %all-to-all-done.2 = bf16[4,8,24,1536]{3,2,1,0:T(8,128)(2,1)} async-done(((bf16[4,8,24,1536]{3,2,1,0:T(8,128)(2,1)}), bf16[4,8,24,1536]{3,2,1,0:T(8,128)(2,1)}, u32[]{:S(2)}, u32[]{:S(2)}) %all-to-all-start.2) | async-done | bytes 2359328 | tf_op jit(solution)/shard_map/all_to_all | solution.py:565
  91.5 3.3 pad_maximum_fusion.1
  97.5 2.3 collective-permute-done.5
  99.8 3.1 select_bitcast_fusion.1
  105.9 4.1 shard_map.246
  112.0 4.7 shard_map.247
  117.4 13.4 %collective-permute-done.6 = bf16[256,1536]{1,0:T(8,128)(2,1)S(1)} collective-permute-done((bf16[256,1536]{1,0:T(8,128)(2,1)S(1)}, bf16[256,1536]{1,0:T(8,128)(2,1)S(1)}, u32[]{:S(2)}, u32[]{:S(2)}) %collective-permute-start.6) | collective-permute-done | bytes 786464 | tf_op jit(solution)/shard_map/ppermute | solution.py:48
  134.7 17.1 %collective-permute-done.7 = bf16[256,1536]{1,0:T(8,128)(2,1)} collective-permute-done((bf16[256,1536]{1,0:T(8,128)(2,1)}, bf16[256,1536]{1,0:T(8,128)(2,1)}, u32[]{:S(2)}, u32[]{:S(2)}) %collective-permute-start.7) | collective-permute-done | bytes 786464 | tf_op jit(solution)/shard_map/ppermute | solution.py:48
  156.4 2.8 convolution_convert_fusion.1
  159.2 3.9 all-to-all-start.3
  165.5 29.6 %all-to-all-done.3 = bf16[16,48,1536]{2,1,0:T(8,128)(2,1)S(1)} async-done(((bf16[16,48,1536]{2,1,0:T(8,128)(2,1)}), bf16[16,48,1536]{2,1,0:T(8,128)(2,1)S(1)}, u32[]{:S(2)}, u32[]{:S(2)}) %all-to-all-start.3) | async-done | bytes 2359328 | tf_op jit(solution)/shard_map/all_to_all | solution.py:97
  196.5 13.6 %shard_map.248 = (f32[768,1024]{1,0:T(8,128)}, f32[768,1024]{1,0:T(8,128)}, bf16[768,1024]{1,0:T(8,128)(2,1)}, bf16[768,1536]{1,0:T(8,128)(2,1)}) custom-call(bf16[768,1536]{1,0:T(8,128)(2,1)} %bitcast.155, bf16[4,2,3,384,512]{4,3,2,1,0:T(8,128)(2,1)} %bitcast.149, bf16[4,2,3,384,512]{4,3,2,1,0:T(8,128)(2,1)} %bitcast.150, bf16[4,2,3,384,512]{4,3,2,1,0:T(8,128)(2,1)} %bitcast.151), custom_call_target="tpu_custom_call" | custom-call | flops 7247757312 | bytes 20000000 | tf_op jit(solution)/shard_map/pallas_call | solution.py:388
  210.2 37.5 %all_to_all.40 = bf16[16,48,1536]{2,1,0:T(8,128)(2,1)S(1)} all-to-all(bf16[16,48,1536]{2,1,0:T(8,128)(2,1)} %bitcast.174), channel_id=1, replica_groups=mesh['h'=2,'x'=4,'c'=2,'y'=4,'t'=2] {'h','x','c'}, dimensions={0} | all-to-all | bytes 4718592 | tf_op jit(solution)/shard_map/all_to_all | solution.py:97
  250.3 35.3 %collective-permute-done.8 = bf16[512,1536]{1,0:T(8,128)(2,1)S(1)} collective-permute-done((bf16[512,1536]{1,0:T(8,128)(2,1)S(1)}, bf16[512,1536]{1,0:T(8,128)(2,1)S(1)}, u32[]{:S(2)}, u32[]{:S(2)}) %collective-permute-start.8) | collective-permute-done | bytes 1572896 | tf_op jit(solution)/shard_map/ppermute | solution.py:48
  285.6 2.0 fusion.7
  288.0 2.8 convolution_convert_fusion
  290.8 4.5 all-to-all-start.5
  295.3 3.8 select_reduce_fusion.1
  299.8 20.2 %collective-permute-done.9 = f32[2,512]{1,0:T(2,128)S(1)} collective-permute-done((f32[2,512]{1,0:T(2,128)S(1)}, f32[2,512]{1,0:T(2,128)S(1)}, u32[]{:S(2)}, u32[]{:S(2)}) %collective-permute-start.9) | collective-permute-done | bytes 4128 | tf_op jit(solution)/shard_map/ppermute | solution.py:48
  320.0 7.3 %all-to-all-done.5 = bf16[16,48,1536]{2,1,0:T(8,128)(2,1)} async-done(((bf16[16,48,1536]{2,1,0:T(8,128)(2,1)}), bf16[16,48,1536]{2,1,0:T(8,128)(2,1)}, u32[]{:S(2)}, u32[]{:S(2)}) %all-to-all-start.5) | async-done | bytes 2359328 | tf_op jit(solution)/shard_map/all_to_all | solution.py:97
  327.4 17.2 %shard_map.249 = (bf16[768,1024]{1,0:T(8,128)(2,1)}, bf16[768,1024]{1,0:T(8,128)(2,1)}, bf16[768,1536]{1,0:T(8,128)(2,1)}) custom-call(bf16[768,1536]{1,0:T(8,128)(2,1)} %bitcast.50.d_ref, f32[768,1024]{1,0:T(8,128)} %get-tuple-element.123.g_ref, f32[768,1024]{1,0:T(8,128)} %get-tuple-element.124.u_ref, bf16[4,2,3,384,512]{4,3,2,1,0:T(8,128)(2,1)} %bitcast.152, ...), custom_call_target="tpu_custom_call" | custom-call | flops 7247757312 | bytes 20000000 | tf_op jit(solution)/shard_map/pallas_call | solution.py:408
  344.5 5.5 all-to-all-start.6
  350.1 13.8 %shard_map.250 = bf16[4,2,3,384,512]{4,3,2,1,0:T(8,128)(2,1)} custom-call(bf16[768,1536]{1,0:T(8,128)(2,1)} %bitcast.156, bf16[768,1536]{1,0:T(8,128)(2,1)} %bitcast.50.d_ref, bf16[768,1024]{1,0:T(8,128)(2,1)} %get-tuple-element.128.dg_ref, bf16[768,1024]{1,0:T(8,128)(2,1)} %get-tuple-element.129.du_ref, bf16[768,1024]{1,0:T(8,128)(2,1)} %get-tuple-element.130.inner_ref), custom_call_target="tpu_custom_call" | custom-call | flops 7247757312 | bytes 20000000 | tf_op jit(solution)/shard_map/pallas_call | solution.py:422
  363.9 12.7 %copy.79 = bf16[4,2,3,384,512]{3,4,2,1,0:T(8,128)(2,1)} copy(bf16[4,2,3,384,512]{4,3,2,1,0:T(8,128)(2,1)} %shard_map.250) | data formatting | bytes 18874368 | tf_op jit(solution)/shard_map/pallas_call | solution.py:422
  376.6 5.6 all-to-all-done.6
  382.2 3.3 convolution_convert_fusion.2
  390.9 30.9 %collective-permute-done.10 = bf16[512,1536]{1,0:T(8,128)(2,1)S(1)} collective-permute-done((bf16[512,1536]{1,0:T(8,128)(2,1)S(1)}, bf16[512,1536]{1,0:T(8,128)(2,1)S(1)}, u32[]{:S(2)}, u32[]{:S(2)}) %collective-permute-start.10) | collective-permute-done | bytes 1572896 | tf_op jit(solution)/shard_map/ppermute | solution.py:48
  423.7 3.3 fusion.75
  427.0 2.3 fusion.24.d_ref
  429.3 7.2 %shard_map.251 = (bf16[384,512]{1,0:T(8,128)(2,1)}, bf16[2,128,512]{2,1,0:T(8,128)(2,1)}, bf16[2,128,512]{2,1,0:T(8,128)(2,1)}, bf16[2,128,512]{2,1,0:T(8,128)(2,1)}, bf16[2,128,512]{2,1,0:T(8,128)(2,1)}) custom-call(s32[1]{0:T(128)} %bitcast.y_ref, bf16[768,512]{1,0:T(8,128)(2,1)} %copy-done.11, bf16[768,512]{1,0:T(8,128)(2,1)} %fusion.24.d_ref, ...), custom_call_target="tpu_custom_call" | custom-call | flops 149999992832 | bytes 6000000 | tf_op jit(solution)/shard_map/pallas_call | solution.py:274
  436.5 38.0 %reduce-scatter.2.cloned.1.call-done = bf16[1,2,3,384,512]{3,4,2,1,0:T(8,128)(2,1)} async-done(((bf16[4,2,3,384,512]{3,4,2,1,0:T(8,128)(2,1)}), bf16[1,2,3,384,512]{3,4,2,1,0:T(8,128)(2,1)}) %reduce-scatter.2.cloned.1.call-update) | async-done | bytes 2359312 | tf_op jit(solution)/shard_map/reduce_scatter | solution.py:667
  482.6 7.0 %shard_map.252 = (bf16[384,512]{1,0:T(8,128)(2,1)}, bf16[2,128,512]{2,1,0:T(8,128)(2,1)}, bf16[2,128,512]{2,1,0:T(8,128)(2,1)}, bf16[2,128,512]{2,1,0:T(8,128)(2,1)}, bf16[2,128,512]{2,1,0:T(8,128)(2,1)}) custom-call(s32[1]{0:T(128)} %bitcast.y_ref, bf16[768,512]{1,0:T(8,128)(2,1)} %copy-done.11, bf16[768,512]{1,0:T(8,128)(2,1)} %fusion.24.d_ref, ...), custom_call_target="tpu_custom_call" | custom-call | flops 149999992832 | bytes 6000000 | tf_op jit(solution)/shard_map/pallas_call | solution.py:274
  490.7 4.0 collective-permute-done.13
  494.7 6.0 collective-permute-done.14
  507.6 8.4 %shard_map.253 = (bf16[4,4,2,24,1664]{4,3,2,1,0:T(8,128)(2,1)}, bf16[4,4,2,24,1664]{4,3,2,1,0:T(8,128)(2,1)}) custom-call(s32[1]{0:T(128)} %bitcast.55.core_ref, bf16[512,1536]{1,0:T(8,128)(2,1)} %copy-done.35, bf16[512,1536]{1,0:T(8,128)(2,1)} %copy-done, bf16[512,1536]{1,0:T(8,128)(2,1)} %copy-done.27, f32[8,1536]{1,0:T(8,128)} %maximum_maximum_fusion.refs_3_, ...), custom_call_target="tpu_custom_call" | custom-call | flops 20000000000 | bytes 10000000 | tf_op jit(solution)/shard_map/pallas_call | solution.py:484
  516.0 4.8 fusion.12
  527.3 1.8 fusion.10
  529.2 2.4 shard_map.254
  531.6 3.7 fusion.52
  537.9 2.7 collective-permute-start.21
  542.0 2.4 add_convert_fusion
  544.4 11.8 %all-to-all-start.7 = ((bf16[4,4,2,24,640]{4,3,2,1,0:T(8,128)(2,1)}), bf16[4,4,2,24,640]{4,3,2,1,0:T(8,128)(2,1)S(1)}, u32[]{:S(2)}, u32[]{:S(2)}) async-start(bf16[4,4,2,24,640]{4,3,2,1,0:T(8,128)(2,1)} %add_convert_fusion), calls=%async_computation.8 | async-start | bytes 1966080 | tf_op jit(solution)/shard_map/all_to_all | solution.py:760
  558.7 2.3 copy.83
  562.1 2.1 fusion.41
  564.3 4.4 collective-permute-done.21
  568.7 4.0 collective-permute-done.24
  574.4 1.8 collective-permute-start.30
  576.2 1.8 collective-permute-start.29
  578.0 1.8 add_convert_fusion.4
  579.8 3.8 collective-permute-start.25
  583.6 5.9 collective-permute-start.27
  591.0 2.8 collective-permute-done.25
  595.2 2.0 collective-permute-done.26
  597.3 2.8 fusion.11
  600.2 3.3 collective-permute-start.31
  603.4 4.8 fusion.6
  (269 shorter events, 86.5 us)
Async XLA Ops:
  11.4 22.8 %all-to-all-start = ((bf16[8,24,2176]{2,1,0:T(8,128)(2,1)}), bf16[8,24,2176]{2,1,0:T(8,128)(2,1)S(1)}, u32[]{:S(2)}, u32[]{:S(2)}) async-start(bf16[8,24,2176]{2,1,0:T(8,128)(2,1)} %broadcast_in_dim.149), calls=%async_computation | async-start | bytes 1671168 | tf_op jit(solution)/shard_map/all_to_all | solution.py:57
  35.5 18.5 %all-to-all-start.1 = ((bf16[4,8,24,640]{3,2,1,0:T(8,128)(2,1)}), bf16[4,8,24,640]{3,2,1,0:T(8,128)(2,1)S(1)}, u32[]{:S(2)}, u32[]{:S(2)}) async-start(bf16[4,8,24,640]{3,2,1,0:T(8,128)(2,1)} %broadcast_in_dim.150), calls=%async_computation.1 | async-start | bytes 1966080 | tf_op jit(solution)/shard_map/all_to_all | solution.py:62
  39.8 15.8 %copy-start.17 = (bf16[512,1536]{1,0:T(8,128)(2,1)S(1)}, bf16[512,1536]{1,0:T(8,128)(2,1)}, u32[]{:S(2)}) copy-start(bf16[512,1536]{1,0:T(8,128)(2,1)} %param.15) | copy-start | bytes 4718596
  55.6 6.1 collective-permute-start
  56.0 28.8 %collective-permute-start.4 = (bf16[3,384,512]{2,1,0:T(8,128)(2,1)}, bf16[3,384,512]{2,1,0:T(8,128)(2,1)}, u32[]{:S(2)}, u32[]{:S(2)}) collective-permute-start(bf16[3,384,512]{2,1,0:T(8,128)(2,1)} %pad_maximum_fusion.3), channel_id=1, source_target_pairs={{0,1},{1,0},{2,3},{3,2},{4,5},{5,4},{6,7},{7,6},{8,9},{9,8},{10,11... | collective-permute-start | bytes 3538952 | tf_op jit(solution)/shard_map/ppermute | solution.py:48
  57.1 34.4 %all-to-all-start.2 = ((bf16[4,8,24,1536]{3,2,1,0:T(8,128)(2,1)}), bf16[4,8,24,1536]{3,2,1,0:T(8,128)(2,1)}, u32[]{:S(2)}, u32[]{:S(2)}) async-start(bf16[4,8,24,1536]{3,2,1,0:T(8,128)(2,1)} %broadcast_in_dim.151), calls=%async_computation.2 | async-start | bytes 4718592 | tf_op jit(solution)/shard_map/all_to_all | solution.py:565
  61.6 133.4 %all-gather.3.cloned.1.call-start = ((), (), s32[]{:S(2)}) async-start(), calls=%async_computation.10 | async-start | bytes 11796480 | tf_op jit(solution)/shard_map/all_gather | solution.py:591
  64.3 39.6 %copy-start = (bf16[512,1536]{1,0:T(8,128)(2,1)}, bf16[512,1536]{1,0:T(8,128)(2,1)S(1)}, u32[]{:S(2)}) copy-start(bf16[512,1536]{1,0:T(8,128)(2,1)S(1)} %fusion.2.refs_1_.refs_0_) | copy-start | bytes 4718596
  65.3 46.7 %copy-start.4 = (bf16[512,512]{1,0:T(8,128)(2,1)}, bf16[512,512]{1,0:T(8,128)(2,1)S(1)}, u32[]{:S(2)}) copy-start(bf16[512,512]{1,0:T(8,128)(2,1)S(1)} %fusion.34) | copy-start | bytes 1572868
  65.3 29.4 %collective-permute-start.3 = (bf16[2,256,512]{2,1,0:T(8,128)(2,1)S(1)}, bf16[2,256,512]{2,1,0:T(8,128)(2,1)S(1)}, u32[]{:S(2)}, u32[]{:S(2)}) collective-permute-start(bf16[2,256,512]{2,1,0:T(8,128)(2,1)S(1)} %bitcast.142), channel_id=1, source_target_pairs={{0,6},{1,7},{8,14},{9,15},{16,22},{17,23},{24,30},{25,31},{32,38},... | collective-permute-start | bytes 1572872 | tf_op jit(solution)/shard_map/ppermute | solution.py:579
  66.7 28.1 %collective-permute-start.2 = (bf16[2,256,512]{2,1,0:T(8,128)(2,1)S(1)}, bf16[2,256,512]{2,1,0:T(8,128)(2,1)S(1)}, u32[]{:S(2)}, u32[]{:S(2)}) collective-permute-start(bf16[2,256,512]{2,1,0:T(8,128)(2,1)S(1)} %bitcast.143), channel_id=1, source_target_pairs={{0,4},{2,6},{1,5},{3,7},{8,12},{10,14},{9,13},{11,15},{16,20},{18,... | collective-permute-start | bytes 1572872 | tf_op jit(solution)/shard_map/ppermute | solution.py:579
  69.1 25.7 %collective-permute-start.1 = (bf16[2,256,512]{2,1,0:T(8,128)(2,1)S(1)}, bf16[2,256,512]{2,1,0:T(8,128)(2,1)}, u32[]{:S(2)}, u32[]{:S(2)}) collective-permute-start(bf16[2,256,512]{2,1,0:T(8,128)(2,1)S(1)} %bitcast.144), channel_id=1, source_target_pairs={{0,2},{2,4},{4,6},{1,3},{3,5},{5,7},{8,10},{10,12},{12,14},{9,11},... | collective-permute-start | bytes 1572872 | tf_op jit(solution)/shard_map/ppermute | solution.py:579
  94.9 5.0 collective-permute-start.5
  96.8 15.2 %copy-start.2 = (s32[2048,1]{1,0:T(8,128)}, s32[2048,1]{1,0:T(8,128)S(1)}, u32[]{:S(2)}) copy-start(s32[2048,1]{1,0:T(8,128)S(1)} %copy.76.seg_k) | copy-start | bytes 24580
  97.5 152.7 %copy-start.3 = (s32[1,512]{1,0:T(1,128)}, s32[1,512]{1,0:T(1,128)S(1)}, u32[]{:S(2)}) copy-start(s32[1,512]{1,0:T(1,128)S(1)} %get-tuple-element.262.seg_q) | copy-start | bytes 6148
  103.8 27.0 %copy-start.29 = (bf16[2,4,2,96,1536]{4,3,2,1,0:T(8,128)(2,1)}, bf16[2,4,2,96,1536]{4,3,2,1,0:T(8,128)(2,1)S(1)}, u32[]{:S(2)}) copy-start(bf16[2,4,2,96,1536]{4,3,2,1,0:T(8,128)(2,1)S(1)} %copy.75) | copy-start | bytes 14155780
  110.9 19.9 %collective-permute-start.6 = (bf16[256,1536]{1,0:T(8,128)(2,1)S(1)}, bf16[256,1536]{1,0:T(8,128)(2,1)S(1)}, u32[]{:S(2)}, u32[]{:S(2)}) collective-permute-start(bf16[256,1536]{1,0:T(8,128)(2,1)S(1)} %convolution_convert_fusion.5), channel_id=1, source_target_pairs={{0,1},{1,0},{2,3},{3,2},{4,5},{5,4},{6,7},{7,6},{8,9},{9,8},{10,11... | collective-permute-start | bytes 2359304 | tf_op jit(solution)/shard_map/ppermute | solution.py:48
  117.4 17.3 %copy-start.10 = (bf16[768,256]{1,0:T(8,128)(2,1)}, bf16[768,256]{1,0:T(8,128)(2,1)S(1)}, u32[]{:S(2)}) copy-start(bf16[768,256]{1,0:T(8,128)(2,1)S(1)} %get-tuple-element.116.o_1.refs_5_) | copy-start | bytes 1179652
  117.4 15.9 %copy-start.53 = (s32[512,2]{0,1:T(2,128)S(1)}, s32[512,2]{0,1:T(2,128)}, u32[]{:S(2)}) copy-start(s32[512,2]{0,1:T(2,128)} %param.18) | copy-start | bytes 12292
  132.6 19.2 %collective-permute-start.7 = (bf16[256,1536]{1,0:T(8,128)(2,1)}, bf16[256,1536]{1,0:T(8,128)(2,1)}, u32[]{:S(2)}, u32[]{:S(2)}) collective-permute-start(bf16[256,1536]{1,0:T(8,128)(2,1)} %convolution_convert_fusion.4), channel_id=1, source_target_pairs={{0,1},{1,0},{2,3},{3,2},{4,5},{5,4},{6,7},{7,6},{8,9},{9,8},{10,11... | collective-permute-start | bytes 2359304 | tf_op jit(solution)/shard_map/ppermute | solution.py:48
  134.7 18.7 %copy-start.18 = (bf16[512,1536]{1,0:T(8,128)(2,1)S(1)}, bf16[512,1536]{1,0:T(8,128)(2,1)}, u32[]{:S(2)}) copy-start(bf16[512,1536]{1,0:T(8,128)(2,1)} %param.15) | copy-start | bytes 4718596
  159.2 35.9 %all-to-all-start.3 = ((bf16[16,48,1536]{2,1,0:T(8,128)(2,1)}), bf16[16,48,1536]{2,1,0:T(8,128)(2,1)S(1)}, u32[]{:S(2)}, u32[]{:S(2)}) async-start(bf16[16,48,1536]{2,1,0:T(8,128)(2,1)} %bitcast.173), calls=%async_computation.3 | async-start | bytes 4718592 | tf_op jit(solution)/shard_map/all_to_all | solution.py:97
  210.2 37.5 %copy-start.37 = (bf16[512,768]{1,0:T(8,128)(2,1)S(1)}, bf16[512,768]{1,0:T(8,128)(2,1)}, u32[]{:S(2)}) copy-start(bf16[512,768]{1,0:T(8,128)(2,1)} %add_convert_fusion.2) | copy-start | bytes 2359300
  247.7 37.9 %copy-start.15 = (f32[512,1536]{1,0:T(8,128)S(1)}, f32[512,1536]{1,0:T(8,128)}, u32[]{:S(2)}) copy-start(f32[512,1536]{1,0:T(8,128)} %copy-done.14) | copy-start | bytes 9437188
  247.7 37.9 %copy-start.21 = (bf16[512,1536]{1,0:T(8,128)(2,1)S(1)}, bf16[512,1536]{1,0:T(8,128)(2,1)}, u32[]{:S(2)}) copy-start(bf16[512,1536]{1,0:T(8,128)(2,1)} %param.16) | copy-start | bytes 4718596
  249.1 36.5 %collective-permute-start.8 = (bf16[512,1536]{1,0:T(8,128)(2,1)S(1)}, bf16[512,1536]{1,0:T(8,128)(2,1)S(1)}, u32[]{:S(2)}, u32[]{:S(2)}) collective-permute-start(bf16[512,1536]{1,0:T(8,128)(2,1)S(1)} %convolution_convert_fusion.3), channel_id=1, source_target_pairs={{0,1},{1,0},{2,3},{3,2},{4,5},{5,4},{6,7},{7,6},{8,9},{9,8},{10,11... | collective-permute-start | bytes 4718600 | tf_op jit(solution)/shard_map/ppermute | solution.py:48
  287.6 136.1 %copy-start.20 = (f32[512,1536]{1,0:T(8,128)}, f32[512,1536]{1,0:T(8,128)S(1)}, u32[]{:S(2)}) copy-start(f32[512,1536]{1,0:T(8,128)S(1)} %get-tuple-element.260) | copy-start | bytes 9437188
  290.8 36.5 %all-to-all-start.5 = ((bf16[16,48,1536]{2,1,0:T(8,128)(2,1)}), bf16[16,48,1536]{2,1,0:T(8,128)(2,1)}, u32[]{:S(2)}, u32[]{:S(2)}) async-start(bf16[16,48,1536]{2,1,0:T(8,128)(2,1)} %bitcast.172), calls=%async_computation.5 | async-start | bytes 4718592 | tf_op jit(solution)/shard_map/all_to_all | solution.py:97
  299.1 20.9 %collective-permute-start.9 = (f32[2,512]{1,0:T(2,128)S(1)}, f32[2,512]{1,0:T(2,128)S(1)}, u32[]{:S(2)}, u32[]{:S(2)}) collective-permute-start(f32[2,512]{1,0:T(2,128)S(1)} %pad_maximum_fusion.6), channel_id=1, source_target_pairs={{0,1},{1,0},{2,3},{3,2},{4,5},{5,4},{6,7},{7,6},{8,9},{9,8},{10,11... | collective-permute-start | bytes 12296 | tf_op jit(solution)/shard_map/ppermute | solution.py:48
  344.5 37.6 %all-to-all-start.6 = ((bf16[16,48,1536]{2,1,0:T(8,128)(2,1)}), bf16[16,48,1536]{2,1,0:T(8,128)(2,1)}, u32[]{:S(2)}, u32[]{:S(2)}) async-start(bf16[16,48,1536]{2,1,0:T(8,128)(2,1)} %bitcast.171), calls=%async_computation.6 | async-start | bytes 4718592 | tf_op jit(solution)/shard_map/all_to_all | solution.py:97
  350.1 124.5 %reduce-scatter.2.cloned.1.call-start = ((), (), s32[]{:S(2)}) async-start(), calls=%async_computation.9 | async-start | bytes 11796480 | tf_op jit(solution)/shard_map/reduce_scatter | solution.py:667
  385.5 36.4 %copy-start.16 = (f32[512,1536]{1,0:T(8,128)S(1)}, f32[512,1536]{1,0:T(8,128)}, u32[]{:S(2)}) copy-start(f32[512,1536]{1,0:T(8,128)} %copy-done.14) | copy-start | bytes 9437188
  385.5 36.3 %collective-permute-start.10 = (bf16[512,1536]{1,0:T(8,128)(2,1)S(1)}, bf16[512,1536]{1,0:T(8,128)(2,1)S(1)}, u32[]{:S(2)}, u32[]{:S(2)}) collective-permute-start(bf16[512,1536]{1,0:T(8,128)(2,1)S(1)} %convolution_convert_fusion.2), channel_id=1, source_target_pairs={{0,1},{1,0},{2,3},{3,2},{4,5},{5,4},{6,7},{7,6},{8,9},{9,8},{10,11... | collective-permute-start | bytes 4718600 | tf_op jit(solution)/shard_map/ppermute | solution.py:48
  390.9 32.8 %copy-start.22 = (bf16[512,1536]{1,0:T(8,128)(2,1)S(1)}, bf16[512,1536]{1,0:T(8,128)(2,1)}, u32[]{:S(2)}) copy-start(bf16[512,1536]{1,0:T(8,128)(2,1)} %param.16) | copy-start | bytes 4718596
  475.9 14.7 %collective-permute-start.11 = (bf16[2,128,512]{2,1,0:T(8,128)(2,1)}, bf16[2,128,512]{2,1,0:T(8,128)(2,1)}, u32[]{:S(2)}, u32[]{:S(2)}) collective-permute-start(bf16[2,128,512]{2,1,0:T(8,128)(2,1)} %get-tuple-element.146), channel_id=1, source_target_pairs={{2,0},{4,2},{6,4},{3,1},{5,3},{7,5},{10,8},{12,10},{14,12},{11,9},... | collective-permute-start | bytes 786440 | tf_op jit(solution)/shard_map/ppermute | solution.py:691
  477.2 13.4 %collective-permute-start.12 = (bf16[2,128,512]{2,1,0:T(8,128)(2,1)}, bf16[2,128,512]{2,1,0:T(8,128)(2,1)}, u32[]{:S(2)}, u32[]{:S(2)}) collective-permute-start(bf16[2,128,512]{2,1,0:T(8,128)(2,1)} %get-tuple-element.147), channel_id=1, source_target_pairs={{4,0},{6,2},{5,1},{7,3},{12,8},{14,10},{13,9},{15,11},{20,16},{22,... | collective-permute-start | bytes 786440 | tf_op jit(solution)/shard_map/ppermute | solution.py:691
  478.5 16.1 %collective-permute-start.13 = (bf16[2,128,512]{2,1,0:T(8,128)(2,1)}, bf16[2,128,512]{2,1,0:T(8,128)(2,1)}, u32[]{:S(2)}, u32[]{:S(2)}) collective-permute-start(bf16[2,128,512]{2,1,0:T(8,128)(2,1)} %get-tuple-element.148), channel_id=1, source_target_pairs={{6,0},{7,1},{14,8},{15,9},{22,16},{23,17},{30,24},{31,25},{38,32},... | collective-permute-start | bytes 786440 | tf_op jit(solution)/shard_map/ppermute | solution.py:691
  480.8 19.8 %collective-permute-start.14 = (bf16[2,384,512]{1,2,0:T(8,128)(2,1)}, bf16[2,384,512]{1,2,0:T(8,128)(2,1)}, u32[]{:S(2)}, u32[]{:S(2)}) collective-permute-start(bf16[2,384,512]{1,2,0:T(8,128)(2,1)} %slice.138), channel_id=1, source_target_pairs={{0,1},{1,0},{2,3},{3,2},{4,5},{5,4},{6,7},{7,6},{8,9},{9,8},{10,11... | collective-permute-start | bytes 2359304 | tf_op jit(solution)/shard_map/ppermute | solution.py:48
  482.6 18.1 %copy-start.46 = (bf16[16,512]{1,0:T(8,128)(2,1)S(1)}, bf16[16,512]{1,0:T(8,128)(2,1)}, u32[]{:S(2)}) copy-start(bf16[16,512]{1,0:T(8,128)(2,1)} %copy-done.45) | copy-start | bytes 49156
  482.6 24.3 %copy-start.51 = (f32[1,1536]{1,0:T(1,128)S(1)}, f32[1,1536]{1,0:T(1,128)}, u32[]{:S(2)}) copy-start(f32[1,1536]{1,0:T(1,128)} %broadcast_in_dim.171) | copy-start | bytes 18436
  482.6 24.3 %copy-start.55 = (f32[8]{0:T(128)S(1)}, f32[8]{0:T(128)}, u32[]{:S(2)}) copy-start(f32[8]{0:T(128)} %pad.11.clone) | copy-start | bytes 100
  482.6 24.3 %copy-start.56 = (f32[8]{0:T(128)S(1)}, f32[8]{0:T(128)}, u32[]{:S(2)}) copy-start(f32[8]{0:T(128)} %pad.10.clone) | copy-start | bytes 100
  482.6 24.3 %copy-start.57 = (f32[8]{0:T(128)S(1)}, f32[8]{0:T(128)}, u32[]{:S(2)}) copy-start(f32[8]{0:T(128)} %pad.9.clone) | copy-start | bytes 100
  501.3 19.5 %collective-permute-start.15 = (bf16[2,128,512]{2,1,0:T(8,128)(2,1)}, bf16[2,128,512]{2,1,0:T(8,128)(2,1)S(1)}, u32[]{:S(2)}, u32[]{:S(2)}) collective-permute-start(bf16[2,128,512]{2,1,0:T(8,128)(2,1)} %get-tuple-element.151), channel_id=1, source_target_pairs={{2,0},{4,2},{6,4},{3,1},{5,3},{7,5},{10,8},{12,10},{14,12},{11,9},... | collective-permute-start | bytes 786440 | tf_op jit(solution)/shard_map/ppermute | solution.py:691
  502.6 18.2 %collective-permute-start.16 = (bf16[2,128,512]{2,1,0:T(8,128)(2,1)}, bf16[2,128,512]{2,1,0:T(8,128)(2,1)S(1)}, u32[]{:S(2)}, u32[]{:S(2)}) collective-permute-start(bf16[2,128,512]{2,1,0:T(8,128)(2,1)} %get-tuple-element.152), channel_id=1, source_target_pairs={{4,0},{6,2},{5,1},{7,3},{12,8},{14,10},{13,9},{15,11},{20,16},{22,... | collective-permute-start | bytes 786440 | tf_op jit(solution)/shard_map/ppermute | solution.py:691
  503.9 18.5 %collective-permute-start.17 = (bf16[2,128,512]{2,1,0:T(8,128)(2,1)}, bf16[2,128,512]{2,1,0:T(8,128)(2,1)}, u32[]{:S(2)}, u32[]{:S(2)}) collective-permute-start(bf16[2,128,512]{2,1,0:T(8,128)(2,1)} %get-tuple-element.153), channel_id=1, source_target_pairs={{6,0},{7,1},{14,8},{15,9},{22,16},{23,17},{30,24},{31,25},{38,32},... | collective-permute-start | bytes 786440 | tf_op jit(solution)/shard_map/ppermute | solution.py:691
  505.2 17.2 %collective-permute-start.18 = (bf16[384,512]{0,1:T(8,128)(2,1)S(1)}, bf16[384,512]{0,1:T(8,128)(2,1)S(1)}, u32[]{:S(2)}, u32[]{:S(2)}) collective-permute-start(bf16[384,512]{0,1:T(8,128)(2,1)S(1)} %slice_bitcast_fusion.3), channel_id=1, source_target_pairs={{0,1},{1,0},{2,3},{3,2},{4,5},{5,4},{6,7},{7,6},{8,9},{9,8},{10,11... | collective-permute-start | bytes 1179656 | tf_op jit(solution)/shard_map/ppermute | solution.py:48
  522.4 9.2 %collective-permute-start.19 = (bf16[4,4,2,24,1664]{4,3,2,1,0:T(8,128)(2,1)}, bf16[4,4,2,24,1664]{4,3,2,1,0:T(8,128)(2,1)}, u32[]{:S(2)}, u32[]{:S(2)}) collective-permute-start(bf16[4,4,2,24,1664]{4,3,2,1,0:T(8,128)(2,1)} %get-tuple-element.174), channel_id=1, source_target_pairs={{0,8},{8,0},{1,9},{9,1},{2,10},{10,2},{3,11},{11,3},{4,12},{12,4},... | collective-permute-start | bytes 7667720 | tf_op jit(solution)/shard_map/ppermute | solution.py:48
  535.3 6.7 %collective-permute-start.23 = (bf16[4,4,2,24,640]{4,3,2,1,0:T(8,128)(2,1)S(1)}, bf16[4,4,2,24,640]{4,3,2,1,0:T(8,128)(2,1)}, u32[]{:S(2)}, u32[]{:S(2)}) collective-permute-start(bf16[4,4,2,24,640]{4,3,2,1,0:T(8,128)(2,1)S(1)} %get-tuple-element.180), channel_id=1, source_target_pairs={{0,8},{8,0},{1,9},{9,1},{2,10},{10,2},{3,11},{11,3},{4,12},{12,4},... | collective-permute-start | bytes 2949128 | tf_op jit(solution)/shard_map/ppermute | solution.py:48
  535.7 37.0 %collective-permute-start.24 = (bf16[512,1536]{1,0:T(8,128)(2,1)}, bf16[512,1536]{1,0:T(8,128)(2,1)}, u32[]{:S(2)}, u32[]{:S(2)}) collective-permute-start(bf16[512,1536]{1,0:T(8,128)(2,1)} %get-tuple-element.182), channel_id=1, source_target_pairs={{0,1},{1,0},{2,3},{3,2},{4,5},{5,4},{6,7},{7,6},{8,9},{9,8},{10,11... | collective-permute-start | bytes 4718600 | tf_op jit(solution)/shard_map/ppermute | solution.py:48
  536.4 27.9 %collective-permute-start.20 = (bf16[4,2,24,1664]{3,2,1,0:T(8,128)(2,1)}, bf16[4,2,24,1664]{3,2,1,0:T(8,128)(2,1)}, u32[]{:S(2)}, u32[]{:S(2)}) collective-permute-start(bf16[4,2,24,1664]{3,2,1,0:T(8,128)(2,1)} %get-tuple-element.176), channel_id=1, source_target_pairs={{0,16},{16,32},{32,48},{48,0},{1,17},{17,33},{33,49},{49,1},{2,18}... | collective-permute-start | bytes 1916936 | tf_op jit(solution)/shard_map/ppermute | solution.py:515
  537.9 30.8 %collective-permute-start.21 = (bf16[4,2,24,1664]{3,2,1,0:T(8,128)(2,1)}, bf16[4,2,24,1664]{3,2,1,0:T(8,128)(2,1)}, u32[]{:S(2)}, u32[]{:S(2)}) collective-permute-start(bf16[4,2,24,1664]{3,2,1,0:T(8,128)(2,1)} %get-tuple-element.177), channel_id=1, source_target_pairs={{0,32},{16,48},{32,0},{48,16},{1,33},{17,49},{33,1},{49,17},{2,34}... | collective-permute-start | bytes 1916936 | tf_op jit(solution)/shard_map/ppermute | solution.py:515
  540.6 28.1 %collective-permute-start.22 = (bf16[4,2,24,1664]{3,2,1,0:T(8,128)(2,1)}, bf16[4,2,24,1664]{3,2,1,0:T(8,128)(2,1)}, u32[]{:S(2)}, u32[]{:S(2)}) collective-permute-start(bf16[4,2,24,1664]{3,2,1,0:T(8,128)(2,1)} %get-tuple-element.178), channel_id=1, source_target_pairs={{0,48},{16,0},{32,16},{48,32},{1,49},{17,1},{33,17},{49,33},{2,50}... | collective-permute-start | bytes 1916936 | tf_op jit(solution)/shard_map/ppermute | solution.py:515
  544.4 28.3 %all-to-all-start.7 = ((bf16[4,4,2,24,640]{4,3,2,1,0:T(8,128)(2,1)}), bf16[4,4,2,24,640]{4,3,2,1,0:T(8,128)(2,1)S(1)}, u32[]{:S(2)}, u32[]{:S(2)}) async-start(bf16[4,4,2,24,640]{4,3,2,1,0:T(8,128)(2,1)} %add_convert_fusion), calls=%async_computation.8 | async-start | bytes 1966080 | tf_op jit(solution)/shard_map/all_to_all | solution.py:760
  562.1 15.8 %copy-start.32 = (bf16[4,2,24,1664]{3,2,1,0:T(8,128)(2,1)S(1)}, bf16[4,2,24,1664]{3,2,1,0:T(8,128)(2,1)}, u32[]{:S(2)}) copy-start(bf16[4,2,24,1664]{3,2,1,0:T(8,128)(2,1)} %get-tuple-element.183) | copy-start | bytes 1916932
  572.9 16.7 %collective-permute-start.28 = (bf16[2,24,640]{2,1,0:T(8,128)(2,1)S(1)}, bf16[2,24,640]{2,1,0:T(8,128)(2,1)S(1)}, u32[]{:S(2)}, u32[]{:S(2)}) collective-permute-start(bf16[2,24,640]{2,1,0:T(8,128)(2,1)S(1)} %get-tuple-element.282), channel_id=1, source_target_pairs={{0,16},{16,32},{32,48},{48,0},{1,17},{17,33},{33,49},{49,1},{2,18}... | collective-permute-start | bytes 184328 | tf_op jit(solution)/shard_map/ppermute | solution.py:84
  574.4 16.5 %collective-permute-start.30 = (bf16[2,24,640]{2,1,0:T(8,128)(2,1)S(1)}, bf16[2,24,640]{2,1,0:T(8,128)(2,1)S(1)}, u32[]{:S(2)}, u32[]{:S(2)}) collective-permute-start(bf16[2,24,640]{2,1,0:T(8,128)(2,1)S(1)} %get-tuple-element.283), channel_id=1, source_target_pairs={{0,48},{16,0},{32,16},{48,32},{1,49},{17,1},{33,17},{49,33},{2,50}... | collective-permute-start | bytes 184328 | tf_op jit(solution)/shard_map/ppermute | solution.py:84
  576.2 21.1 %copy-start.48 = (f32[1536]{0:T(1024)S(1)}, f32[1536]{0:T(1024)}, u32[]{:S(2)}) copy-start(f32[1536]{0:T(1024)} %copy-done.47) | copy-start | bytes 18436
  576.2 14.8 %collective-permute-start.29 = (bf16[2,24,640]{2,1,0:T(8,128)(2,1)S(1)}, bf16[2,24,640]{2,1,0:T(8,128)(2,1)S(1)}, u32[]{:S(2)}, u32[]{:S(2)}) collective-permute-start(bf16[2,24,640]{2,1,0:T(8,128)(2,1)S(1)} %get-tuple-element.284), channel_id=1, source_target_pairs={{0,32},{16,48},{32,0},{48,16},{1,33},{17,49},{33,1},{49,17},{2,34}... | collective-permute-start | bytes 184328 | tf_op jit(solution)/shard_map/ppermute | solution.py:84
  579.8 14.0 %collective-permute-start.25 = (bf16[2,24,1664]{2,1,0:T(8,128)(2,1)S(1)}, bf16[2,24,1664]{2,1,0:T(8,128)(2,1)S(1)}, u32[]{:S(2)}, u32[]{:S(2)}) collective-permute-start(bf16[2,24,1664]{2,1,0:T(8,128)(2,1)S(1)} %get-tuple-element.279), channel_id=1, source_target_pairs={{0,2},{2,4},{4,6},{6,0},{1,3},{3,5},{5,7},{7,1},{8,10},{10,12},{12... | collective-permute-start | bytes 479240 | tf_op jit(solution)/shard_map/ppermute | solution.py:84
  583.6 11.5 %collective-permute-start.27 = (bf16[2,24,1664]{2,1,0:T(8,128)(2,1)S(1)}, bf16[2,24,1664]{2,1,0:T(8,128)(2,1)S(1)}, u32[]{:S(2)}, u32[]{:S(2)}) collective-permute-start(bf16[2,24,1664]{2,1,0:T(8,128)(2,1)S(1)} %get-tuple-element.280), channel_id=1, source_target_pairs={{0,6},{2,0},{4,2},{6,4},{1,7},{3,1},{5,3},{7,5},{8,14},{10,8},{12,... | collective-permute-start | bytes 479240 | tf_op jit(solution)/shard_map/ppermute | solution.py:84
  589.6 7.6 %collective-permute-start.26 = (bf16[2,24,1664]{2,1,0:T(8,128)(2,1)S(1)}, bf16[2,24,1664]{2,1,0:T(8,128)(2,1)S(1)}, u32[]{:S(2)}, u32[]{:S(2)}) collective-permute-start(bf16[2,24,1664]{2,1,0:T(8,128)(2,1)S(1)} %get-tuple-element.281), channel_id=1, source_target_pairs={{0,4},{2,6},{4,0},{6,2},{1,5},{3,7},{5,1},{7,3},{8,12},{10,14},{12... | collective-permute-start | bytes 479240 | tf_op jit(solution)/shard_map/ppermute | solution.py:84
  600.2 8.1 %collective-permute-start.31 = (bf16[24,2304]{1,0:T(8,128)(2,1)S(1)}, bf16[24,2304]{1,0:T(8,128)(2,1)S(1)}, u32[]{:S(2)}, u32[]{:S(2)}) collective-permute-start(bf16[24,2304]{1,0:T(8,128)(2,1)S(1)} %dynamic-slice_bitcast_fusion.3), channel_id=1, source_target_pairs={{0,64},{64,0},{1,65},{65,1},{2,66},{66,2},{3,67},{67,3},{4,68},{68... | collective-permute-start | bytes 331784 | tf_op jit(solution)/shard_map/ppermute | solution.py:84
  610.9 3.9 collective-permute-start.32
  (40 other events, 163.8 us)
Sparse Core Ops, SparseCore 0:
  95.0 89.6 all-gather.2
  376.7 97.7 reduce-scatter.1

commit v5 on v4

--- a/solution.py
+++ b/solution.py
@@ -4,7 +4,6 @@
 import jax.numpy as jnp
 from jax import lax
 from jax.experimental import pallas as pl
-from jax.experimental.layout import Layout, with_layout_constraint
 from jax.experimental.pallas import tpu as pltpu
 from jax.sharding import Mesh
 from jax.sharding import PartitionSpec as P
@@ -489,7 +488,7 @@
         out_shape=[out, out],
         scratch_shapes=[pltpu.VMEM((384, cols), F32)],
         compiler_params=pltpu.CompilerParams(
-            vmem_limit_bytes=(60 if len(arrays) > 4 else 40) << 20
+            vmem_limit_bytes=40 << 20
         ),
         cost_estimate=pl.CostEstimate(
             flops=flops, bytes_accessed=flops // 2000, transcendentals=0
@@ -759,7 +758,7 @@
     paired_two = both(own_two, swap(theirs_two, "c")).astype(BF)
     ring_two = lax.all_to_all(paired_two, "y", 0, 0, tiled=True)
     grad_wide = keep[:2].astype(F32) + given_0.astype(F32)
-    own_down = with_layout_constraint(both(keep[2], given_1).T, Layout(major_to_minor=(0, 1)))
+    own_down = both(keep[2], given_1).T
     *parts_one, ring_two, own_down, other = lax.optimization_barrier(
         (*parts_one, ring_two, own_down, other)
     )

time: 634 us -> 627 us (0.989)
    pallas_call x1 -> x0, local copies, waits for them, and re-layouts: 12.7 us -> none  [expert_grads(): pl.pallas_call(expert_grads_kernel, in_specs=[whole, whole, column, colum...]
    all_to_all x3, waiting for transfers between devices: 42.5 us -> 54.8 us  [exchange_slots(): lax.all_to_all(rows.reshape(EXPERTS, -1, width), ('h', 'x', 'c'), 0, 0, t...]
    reduce_scatter x1, waiting for transfers between devices: 38 us -> 27.4 us  [local(): grad_experts = lax.psum_scatter(grad_parts, 'y', scatter_dimension=0)]
    unnamed x130 -> x159, local copies, waits for them, and re-layouts: 11.9 us -> 20.2 us
  transfers between devices with their start and end apart: 42 -> 42, of which waited for: 22 -> 20; matrix products, arithmetic and copies ran while one was open for 15% -> 12% of each run, Pallas kernels for 8% -> 7%
where the time goes in v5:
time: 627 us; the launch traced here: 617 us
  waiting for transfers between devices  272 us (43%)
  starting transfers between devices  94.2 us (15%)
  Pallas kernels  77 us (12%)
  other arithmetic  50.6 us (8%)
  local copies, waits for them, and re-layouts  40.4 us (6%)
  blocking collectives  37.5 us (6%)
  matrix products  26.7 us (4%)
  between operations  19.3 us (3%)
    ppermute x14, waiting for transfers between devices, swap(): return lax.ppermute(value, axis, [(0, 1), (1, 0)])  141 us
    all_to_all x3, waiting for transfers between devices, exchange_slots(): lax.all_to_all(rows.reshape(EXPERTS, -1, width), ('h', 'x', 'c'), 0, 0, t...  54.8 us
    all_to_all x1, blocking collectives, exchange_slots(): lax.all_to_all(rows.reshape(EXPERTS, -1, width), ('h', 'x', 'c'), 0, 0, t...  37.5 us
    reduce_scatter x1, waiting for transfers between devices, local(): grad_experts = lax.psum_scatter(grad_parts, 'y', scatter_dimension=0)  27.4 us
    dot_general x16, matrix products, dot(): lax.dot_general(left, right, (((left_dim,), (right_dim,)), ((), ())), pre...  26.7 us
    unnamed x159, local copies, waits for them, and re-layouts  20.2 us
    ppermute x7, starting transfers between devices, axis_parts(): lax.ppermute(block, axis, [(i, (i + r) % size) for i in range(size)])  20.2 us
    pallas_call x1, Pallas kernels, run_experts_back(): pl.pallas_call(experts_back_kernel, in_specs=[whole, column, column] + we...  17.1 us
  transfers between devices with their start and end apart: 42, of which 20 were waited for; matrix products, arithmetic and copies ran while one was open for 12% of the time, Pallas kernels for 7%

profile of v5, /device:TPU:0, one launch (start us, length us, event | category | flops | bytes accessed | tf_op | source)
XLA Modules:
  0.0 617.4 jit_solution(4600294928915745182)
XLA Ops:
  11.4 7.9 %all-to-all-start = ((bf16[8,24,2176]{2,1,0:T(8,128)(2,1)}), bf16[8,24,2176]{2,1,0:T(8,128)(2,1)S(1)}, u32[]{:S(2)}, u32[]{:S(2)}) async-start(bf16[8,24,2176]{2,1,0:T(8,128)(2,1)} %broadcast_in_dim.149), calls=%async_computation | async-start | bytes 1671168 | tf_op jit(solution)/shard_map/all_to_all | solution.py:56
  20.7 13.6 %all-to-all-done = bf16[8,24,2176]{2,1,0:T(8,128)(2,1)S(1)} async-done(((bf16[8,24,2176]{2,1,0:T(8,128)(2,1)}), bf16[8,24,2176]{2,1,0:T(8,128)(2,1)S(1)}, u32[]{:S(2)}, u32[]{:S(2)}) %all-to-all-start) | async-done | bytes 835616 | tf_op jit(solution)/shard_map/all_to_all | solution.py:56
  35.4 4.3 all-to-all-start.1
  41.0 13.0 %all-to-all-done.1 = bf16[4,8,24,640]{3,2,1,0:T(8,128)(2,1)S(1)} async-done(((bf16[4,8,24,640]{3,2,1,0:T(8,128)(2,1)}), bf16[4,8,24,640]{3,2,1,0:T(8,128)(2,1)S(1)}, u32[]{:S(2)}, u32[]{:S(2)}) %all-to-all-start.1) | async-done | bytes 983072 | tf_op jit(solution)/shard_map/all_to_all | solution.py:61
  57.1 4.5 all-to-all-start.2
  68.0 2.4 collective-permute-start.2
  70.4 2.1 collective-permute-start.1
  72.5 12.2 %collective-permute-done.4 = bf16[3,384,512]{2,1,0:T(8,128)(2,1)} collective-permute-done((bf16[3,384,512]{2,1,0:T(8,128)(2,1)}, bf16[3,384,512]{2,1,0:T(8,128)(2,1)}, u32[]{:S(2)}, u32[]{:S(2)}) %collective-permute-start.4) | collective-permute-done | bytes 1179680 | tf_op jit(solution)/shard_map/ppermute | solution.py:47
  84.7 6.7 %all-to-all-done.2 = bf16[4,8,24,1536]{3,2,1,0:T(8,128)(2,1)} async-done(((bf16[4,8,24,1536]{3,2,1,0:T(8,128)(2,1)}), bf16[4,8,24,1536]{3,2,1,0:T(8,128)(2,1)}, u32[]{:S(2)}, u32[]{:S(2)}) %all-to-all-start.2) | async-done | bytes 2359328 | tf_op jit(solution)/shard_map/all_to_all | solution.py:564
  91.5 3.2 pad_maximum_fusion.1
  97.4 2.3 collective-permute-done.5
  99.7 2.7 select_bitcast_fusion.1
  105.5 4.1 shard_map.246
  111.7 4.7 shard_map.247
  116.5 13.8 %collective-permute-done.6 = bf16[256,1536]{1,0:T(8,128)(2,1)S(1)} collective-permute-done((bf16[256,1536]{1,0:T(8,128)(2,1)S(1)}, bf16[256,1536]{1,0:T(8,128)(2,1)S(1)}, u32[]{:S(2)}, u32[]{:S(2)}) %collective-permute-start.6) | collective-permute-done | bytes 786464 | tf_op jit(solution)/shard_map/ppermute | solution.py:47
  133.6 16.7 %collective-permute-done.7 = bf16[256,1536]{1,0:T(8,128)(2,1)} collective-permute-done((bf16[256,1536]{1,0:T(8,128)(2,1)S(1)}, bf16[256,1536]{1,0:T(8,128)(2,1)}, u32[]{:S(2)}, u32[]{:S(2)}) %collective-permute-start.7) | collective-permute-done | bytes 786464 | tf_op jit(solution)/shard_map/ppermute | solution.py:47
  154.6 2.8 convolution_convert_fusion.1
  157.4 3.9 all-to-all-start.3
  163.7 29.6 %all-to-all-done.3 = bf16[16,48,1536]{2,1,0:T(8,128)(2,1)S(1)} async-done(((bf16[16,48,1536]{2,1,0:T(8,128)(2,1)}), bf16[16,48,1536]{2,1,0:T(8,128)(2,1)S(1)}, u32[]{:S(2)}, u32[]{:S(2)}) %all-to-all-start.3) | async-done | bytes 2359328 | tf_op jit(solution)/shard_map/all_to_all | solution.py:96
  194.7 13.6 %shard_map.248 = (f32[768,1024]{1,0:T(8,128)}, f32[768,1024]{1,0:T(8,128)}, bf16[768,1024]{1,0:T(8,128)(2,1)}, bf16[768,1536]{1,0:T(8,128)(2,1)}) custom-call(bf16[768,1536]{1,0:T(8,128)(2,1)} %bitcast.155, bf16[4,2,3,384,512]{4,3,2,1,0:T(8,128)(2,1)} %bitcast.149, bf16[4,2,3,384,512]{4,3,2,1,0:T(8,128)(2,1)} %bitcast.150, bf16[4,2,3,384,512]{4,3,2,1,0:T(8,128)(2,1)} %bitcast.151), custom_call_target="tpu_custom_call" | custom-call | flops 7247757312 | bytes 20000000 | tf_op jit(solution)/shard_map/pallas_call | solution.py:387
  208.4 37.5 %all_to_all.40 = bf16[16,48,1536]{2,1,0:T(8,128)(2,1)S(1)} all-to-all(bf16[16,48,1536]{2,1,0:T(8,128)(2,1)} %bitcast.175), channel_id=1, replica_groups=mesh['h'=2,'x'=4,'c'=2,'y'=4,'t'=2] {'h','x','c'}, dimensions={0} | all-to-all | bytes 4718592 | tf_op jit(solution)/shard_map/all_to_all | solution.py:96
  248.6 35.2 %collective-permute-done.8 = bf16[512,1536]{1,0:T(8,128)(2,1)S(1)} collective-permute-done((bf16[512,1536]{1,0:T(8,128)(2,1)S(1)}, bf16[512,1536]{1,0:T(8,128)(2,1)S(1)}, u32[]{:S(2)}, u32[]{:S(2)}) %collective-permute-start.8) | collective-permute-done | bytes 1572896 | tf_op jit(solution)/shard_map/ppermute | solution.py:47
  283.8 2.0 fusion.7
  286.2 2.9 convolution_convert_fusion
  289.1 4.4 all-to-all-start.5
  293.6 3.8 select_reduce_fusion.1
  298.3 20.2 %collective-permute-done.9 = f32[2,512]{1,0:T(2,128)S(1)} collective-permute-done((f32[2,512]{1,0:T(2,128)S(1)}, f32[2,512]{1,0:T(2,128)S(1)}, u32[]{:S(2)}, u32[]{:S(2)}) %collective-permute-start.9) | collective-permute-done | bytes 4128 | tf_op jit(solution)/shard_map/ppermute | solution.py:47
  318.5 7.1 %all-to-all-done.5 = bf16[16,48,1536]{2,1,0:T(8,128)(2,1)} async-done(((bf16[16,48,1536]{2,1,0:T(8,128)(2,1)}), bf16[16,48,1536]{2,1,0:T(8,128)(2,1)}, u32[]{:S(2)}, u32[]{:S(2)}) %all-to-all-start.5) | async-done | bytes 2359328 | tf_op jit(solution)/shard_map/all_to_all | solution.py:96
  325.6 17.1 %shard_map.249 = (bf16[768,1024]{1,0:T(8,128)(2,1)}, bf16[768,1024]{1,0:T(8,128)(2,1)}, bf16[768,1536]{1,0:T(8,128)(2,1)}) custom-call(bf16[768,1536]{1,0:T(8,128)(2,1)} %bitcast.50.d_ref, f32[768,1024]{1,0:T(8,128)} %get-tuple-element.123.g_ref, f32[768,1024]{1,0:T(8,128)} %get-tuple-element.124.u_ref, bf16[4,2,3,384,512]{4,3,2,1,0:T(8,128)(2,1)} %bitcast.152, ...), custom_call_target="tpu_custom_call" | custom-call | flops 7247757312 | bytes 20000000 | tf_op jit(solution)/shard_map/pallas_call | solution.py:407
  342.7 5.5 all-to-all-start.6
  348.3 13.9 %shard_map.250 = bf16[4,2,3,384,512]{4,3,2,1,0:T(8,128)(2,1)} custom-call(bf16[768,1536]{1,0:T(8,128)(2,1)} %bitcast.156, bf16[768,1536]{1,0:T(8,128)(2,1)} %bitcast.50.d_ref, bf16[768,1024]{1,0:T(8,128)(2,1)} %get-tuple-element.128.dg_ref, bf16[768,1024]{1,0:T(8,128)(2,1)} %get-tuple-element.129.du_ref, bf16[768,1024]{1,0:T(8,128)(2,1)} %get-tuple-element.130.inner_ref), custom_call_target="tpu_custom_call" | custom-call | flops 7247757312 | bytes 20000000 | tf_op jit(solution)/shard_map/pallas_call | solution.py:421
  362.3 18.1 %all-to-all-done.6 = bf16[16,48,1536]{2,1,0:T(8,128)(2,1)} async-done(((bf16[16,48,1536]{2,1,0:T(8,128)(2,1)}), bf16[16,48,1536]{2,1,0:T(8,128)(2,1)}, u32[]{:S(2)}, u32[]{:S(2)}) %all-to-all-start.6) | async-done | bytes 2359328 | tf_op jit(solution)/shard_map/all_to_all | solution.py:96
  380.3 3.8 convolution_convert_fusion.2
  389.2 31.0 %collective-permute-done.10 = bf16[512,1536]{1,0:T(8,128)(2,1)S(1)} collective-permute-done((bf16[512,1536]{1,0:T(8,128)(2,1)S(1)}, bf16[512,1536]{1,0:T(8,128)(2,1)S(1)}, u32[]{:S(2)}, u32[]{:S(2)}) %collective-permute-start.10) | collective-permute-done | bytes 1572896 | tf_op jit(solution)/shard_map/ppermute | solution.py:47
  422.1 3.3 fusion.75
  425.4 2.3 fusion.24.d_ref
  427.7 7.0 %shard_map.251 = (bf16[384,512]{1,0:T(8,128)(2,1)}, bf16[2,128,512]{2,1,0:T(8,128)(2,1)}, bf16[2,128,512]{2,1,0:T(8,128)(2,1)}, bf16[2,128,512]{2,1,0:T(8,128)(2,1)}, bf16[2,128,512]{2,1,0:T(8,128)(2,1)}) custom-call(s32[1]{0:T(128)} %bitcast.y_ref, bf16[768,512]{1,0:T(8,128)(2,1)} %copy-done.20, bf16[768,512]{1,0:T(8,128)(2,1)} %fusion.24.d_ref, ...), custom_call_target="tpu_custom_call" | custom-call | flops 149999992832 | bytes 6000000 | tf_op jit(solution)/shard_map/pallas_call | solution.py:273
  434.7 27.4 %reduce-scatter.2.cloned.1.call-done = bf16[1,2,3,384,512]{4,3,2,1,0:T(8,128)(2,1)} async-done(((bf16[4,2,3,384,512]{4,3,2,1,0:T(8,128)(2,1)}), bf16[1,2,3,384,512]{4,3,2,1,0:T(8,128)(2,1)}) %reduce-scatter.2.cloned.1.call-update) | async-done | bytes 2359312 | tf_op jit(solution)/shard_map/reduce_scatter | solution.py:666
  468.3 1.7 collective-permute-start.14
  470.1 7.1 %shard_map.252 = (bf16[384,512]{1,0:T(8,128)(2,1)}, bf16[2,128,512]{2,1,0:T(8,128)(2,1)}, bf16[2,128,512]{2,1,0:T(8,128)(2,1)}, bf16[2,128,512]{2,1,0:T(8,128)(2,1)}, bf16[2,128,512]{2,1,0:T(8,128)(2,1)}) custom-call(s32[1]{0:T(128)} %bitcast.y_ref, bf16[768,512]{1,0:T(8,128)(2,1)} %copy-done.20, bf16[768,512]{1,0:T(8,128)(2,1)} %fusion.24.d_ref, ...), custom_call_target="tpu_custom_call" | custom-call | flops 149999992832 | bytes 6000000 | tf_op jit(solution)/shard_map/pallas_call | solution.py:273
  478.2 4.0 collective-permute-done.13
  482.2 5.9 collective-permute-done.14
  500.6 6.3 %shard_map.253 = (bf16[4,4,2,24,1664]{4,3,2,1,0:T(8,128)(2,1)S(1)}, bf16[4,4,2,24,1664]{4,3,2,1,0:T(8,128)(2,1)}) custom-call(s32[1]{0:T(128)} %bitcast.55.core_ref, bf16[512,1536]{1,0:T(8,128)(2,1)S(1)} %copy-done.3, bf16[512,1536]{1,0:T(8,128)(2,1)S(1)} %copy-done.5, bf16[512,1536]{1,0:T(8,128)(2,1)S(1)} %copy-done.1, ...), custom_call_target="tpu_custom_call" | custom-call | flops 20000000000 | bytes 10000000 | tf_op jit(solution)/shard_map/pallas_call | solution.py:483
  506.8 3.1 fusion.12
  516.1 1.8 fusion.10
  517.9 3.1 shard_map.254
  521.0 3.5 fusion.52
  527.2 2.7 collective-permute-start.21
  531.4 2.4 add_convert_fusion
  533.8 12.7 %all-to-all-start.7 = ((bf16[4,4,2,24,640]{4,3,2,1,0:T(8,128)(2,1)}), bf16[4,4,2,24,640]{4,3,2,1,0:T(8,128)(2,1)S(1)}, u32[]{:S(2)}, u32[]{:S(2)}) async-start(bf16[4,4,2,24,640]{4,3,2,1,0:T(8,128)(2,1)} %add_convert_fusion), calls=%async_computation.8 | async-start | bytes 1966080 | tf_op jit(solution)/shard_map/all_to_all | solution.py:759
  546.5 1.7 convert_add_fusion.1
  549.4 2.0 fusion.41
  551.4 6.5 %collective-permute-done.21 = bf16[4,2,24,1664]{3,2,1,0:T(8,128)(2,1)} collective-permute-done((bf16[4,2,24,1664]{3,2,1,0:T(8,128)(2,1)}, bf16[4,2,24,1664]{3,2,1,0:T(8,128)(2,1)}, u32[]{:S(2)}, u32[]{:S(2)}) %collective-permute-start.21) | collective-permute-done | bytes 639008 | tf_op jit(solution)/shard_map/ppermute | solution.py:514
  557.9 3.9 collective-permute-done.24
  564.1 1.8 collective-permute-start.30
  565.9 1.8 collective-permute-start.29
  567.7 2.0 add_convert_fusion.4
  571.3 3.0 collective-permute-start.25
  574.3 7.4 %collective-permute-start.27 = (bf16[2,24,1664]{2,1,0:T(8,128)(2,1)}, bf16[2,24,1664]{2,1,0:T(8,128)(2,1)}, u32[]{:S(2)}, u32[]{:S(2)}) collective-permute-start(bf16[2,24,1664]{2,1,0:T(8,128)(2,1)} %get-tuple-element.280), channel_id=1, source_target_pairs={{0,6},{2,0},{4,2},{6,4},{1,7},{3,1},{5,3},{7,5},{8,14},{10,8},{12,... | collective-permute-start | bytes 479240 | tf_op jit(solution)/shard_map/ppermute | solution.py:83
  581.7 2.3 copy.75
  586.5 4.2 collective-permute-done.26
  592.0 2.3 fusion.11
  594.4 3.3 collective-permute-start.31
  597.7 4.4 fusion.6
  (297 shorter events, 90.8 us)
Async XLA Ops:
  11.4 22.8 %all-to-all-start = ((bf16[8,24,2176]{2,1,0:T(8,128)(2,1)}), bf16[8,24,2176]{2,1,0:T(8,128)(2,1)S(1)}, u32[]{:S(2)}, u32[]{:S(2)}) async-start(bf16[8,24,2176]{2,1,0:T(8,128)(2,1)} %broadcast_in_dim.149), calls=%async_computation | async-start | bytes 1671168 | tf_op jit(solution)/shard_map/all_to_all | solution.py:56
  35.4 18.5 %all-to-all-start.1 = ((bf16[4,8,24,640]{3,2,1,0:T(8,128)(2,1)}), bf16[4,8,24,640]{3,2,1,0:T(8,128)(2,1)S(1)}, u32[]{:S(2)}, u32[]{:S(2)}) async-start(bf16[4,8,24,640]{3,2,1,0:T(8,128)(2,1)} %broadcast_in_dim.150), calls=%async_computation.1 | async-start | bytes 1966080 | tf_op jit(solution)/shard_map/all_to_all | solution.py:61
  39.7 15.8 %copy-start.26 = (bf16[512,1536]{1,0:T(8,128)(2,1)S(1)}, bf16[512,1536]{1,0:T(8,128)(2,1)}, u32[]{:S(2)}) copy-start(bf16[512,1536]{1,0:T(8,128)(2,1)} %param.15) | copy-start | bytes 4718596
  55.6 6.1 collective-permute-start
  56.0 28.8 %collective-permute-start.4 = (bf16[3,384,512]{2,1,0:T(8,128)(2,1)}, bf16[3,384,512]{2,1,0:T(8,128)(2,1)}, u32[]{:S(2)}, u32[]{:S(2)}) collective-permute-start(bf16[3,384,512]{2,1,0:T(8,128)(2,1)} %pad_maximum_fusion.3), channel_id=1, source_target_pairs={{0,1},{1,0},{2,3},{3,2},{4,5},{5,4},{6,7},{7,6},{8,9},{9,8},{10,11... | collective-permute-start | bytes 3538952 | tf_op jit(solution)/shard_map/ppermute | solution.py:47
  57.1 34.4 %all-to-all-start.2 = ((bf16[4,8,24,1536]{3,2,1,0:T(8,128)(2,1)}), bf16[4,8,24,1536]{3,2,1,0:T(8,128)(2,1)}, u32[]{:S(2)}, u32[]{:S(2)}) async-start(bf16[4,8,24,1536]{3,2,1,0:T(8,128)(2,1)} %broadcast_in_dim.151), calls=%async_computation.2 | async-start | bytes 4718592 | tf_op jit(solution)/shard_map/all_to_all | solution.py:564
  61.6 131.7 %all-gather.3.cloned.1.call-start = ((), (), s32[]{:S(2)}) async-start(), calls=%async_computation.10 | async-start | bytes 11796480 | tf_op jit(solution)/shard_map/all_gather | solution.py:590
  65.6 37.7 %copy-start.4 = (bf16[512,1536]{1,0:T(8,128)(2,1)}, bf16[512,1536]{1,0:T(8,128)(2,1)S(1)}, u32[]{:S(2)}) copy-start(bf16[512,1536]{1,0:T(8,128)(2,1)S(1)} %fusion.2.refs_1_.refs_0_) | copy-start | bytes 4718596
  66.7 45.1 %copy-start.9 = (bf16[512,512]{1,0:T(8,128)(2,1)}, bf16[512,512]{1,0:T(8,128)(2,1)S(1)}, u32[]{:S(2)}) copy-start(bf16[512,512]{1,0:T(8,128)(2,1)S(1)} %fusion.34) | copy-start | bytes 1572868
  66.7 28.0 %collective-permute-start.3 = (bf16[2,256,512]{2,1,0:T(8,128)(2,1)S(1)}, bf16[2,256,512]{2,1,0:T(8,128)(2,1)S(1)}, u32[]{:S(2)}, u32[]{:S(2)}) collective-permute-start(bf16[2,256,512]{2,1,0:T(8,128)(2,1)S(1)} %bitcast.142), channel_id=1, source_target_pairs={{0,6},{1,7},{8,14},{9,15},{16,22},{17,23},{24,30},{25,31},{32,38},... | collective-permute-start | bytes 1572872 | tf_op jit(solution)/shard_map/ppermute | solution.py:578
  68.0 26.7 %collective-permute-start.2 = (bf16[2,256,512]{2,1,0:T(8,128)(2,1)S(1)}, bf16[2,256,512]{2,1,0:T(8,128)(2,1)S(1)}, u32[]{:S(2)}, u32[]{:S(2)}) collective-permute-start(bf16[2,256,512]{2,1,0:T(8,128)(2,1)S(1)} %bitcast.143), channel_id=1, source_target_pairs={{0,4},{2,6},{1,5},{3,7},{8,12},{10,14},{9,13},{11,15},{16,20},{18,... | collective-permute-start | bytes 1572872 | tf_op jit(solution)/shard_map/ppermute | solution.py:578
  70.4 24.3 %collective-permute-start.1 = (bf16[2,256,512]{2,1,0:T(8,128)(2,1)S(1)}, bf16[2,256,512]{2,1,0:T(8,128)(2,1)}, u32[]{:S(2)}, u32[]{:S(2)}) collective-permute-start(bf16[2,256,512]{2,1,0:T(8,128)(2,1)S(1)} %bitcast.144), channel_id=1, source_target_pairs={{0,2},{2,4},{4,6},{1,3},{3,5},{5,7},{8,10},{10,12},{12,14},{9,11},... | collective-permute-start | bytes 1572872 | tf_op jit(solution)/shard_map/ppermute | solution.py:578
  94.7 5.0 collective-permute-start.5
  97.4 151.2 %copy-start.8 = (s32[1,512]{1,0:T(1,128)}, s32[1,512]{1,0:T(1,128)S(1)}, u32[]{:S(2)}) copy-start(s32[1,512]{1,0:T(1,128)S(1)} %get-tuple-element.262.seg_q) | copy-start | bytes 6148
  103.3 27.1 %copy-start.38 = (bf16[2,4,2,96,1536]{4,3,2,1,0:T(8,128)(2,1)}, bf16[2,4,2,96,1536]{4,3,2,1,0:T(8,128)(2,1)S(1)}, u32[]{:S(2)}) copy-start(bf16[2,4,2,96,1536]{4,3,2,1,0:T(8,128)(2,1)S(1)} %copy.69) | copy-start | bytes 14155780
  110.4 19.9 %collective-permute-start.6 = (bf16[256,1536]{1,0:T(8,128)(2,1)S(1)}, bf16[256,1536]{1,0:T(8,128)(2,1)S(1)}, u32[]{:S(2)}, u32[]{:S(2)}) collective-permute-start(bf16[256,1536]{1,0:T(8,128)(2,1)S(1)} %convolution_convert_fusion.5), channel_id=1, source_target_pairs={{0,1},{1,0},{2,3},{3,2},{4,5},{5,4},{6,7},{7,6},{8,9},{9,8},{10,11... | collective-permute-start | bytes 2359304 | tf_op jit(solution)/shard_map/ppermute | solution.py:47
  116.5 17.1 %copy-start.16 = (bf16[768,256]{1,0:T(8,128)(2,1)}, bf16[768,256]{1,0:T(8,128)(2,1)S(1)}, u32[]{:S(2)}) copy-start(bf16[768,256]{1,0:T(8,128)(2,1)S(1)} %get-tuple-element.116.o_1.refs_5_) | copy-start | bytes 1179652
  116.5 17.1 %copy-start.22 = (f32[4,8,256]{2,1,0:T(8,128)}, f32[4,8,256]{2,1,0:T(8,128)S(1)}, u32[]{:S(2)}) copy-start(f32[4,8,256]{2,1,0:T(8,128)S(1)} %get-tuple-element.134.lse_1) | copy-start | bytes 98308
  131.2 19.0 %collective-permute-start.7 = (bf16[256,1536]{1,0:T(8,128)(2,1)S(1)}, bf16[256,1536]{1,0:T(8,128)(2,1)}, u32[]{:S(2)}, u32[]{:S(2)}) collective-permute-start(bf16[256,1536]{1,0:T(8,128)(2,1)S(1)} %convolution_convert_fusion.4), channel_id=1, source_target_pairs={{0,1},{1,0},{2,3},{3,2},{4,5},{5,4},{6,7},{7,6},{8,9},{9,8},{10,11... | collective-permute-start | bytes 2359304 | tf_op jit(solution)/shard_map/ppermute | solution.py:47
  132.2 22.2 %copy-start.67 = (s32[1,512]{1,0:T(1,128)}, s32[1,512]{1,0:T(1,128)S(1)}, u32[]{:S(2)}) copy-start(s32[1,512]{1,0:T(1,128)S(1)} %get-tuple-element.304) | copy-start | bytes 6148
  133.6 18.0 %copy-start.27 = (bf16[512,1536]{1,0:T(8,128)(2,1)S(1)}, bf16[512,1536]{1,0:T(8,128)(2,1)}, u32[]{:S(2)}) copy-start(bf16[512,1536]{1,0:T(8,128)(2,1)} %param.15) | copy-start | bytes 4718596
  157.4 35.9 %all-to-all-start.3 = ((bf16[16,48,1536]{2,1,0:T(8,128)(2,1)}), bf16[16,48,1536]{2,1,0:T(8,128)(2,1)S(1)}, u32[]{:S(2)}, u32[]{:S(2)}) async-start(bf16[16,48,1536]{2,1,0:T(8,128)(2,1)} %bitcast.174), calls=%async_computation.3 | async-start | bytes 4718592 | tf_op jit(solution)/shard_map/all_to_all | solution.py:96
  208.4 37.5 %copy-start.47 = (bf16[512,768]{1,0:T(8,128)(2,1)S(1)}, bf16[512,768]{1,0:T(8,128)(2,1)}, u32[]{:S(2)}) copy-start(bf16[512,768]{1,0:T(8,128)(2,1)} %add_convert_fusion.2) | copy-start | bytes 2359300
  245.9 37.9 %copy-start.24 = (f32[512,1536]{1,0:T(8,128)S(1)}, f32[512,1536]{1,0:T(8,128)}, u32[]{:S(2)}) copy-start(f32[512,1536]{1,0:T(8,128)} %copy-done.23) | copy-start | bytes 9437188
  245.9 37.9 %copy-start.31 = (bf16[512,1536]{1,0:T(8,128)(2,1)S(1)}, bf16[512,1536]{1,0:T(8,128)(2,1)}, u32[]{:S(2)}) copy-start(bf16[512,1536]{1,0:T(8,128)(2,1)} %param.16) | copy-start | bytes 4718596
  247.3 36.5 %collective-permute-start.8 = (bf16[512,1536]{1,0:T(8,128)(2,1)S(1)}, bf16[512,1536]{1,0:T(8,128)(2,1)S(1)}, u32[]{:S(2)}, u32[]{:S(2)}) collective-permute-start(bf16[512,1536]{1,0:T(8,128)(2,1)S(1)} %convolution_convert_fusion.3), channel_id=1, source_target_pairs={{0,1},{1,0},{2,3},{3,2},{4,5},{5,4},{6,7},{7,6},{8,9},{9,8},{10,11... | collective-permute-start | bytes 4718600 | tf_op jit(solution)/shard_map/ppermute | solution.py:47
  285.8 136.3 %copy-start.30 = (f32[512,1536]{1,0:T(8,128)}, f32[512,1536]{1,0:T(8,128)S(1)}, u32[]{:S(2)}) copy-start(f32[512,1536]{1,0:T(8,128)S(1)} %get-tuple-element.260) | copy-start | bytes 9437188
  289.1 36.5 %all-to-all-start.5 = ((bf16[16,48,1536]{2,1,0:T(8,128)(2,1)}), bf16[16,48,1536]{2,1,0:T(8,128)(2,1)}, u32[]{:S(2)}, u32[]{:S(2)}) async-start(bf16[16,48,1536]{2,1,0:T(8,128)(2,1)} %bitcast.173), calls=%async_computation.5 | async-start | bytes 4718592 | tf_op jit(solution)/shard_map/all_to_all | solution.py:96
  297.3 21.1 %collective-permute-start.9 = (f32[2,512]{1,0:T(2,128)S(1)}, f32[2,512]{1,0:T(2,128)S(1)}, u32[]{:S(2)}, u32[]{:S(2)}) collective-permute-start(f32[2,512]{1,0:T(2,128)S(1)} %pad_maximum_fusion.6), channel_id=1, source_target_pairs={{0,1},{1,0},{2,3},{3,2},{4,5},{5,4},{6,7},{7,6},{8,9},{9,8},{10,11... | collective-permute-start | bytes 12296 | tf_op jit(solution)/shard_map/ppermute | solution.py:47
  342.7 37.6 %all-to-all-start.6 = ((bf16[16,48,1536]{2,1,0:T(8,128)(2,1)}), bf16[16,48,1536]{2,1,0:T(8,128)(2,1)}, u32[]{:S(2)}, u32[]{:S(2)}) async-start(bf16[16,48,1536]{2,1,0:T(8,128)(2,1)} %bitcast.172), calls=%async_computation.6 | async-start | bytes 4718592 | tf_op jit(solution)/shard_map/all_to_all | solution.py:96
  348.3 113.8 %reduce-scatter.2.cloned.1.call-start = ((), (), s32[]{:S(2)}) async-start(), calls=%async_computation.9 | async-start | bytes 11796480 | tf_op jit(solution)/shard_map/reduce_scatter | solution.py:666
  384.2 36.1 %copy-start.25 = (f32[512,1536]{1,0:T(8,128)S(1)}, f32[512,1536]{1,0:T(8,128)}, u32[]{:S(2)}) copy-start(f32[512,1536]{1,0:T(8,128)} %copy-done.23) | copy-start | bytes 9437188
  384.2 36.1 %collective-permute-start.10 = (bf16[512,1536]{1,0:T(8,128)(2,1)S(1)}, bf16[512,1536]{1,0:T(8,128)(2,1)S(1)}, u32[]{:S(2)}, u32[]{:S(2)}) collective-permute-start(bf16[512,1536]{1,0:T(8,128)(2,1)S(1)} %convolution_convert_fusion.2), channel_id=1, source_target_pairs={{0,1},{1,0},{2,3},{3,2},{4,5},{5,4},{6,7},{7,6},{8,9},{9,8},{10,11... | collective-permute-start | bytes 4718600 | tf_op jit(solution)/shard_map/ppermute | solution.py:47
  389.2 32.9 %copy-start.32 = (bf16[512,1536]{1,0:T(8,128)(2,1)S(1)}, bf16[512,1536]{1,0:T(8,128)(2,1)}, u32[]{:S(2)}) copy-start(bf16[512,1536]{1,0:T(8,128)(2,1)} %param.16) | copy-start | bytes 4718596
  463.4 14.7 %collective-permute-start.11 = (bf16[2,128,512]{2,1,0:T(8,128)(2,1)}, bf16[2,128,512]{2,1,0:T(8,128)(2,1)}, u32[]{:S(2)}, u32[]{:S(2)}) collective-permute-start(bf16[2,128,512]{2,1,0:T(8,128)(2,1)} %get-tuple-element.146), channel_id=1, source_target_pairs={{2,0},{4,2},{6,4},{3,1},{5,3},{7,5},{10,8},{12,10},{14,12},{11,9},... | collective-permute-start | bytes 786440 | tf_op jit(solution)/shard_map/ppermute | solution.py:690
  464.7 13.4 %collective-permute-start.12 = (bf16[2,128,512]{2,1,0:T(8,128)(2,1)}, bf16[2,128,512]{2,1,0:T(8,128)(2,1)}, u32[]{:S(2)}, u32[]{:S(2)}) collective-permute-start(bf16[2,128,512]{2,1,0:T(8,128)(2,1)} %get-tuple-element.147), channel_id=1, source_target_pairs={{4,0},{6,2},{5,1},{7,3},{12,8},{14,10},{13,9},{15,11},{20,16},{22,... | collective-permute-start | bytes 786440 | tf_op jit(solution)/shard_map/ppermute | solution.py:690
  466.0 16.1 %collective-permute-start.13 = (bf16[2,128,512]{2,1,0:T(8,128)(2,1)}, bf16[2,128,512]{2,1,0:T(8,128)(2,1)}, u32[]{:S(2)}, u32[]{:S(2)}) collective-permute-start(bf16[2,128,512]{2,1,0:T(8,128)(2,1)} %get-tuple-element.148), channel_id=1, source_target_pairs={{6,0},{7,1},{14,8},{15,9},{22,16},{23,17},{30,24},{31,25},{38,32},... | collective-permute-start | bytes 786440 | tf_op jit(solution)/shard_map/ppermute | solution.py:690
  468.3 19.8 %collective-permute-start.14 = (bf16[2,384,512]{2,1,0:T(8,128)(2,1)}, bf16[2,384,512]{2,1,0:T(8,128)(2,1)}, u32[]{:S(2)}, u32[]{:S(2)}) collective-permute-start(bf16[2,384,512]{2,1,0:T(8,128)(2,1)} %slice.138), channel_id=1, source_target_pairs={{0,1},{1,0},{2,3},{3,2},{4,5},{5,4},{6,7},{7,6},{8,9},{9,8},{10,11... | collective-permute-start | bytes 2359304 | tf_op jit(solution)/shard_map/ppermute | solution.py:47
  470.0 18.1 %copy-start.60 = (bf16[16,512]{1,0:T(8,128)(2,1)S(1)}, bf16[16,512]{1,0:T(8,128)(2,1)}, u32[]{:S(2)}) copy-start(bf16[16,512]{1,0:T(8,128)(2,1)} %copy-done.59) | copy-start | bytes 49156
  470.0 23.6 %copy-start.66 = (f32[1,1536]{1,0:T(1,128)S(1)}, f32[1,1536]{1,0:T(1,128)}, u32[]{:S(2)}) copy-start(f32[1,1536]{1,0:T(1,128)} %broadcast_in_dim.171) | copy-start | bytes 18436
  470.0 23.6 %copy-start.72 = (f32[8]{0:T(128)S(1)}, f32[8]{0:T(128)}, u32[]{:S(2)}) copy-start(f32[8]{0:T(128)} %pad.11.clone) | copy-start | bytes 100
  470.0 23.6 %copy-start.73 = (f32[8]{0:T(128)S(1)}, f32[8]{0:T(128)}, u32[]{:S(2)}) copy-start(f32[8]{0:T(128)} %pad.10.clone) | copy-start | bytes 100
  470.0 23.6 %copy-start.74 = (f32[8]{0:T(128)S(1)}, f32[8]{0:T(128)}, u32[]{:S(2)}) copy-start(f32[8]{0:T(128)} %pad.9.clone) | copy-start | bytes 100
  470.0 23.7 %copy-start.1 = (bf16[512,1536]{1,0:T(8,128)(2,1)S(1)}, bf16[512,1536]{1,0:T(8,128)(2,1)}, u32[]{:S(2)}) copy-start(bf16[512,1536]{1,0:T(8,128)(2,1)} %copy-done) | copy-start | bytes 4718596
  488.1 21.8 %collective-permute-start.15 = (bf16[2,128,512]{2,1,0:T(8,128)(2,1)}, bf16[2,128,512]{2,1,0:T(8,128)(2,1)S(1)}, u32[]{:S(2)}, u32[]{:S(2)}) collective-permute-start(bf16[2,128,512]{2,1,0:T(8,128)(2,1)} %get-tuple-element.151), channel_id=1, source_target_pairs={{2,0},{4,2},{6,4},{3,1},{5,3},{7,5},{10,8},{12,10},{14,12},{11,9},... | collective-permute-start | bytes 786440 | tf_op jit(solution)/shard_map/ppermute | solution.py:690
  489.4 20.5 %collective-permute-start.16 = (bf16[2,128,512]{2,1,0:T(8,128)(2,1)}, bf16[2,128,512]{2,1,0:T(8,128)(2,1)S(1)}, u32[]{:S(2)}, u32[]{:S(2)}) collective-permute-start(bf16[2,128,512]{2,1,0:T(8,128)(2,1)} %get-tuple-element.152), channel_id=1, source_target_pairs={{4,0},{6,2},{5,1},{7,3},{12,8},{14,10},{13,9},{15,11},{20,16},{22,... | collective-permute-start | bytes 786440 | tf_op jit(solution)/shard_map/ppermute | solution.py:690
  490.7 19.2 %collective-permute-start.17 = (bf16[2,128,512]{2,1,0:T(8,128)(2,1)}, bf16[2,128,512]{2,1,0:T(8,128)(2,1)S(1)}, u32[]{:S(2)}, u32[]{:S(2)}) collective-permute-start(bf16[2,128,512]{2,1,0:T(8,128)(2,1)} %get-tuple-element.153), channel_id=1, source_target_pairs={{6,0},{7,1},{14,8},{15,9},{22,16},{23,17},{30,24},{31,25},{38,32},... | collective-permute-start | bytes 786440 | tf_op jit(solution)/shard_map/ppermute | solution.py:690
  492.0 18.0 %collective-permute-start.18 = (bf16[384,512]{1,0:T(8,128)(2,1)S(1)}, bf16[384,512]{1,0:T(8,128)(2,1)S(1)}, u32[]{:S(2)}, u32[]{:S(2)}) collective-permute-start(bf16[384,512]{1,0:T(8,128)(2,1)S(1)} %slice_bitcast_fusion.3), channel_id=1, source_target_pairs={{0,1},{1,0},{2,3},{3,2},{4,5},{5,4},{6,7},{7,6},{8,9},{9,8},{10,11... | collective-permute-start | bytes 1179656 | tf_op jit(solution)/shard_map/ppermute | solution.py:47
  510.9 10.1 %collective-permute-start.19 = (bf16[4,4,2,24,1664]{4,3,2,1,0:T(8,128)(2,1)}, bf16[4,4,2,24,1664]{4,3,2,1,0:T(8,128)(2,1)}, u32[]{:S(2)}, u32[]{:S(2)}) collective-permute-start(bf16[4,4,2,24,1664]{4,3,2,1,0:T(8,128)(2,1)} %get-tuple-element.174), channel_id=1, source_target_pairs={{0,8},{8,0},{1,9},{9,1},{2,10},{10,2},{3,11},{11,3},{4,12},{12,4},... | collective-permute-start | bytes 7667720 | tf_op jit(solution)/shard_map/ppermute | solution.py:47
  524.5 6.8 %collective-permute-start.23 = (bf16[4,4,2,24,640]{4,3,2,1,0:T(8,128)(2,1)}, bf16[4,4,2,24,640]{4,3,2,1,0:T(8,128)(2,1)}, u32[]{:S(2)}, u32[]{:S(2)}) collective-permute-start(bf16[4,4,2,24,640]{4,3,2,1,0:T(8,128)(2,1)} %get-tuple-element.180), channel_id=1, source_target_pairs={{0,8},{8,0},{1,9},{9,1},{2,10},{10,2},{3,11},{11,3},{4,12},{12,4},... | collective-permute-start | bytes 2949128 | tf_op jit(solution)/shard_map/ppermute | solution.py:47
  525.0 36.7 %collective-permute-start.24 = (bf16[512,1536]{1,0:T(8,128)(2,1)}, bf16[512,1536]{1,0:T(8,128)(2,1)S(1)}, u32[]{:S(2)}, u32[]{:S(2)}) collective-permute-start(bf16[512,1536]{1,0:T(8,128)(2,1)} %get-tuple-element.182), channel_id=1, source_target_pairs={{0,1},{1,0},{2,3},{3,2},{4,5},{5,4},{6,7},{7,6},{8,9},{9,8},{10,11... | collective-permute-start | bytes 4718600 | tf_op jit(solution)/shard_map/ppermute | solution.py:47
  525.8 25.7 %collective-permute-start.20 = (bf16[4,2,24,1664]{3,2,1,0:T(8,128)(2,1)}, bf16[4,2,24,1664]{3,2,1,0:T(8,128)(2,1)}, u32[]{:S(2)}, u32[]{:S(2)}) collective-permute-start(bf16[4,2,24,1664]{3,2,1,0:T(8,128)(2,1)} %get-tuple-element.176), channel_id=1, source_target_pairs={{0,16},{16,32},{32,48},{48,0},{1,17},{17,33},{33,49},{49,1},{2,18}... | collective-permute-start | bytes 1916936 | tf_op jit(solution)/shard_map/ppermute | solution.py:514
  527.2 30.7 %collective-permute-start.21 = (bf16[4,2,24,1664]{3,2,1,0:T(8,128)(2,1)}, bf16[4,2,24,1664]{3,2,1,0:T(8,128)(2,1)}, u32[]{:S(2)}, u32[]{:S(2)}) collective-permute-start(bf16[4,2,24,1664]{3,2,1,0:T(8,128)(2,1)} %get-tuple-element.177), channel_id=1, source_target_pairs={{0,32},{16,48},{32,0},{48,16},{1,33},{17,49},{33,1},{49,17},{2,34}... | collective-permute-start | bytes 1916936 | tf_op jit(solution)/shard_map/ppermute | solution.py:514
  529.9 28.0 %collective-permute-start.22 = (bf16[4,2,24,1664]{3,2,1,0:T(8,128)(2,1)}, bf16[4,2,24,1664]{3,2,1,0:T(8,128)(2,1)}, u32[]{:S(2)}, u32[]{:S(2)}) collective-permute-start(bf16[4,2,24,1664]{3,2,1,0:T(8,128)(2,1)} %get-tuple-element.178), channel_id=1, source_target_pairs={{0,48},{16,0},{32,16},{48,32},{1,49},{17,1},{33,17},{49,33},{2,50}... | collective-permute-start | bytes 1916936 | tf_op jit(solution)/shard_map/ppermute | solution.py:514
  533.8 28.0 %all-to-all-start.7 = ((bf16[4,4,2,24,640]{4,3,2,1,0:T(8,128)(2,1)}), bf16[4,4,2,24,640]{4,3,2,1,0:T(8,128)(2,1)S(1)}, u32[]{:S(2)}, u32[]{:S(2)}) async-start(bf16[4,4,2,24,640]{4,3,2,1,0:T(8,128)(2,1)} %add_convert_fusion), calls=%async_computation.8 | async-start | bytes 1966080 | tf_op jit(solution)/shard_map/all_to_all | solution.py:759
  562.7 21.3 %collective-permute-start.28 = (bf16[2,24,640]{2,1,0:T(8,128)(2,1)}, bf16[2,24,640]{2,1,0:T(8,128)(2,1)}, u32[]{:S(2)}, u32[]{:S(2)}) collective-permute-start(bf16[2,24,640]{2,1,0:T(8,128)(2,1)} %get-tuple-element.282), channel_id=1, source_target_pairs={{0,16},{16,32},{32,48},{48,0},{1,17},{17,33},{33,49},{49,1},{2,18}... | collective-permute-start | bytes 184328 | tf_op jit(solution)/shard_map/ppermute | solution.py:83
  564.1 21.3 %collective-permute-start.30 = (bf16[2,24,640]{2,1,0:T(8,128)(2,1)}, bf16[2,24,640]{2,1,0:T(8,128)(2,1)}, u32[]{:S(2)}, u32[]{:S(2)}) collective-permute-start(bf16[2,24,640]{2,1,0:T(8,128)(2,1)} %get-tuple-element.283), channel_id=1, source_target_pairs={{0,48},{16,0},{32,16},{48,32},{1,49},{17,1},{33,17},{49,33},{2,50}... | collective-permute-start | bytes 184328 | tf_op jit(solution)/shard_map/ppermute | solution.py:83
  565.9 19.5 %collective-permute-start.29 = (bf16[2,24,640]{2,1,0:T(8,128)(2,1)}, bf16[2,24,640]{2,1,0:T(8,128)(2,1)}, u32[]{:S(2)}, u32[]{:S(2)}) collective-permute-start(bf16[2,24,640]{2,1,0:T(8,128)(2,1)} %get-tuple-element.284), channel_id=1, source_target_pairs={{0,32},{16,48},{32,0},{48,16},{1,33},{17,49},{33,1},{49,17},{2,34}... | collective-permute-start | bytes 184328 | tf_op jit(solution)/shard_map/ppermute | solution.py:83
  570.5 21.4 %copy-start.29 = (bf16[512,1536]{1,0:T(8,128)(2,1)S(1)}, bf16[512,1536]{1,0:T(8,128)(2,1)}, u32[]{:S(2)}) copy-start(bf16[512,1536]{1,0:T(8,128)(2,1)} %param.15) | copy-start | bytes 4718596
  571.3 15.1 %collective-permute-start.25 = (bf16[2,24,1664]{2,1,0:T(8,128)(2,1)}, bf16[2,24,1664]{2,1,0:T(8,128)(2,1)}, u32[]{:S(2)}, u32[]{:S(2)}) collective-permute-start(bf16[2,24,1664]{2,1,0:T(8,128)(2,1)} %get-tuple-element.279), channel_id=1, source_target_pairs={{0,2},{2,4},{4,6},{6,0},{1,3},{3,5},{5,7},{7,1},{8,10},{10,12},{12... | collective-permute-start | bytes 479240 | tf_op jit(solution)/shard_map/ppermute | solution.py:83
  574.3 12.2 %collective-permute-start.27 = (bf16[2,24,1664]{2,1,0:T(8,128)(2,1)}, bf16[2,24,1664]{2,1,0:T(8,128)(2,1)}, u32[]{:S(2)}, u32[]{:S(2)}) collective-permute-start(bf16[2,24,1664]{2,1,0:T(8,128)(2,1)} %get-tuple-element.280), channel_id=1, source_target_pairs={{0,6},{2,0},{4,2},{6,4},{1,7},{3,1},{5,3},{7,5},{8,14},{10,8},{12,... | collective-permute-start | bytes 479240 | tf_op jit(solution)/shard_map/ppermute | solution.py:83
  584.0 6.8 %collective-permute-start.26 = (bf16[2,24,1664]{2,1,0:T(8,128)(2,1)S(1)}, bf16[2,24,1664]{2,1,0:T(8,128)(2,1)S(1)}, u32[]{:S(2)}, u32[]{:S(2)}) collective-permute-start(bf16[2,24,1664]{2,1,0:T(8,128)(2,1)S(1)} %get-tuple-element.281), channel_id=1, source_target_pairs={{0,4},{2,6},{4,0},{6,2},{1,5},{3,7},{5,1},{7,3},{8,12},{10,14},{12... | collective-permute-start | bytes 479240 | tf_op jit(solution)/shard_map/ppermute | solution.py:83
  594.4 7.7 %collective-permute-start.31 = (bf16[24,2304]{1,0:T(8,128)(2,1)S(1)}, bf16[24,2304]{1,0:T(8,128)(2,1)S(1)}, u32[]{:S(2)}, u32[]{:S(2)}) collective-permute-start(bf16[24,2304]{1,0:T(8,128)(2,1)S(1)} %dynamic-slice_bitcast_fusion.3), channel_id=1, source_target_pairs={{0,64},{64,0},{1,65},{65,1},{2,66},{66,2},{3,67},{67,3},{4,68},{68... | collective-permute-start | bytes 331784 | tf_op jit(solution)/shard_map/ppermute | solution.py:83
  604.7 3.8 collective-permute-start.32
  (55 other events, 209.5 us)
Sparse Core Ops, SparseCore 0:
  94.9 91.0 all-gather.2
  362.4 99.6 reduce-scatter.1

commit v6 on v4

--- a/solution.py
+++ b/solution.py
@@ -4,7 +4,6 @@
 import jax.numpy as jnp
 from jax import lax
 from jax.experimental import pallas as pl
-from jax.experimental.layout import Layout, with_layout_constraint
 from jax.experimental.pallas import tpu as pltpu
 from jax.sharding import Mesh
 from jax.sharding import PartitionSpec as P
@@ -373,7 +372,7 @@
     return dict(
         grid=(hidden // HALF,),
         scratch_shapes=[pltpu.VMEM((rows, width), F32)],
-        compiler_params=pltpu.CompilerParams(vmem_limit_bytes=60 << 20),
+        compiler_params=pltpu.CompilerParams(vmem_limit_bytes=40 << 20),
         cost_estimate=pl.CostEstimate(
             flops=6 * rows * width * hidden, bytes_accessed=20_000_000, transcendentals=rows * hidden
         ),
@@ -497,6 +496,22 @@
     )(jnp.full((1,), lax.axis_index("c"), jnp.int32), *arrays)
 
 
+def turned_sum_kernel(left_ref, right_ref, out_ref):
+    out_ref[...] = both(left_ref[...], right_ref[...]).T
+
+
+def turned_sum(left, right):
+    rows, cols = left.shape
+    return pl.pallas_call(
+        turned_sum_kernel,
+        out_shape=jax.ShapeDtypeStruct((cols, rows), F32),
+        compiler_params=pltpu.CompilerParams(vmem_limit_bytes=16 << 20),
+        cost_estimate=pl.CostEstimate(
+            flops=2 * rows * cols, bytes_accessed=8 * rows * cols, transcendentals=0
+        ),
+    )(left, right)
+
+
 def pair_blocks(own, theirs, axis):
     received = swap(theirs, "c")
     me = lax.axis_index(axis)
@@ -728,15 +743,14 @@
         feat_width // 2 + 128 + q_width,
         20_000_000_000,
     )
-    d_act_query = dot(jnp.concatenate([back_0[0], back_1[0]]), full_query, 0, 1)
-    o1, o2, o3, given_1, own_one, theirs_one, d_act_query = lax.optimization_barrier(
-        (*others_1, given_1, own_one, theirs_one, d_act_query)
+    o1, o2, o3, given_1, own_one, theirs_one, dq_0, dq_1 = lax.optimization_barrier(
+        (*others_1, given_1, own_one, theirs_one, back_0[0], back_1[0])
     )
 
     d_kv_t = jnp.concatenate(
         [added([back_0[1], *others_0]), added([back_1[1], o1, o2, o3])], axis=1
     ).reshape(2 * k_width, tok_rows).astype(BF)
-    d_act_part = d_act_query + dot(d_kv_t, full_kv, 0, 1)
+    d_act_part = dot(jnp.concatenate([dq_0, dq_1]), full_query, 0, 1) + dot(d_kv_t, full_kv, 0, 1)
     part = d_act_part.astype(BF)
     blocks_one = pair_blocks(own_one, theirs_one, "x")
     gain_row = jnp.sum(d_act_part * resid_in * scale_one, axis=0, keepdims=True)
@@ -759,7 +773,7 @@
     paired_two = both(own_two, swap(theirs_two, "c")).astype(BF)
     ring_two = lax.all_to_all(paired_two, "y", 0, 0, tiled=True)
     grad_wide = keep[:2].astype(F32) + given_0.astype(F32)
-    own_down = with_layout_constraint(both(keep[2], given_1).T, Layout(major_to_minor=(0, 1)))
+    own_down = turned_sum(keep[2], given_1)
     *parts_one, ring_two, own_down, other = lax.optimization_barrier(
         (*parts_one, ring_two, own_down, other)
     )

time: 634 us -> 622 us (0.981)
  waiting for transfers between devices: 273 us -> 288 us
  starting transfers between devices: 92 us -> 81.8 us
  other arithmetic: 50.8 us -> 41.7 us
    pallas_call x1 -> x0, local copies, waits for them, and re-layouts: 12.7 us -> none  [expert_grads(): pl.pallas_call(expert_grads_kernel, in_specs=[whole, whole, column, colum...]
    unnamed x130 -> x152, local copies, waits for them, and re-layouts: 11.9 us -> 22.6 us
    all_to_all x3, waiting for transfers between devices: 42.5 us -> 52 us  [exchange_slots(): lax.all_to_all(rows.reshape(EXPERTS, -1, width), ('h', 'x', 'c'), 0, 0, t...]
    ppermute x3, waiting for transfers between devices: 4.38 us -> 12.6 us  [send_blocks(): lax.ppermute(blocks[r], axis, [(i, (i + r) % 4) for i in range(4)])]
    reduce_scatter x1, waiting for transfers between devices: 38 us -> 30.8 us  [local(): grad_experts = lax.psum_scatter(grad_parts, 'y', scatter_dimension=0)]
  transfers between devices with their start and end apart: 42 -> 42, of which waited for: 22 -> 22; matrix products, arithmetic and copies ran while one was open for 15% -> 11% of each run, Pallas kernels for 8% -> 8%
where the time goes in v6:
time: 622 us; the launch traced here: 612 us
  waiting for transfers between devices  288 us (46%)
  starting transfers between devices  81.8 us (13%)
  Pallas kernels  73.4 us (12%)
  local copies, waits for them, and re-layouts  43 us (7%)
  other arithmetic  41.7 us (7%)
  blocking collectives  37.4 us (6%)
  matrix products  27.6 us (4%)
  between operations  19.4 us (3%)
    ppermute x14, waiting for transfers between devices, swap(): return lax.ppermute(value, axis, [(0, 1), (1, 0)])  143 us
    all_to_all x3, waiting for transfers between devices, exchange_slots(): lax.all_to_all(rows.reshape(EXPERTS, -1, width), ('h', 'x', 'c'), 0, 0, t...  52 us
    all_to_all x1, blocking collectives, exchange_slots(): lax.all_to_all(rows.reshape(EXPERTS, -1, width), ('h', 'x', 'c'), 0, 0, t...  37.4 us
    reduce_scatter x1, waiting for transfers between devices, local(): grad_experts = lax.psum_scatter(grad_parts, 'y', scatter_dimension=0)  30.8 us
    dot_general x16, matrix products, dot(): lax.dot_general(left, right, (((left_dim,), (right_dim,)), ((), ())), pre...  27.6 us
    unnamed x152, local copies, waits for them, and re-layouts  22.6 us
    pallas_call x1, Pallas kernels, run_experts_back(): pl.pallas_call(experts_back_kernel, in_specs=[whole, column, column] + we...  14.9 us
    ppermute x7, starting transfers between devices, axis_parts(): lax.ppermute(block, axis, [(i, (i + r) % size) for i in range(size)])  14.3 us
  transfers between devices with their start and end apart: 42, of which 22 were waited for; matrix products, arithmetic and copies ran while one was open for 11% of the time, Pallas kernels for 8%

profile of v6, /device:TPU:0, one launch (start us, length us, event | category | flops | bytes accessed | tf_op | source)
XLA Modules:
  0.0 612.3 jit_solution(18425339133076146717)
XLA Ops:
  11.4 7.9 %all-to-all-start = ((bf16[8,24,2176]{2,1,0:T(8,128)(2,1)}), bf16[8,24,2176]{2,1,0:T(8,128)(2,1)S(1)}, u32[]{:S(2)}, u32[]{:S(2)}) async-start(bf16[8,24,2176]{2,1,0:T(8,128)(2,1)} %broadcast_in_dim.149), calls=%async_computation | async-start | bytes 1671168 | tf_op jit(solution)/shard_map/all_to_all | solution.py:56
  20.7 13.6 %all-to-all-done = bf16[8,24,2176]{2,1,0:T(8,128)(2,1)S(1)} async-done(((bf16[8,24,2176]{2,1,0:T(8,128)(2,1)}), bf16[8,24,2176]{2,1,0:T(8,128)(2,1)S(1)}, u32[]{:S(2)}, u32[]{:S(2)}) %all-to-all-start) | async-done | bytes 835616 | tf_op jit(solution)/shard_map/all_to_all | solution.py:56
  35.5 4.3 all-to-all-start.1
  41.0 13.0 %all-to-all-done.1 = bf16[4,8,24,640]{3,2,1,0:T(8,128)(2,1)S(1)} async-done(((bf16[4,8,24,640]{3,2,1,0:T(8,128)(2,1)}), bf16[4,8,24,640]{3,2,1,0:T(8,128)(2,1)S(1)}, u32[]{:S(2)}, u32[]{:S(2)}) %all-to-all-start.1) | async-done | bytes 983072 | tf_op jit(solution)/shard_map/all_to_all | solution.py:61
  57.1 4.5 all-to-all-start.2
  67.6 2.4 collective-permute-start.2
  70.0 2.1 collective-permute-start.1
  72.1 12.7 %collective-permute-done.4 = bf16[3,384,512]{2,1,0:T(8,128)(2,1)} collective-permute-done((bf16[3,384,512]{2,1,0:T(8,128)(2,1)}, bf16[3,384,512]{2,1,0:T(8,128)(2,1)}, u32[]{:S(2)}, u32[]{:S(2)}) %collective-permute-start.4) | collective-permute-done | bytes 1179680 | tf_op jit(solution)/shard_map/ppermute | solution.py:47
  84.8 6.7 %all-to-all-done.2 = bf16[4,8,24,1536]{3,2,1,0:T(8,128)(2,1)} async-done(((bf16[4,8,24,1536]{3,2,1,0:T(8,128)(2,1)}), bf16[4,8,24,1536]{3,2,1,0:T(8,128)(2,1)}, u32[]{:S(2)}, u32[]{:S(2)}) %all-to-all-start.2) | async-done | bytes 2359328 | tf_op jit(solution)/shard_map/all_to_all | solution.py:580
  91.5 3.2 pad_maximum_fusion.1
  97.4 2.3 collective-permute-done.5
  99.7 2.7 select_bitcast_fusion.1
  105.4 4.1 shard_map.246
  112.3 4.7 shard_map.247
  117.1 13.9 %collective-permute-done.6 = bf16[256,1536]{1,0:T(8,128)(2,1)S(1)} collective-permute-done((bf16[256,1536]{1,0:T(8,128)(2,1)S(1)}, bf16[256,1536]{1,0:T(8,128)(2,1)S(1)}, u32[]{:S(2)}, u32[]{:S(2)}) %collective-permute-start.6) | collective-permute-done | bytes 786464 | tf_op jit(solution)/shard_map/ppermute | solution.py:47
  133.1 17.8 %collective-permute-done.7 = bf16[256,1536]{1,0:T(8,128)(2,1)S(1)} collective-permute-done((bf16[256,1536]{1,0:T(8,128)(2,1)S(1)}, bf16[256,1536]{1,0:T(8,128)(2,1)S(1)}, u32[]{:S(2)}, u32[]{:S(2)}) %collective-permute-start.7) | collective-permute-done | bytes 786464 | tf_op jit(solution)/shard_map/ppermute | solution.py:47
  154.1 2.8 convolution_convert_fusion.1
  156.9 3.9 all-to-all-start.3
  162.3 30.4 %all-to-all-done.3 = bf16[16,48,1536]{2,1,0:T(8,128)(2,1)S(1)} async-done(((bf16[16,48,1536]{2,1,0:T(8,128)(2,1)}), bf16[16,48,1536]{2,1,0:T(8,128)(2,1)S(1)}, u32[]{:S(2)}, u32[]{:S(2)}) %all-to-all-start.3) | async-done | bytes 2359328 | tf_op jit(solution)/shard_map/all_to_all | solution.py:96
  192.7 12.1 %shard_map.248 = (f32[768,1024]{1,0:T(8,128)S(1)}, f32[768,1024]{1,0:T(8,128)S(1)}, bf16[768,1024]{1,0:T(8,128)(2,1)S(1)}, bf16[768,1536]{1,0:T(8,128)(2,1)S(1)}) custom-call(bf16[768,1536]{1,0:T(8,128)(2,1)S(1)} %bitcast.137, bf16[4,2,3,384,512]{4,3,2,1,0:T(8,128)(2,1)} %bitcast.150, bf16[4,2,3,384,512]{4,3,2,1,0:T(8,128)(2,1)} %bitcast.151, ...), custom_call_target="tpu_custom_call" | custom-call | flops 7247757312 | bytes 20000000 | tf_op jit(solution)/shard_map/pallas_call | solution.py:387
  206.5 37.4 %all_to_all.40 = bf16[16,48,1536]{2,1,0:T(8,128)(2,1)S(1)} all-to-all(bf16[16,48,1536]{2,1,0:T(8,128)(2,1)S(1)} %bitcast.140), channel_id=1, replica_groups=mesh['h'=2,'x'=4,'c'=2,'y'=4,'t'=2] {'h','x','c'}, dimensions={0} | all-to-all | bytes 4718592 | tf_op jit(solution)/shard_map/all_to_all | solution.py:96
  246.7 35.1 %collective-permute-done.8 = bf16[512,1536]{1,0:T(8,128)(2,1)S(1)} collective-permute-done((bf16[512,1536]{1,0:T(8,128)(2,1)S(1)}, bf16[512,1536]{1,0:T(8,128)(2,1)S(1)}, u32[]{:S(2)}, u32[]{:S(2)}) %collective-permute-start.8) | collective-permute-done | bytes 1572896 | tf_op jit(solution)/shard_map/ppermute | solution.py:47
  281.8 2.0 fusion.7
  285.4 2.8 convolution_convert_fusion
  288.2 3.7 all-to-all-start.5
  292.0 3.8 select_reduce_fusion.1
  296.7 20.3 %collective-permute-done.9 = f32[2,512]{1,0:T(2,128)S(1)} collective-permute-done((f32[2,512]{1,0:T(2,128)S(1)}, f32[2,512]{1,0:T(2,128)S(1)}, u32[]{:S(2)}, u32[]{:S(2)}) %collective-permute-start.9) | collective-permute-done | bytes 4128 | tf_op jit(solution)/shard_map/ppermute | solution.py:47
  316.9 7.0 %all-to-all-done.5 = bf16[16,48,1536]{2,1,0:T(8,128)(2,1)S(1)} async-done(((bf16[16,48,1536]{2,1,0:T(8,128)(2,1)}), bf16[16,48,1536]{2,1,0:T(8,128)(2,1)S(1)}, u32[]{:S(2)}, u32[]{:S(2)}) %all-to-all-start.5) | async-done | bytes 2359328 | tf_op jit(solution)/shard_map/all_to_all | solution.py:96
  324.0 1.9 copy-done.3
  325.9 1.9 copy-done.5
  327.8 14.9 %shard_map.249 = (bf16[768,1024]{1,0:T(8,128)(2,1)S(1)}, bf16[768,1024]{1,0:T(8,128)(2,1)S(1)}, bf16[768,1536]{1,0:T(8,128)(2,1)S(1)}) custom-call(bf16[768,1536]{1,0:T(8,128)(2,1)S(1)} %bitcast.135, f32[768,1024]{1,0:T(8,128)S(1)} %copy-done.3, f32[768,1024]{1,0:T(8,128)S(1)} %copy-done.5, bf16[4,2,3,384,512]{4,3,2,1,0:T(8,128)(2,1)} %bitcast.153, ...), custom_call_target="tpu_custom_call" | custom-call | flops 7247757312 | bytes 20000000 | tf_op jit(solution)/shard_map/pallas_call | solution.py:407
  346.4 5.5 all-to-all-start.6
  357.8 11.6 %shard_map.250 = bf16[4,2,3,384,512]{4,3,2,1,0:T(8,128)(2,1)} custom-call(bf16[768,1536]{1,0:T(8,128)(2,1)S(1)} %bitcast.138, bf16[768,1536]{1,0:T(8,128)(2,1)S(1)} %bitcast.136, bf16[768,1024]{1,0:T(8,128)(2,1)S(1)} %copy-done.14, bf16[768,1024]{1,0:T(8,128)(2,1)S(1)} %copy-done.16, bf16[768,1024]{1,0:T(8,128)(2,1)S(1)} %copy-done.12), custom_call_target="tpu_custom_call" | custom-call | flops 7247757312 | bytes 20000000 | tf_op jit(solution)/shard_map/pallas_call | solution.py:421
  369.4 14.5 %all-to-all-done.6 = bf16[16,48,1536]{2,1,0:T(8,128)(2,1)} async-done(((bf16[16,48,1536]{2,1,0:T(8,128)(2,1)}), bf16[16,48,1536]{2,1,0:T(8,128)(2,1)}, u32[]{:S(2)}, u32[]{:S(2)}) %all-to-all-start.6) | async-done | bytes 2359328 | tf_op jit(solution)/shard_map/all_to_all | solution.py:96
  384.0 3.0 convolution_convert_fusion.2
  391.9 31.5 %collective-permute-done.10 = bf16[512,1536]{1,0:T(8,128)(2,1)S(1)} collective-permute-done((bf16[512,1536]{1,0:T(8,128)(2,1)S(1)}, bf16[512,1536]{1,0:T(8,128)(2,1)S(1)}, u32[]{:S(2)}, u32[]{:S(2)}) %collective-permute-start.10) | collective-permute-done | bytes 1572896 | tf_op jit(solution)/shard_map/ppermute | solution.py:47
  425.2 3.3 fusion.73
  428.6 2.3 fusion.24.d_ref
  430.9 7.0 %shard_map.251 = (bf16[384,512]{1,0:T(8,128)(2,1)}, bf16[2,128,512]{2,1,0:T(8,128)(2,1)}, bf16[2,128,512]{2,1,0:T(8,128)(2,1)}, bf16[2,128,512]{2,1,0:T(8,128)(2,1)}, bf16[2,128,512]{2,1,0:T(8,128)(2,1)}) custom-call(s32[1]{0:T(128)} %bitcast.y_ref, bf16[768,512]{1,0:T(8,128)(2,1)} %copy-done.24, bf16[768,512]{1,0:T(8,128)(2,1)} %fusion.24.d_ref, ...), custom_call_target="tpu_custom_call" | custom-call | flops 149999992832 | bytes 6000000 | tf_op jit(solution)/shard_map/pallas_call | solution.py:273
  437.9 30.8 %reduce-scatter.2.cloned.1.call-done = bf16[1,2,3,384,512]{4,3,2,1,0:T(8,128)(2,1)} async-done(((bf16[4,2,3,384,512]{4,3,2,1,0:T(8,128)(2,1)}), bf16[1,2,3,384,512]{4,3,2,1,0:T(8,128)(2,1)}) %reduce-scatter.2.cloned.1.call-update) | async-done | bytes 2359312 | tf_op jit(solution)/shard_map/reduce_scatter | solution.py:682
  475.0 1.7 collective-permute-start.14
  476.7 7.0 %shard_map.252 = (bf16[384,512]{1,0:T(8,128)(2,1)}, bf16[2,128,512]{2,1,0:T(8,128)(2,1)}, bf16[2,128,512]{2,1,0:T(8,128)(2,1)}, bf16[2,128,512]{2,1,0:T(8,128)(2,1)}, bf16[2,128,512]{2,1,0:T(8,128)(2,1)}) custom-call(s32[1]{0:T(128)} %bitcast.y_ref, bf16[768,512]{1,0:T(8,128)(2,1)} %copy-done.24, bf16[768,512]{1,0:T(8,128)(2,1)} %fusion.24.d_ref, ...), custom_call_target="tpu_custom_call" | custom-call | flops 149999992832 | bytes 6000000 | tf_op jit(solution)/shard_map/pallas_call | solution.py:273
  484.7 4.1 collective-permute-done.13
  488.8 5.9 collective-permute-done.14
  501.7 8.4 %shard_map.253 = (bf16[4,4,2,24,1664]{4,3,2,1,0:T(8,128)(2,1)}, bf16[4,4,2,24,1664]{4,3,2,1,0:T(8,128)(2,1)}) custom-call(s32[1]{0:T(128)} %bitcast.55.core_ref, bf16[512,1536]{1,0:T(8,128)(2,1)} %copy-done.47, bf16[512,1536]{1,0:T(8,128)(2,1)} %copy-done.7, bf16[512,1536]{1,0:T(8,128)(2,1)} %copy-done.41, f32[8,1536]{1,0:T(8,128)} %maximum_maximum_fusion.refs_3_, ...), custom_call_target="tpu_custom_call" | custom-call | flops 20000000000 | bytes 10000000 | tf_op jit(solution)/shard_map/pallas_call | solution.py:483
  510.1 6.2 %collective-permute-done.17 = bf16[2,128,512]{2,1,0:T(8,128)(2,1)S(1)} collective-permute-done((bf16[2,128,512]{2,1,0:T(8,128)(2,1)}, bf16[2,128,512]{2,1,0:T(8,128)(2,1)S(1)}, u32[]{:S(2)}, u32[]{:S(2)}) %collective-permute-start.17) | collective-permute-done | bytes 262176 | tf_op jit(solution)/shard_map/ppermute | solution.py:706
  517.8 3.3 fusion.12
  521.1 2.6 fusion.10
  523.8 2.4 shard_map.254
  526.2 3.4 fusion.50
  532.4 2.7 collective-permute-start.21
  536.5 2.4 add_convert_fusion
  538.9 6.5 %all-to-all-start.7 = ((bf16[4,4,2,24,640]{4,3,2,1,0:T(8,128)(2,1)}), bf16[4,4,2,24,640]{4,3,2,1,0:T(8,128)(2,1)S(1)}, u32[]{:S(2)}, u32[]{:S(2)}) async-start(bf16[4,4,2,24,640]{4,3,2,1,0:T(8,128)(2,1)} %add_convert_fusion), calls=%async_computation.8 | async-start | bytes 1966080 | tf_op jit(solution)/shard_map/all_to_all | solution.py:774
  550.4 12.6 %collective-permute-done.21 = bf16[4,2,24,1664]{3,2,1,0:T(8,128)(2,1)} collective-permute-done((bf16[4,2,24,1664]{3,2,1,0:T(8,128)(2,1)}, bf16[4,2,24,1664]{3,2,1,0:T(8,128)(2,1)}, u32[]{:S(2)}, u32[]{:S(2)}) %collective-permute-start.21) | collective-permute-done | bytes 639008 | tf_op jit(solution)/shard_map/ppermute | solution.py:530
  563.0 3.8 collective-permute-done.24
  568.6 1.8 collective-permute-start.30
  570.3 1.8 collective-permute-start.29
  572.1 1.8 add_convert_fusion.3
  573.9 4.0 collective-permute-start.25
  580.1 3.3 collective-permute-done.25
  583.7 2.1 collective-permute-done.26
  586.0 2.9 fusion.11
  588.9 3.1 collective-permute-start.31
  591.9 4.8 fusion.6
  (290 shorter events, 88.9 us)
Async XLA Ops:
  11.4 22.8 %all-to-all-start = ((bf16[8,24,2176]{2,1,0:T(8,128)(2,1)}), bf16[8,24,2176]{2,1,0:T(8,128)(2,1)S(1)}, u32[]{:S(2)}, u32[]{:S(2)}) async-start(bf16[8,24,2176]{2,1,0:T(8,128)(2,1)} %broadcast_in_dim.149), calls=%async_computation | async-start | bytes 1671168 | tf_op jit(solution)/shard_map/all_to_all | solution.py:56
  35.5 18.5 %all-to-all-start.1 = ((bf16[4,8,24,640]{3,2,1,0:T(8,128)(2,1)}), bf16[4,8,24,640]{3,2,1,0:T(8,128)(2,1)S(1)}, u32[]{:S(2)}, u32[]{:S(2)}) async-start(bf16[4,8,24,640]{3,2,1,0:T(8,128)(2,1)} %broadcast_in_dim.150), calls=%async_computation.1 | async-start | bytes 1966080 | tf_op jit(solution)/shard_map/all_to_all | solution.py:61
  39.8 15.8 %copy-start.30 = (bf16[512,1536]{1,0:T(8,128)(2,1)S(1)}, bf16[512,1536]{1,0:T(8,128)(2,1)}, u32[]{:S(2)}) copy-start(bf16[512,1536]{1,0:T(8,128)(2,1)} %param.15) | copy-start | bytes 4718596
  55.6 6.1 collective-permute-start
  56.0 28.8 %collective-permute-start.4 = (bf16[3,384,512]{2,1,0:T(8,128)(2,1)}, bf16[3,384,512]{2,1,0:T(8,128)(2,1)}, u32[]{:S(2)}, u32[]{:S(2)}) collective-permute-start(bf16[3,384,512]{2,1,0:T(8,128)(2,1)} %pad_maximum_fusion.3), channel_id=1, source_target_pairs={{0,1},{1,0},{2,3},{3,2},{4,5},{5,4},{6,7},{7,6},{8,9},{9,8},{10,11... | collective-permute-start | bytes 3538952 | tf_op jit(solution)/shard_map/ppermute | solution.py:47
  57.1 34.4 %all-to-all-start.2 = ((bf16[4,8,24,1536]{3,2,1,0:T(8,128)(2,1)}), bf16[4,8,24,1536]{3,2,1,0:T(8,128)(2,1)}, u32[]{:S(2)}, u32[]{:S(2)}) async-start(bf16[4,8,24,1536]{3,2,1,0:T(8,128)(2,1)} %broadcast_in_dim.151), calls=%async_computation.2 | async-start | bytes 4718592 | tf_op jit(solution)/shard_map/all_to_all | solution.py:580
  61.6 131.1 %all-gather.3.cloned.1.call-start = ((), (), s32[]{:S(2)}) async-start(), calls=%async_computation.10 | async-start | bytes 11796480 | tf_op jit(solution)/shard_map/all_gather | solution.py:606
  65.1 38.0 %copy-start.7 = (bf16[512,1536]{1,0:T(8,128)(2,1)}, bf16[512,1536]{1,0:T(8,128)(2,1)S(1)}, u32[]{:S(2)}) copy-start(bf16[512,1536]{1,0:T(8,128)(2,1)S(1)} %fusion.2.refs_1_.refs_0_) | copy-start | bytes 4718596
  66.2 46.1 %copy-start.17 = (bf16[512,512]{1,0:T(8,128)(2,1)}, bf16[512,512]{1,0:T(8,128)(2,1)S(1)}, u32[]{:S(2)}) copy-start(bf16[512,512]{1,0:T(8,128)(2,1)S(1)} %fusion.33) | copy-start | bytes 1572868
  66.2 28.5 %collective-permute-start.3 = (bf16[2,256,512]{2,1,0:T(8,128)(2,1)S(1)}, bf16[2,256,512]{2,1,0:T(8,128)(2,1)S(1)}, u32[]{:S(2)}, u32[]{:S(2)}) collective-permute-start(bf16[2,256,512]{2,1,0:T(8,128)(2,1)S(1)} %bitcast.143), channel_id=1, source_target_pairs={{0,6},{1,7},{8,14},{9,15},{16,22},{17,23},{24,30},{25,31},{32,38},... | collective-permute-start | bytes 1572872 | tf_op jit(solution)/shard_map/ppermute | solution.py:594
  67.6 27.2 %collective-permute-start.2 = (bf16[2,256,512]{2,1,0:T(8,128)(2,1)S(1)}, bf16[2,256,512]{2,1,0:T(8,128)(2,1)S(1)}, u32[]{:S(2)}, u32[]{:S(2)}) collective-permute-start(bf16[2,256,512]{2,1,0:T(8,128)(2,1)S(1)} %bitcast.144), channel_id=1, source_target_pairs={{0,4},{2,6},{1,5},{3,7},{8,12},{10,14},{9,13},{11,15},{16,20},{18,... | collective-permute-start | bytes 1572872 | tf_op jit(solution)/shard_map/ppermute | solution.py:594
  70.0 24.8 %collective-permute-start.1 = (bf16[2,256,512]{2,1,0:T(8,128)(2,1)S(1)}, bf16[2,256,512]{2,1,0:T(8,128)(2,1)}, u32[]{:S(2)}, u32[]{:S(2)}) collective-permute-start(bf16[2,256,512]{2,1,0:T(8,128)(2,1)S(1)} %bitcast.145), channel_id=1, source_target_pairs={{0,2},{2,4},{4,6},{1,3},{3,5},{5,7},{8,10},{10,12},{12,14},{9,11},... | collective-permute-start | bytes 1572872 | tf_op jit(solution)/shard_map/ppermute | solution.py:594
  94.8 5.0 collective-permute-start.5
  97.4 149.2 %copy-start.10 = (s32[1,512]{1,0:T(1,128)}, s32[1,512]{1,0:T(1,128)S(1)}, u32[]{:S(2)}) copy-start(s32[1,512]{1,0:T(1,128)S(1)} %get-tuple-element.264.seg_q) | copy-start | bytes 6148
  103.2 27.9 %copy-start.43 = (bf16[2,4,2,96,1536]{4,3,2,1,0:T(8,128)(2,1)}, bf16[2,4,2,96,1536]{4,3,2,1,0:T(8,128)(2,1)S(1)}, u32[]{:S(2)}) copy-start(bf16[2,4,2,96,1536]{4,3,2,1,0:T(8,128)(2,1)S(1)} %copy.66) | copy-start | bytes 14155780
  111.1 19.9 %collective-permute-start.6 = (bf16[256,1536]{1,0:T(8,128)(2,1)S(1)}, bf16[256,1536]{1,0:T(8,128)(2,1)S(1)}, u32[]{:S(2)}, u32[]{:S(2)}) collective-permute-start(bf16[256,1536]{1,0:T(8,128)(2,1)S(1)} %convolution_convert_fusion.5), channel_id=1, source_target_pairs={{0,1},{1,0},{2,3},{3,2},{4,5},{5,4},{6,7},{7,6},{8,9},{9,8},{10,11... | collective-permute-start | bytes 2359304 | tf_op jit(solution)/shard_map/ppermute | solution.py:47
  117.1 15.8 %copy-start.65 = (s32[512,2]{0,1:T(2,128)S(1)}, s32[512,2]{0,1:T(2,128)}, u32[]{:S(2)}) copy-start(s32[512,2]{0,1:T(2,128)} %param.18) | copy-start | bytes 12292
  131.9 19.0 %collective-permute-start.7 = (bf16[256,1536]{1,0:T(8,128)(2,1)S(1)}, bf16[256,1536]{1,0:T(8,128)(2,1)S(1)}, u32[]{:S(2)}, u32[]{:S(2)}) collective-permute-start(bf16[256,1536]{1,0:T(8,128)(2,1)S(1)} %convolution_convert_fusion.4), channel_id=1, source_target_pairs={{0,1},{1,0},{2,3},{3,2},{4,5},{5,4},{6,7},{7,6},{8,9},{9,8},{10,11... | collective-permute-start | bytes 2359304 | tf_op jit(solution)/shard_map/ppermute | solution.py:47
  133.1 18.0 %copy-start.31 = (bf16[512,1536]{1,0:T(8,128)(2,1)S(1)}, bf16[512,1536]{1,0:T(8,128)(2,1)}, u32[]{:S(2)}) copy-start(bf16[512,1536]{1,0:T(8,128)(2,1)} %param.15) | copy-start | bytes 4718596
  156.9 35.9 %all-to-all-start.3 = ((bf16[16,48,1536]{2,1,0:T(8,128)(2,1)}), bf16[16,48,1536]{2,1,0:T(8,128)(2,1)S(1)}, u32[]{:S(2)}, u32[]{:S(2)}) async-start(bf16[16,48,1536]{2,1,0:T(8,128)(2,1)} %bitcast.171), calls=%async_computation.3 | async-start | bytes 4718592 | tf_op jit(solution)/shard_map/all_to_all | solution.py:96
  206.5 37.4 %copy-start.2 = (f32[768,1024]{1,0:T(8,128)}, f32[768,1024]{1,0:T(8,128)S(1)}, u32[]{:S(2)}) copy-start(f32[768,1024]{1,0:T(8,128)S(1)} %get-tuple-element.124.g_ref) | copy-start | bytes 9437188
  206.5 37.4 %copy-start.11 = (bf16[768,1024]{1,0:T(8,128)(2,1)}, bf16[768,1024]{1,0:T(8,128)(2,1)S(1)}, u32[]{:S(2)}) copy-start(bf16[768,1024]{1,0:T(8,128)(2,1)S(1)} %get-tuple-element.131.inner_ref) | copy-start | bytes 4718596
  206.5 37.4 %copy-start.51 = (bf16[512,768]{1,0:T(8,128)(2,1)S(1)}, bf16[512,768]{1,0:T(8,128)(2,1)}, u32[]{:S(2)}) copy-start(bf16[512,768]{1,0:T(8,128)(2,1)} %add_convert_fusion.2) | copy-start | bytes 2359300
  243.9 37.9 %copy-start.28 = (f32[512,1536]{1,0:T(8,128)S(1)}, f32[512,1536]{1,0:T(8,128)}, u32[]{:S(2)}) copy-start(f32[512,1536]{1,0:T(8,128)} %copy-done.27) | copy-start | bytes 9437188
  243.9 37.9 %copy-start.36 = (bf16[512,1536]{1,0:T(8,128)(2,1)S(1)}, bf16[512,1536]{1,0:T(8,128)(2,1)}, u32[]{:S(2)}) copy-start(bf16[512,1536]{1,0:T(8,128)(2,1)} %param.16) | copy-start | bytes 4718596
  245.4 36.4 %collective-permute-start.8 = (bf16[512,1536]{1,0:T(8,128)(2,1)S(1)}, bf16[512,1536]{1,0:T(8,128)(2,1)S(1)}, u32[]{:S(2)}, u32[]{:S(2)}) collective-permute-start(bf16[512,1536]{1,0:T(8,128)(2,1)S(1)} %convolution_convert_fusion.3), channel_id=1, source_target_pairs={{0,1},{1,0},{2,3},{3,2},{4,5},{5,4},{6,7},{7,6},{8,9},{9,8},{10,11... | collective-permute-start | bytes 4718600 | tf_op jit(solution)/shard_map/ppermute | solution.py:47
  288.2 35.7 %all-to-all-start.5 = ((bf16[16,48,1536]{2,1,0:T(8,128)(2,1)}), bf16[16,48,1536]{2,1,0:T(8,128)(2,1)S(1)}, u32[]{:S(2)}, u32[]{:S(2)}) async-start(bf16[16,48,1536]{2,1,0:T(8,128)(2,1)} %bitcast.170), calls=%async_computation.5 | async-start | bytes 4718592 | tf_op jit(solution)/shard_map/all_to_all | solution.py:96
  295.8 21.2 %collective-permute-start.9 = (f32[2,512]{1,0:T(2,128)S(1)}, f32[2,512]{1,0:T(2,128)S(1)}, u32[]{:S(2)}, u32[]{:S(2)}) collective-permute-start(f32[2,512]{1,0:T(2,128)S(1)} %pad_maximum_fusion.6), channel_id=1, source_target_pairs={{0,1},{1,0},{2,3},{3,2},{4,5},{5,4},{6,7},{7,6},{8,9},{9,8},{10,11... | collective-permute-start | bytes 12296 | tf_op jit(solution)/shard_map/ppermute | solution.py:47
  346.4 37.6 %all-to-all-start.6 = ((bf16[16,48,1536]{2,1,0:T(8,128)(2,1)}), bf16[16,48,1536]{2,1,0:T(8,128)(2,1)}, u32[]{:S(2)}, u32[]{:S(2)}) async-start(bf16[16,48,1536]{2,1,0:T(8,128)(2,1)} %bitcast.139), calls=%async_computation.6 | async-start | bytes 4718592 | tf_op jit(solution)/shard_map/all_to_all | solution.py:96
  351.9 116.9 %reduce-scatter.2.cloned.1.call-start = ((), (), s32[]{:S(2)}) async-start(), calls=%async_computation.9 | async-start | bytes 11796480 | tf_op jit(solution)/shard_map/reduce_scatter | solution.py:682
  387.0 36.4 %copy-start.29 = (f32[512,1536]{1,0:T(8,128)S(1)}, f32[512,1536]{1,0:T(8,128)}, u32[]{:S(2)}) copy-start(f32[512,1536]{1,0:T(8,128)} %copy-done.27) | copy-start | bytes 9437188
  387.1 36.3 %collective-permute-start.10 = (bf16[512,1536]{1,0:T(8,128)(2,1)S(1)}, bf16[512,1536]{1,0:T(8,128)(2,1)S(1)}, u32[]{:S(2)}, u32[]{:S(2)}) collective-permute-start(bf16[512,1536]{1,0:T(8,128)(2,1)S(1)} %convolution_convert_fusion.2), channel_id=1, source_target_pairs={{0,1},{1,0},{2,3},{3,2},{4,5},{5,4},{6,7},{7,6},{8,9},{9,8},{10,11... | collective-permute-start | bytes 4718600 | tf_op jit(solution)/shard_map/ppermute | solution.py:47
  391.3 33.3 %copy-start.57 = (bf16[16,512]{1,0:T(8,128)(2,1)}, bf16[16,512]{1,0:T(8,128)(2,1)S(1)}, u32[]{:S(2)}) copy-start(bf16[16,512]{1,0:T(8,128)(2,1)S(1)} %multiply_convert_fusion.2) | copy-start | bytes 49156
  391.9 33.3 %copy-start.35 = (f32[512,1536]{1,0:T(8,128)S(1)}, f32[512,1536]{1,0:T(8,128)}, u32[]{:S(2)}) copy-start(f32[512,1536]{1,0:T(8,128)} %copy-done.34) | copy-start | bytes 9437188
  391.9 33.3 %copy-start.37 = (bf16[512,1536]{1,0:T(8,128)(2,1)S(1)}, bf16[512,1536]{1,0:T(8,128)(2,1)}, u32[]{:S(2)}) copy-start(bf16[512,1536]{1,0:T(8,128)(2,1)} %param.16) | copy-start | bytes 4718596
  470.1 14.6 %collective-permute-start.11 = (bf16[2,128,512]{2,1,0:T(8,128)(2,1)}, bf16[2,128,512]{2,1,0:T(8,128)(2,1)}, u32[]{:S(2)}, u32[]{:S(2)}) collective-permute-start(bf16[2,128,512]{2,1,0:T(8,128)(2,1)} %get-tuple-element.147), channel_id=1, source_target_pairs={{2,0},{4,2},{6,4},{3,1},{5,3},{7,5},{10,8},{12,10},{14,12},{11,9},... | collective-permute-start | bytes 786440 | tf_op jit(solution)/shard_map/ppermute | solution.py:706
  471.4 13.3 %collective-permute-start.12 = (bf16[2,128,512]{2,1,0:T(8,128)(2,1)}, bf16[2,128,512]{2,1,0:T(8,128)(2,1)}, u32[]{:S(2)}, u32[]{:S(2)}) collective-permute-start(bf16[2,128,512]{2,1,0:T(8,128)(2,1)} %get-tuple-element.148), channel_id=1, source_target_pairs={{4,0},{6,2},{5,1},{7,3},{12,8},{14,10},{13,9},{15,11},{20,16},{22,... | collective-permute-start | bytes 786440 | tf_op jit(solution)/shard_map/ppermute | solution.py:706
  472.7 16.1 %collective-permute-start.13 = (bf16[2,128,512]{2,1,0:T(8,128)(2,1)}, bf16[2,128,512]{2,1,0:T(8,128)(2,1)}, u32[]{:S(2)}, u32[]{:S(2)}) collective-permute-start(bf16[2,128,512]{2,1,0:T(8,128)(2,1)} %get-tuple-element.149), channel_id=1, source_target_pairs={{6,0},{7,1},{14,8},{15,9},{22,16},{23,17},{30,24},{31,25},{38,32},... | collective-permute-start | bytes 786440 | tf_op jit(solution)/shard_map/ppermute | solution.py:706
  475.0 19.8 %collective-permute-start.14 = (bf16[2,384,512]{2,1,0:T(8,128)(2,1)}, bf16[2,384,512]{2,1,0:T(8,128)(2,1)}, u32[]{:S(2)}, u32[]{:S(2)}) collective-permute-start(bf16[2,384,512]{2,1,0:T(8,128)(2,1)} %slice.138), channel_id=1, source_target_pairs={{0,1},{1,0},{2,3},{3,2},{4,5},{5,4},{6,7},{7,6},{8,9},{9,8},{10,11... | collective-permute-start | bytes 2359304 | tf_op jit(solution)/shard_map/ppermute | solution.py:47
  476.7 18.1 %copy-start.58 = (bf16[16,512]{1,0:T(8,128)(2,1)S(1)}, bf16[16,512]{1,0:T(8,128)(2,1)}, u32[]{:S(2)}) copy-start(bf16[16,512]{1,0:T(8,128)(2,1)} %copy-done.57) | copy-start | bytes 49156
  476.7 24.3 %copy-start.63 = (f32[1,1536]{1,0:T(1,128)S(1)}, f32[1,1536]{1,0:T(1,128)}, u32[]{:S(2)}) copy-start(f32[1,1536]{1,0:T(1,128)} %broadcast_in_dim.171) | copy-start | bytes 18436
  476.7 24.3 %copy-start.67 = (f32[8]{0:T(128)S(1)}, f32[8]{0:T(128)}, u32[]{:S(2)}) copy-start(f32[8]{0:T(128)} %pad.11.clone) | copy-start | bytes 100
  476.7 24.3 %copy-start.68 = (f32[8]{0:T(128)S(1)}, f32[8]{0:T(128)}, u32[]{:S(2)}) copy-start(f32[8]{0:T(128)} %pad.10.clone) | copy-start | bytes 100
  476.7 24.3 %copy-start.69 = (f32[8]{0:T(128)S(1)}, f32[8]{0:T(128)}, u32[]{:S(2)}) copy-start(f32[8]{0:T(128)} %pad.9.clone) | copy-start | bytes 100
  495.5 14.7 %collective-permute-start.15 = (bf16[2,128,512]{2,1,0:T(8,128)(2,1)}, bf16[2,128,512]{2,1,0:T(8,128)(2,1)S(1)}, u32[]{:S(2)}, u32[]{:S(2)}) collective-permute-start(bf16[2,128,512]{2,1,0:T(8,128)(2,1)} %get-tuple-element.152), channel_id=1, source_target_pairs={{2,0},{4,2},{6,4},{3,1},{5,3},{7,5},{10,8},{12,10},{14,12},{11,9},... | collective-permute-start | bytes 786440 | tf_op jit(solution)/shard_map/ppermute | solution.py:706
  496.7 13.4 %collective-permute-start.16 = (bf16[2,128,512]{2,1,0:T(8,128)(2,1)}, bf16[2,128,512]{2,1,0:T(8,128)(2,1)S(1)}, u32[]{:S(2)}, u32[]{:S(2)}) collective-permute-start(bf16[2,128,512]{2,1,0:T(8,128)(2,1)} %get-tuple-element.153), channel_id=1, source_target_pairs={{4,0},{6,2},{5,1},{7,3},{12,8},{14,10},{13,9},{15,11},{20,16},{22,... | collective-permute-start | bytes 786440 | tf_op jit(solution)/shard_map/ppermute | solution.py:706
  498.0 18.3 %collective-permute-start.17 = (bf16[2,128,512]{2,1,0:T(8,128)(2,1)}, bf16[2,128,512]{2,1,0:T(8,128)(2,1)S(1)}, u32[]{:S(2)}, u32[]{:S(2)}) collective-permute-start(bf16[2,128,512]{2,1,0:T(8,128)(2,1)} %get-tuple-element.154), channel_id=1, source_target_pairs={{6,0},{7,1},{14,8},{15,9},{22,16},{23,17},{30,24},{31,25},{38,32},... | collective-permute-start | bytes 786440 | tf_op jit(solution)/shard_map/ppermute | solution.py:706
  499.3 17.0 %collective-permute-start.18 = (bf16[384,512]{1,0:T(8,128)(2,1)S(1)}, bf16[384,512]{1,0:T(8,128)(2,1)S(1)}, u32[]{:S(2)}, u32[]{:S(2)}) collective-permute-start(bf16[384,512]{1,0:T(8,128)(2,1)S(1)} %slice_bitcast_fusion.3), channel_id=1, source_target_pairs={{0,1},{1,0},{2,3},{3,2},{4,5},{5,4},{6,7},{7,6},{8,9},{9,8},{10,11... | collective-permute-start | bytes 1179656 | tf_op jit(solution)/shard_map/ppermute | solution.py:47
  501.7 15.9 %copy-start.56 = (bf16[2,128,512]{2,1,0:T(8,128)(2,1)S(1)}, bf16[2,128,512]{2,1,0:T(8,128)(2,1)}, u32[]{:S(2)}) copy-start(bf16[2,128,512]{2,1,0:T(8,128)(2,1)} %get-tuple-element.169) | copy-start | bytes 786436
  516.3 9.9 %collective-permute-start.19 = (bf16[4,4,2,24,1664]{4,3,2,1,0:T(8,128)(2,1)}, bf16[4,4,2,24,1664]{4,3,2,1,0:T(8,128)(2,1)}, u32[]{:S(2)}, u32[]{:S(2)}) collective-permute-start(bf16[4,4,2,24,1664]{4,3,2,1,0:T(8,128)(2,1)} %get-tuple-element.176), channel_id=1, source_target_pairs={{0,8},{8,0},{1,9},{9,1},{2,10},{10,2},{3,11},{11,3},{4,12},{12,4},... | collective-permute-start | bytes 7667720 | tf_op jit(solution)/shard_map/ppermute | solution.py:47
  529.6 6.9 %collective-permute-start.23 = (bf16[4,4,2,24,640]{4,3,2,1,0:T(8,128)(2,1)S(1)}, bf16[4,4,2,24,640]{4,3,2,1,0:T(8,128)(2,1)}, u32[]{:S(2)}, u32[]{:S(2)}) collective-permute-start(bf16[4,4,2,24,640]{4,3,2,1,0:T(8,128)(2,1)S(1)} %get-tuple-element.182), channel_id=1, source_target_pairs={{0,8},{8,0},{1,9},{9,1},{2,10},{10,2},{3,11},{11,3},{4,12},{12,4},... | collective-permute-start | bytes 2949128 | tf_op jit(solution)/shard_map/ppermute | solution.py:47
  530.2 36.6 %collective-permute-start.24 = (bf16[512,1536]{1,0:T(8,128)(2,1)}, bf16[512,1536]{1,0:T(8,128)(2,1)}, u32[]{:S(2)}, u32[]{:S(2)}) collective-permute-start(bf16[512,1536]{1,0:T(8,128)(2,1)} %get-tuple-element.184), channel_id=1, source_target_pairs={{0,1},{1,0},{2,3},{3,2},{4,5},{5,4},{6,7},{7,6},{8,9},{9,8},{10,11... | collective-permute-start | bytes 4718600 | tf_op jit(solution)/shard_map/ppermute | solution.py:47
  530.7 19.8 %collective-permute-start.20 = (bf16[4,2,24,1664]{3,2,1,0:T(8,128)(2,1)}, bf16[4,2,24,1664]{3,2,1,0:T(8,128)(2,1)}, u32[]{:S(2)}, u32[]{:S(2)}) collective-permute-start(bf16[4,2,24,1664]{3,2,1,0:T(8,128)(2,1)} %get-tuple-element.178), channel_id=1, source_target_pairs={{0,16},{16,32},{32,48},{48,0},{1,17},{17,33},{33,49},{49,1},{2,18}... | collective-permute-start | bytes 1916936 | tf_op jit(solution)/shard_map/ppermute | solution.py:530
  532.4 30.7 %collective-permute-start.21 = (bf16[4,2,24,1664]{3,2,1,0:T(8,128)(2,1)}, bf16[4,2,24,1664]{3,2,1,0:T(8,128)(2,1)}, u32[]{:S(2)}, u32[]{:S(2)}) collective-permute-start(bf16[4,2,24,1664]{3,2,1,0:T(8,128)(2,1)} %get-tuple-element.179), channel_id=1, source_target_pairs={{0,32},{16,48},{32,0},{48,16},{1,33},{17,49},{33,1},{49,17},{2,34}... | collective-permute-start | bytes 1916936 | tf_op jit(solution)/shard_map/ppermute | solution.py:530
  535.0 28.0 %collective-permute-start.22 = (bf16[4,2,24,1664]{3,2,1,0:T(8,128)(2,1)}, bf16[4,2,24,1664]{3,2,1,0:T(8,128)(2,1)}, u32[]{:S(2)}, u32[]{:S(2)}) collective-permute-start(bf16[4,2,24,1664]{3,2,1,0:T(8,128)(2,1)} %get-tuple-element.180), channel_id=1, source_target_pairs={{0,48},{16,0},{32,16},{48,32},{1,49},{17,1},{33,17},{49,33},{2,50}... | collective-permute-start | bytes 1916936 | tf_op jit(solution)/shard_map/ppermute | solution.py:530
  538.9 27.9 %all-to-all-start.7 = ((bf16[4,4,2,24,640]{4,3,2,1,0:T(8,128)(2,1)}), bf16[4,4,2,24,640]{4,3,2,1,0:T(8,128)(2,1)S(1)}, u32[]{:S(2)}, u32[]{:S(2)}) async-start(bf16[4,4,2,24,640]{4,3,2,1,0:T(8,128)(2,1)} %add_convert_fusion), calls=%async_computation.8 | async-start | bytes 1966080 | tf_op jit(solution)/shard_map/all_to_all | solution.py:774
  567.0 11.5 %collective-permute-start.28 = (bf16[2,24,640]{2,1,0:T(8,128)(2,1)S(1)}, bf16[2,24,640]{2,1,0:T(8,128)(2,1)S(1)}, u32[]{:S(2)}, u32[]{:S(2)}) collective-permute-start(bf16[2,24,640]{2,1,0:T(8,128)(2,1)S(1)} %get-tuple-element.284), channel_id=1, source_target_pairs={{0,16},{16,32},{32,48},{48,0},{1,17},{17,33},{33,49},{49,1},{2,18}... | collective-permute-start | bytes 184328 | tf_op jit(solution)/shard_map/ppermute | solution.py:83
  568.6 11.5 %collective-permute-start.30 = (bf16[2,24,640]{2,1,0:T(8,128)(2,1)S(1)}, bf16[2,24,640]{2,1,0:T(8,128)(2,1)S(1)}, u32[]{:S(2)}, u32[]{:S(2)}) collective-permute-start(bf16[2,24,640]{2,1,0:T(8,128)(2,1)S(1)} %get-tuple-element.285), channel_id=1, source_target_pairs={{0,48},{16,0},{32,16},{48,32},{1,49},{17,1},{33,17},{49,33},{2,50}... | collective-permute-start | bytes 184328 | tf_op jit(solution)/shard_map/ppermute | solution.py:83
  570.3 9.7 %collective-permute-start.29 = (bf16[2,24,640]{2,1,0:T(8,128)(2,1)S(1)}, bf16[2,24,640]{2,1,0:T(8,128)(2,1)S(1)}, u32[]{:S(2)}, u32[]{:S(2)}) collective-permute-start(bf16[2,24,640]{2,1,0:T(8,128)(2,1)S(1)} %get-tuple-element.286), channel_id=1, source_target_pairs={{0,32},{16,48},{32,0},{48,16},{1,33},{17,49},{33,1},{49,17},{2,34}... | collective-permute-start | bytes 184328 | tf_op jit(solution)/shard_map/ppermute | solution.py:83
  573.9 9.5 %collective-permute-start.25 = (bf16[2,24,1664]{2,1,0:T(8,128)(2,1)S(1)}, bf16[2,24,1664]{2,1,0:T(8,128)(2,1)S(1)}, u32[]{:S(2)}, u32[]{:S(2)}) collective-permute-start(bf16[2,24,1664]{2,1,0:T(8,128)(2,1)S(1)} %get-tuple-element.281), channel_id=1, source_target_pairs={{0,2},{2,4},{4,6},{6,0},{1,3},{3,5},{5,7},{7,1},{8,10},{10,12},{12... | collective-permute-start | bytes 479240 | tf_op jit(solution)/shard_map/ppermute | solution.py:83
  577.9 5.8 collective-permute-start.27
  578.5 7.3 %collective-permute-start.26 = (bf16[2,24,1664]{2,1,0:T(8,128)(2,1)S(1)}, bf16[2,24,1664]{2,1,0:T(8,128)(2,1)S(1)}, u32[]{:S(2)}, u32[]{:S(2)}) collective-permute-start(bf16[2,24,1664]{2,1,0:T(8,128)(2,1)S(1)} %get-tuple-element.283), channel_id=1, source_target_pairs={{0,4},{2,6},{4,0},{6,2},{1,5},{3,7},{5,1},{7,3},{8,12},{10,14},{12... | collective-permute-start | bytes 479240 | tf_op jit(solution)/shard_map/ppermute | solution.py:83
  588.9 7.9 %collective-permute-start.31 = (bf16[24,2304]{1,0:T(8,128)(2,1)S(1)}, bf16[24,2304]{1,0:T(8,128)(2,1)S(1)}, u32[]{:S(2)}, u32[]{:S(2)}) collective-permute-start(bf16[24,2304]{1,0:T(8,128)(2,1)S(1)} %dynamic-slice_bitcast_fusion.3), channel_id=1, source_target_pairs={{0,64},{64,0},{1,65},{65,1},{2,66},{66,2},{3,67},{67,3},{4,68},{68... | collective-permute-start | bytes 331784 | tf_op jit(solution)/shard_map/ppermute | solution.py:83
  599.4 3.9 collective-permute-start.32
  (52 other events, 254.8 us)
Sparse Core Ops, SparseCore 0:
  94.9 90.5 all-gather.2
  369.6 99.1 reduce-scatter.1

commit v7 on v6

--- a/solution.py
+++ b/solution.py
@@ -372,7 +372,7 @@
     return dict(
         grid=(hidden // HALF,),
         scratch_shapes=[pltpu.VMEM((rows, width), F32)],
-        compiler_params=pltpu.CompilerParams(vmem_limit_bytes=40 << 20),
+        compiler_params=pltpu.CompilerParams(vmem_limit_bytes=60 << 20),
         cost_estimate=pl.CostEstimate(
             flops=6 * rows * width * hidden, bytes_accessed=20_000_000, transcendentals=rows * hidden
         ),
@@ -383,6 +383,7 @@
     rows, width = x.shape
     hidden = 2 * experts_full.shape[4]
     common, whole, weights, column = expert_specs(rows, width, hidden)
+    common["compiler_params"] = pltpu.CompilerParams(vmem_limit_bytes=40 << 20)
     wide = jax.ShapeDtypeStruct((rows, hidden), F32)
     return pl.pallas_call(
         experts_kernel,

time: 622 us -> 613 us (0.986)
  local copies, waits for them, and re-layouts: 43 us -> 29.6 us
    unnamed x152 -> x132, local copies, waits for them, and re-layouts: 22.6 us -> 9.01 us
where the time goes in v7:
time: 613 us; the launch traced here: 604 us
  waiting for transfers between devices  286 us (47%)
  starting transfers between devices  81.9 us (13%)
  Pallas kernels  77.9 us (13%)
  other arithmetic  42.7 us (7%)
  blocking collectives  37.4 us (6%)
  local copies, waits for them, and re-layouts  29.6 us (5%)
  matrix products  28.6 us (5%)
  between operations  19.4 us (3%)
    ppermute x14, waiting for transfers between devices, swap(): return lax.ppermute(value, axis, [(0, 1), (1, 0)])  143 us
    all_to_all x3, waiting for transfers between devices, exchange_slots(): lax.all_to_all(rows.reshape(EXPERTS, -1, width), ('h', 'x', 'c'), 0, 0, t...  54.9 us
    all_to_all x1, blocking collectives, exchange_slots(): lax.all_to_all(rows.reshape(EXPERTS, -1, width), ('h', 'x', 'c'), 0, 0, t...  37.4 us
    dot_general x16, matrix products, dot(): lax.dot_general(left, right, (((left_dim,), (right_dim,)), ((), ())), pre...  28.6 us
    reduce_scatter x1, waiting for transfers between devices, local(): grad_experts = lax.psum_scatter(grad_parts, 'y', scatter_dimension=0)  26.1 us
    pallas_call x1, Pallas kernels, run_experts_back(): pl.pallas_call(experts_back_kernel, in_specs=[whole, column, column] + we...  17.1 us
    ppermute x7, starting transfers between devices, axis_parts(): lax.ppermute(block, axis, [(i, (i + r) % size) for i in range(size)])  14.2 us
    pallas_call x2, Pallas kernels, attend_back(): pl.pallas_call(bwd_kernel, grid=(count,), in_specs=[pl.BlockSpec(memory_s...  14 us
  transfers between devices with their start and end apart: 42, of which 22 were waited for; matrix products, arithmetic and copies ran while one was open for 11% of the time, Pallas kernels for 8%

profile of v7, /device:TPU:0, one launch (start us, length us, event | category | flops | bytes accessed | tf_op | source)
XLA Modules:
  0.0 603.7 jit_solution(15087197637093039600)
XLA Ops:
  11.4 7.9 %all-to-all-start = ((bf16[8,24,2176]{2,1,0:T(8,128)(2,1)}), bf16[8,24,2176]{2,1,0:T(8,128)(2,1)S(1)}, u32[]{:S(2)}, u32[]{:S(2)}) async-start(bf16[8,24,2176]{2,1,0:T(8,128)(2,1)} %broadcast_in_dim.149), calls=%async_computation | async-start | bytes 1671168 | tf_op jit(solution)/shard_map/all_to_all | solution.py:56
  20.7 13.6 %all-to-all-done = bf16[8,24,2176]{2,1,0:T(8,128)(2,1)S(1)} async-done(((bf16[8,24,2176]{2,1,0:T(8,128)(2,1)}), bf16[8,24,2176]{2,1,0:T(8,128)(2,1)S(1)}, u32[]{:S(2)}, u32[]{:S(2)}) %all-to-all-start) | async-done | bytes 835616 | tf_op jit(solution)/shard_map/all_to_all | solution.py:56
  35.5 4.3 all-to-all-start.1
  41.0 13.0 %all-to-all-done.1 = bf16[4,8,24,640]{3,2,1,0:T(8,128)(2,1)S(1)} async-done(((bf16[4,8,24,640]{3,2,1,0:T(8,128)(2,1)}), bf16[4,8,24,640]{3,2,1,0:T(8,128)(2,1)S(1)}, u32[]{:S(2)}, u32[]{:S(2)}) %all-to-all-start.1) | async-done | bytes 983072 | tf_op jit(solution)/shard_map/all_to_all | solution.py:61
  57.1 4.5 all-to-all-start.2
  67.5 2.4 collective-permute-start.2
  69.9 2.1 collective-permute-start.1
  72.0 12.8 %collective-permute-done.4 = bf16[3,384,512]{2,1,0:T(8,128)(2,1)} collective-permute-done((bf16[3,384,512]{2,1,0:T(8,128)(2,1)}, bf16[3,384,512]{2,1,0:T(8,128)(2,1)}, u32[]{:S(2)}, u32[]{:S(2)}) %collective-permute-start.4) | collective-permute-done | bytes 1179680 | tf_op jit(solution)/shard_map/ppermute | solution.py:47
  84.8 6.7 %all-to-all-done.2 = bf16[4,8,24,1536]{3,2,1,0:T(8,128)(2,1)} async-done(((bf16[4,8,24,1536]{3,2,1,0:T(8,128)(2,1)}), bf16[4,8,24,1536]{3,2,1,0:T(8,128)(2,1)}, u32[]{:S(2)}, u32[]{:S(2)}) %all-to-all-start.2) | async-done | bytes 2359328 | tf_op jit(solution)/shard_map/all_to_all | solution.py:581
  91.5 3.2 pad_maximum_fusion.1
  97.4 2.3 collective-permute-done.5
  99.7 2.7 select_bitcast_fusion.1
  105.5 4.1 shard_map.246
  111.8 4.8 shard_map.247
  116.6 13.9 %collective-permute-done.6 = bf16[256,1536]{1,0:T(8,128)(2,1)S(1)} collective-permute-done((bf16[256,1536]{1,0:T(8,128)(2,1)S(1)}, bf16[256,1536]{1,0:T(8,128)(2,1)S(1)}, u32[]{:S(2)}, u32[]{:S(2)}) %collective-permute-start.6) | collective-permute-done | bytes 786464 | tf_op jit(solution)/shard_map/ppermute | solution.py:47
  132.5 17.8 %collective-permute-done.7 = bf16[256,1536]{1,0:T(8,128)(2,1)S(1)} collective-permute-done((bf16[256,1536]{1,0:T(8,128)(2,1)S(1)}, bf16[256,1536]{1,0:T(8,128)(2,1)S(1)}, u32[]{:S(2)}, u32[]{:S(2)}) %collective-permute-start.7) | collective-permute-done | bytes 786464 | tf_op jit(solution)/shard_map/ppermute | solution.py:47
  153.5 2.8 convolution_convert_fusion.1
  156.3 3.9 all-to-all-start.3
  162.6 29.6 %all-to-all-done.3 = bf16[16,48,1536]{2,1,0:T(8,128)(2,1)S(1)} async-done(((bf16[16,48,1536]{2,1,0:T(8,128)(2,1)}), bf16[16,48,1536]{2,1,0:T(8,128)(2,1)S(1)}, u32[]{:S(2)}, u32[]{:S(2)}) %all-to-all-start.3) | async-done | bytes 2359328 | tf_op jit(solution)/shard_map/all_to_all | solution.py:96
  192.2 12.1 %shard_map.248 = (f32[768,1024]{1,0:T(8,128)S(1)}, f32[768,1024]{1,0:T(8,128)S(1)}, bf16[768,1024]{1,0:T(8,128)(2,1)S(1)}, bf16[768,1536]{1,0:T(8,128)(2,1)S(1)}) custom-call(bf16[768,1536]{1,0:T(8,128)(2,1)S(1)} %bitcast.135, bf16[4,2,3,384,512]{4,3,2,1,0:T(8,128)(2,1)} %bitcast.147, bf16[4,2,3,384,512]{4,3,2,1,0:T(8,128)(2,1)} %bitcast.148, ...), custom_call_target="tpu_custom_call" | custom-call | flops 7247757312 | bytes 20000000 | tf_op jit(solution)/shard_map/pallas_call | solution.py:388
  205.9 37.4 %all_to_all.40 = bf16[16,48,1536]{2,1,0:T(8,128)(2,1)S(1)} all-to-all(bf16[16,48,1536]{2,1,0:T(8,128)(2,1)S(1)} %bitcast.137), channel_id=1, replica_groups=mesh['h'=2,'x'=4,'c'=2,'y'=4,'t'=2] {'h','x','c'}, dimensions={0} | all-to-all | bytes 4718592 | tf_op jit(solution)/shard_map/all_to_all | solution.py:96
  246.0 35.2 %collective-permute-done.8 = bf16[512,1536]{1,0:T(8,128)(2,1)S(1)} collective-permute-done((bf16[512,1536]{1,0:T(8,128)(2,1)S(1)}, bf16[512,1536]{1,0:T(8,128)(2,1)S(1)}, u32[]{:S(2)}, u32[]{:S(2)}) %collective-permute-start.8) | collective-permute-done | bytes 1572896 | tf_op jit(solution)/shard_map/ppermute | solution.py:47
  281.2 1.9 fusion.7
  284.8 2.8 convolution_convert_fusion
  287.6 4.5 all-to-all-start.5
  292.1 3.8 select_reduce_fusion.1
  296.8 20.2 %collective-permute-done.9 = f32[2,512]{1,0:T(2,128)S(1)} collective-permute-done((f32[2,512]{1,0:T(2,128)S(1)}, f32[2,512]{1,0:T(2,128)S(1)}, u32[]{:S(2)}, u32[]{:S(2)}) %collective-permute-start.9) | collective-permute-done | bytes 4128 | tf_op jit(solution)/shard_map/ppermute | solution.py:47
  317.0 7.2 %all-to-all-done.5 = bf16[16,48,1536]{2,1,0:T(8,128)(2,1)} async-done(((bf16[16,48,1536]{2,1,0:T(8,128)(2,1)}), bf16[16,48,1536]{2,1,0:T(8,128)(2,1)}, u32[]{:S(2)}, u32[]{:S(2)}) %all-to-all-start.5) | async-done | bytes 2359328 | tf_op jit(solution)/shard_map/all_to_all | solution.py:96
  324.1 17.1 %shard_map.249 = (bf16[768,1024]{1,0:T(8,128)(2,1)}, bf16[768,1024]{1,0:T(8,128)(2,1)}, bf16[768,1536]{1,0:T(8,128)(2,1)}) custom-call(bf16[768,1536]{1,0:T(8,128)(2,1)} %bitcast.50.d_ref, f32[768,1024]{1,0:T(8,128)} %copy-done.1, f32[768,1024]{1,0:T(8,128)} %copy-done.2, bf16[4,2,3,384,512]{4,3,2,1,0:T(8,128)(2,1)} %bitcast.150, ...), custom_call_target="tpu_custom_call" | custom-call | flops 7247757312 | bytes 20000000 | tf_op jit(solution)/shard_map/pallas_call | solution.py:408
  341.3 5.5 all-to-all-start.6
  346.9 13.9 %shard_map.250 = bf16[4,2,3,384,512]{4,3,2,1,0:T(8,128)(2,1)} custom-call(bf16[768,1536]{1,0:T(8,128)(2,1)} %bitcast.136, bf16[768,1536]{1,0:T(8,128)(2,1)} %bitcast.50.d_ref, bf16[768,1024]{1,0:T(8,128)(2,1)} %get-tuple-element.129.dg_ref, bf16[768,1024]{1,0:T(8,128)(2,1)} %get-tuple-element.130.du_ref, bf16[768,1024]{1,0:T(8,128)(2,1)} %copy-done.7), custom_call_target="tpu_custom_call" | custom-call | flops 7247757312 | bytes 20000000 | tf_op jit(solution)/shard_map/pallas_call | solution.py:422
  360.8 18.1 %all-to-all-done.6 = bf16[16,48,1536]{2,1,0:T(8,128)(2,1)} async-done(((bf16[16,48,1536]{2,1,0:T(8,128)(2,1)}), bf16[16,48,1536]{2,1,0:T(8,128)(2,1)}, u32[]{:S(2)}, u32[]{:S(2)}) %all-to-all-start.6) | async-done | bytes 2359328 | tf_op jit(solution)/shard_map/all_to_all | solution.py:96
  378.9 4.1 convolution_convert_fusion.2
  388.0 31.4 %collective-permute-done.10 = bf16[512,1536]{1,0:T(8,128)(2,1)S(1)} collective-permute-done((bf16[512,1536]{1,0:T(8,128)(2,1)S(1)}, bf16[512,1536]{1,0:T(8,128)(2,1)S(1)}, u32[]{:S(2)}, u32[]{:S(2)}) %collective-permute-start.10) | collective-permute-done | bytes 1572896 | tf_op jit(solution)/shard_map/ppermute | solution.py:47
  421.2 3.4 fusion.73
  424.6 2.3 fusion.24.d_ref
  426.9 7.0 %shard_map.251 = (bf16[384,512]{1,0:T(8,128)(2,1)}, bf16[2,128,512]{2,1,0:T(8,128)(2,1)}, bf16[2,128,512]{2,1,0:T(8,128)(2,1)}, bf16[2,128,512]{2,1,0:T(8,128)(2,1)}, bf16[2,128,512]{2,1,0:T(8,128)(2,1)}) custom-call(s32[1]{0:T(128)} %bitcast.y_ref, bf16[768,512]{1,0:T(8,128)(2,1)} %copy-done.15, bf16[768,512]{1,0:T(8,128)(2,1)} %fusion.24.d_ref, ...), custom_call_target="tpu_custom_call" | custom-call | flops 149999992832 | bytes 6000000 | tf_op jit(solution)/shard_map/pallas_call | solution.py:273
  433.9 26.1 %reduce-scatter.2.cloned.1.call-done = bf16[1,2,3,384,512]{4,3,2,1,0:T(8,128)(2,1)} async-done(((bf16[4,2,3,384,512]{4,3,2,1,0:T(8,128)(2,1)}), bf16[1,2,3,384,512]{4,3,2,1,0:T(8,128)(2,1)}) %reduce-scatter.2.cloned.1.call-update) | async-done | bytes 2359312 | tf_op jit(solution)/shard_map/reduce_scatter | solution.py:683
  466.2 1.7 collective-permute-start.14
  468.0 7.0 %shard_map.252 = (bf16[384,512]{1,0:T(8,128)(2,1)}, bf16[2,128,512]{2,1,0:T(8,128)(2,1)}, bf16[2,128,512]{2,1,0:T(8,128)(2,1)}, bf16[2,128,512]{2,1,0:T(8,128)(2,1)}, bf16[2,128,512]{2,1,0:T(8,128)(2,1)}) custom-call(s32[1]{0:T(128)} %bitcast.y_ref, bf16[768,512]{1,0:T(8,128)(2,1)} %copy-done.15, bf16[768,512]{1,0:T(8,128)(2,1)} %fusion.24.d_ref, ...), custom_call_target="tpu_custom_call" | custom-call | flops 149999992832 | bytes 6000000 | tf_op jit(solution)/shard_map/pallas_call | solution.py:273
  476.0 4.1 collective-permute-done.13
  480.1 5.9 collective-permute-done.14
  490.6 1.7 collective-permute-start.18
  493.0 8.4 %shard_map.253 = (bf16[4,4,2,24,1664]{4,3,2,1,0:T(8,128)(2,1)}, bf16[4,4,2,24,1664]{4,3,2,1,0:T(8,128)(2,1)}) custom-call(s32[1]{0:T(128)} %bitcast.55.core_ref, bf16[512,1536]{1,0:T(8,128)(2,1)} %copy-done.37, bf16[512,1536]{1,0:T(8,128)(2,1)} %copy-done.3, bf16[512,1536]{1,0:T(8,128)(2,1)} %copy-done.31, f32[8,1536]{1,0:T(8,128)} %maximum_maximum_fusion.refs_3_, ...), custom_call_target="tpu_custom_call" | custom-call | flops 20000000000 | bytes 10000000 | tf_op jit(solution)/shard_map/pallas_call | solution.py:484
  501.4 6.3 %collective-permute-done.17 = bf16[2,128,512]{2,1,0:T(8,128)(2,1)S(1)} collective-permute-done((bf16[2,128,512]{2,1,0:T(8,128)(2,1)}, bf16[2,128,512]{2,1,0:T(8,128)(2,1)S(1)}, u32[]{:S(2)}, u32[]{:S(2)}) %collective-permute-start.17) | collective-permute-done | bytes 262176 | tf_op jit(solution)/shard_map/ppermute | solution.py:707
  509.2 3.3 fusion.12
  512.5 2.6 fusion.10
  515.2 2.4 shard_map.254
  517.6 3.4 fusion.50
  522.0 1.7 collective-permute-start.20
  523.7 2.7 collective-permute-start.21
  527.9 2.4 add_convert_fusion
  530.3 6.4 %all-to-all-start.7 = ((bf16[4,4,2,24,640]{4,3,2,1,0:T(8,128)(2,1)}), bf16[4,4,2,24,640]{4,3,2,1,0:T(8,128)(2,1)S(1)}, u32[]{:S(2)}, u32[]{:S(2)}) async-start(bf16[4,4,2,24,640]{4,3,2,1,0:T(8,128)(2,1)} %add_convert_fusion), calls=%async_computation.8 | async-start | bytes 1966080 | tf_op jit(solution)/shard_map/all_to_all | solution.py:775
  541.8 12.6 %collective-permute-done.21 = bf16[4,2,24,1664]{3,2,1,0:T(8,128)(2,1)} collective-permute-done((bf16[4,2,24,1664]{3,2,1,0:T(8,128)(2,1)}, bf16[4,2,24,1664]{3,2,1,0:T(8,128)(2,1)}, u32[]{:S(2)}, u32[]{:S(2)}) %collective-permute-start.21) | collective-permute-done | bytes 639008 | tf_op jit(solution)/shard_map/ppermute | solution.py:531
  554.4 3.8 collective-permute-done.24
  560.0 1.8 collective-permute-start.30
  561.7 1.8 collective-permute-start.29
  563.5 1.8 add_convert_fusion.3
  565.3 4.0 collective-permute-start.25
  571.5 3.3 collective-permute-done.25
  575.1 2.1 collective-permute-done.26
  577.4 2.9 fusion.11
  580.3 3.0 collective-permute-start.31
  583.2 4.8 fusion.6
  (270 shorter events, 76.4 us)
Async XLA Ops:
  11.4 22.8 %all-to-all-start = ((bf16[8,24,2176]{2,1,0:T(8,128)(2,1)}), bf16[8,24,2176]{2,1,0:T(8,128)(2,1)S(1)}, u32[]{:S(2)}, u32[]{:S(2)}) async-start(bf16[8,24,2176]{2,1,0:T(8,128)(2,1)} %broadcast_in_dim.149), calls=%async_computation | async-start | bytes 1671168 | tf_op jit(solution)/shard_map/all_to_all | solution.py:56
  35.5 18.5 %all-to-all-start.1 = ((bf16[4,8,24,640]{3,2,1,0:T(8,128)(2,1)}), bf16[4,8,24,640]{3,2,1,0:T(8,128)(2,1)S(1)}, u32[]{:S(2)}, u32[]{:S(2)}) async-start(bf16[4,8,24,640]{3,2,1,0:T(8,128)(2,1)} %broadcast_in_dim.150), calls=%async_computation.1 | async-start | bytes 1966080 | tf_op jit(solution)/shard_map/all_to_all | solution.py:61
  39.8 15.8 %copy-start.20 = (bf16[512,1536]{1,0:T(8,128)(2,1)S(1)}, bf16[512,1536]{1,0:T(8,128)(2,1)}, u32[]{:S(2)}) copy-start(bf16[512,1536]{1,0:T(8,128)(2,1)} %param.15) | copy-start | bytes 4718596
  55.6 6.1 %collective-permute-start = (bf16[4,2,96,640]{3,2,1,0:T(8,128)(2,1)S(1)}, bf16[4,2,96,640]{3,2,1,0:T(8,128)(2,1)}, u32[]{:S(2)}, u32[]{:S(2)}) collective-permute-start(bf16[4,2,96,640]{3,2,1,0:T(8,128)(2,1)S(1)} %bitcast.163), channel_id=1, source_target_pairs={{0,8},{8,0},{1,9},{9,1},{2,10},{10,2},{3,11},{11,3},{4,12},{12,4},... | collective-permute-start | bytes 2949128 | tf_op jit(solution)/shard_map/ppermute | solution.py:47
  56.0 28.8 %collective-permute-start.4 = (bf16[3,384,512]{2,1,0:T(8,128)(2,1)}, bf16[3,384,512]{2,1,0:T(8,128)(2,1)}, u32[]{:S(2)}, u32[]{:S(2)}) collective-permute-start(bf16[3,384,512]{2,1,0:T(8,128)(2,1)} %pad_maximum_fusion.3), channel_id=1, source_target_pairs={{0,1},{1,0},{2,3},{3,2},{4,5},{5,4},{6,7},{7,6},{8,9},{9,8},{10,11... | collective-permute-start | bytes 3538952 | tf_op jit(solution)/shard_map/ppermute | solution.py:47
  57.1 34.4 %all-to-all-start.2 = ((bf16[4,8,24,1536]{3,2,1,0:T(8,128)(2,1)}), bf16[4,8,24,1536]{3,2,1,0:T(8,128)(2,1)}, u32[]{:S(2)}, u32[]{:S(2)}) async-start(bf16[4,8,24,1536]{3,2,1,0:T(8,128)(2,1)} %broadcast_in_dim.151), calls=%async_computation.2 | async-start | bytes 4718592 | tf_op jit(solution)/shard_map/all_to_all | solution.py:581
  61.6 130.6 %all-gather.3.cloned.1.call-start = ((), (), s32[]{:S(2)}) async-start(), calls=%async_computation.10 | async-start | bytes 11796480 | tf_op jit(solution)/shard_map/all_gather | solution.py:607
  65.1 38.2 %copy-start.3 = (bf16[512,1536]{1,0:T(8,128)(2,1)}, bf16[512,1536]{1,0:T(8,128)(2,1)S(1)}, u32[]{:S(2)}) copy-start(bf16[512,1536]{1,0:T(8,128)(2,1)S(1)} %fusion.2.refs_1_.refs_0_) | copy-start | bytes 4718596
  66.2 45.6 %copy-start.8 = (bf16[512,512]{1,0:T(8,128)(2,1)}, bf16[512,512]{1,0:T(8,128)(2,1)S(1)}, u32[]{:S(2)}) copy-start(bf16[512,512]{1,0:T(8,128)(2,1)S(1)} %fusion.33) | copy-start | bytes 1572868
  66.2 28.5 %collective-permute-start.3 = (bf16[2,256,512]{2,1,0:T(8,128)(2,1)S(1)}, bf16[2,256,512]{2,1,0:T(8,128)(2,1)S(1)}, u32[]{:S(2)}, u32[]{:S(2)}) collective-permute-start(bf16[2,256,512]{2,1,0:T(8,128)(2,1)S(1)} %bitcast.140), channel_id=1, source_target_pairs={{0,6},{1,7},{8,14},{9,15},{16,22},{17,23},{24,30},{25,31},{32,38},... | collective-permute-start | bytes 1572872 | tf_op jit(solution)/shard_map/ppermute | solution.py:595
  67.5 27.2 %collective-permute-start.2 = (bf16[2,256,512]{2,1,0:T(8,128)(2,1)S(1)}, bf16[2,256,512]{2,1,0:T(8,128)(2,1)S(1)}, u32[]{:S(2)}, u32[]{:S(2)}) collective-permute-start(bf16[2,256,512]{2,1,0:T(8,128)(2,1)S(1)} %bitcast.141), channel_id=1, source_target_pairs={{0,4},{2,6},{1,5},{3,7},{8,12},{10,14},{9,13},{11,15},{16,20},{18,... | collective-permute-start | bytes 1572872 | tf_op jit(solution)/shard_map/ppermute | solution.py:595
  69.9 24.8 %collective-permute-start.1 = (bf16[2,256,512]{2,1,0:T(8,128)(2,1)S(1)}, bf16[2,256,512]{2,1,0:T(8,128)(2,1)}, u32[]{:S(2)}, u32[]{:S(2)}) collective-permute-start(bf16[2,256,512]{2,1,0:T(8,128)(2,1)S(1)} %bitcast.142), channel_id=1, source_target_pairs={{0,2},{2,4},{4,6},{1,3},{3,5},{5,7},{8,10},{10,12},{12,14},{9,11},... | collective-permute-start | bytes 1572872 | tf_op jit(solution)/shard_map/ppermute | solution.py:595
  94.8 5.0 collective-permute-start.5
  97.4 148.6 %copy-start.6 = (s32[1,512]{1,0:T(1,128)}, s32[1,512]{1,0:T(1,128)S(1)}, u32[]{:S(2)}) copy-start(s32[1,512]{1,0:T(1,128)S(1)} %get-tuple-element.264.seg_q) | copy-start | bytes 6148
  103.3 27.1 %copy-start.33 = (bf16[2,4,2,96,1536]{4,3,2,1,0:T(8,128)(2,1)}, bf16[2,4,2,96,1536]{4,3,2,1,0:T(8,128)(2,1)S(1)}, u32[]{:S(2)}) copy-start(bf16[2,4,2,96,1536]{4,3,2,1,0:T(8,128)(2,1)S(1)} %copy.66) | copy-start | bytes 14155780
  110.5 19.9 %collective-permute-start.6 = (bf16[256,1536]{1,0:T(8,128)(2,1)S(1)}, bf16[256,1536]{1,0:T(8,128)(2,1)S(1)}, u32[]{:S(2)}, u32[]{:S(2)}) collective-permute-start(bf16[256,1536]{1,0:T(8,128)(2,1)S(1)} %convolution_convert_fusion.5), channel_id=1, source_target_pairs={{0,1},{1,0},{2,3},{3,2},{4,5},{5,4},{6,7},{7,6},{8,9},{9,8},{10,11... | collective-permute-start | bytes 2359304 | tf_op jit(solution)/shard_map/ppermute | solution.py:47
  116.6 15.7 %copy-start.55 = (s32[512,2]{0,1:T(2,128)S(1)}, s32[512,2]{0,1:T(2,128)}, u32[]{:S(2)}) copy-start(s32[512,2]{0,1:T(2,128)} %param.18) | copy-start | bytes 12292
  131.3 19.0 %collective-permute-start.7 = (bf16[256,1536]{1,0:T(8,128)(2,1)S(1)}, bf16[256,1536]{1,0:T(8,128)(2,1)S(1)}, u32[]{:S(2)}, u32[]{:S(2)}) collective-permute-start(bf16[256,1536]{1,0:T(8,128)(2,1)S(1)} %convolution_convert_fusion.4), channel_id=1, source_target_pairs={{0,1},{1,0},{2,3},{3,2},{4,5},{5,4},{6,7},{7,6},{8,9},{9,8},{10,11... | collective-permute-start | bytes 2359304 | tf_op jit(solution)/shard_map/ppermute | solution.py:47
  132.5 18.0 %copy-start.21 = (bf16[512,1536]{1,0:T(8,128)(2,1)S(1)}, bf16[512,1536]{1,0:T(8,128)(2,1)}, u32[]{:S(2)}) copy-start(bf16[512,1536]{1,0:T(8,128)(2,1)} %param.15) | copy-start | bytes 4718596
  156.3 35.9 %all-to-all-start.3 = ((bf16[16,48,1536]{2,1,0:T(8,128)(2,1)}), bf16[16,48,1536]{2,1,0:T(8,128)(2,1)S(1)}, u32[]{:S(2)}, u32[]{:S(2)}) async-start(bf16[16,48,1536]{2,1,0:T(8,128)(2,1)} %bitcast.169), calls=%async_computation.3 | async-start | bytes 4718592 | tf_op jit(solution)/shard_map/all_to_all | solution.py:96
  205.9 37.4 %copy-start.1 = (f32[768,1024]{1,0:T(8,128)}, f32[768,1024]{1,0:T(8,128)S(1)}, u32[]{:S(2)}) copy-start(f32[768,1024]{1,0:T(8,128)S(1)} %get-tuple-element.124.g_ref) | copy-start | bytes 9437188
  205.9 37.4 %copy-start.7 = (bf16[768,1024]{1,0:T(8,128)(2,1)}, bf16[768,1024]{1,0:T(8,128)(2,1)S(1)}, u32[]{:S(2)}) copy-start(bf16[768,1024]{1,0:T(8,128)(2,1)S(1)} %get-tuple-element.131.inner_ref) | copy-start | bytes 4718596
  205.9 37.4 %copy-start.41 = (bf16[512,768]{1,0:T(8,128)(2,1)S(1)}, bf16[512,768]{1,0:T(8,128)(2,1)}, u32[]{:S(2)}) copy-start(bf16[512,768]{1,0:T(8,128)(2,1)} %add_convert_fusion.2) | copy-start | bytes 2359300
  243.3 37.9 %copy-start.19 = (f32[512,1536]{1,0:T(8,128)S(1)}, f32[512,1536]{1,0:T(8,128)}, u32[]{:S(2)}) copy-start(f32[512,1536]{1,0:T(8,128)} %copy-done.18) | copy-start | bytes 9437188
  243.3 37.9 %copy-start.26 = (bf16[512,1536]{1,0:T(8,128)(2,1)S(1)}, bf16[512,1536]{1,0:T(8,128)(2,1)}, u32[]{:S(2)}) copy-start(bf16[512,1536]{1,0:T(8,128)(2,1)} %param.16) | copy-start | bytes 4718596
  244.7 36.5 %collective-permute-start.8 = (bf16[512,1536]{1,0:T(8,128)(2,1)S(1)}, bf16[512,1536]{1,0:T(8,128)(2,1)S(1)}, u32[]{:S(2)}, u32[]{:S(2)}) collective-permute-start(bf16[512,1536]{1,0:T(8,128)(2,1)S(1)} %convolution_convert_fusion.3), channel_id=1, source_target_pairs={{0,1},{1,0},{2,3},{3,2},{4,5},{5,4},{6,7},{7,6},{8,9},{9,8},{10,11... | collective-permute-start | bytes 4718600 | tf_op jit(solution)/shard_map/ppermute | solution.py:47
  287.6 36.5 %all-to-all-start.5 = ((bf16[16,48,1536]{2,1,0:T(8,128)(2,1)}), bf16[16,48,1536]{2,1,0:T(8,128)(2,1)}, u32[]{:S(2)}, u32[]{:S(2)}) async-start(bf16[16,48,1536]{2,1,0:T(8,128)(2,1)} %bitcast.168), calls=%async_computation.5 | async-start | bytes 4718592 | tf_op jit(solution)/shard_map/all_to_all | solution.py:96
  295.9 21.1 %collective-permute-start.9 = (f32[2,512]{1,0:T(2,128)S(1)}, f32[2,512]{1,0:T(2,128)S(1)}, u32[]{:S(2)}, u32[]{:S(2)}) collective-permute-start(f32[2,512]{1,0:T(2,128)S(1)} %pad_maximum_fusion.6), channel_id=1, source_target_pairs={{0,1},{1,0},{2,3},{3,2},{4,5},{5,4},{6,7},{7,6},{8,9},{9,8},{10,11... | collective-permute-start | bytes 12296 | tf_op jit(solution)/shard_map/ppermute | solution.py:47
  341.3 37.6 %all-to-all-start.6 = ((bf16[16,48,1536]{2,1,0:T(8,128)(2,1)}), bf16[16,48,1536]{2,1,0:T(8,128)(2,1)}, u32[]{:S(2)}, u32[]{:S(2)}) async-start(bf16[16,48,1536]{2,1,0:T(8,128)(2,1)} %bitcast.167), calls=%async_computation.6 | async-start | bytes 4718592 | tf_op jit(solution)/shard_map/all_to_all | solution.py:96
  346.8 113.2 %reduce-scatter.2.cloned.1.call-start = ((), (), s32[]{:S(2)}) async-start(), calls=%async_computation.9 | async-start | bytes 11796480 | tf_op jit(solution)/shard_map/reduce_scatter | solution.py:683
  383.0 36.4 %collective-permute-start.10 = (bf16[512,1536]{1,0:T(8,128)(2,1)S(1)}, bf16[512,1536]{1,0:T(8,128)(2,1)S(1)}, u32[]{:S(2)}, u32[]{:S(2)}) collective-permute-start(bf16[512,1536]{1,0:T(8,128)(2,1)S(1)} %convolution_convert_fusion.2), channel_id=1, source_target_pairs={{0,1},{1,0},{2,3},{3,2},{4,5},{5,4},{6,7},{7,6},{8,9},{9,8},{10,11... | collective-permute-start | bytes 4718600 | tf_op jit(solution)/shard_map/ppermute | solution.py:47
  388.0 33.2 %copy-start.25 = (f32[512,1536]{1,0:T(8,128)S(1)}, f32[512,1536]{1,0:T(8,128)}, u32[]{:S(2)}) copy-start(f32[512,1536]{1,0:T(8,128)} %copy-done.24) | copy-start | bytes 9437188
  388.0 33.2 %copy-start.27 = (bf16[512,1536]{1,0:T(8,128)(2,1)S(1)}, bf16[512,1536]{1,0:T(8,128)(2,1)}, u32[]{:S(2)}) copy-start(bf16[512,1536]{1,0:T(8,128)(2,1)} %param.16) | copy-start | bytes 4718596
  461.4 14.6 %collective-permute-start.11 = (bf16[2,128,512]{2,1,0:T(8,128)(2,1)}, bf16[2,128,512]{2,1,0:T(8,128)(2,1)}, u32[]{:S(2)}, u32[]{:S(2)}) collective-permute-start(bf16[2,128,512]{2,1,0:T(8,128)(2,1)} %get-tuple-element.147), channel_id=1, source_target_pairs={{2,0},{4,2},{6,4},{3,1},{5,3},{7,5},{10,8},{12,10},{14,12},{11,9},... | collective-permute-start | bytes 786440 | tf_op jit(solution)/shard_map/ppermute | solution.py:707
  462.7 13.4 %collective-permute-start.12 = (bf16[2,128,512]{2,1,0:T(8,128)(2,1)}, bf16[2,128,512]{2,1,0:T(8,128)(2,1)}, u32[]{:S(2)}, u32[]{:S(2)}) collective-permute-start(bf16[2,128,512]{2,1,0:T(8,128)(2,1)} %get-tuple-element.148), channel_id=1, source_target_pairs={{4,0},{6,2},{5,1},{7,3},{12,8},{14,10},{13,9},{15,11},{20,16},{22,... | collective-permute-start | bytes 786440 | tf_op jit(solution)/shard_map/ppermute | solution.py:707
  464.0 16.1 %collective-permute-start.13 = (bf16[2,128,512]{2,1,0:T(8,128)(2,1)}, bf16[2,128,512]{2,1,0:T(8,128)(2,1)}, u32[]{:S(2)}, u32[]{:S(2)}) collective-permute-start(bf16[2,128,512]{2,1,0:T(8,128)(2,1)} %get-tuple-element.149), channel_id=1, source_target_pairs={{6,0},{7,1},{14,8},{15,9},{22,16},{23,17},{30,24},{31,25},{38,32},... | collective-permute-start | bytes 786440 | tf_op jit(solution)/shard_map/ppermute | solution.py:707
  466.2 19.8 %collective-permute-start.14 = (bf16[2,384,512]{2,1,0:T(8,128)(2,1)}, bf16[2,384,512]{2,1,0:T(8,128)(2,1)}, u32[]{:S(2)}, u32[]{:S(2)}) collective-permute-start(bf16[2,384,512]{2,1,0:T(8,128)(2,1)} %slice.138), channel_id=1, source_target_pairs={{0,1},{1,0},{2,3},{3,2},{4,5},{5,4},{6,7},{7,6},{8,9},{9,8},{10,11... | collective-permute-start | bytes 2359304 | tf_op jit(solution)/shard_map/ppermute | solution.py:47
  467.9 18.1 %copy-start.48 = (bf16[16,512]{1,0:T(8,128)(2,1)S(1)}, bf16[16,512]{1,0:T(8,128)(2,1)}, u32[]{:S(2)}) copy-start(bf16[16,512]{1,0:T(8,128)(2,1)} %copy-done.47) | copy-start | bytes 49156
  467.9 24.3 %copy-start.53 = (f32[1,1536]{1,0:T(1,128)S(1)}, f32[1,1536]{1,0:T(1,128)}, u32[]{:S(2)}) copy-start(f32[1,1536]{1,0:T(1,128)} %broadcast_in_dim.171) | copy-start | bytes 18436
  467.9 24.3 %copy-start.57 = (f32[8]{0:T(128)S(1)}, f32[8]{0:T(128)}, u32[]{:S(2)}) copy-start(f32[8]{0:T(128)} %pad.11.clone) | copy-start | bytes 100
  467.9 24.3 %copy-start.58 = (f32[8]{0:T(128)S(1)}, f32[8]{0:T(128)}, u32[]{:S(2)}) copy-start(f32[8]{0:T(128)} %pad.10.clone) | copy-start | bytes 100
  467.9 24.3 %copy-start.59 = (f32[8]{0:T(128)S(1)}, f32[8]{0:T(128)}, u32[]{:S(2)}) copy-start(f32[8]{0:T(128)} %pad.9.clone) | copy-start | bytes 100
  486.7 14.7 %collective-permute-start.15 = (bf16[2,128,512]{2,1,0:T(8,128)(2,1)}, bf16[2,128,512]{2,1,0:T(8,128)(2,1)S(1)}, u32[]{:S(2)}, u32[]{:S(2)}) collective-permute-start(bf16[2,128,512]{2,1,0:T(8,128)(2,1)} %get-tuple-element.152), channel_id=1, source_target_pairs={{2,0},{4,2},{6,4},{3,1},{5,3},{7,5},{10,8},{12,10},{14,12},{11,9},... | collective-permute-start | bytes 786440 | tf_op jit(solution)/shard_map/ppermute | solution.py:707
  488.0 13.4 %collective-permute-start.16 = (bf16[2,128,512]{2,1,0:T(8,128)(2,1)}, bf16[2,128,512]{2,1,0:T(8,128)(2,1)S(1)}, u32[]{:S(2)}, u32[]{:S(2)}) collective-permute-start(bf16[2,128,512]{2,1,0:T(8,128)(2,1)} %get-tuple-element.153), channel_id=1, source_target_pairs={{4,0},{6,2},{5,1},{7,3},{12,8},{14,10},{13,9},{15,11},{20,16},{22,... | collective-permute-start | bytes 786440 | tf_op jit(solution)/shard_map/ppermute | solution.py:707
  489.3 18.4 %collective-permute-start.17 = (bf16[2,128,512]{2,1,0:T(8,128)(2,1)}, bf16[2,128,512]{2,1,0:T(8,128)(2,1)S(1)}, u32[]{:S(2)}, u32[]{:S(2)}) collective-permute-start(bf16[2,128,512]{2,1,0:T(8,128)(2,1)} %get-tuple-element.154), channel_id=1, source_target_pairs={{6,0},{7,1},{14,8},{15,9},{22,16},{23,17},{30,24},{31,25},{38,32},... | collective-permute-start | bytes 786440 | tf_op jit(solution)/shard_map/ppermute | solution.py:707
  490.6 17.1 %collective-permute-start.18 = (bf16[384,512]{1,0:T(8,128)(2,1)S(1)}, bf16[384,512]{1,0:T(8,128)(2,1)S(1)}, u32[]{:S(2)}, u32[]{:S(2)}) collective-permute-start(bf16[384,512]{1,0:T(8,128)(2,1)S(1)} %slice_bitcast_fusion.3), channel_id=1, source_target_pairs={{0,1},{1,0},{2,3},{3,2},{4,5},{5,4},{6,7},{7,6},{8,9},{9,8},{10,11... | collective-permute-start | bytes 1179656 | tf_op jit(solution)/shard_map/ppermute | solution.py:47
  493.0 16.0 %copy-start.46 = (bf16[2,128,512]{2,1,0:T(8,128)(2,1)S(1)}, bf16[2,128,512]{2,1,0:T(8,128)(2,1)}, u32[]{:S(2)}) copy-start(bf16[2,128,512]{2,1,0:T(8,128)(2,1)} %get-tuple-element.169) | copy-start | bytes 786436
  507.7 9.9 %collective-permute-start.19 = (bf16[4,4,2,24,1664]{4,3,2,1,0:T(8,128)(2,1)}, bf16[4,4,2,24,1664]{4,3,2,1,0:T(8,128)(2,1)}, u32[]{:S(2)}, u32[]{:S(2)}) collective-permute-start(bf16[4,4,2,24,1664]{4,3,2,1,0:T(8,128)(2,1)} %get-tuple-element.176), channel_id=1, source_target_pairs={{0,8},{8,0},{1,9},{9,1},{2,10},{10,2},{3,11},{11,3},{4,12},{12,4},... | collective-permute-start | bytes 7667720 | tf_op jit(solution)/shard_map/ppermute | solution.py:47
  521.0 6.9 %collective-permute-start.23 = (bf16[4,4,2,24,640]{4,3,2,1,0:T(8,128)(2,1)S(1)}, bf16[4,4,2,24,640]{4,3,2,1,0:T(8,128)(2,1)}, u32[]{:S(2)}, u32[]{:S(2)}) collective-permute-start(bf16[4,4,2,24,640]{4,3,2,1,0:T(8,128)(2,1)S(1)} %get-tuple-element.182), channel_id=1, source_target_pairs={{0,8},{8,0},{1,9},{9,1},{2,10},{10,2},{3,11},{11,3},{4,12},{12,4},... | collective-permute-start | bytes 2949128 | tf_op jit(solution)/shard_map/ppermute | solution.py:47
  521.6 36.6 %collective-permute-start.24 = (bf16[512,1536]{1,0:T(8,128)(2,1)}, bf16[512,1536]{1,0:T(8,128)(2,1)}, u32[]{:S(2)}, u32[]{:S(2)}) collective-permute-start(bf16[512,1536]{1,0:T(8,128)(2,1)} %get-tuple-element.184), channel_id=1, source_target_pairs={{0,1},{1,0},{2,3},{3,2},{4,5},{5,4},{6,7},{7,6},{8,9},{9,8},{10,11... | collective-permute-start | bytes 4718600 | tf_op jit(solution)/shard_map/ppermute | solution.py:47
  522.0 19.8 %collective-permute-start.20 = (bf16[4,2,24,1664]{3,2,1,0:T(8,128)(2,1)}, bf16[4,2,24,1664]{3,2,1,0:T(8,128)(2,1)}, u32[]{:S(2)}, u32[]{:S(2)}) collective-permute-start(bf16[4,2,24,1664]{3,2,1,0:T(8,128)(2,1)} %get-tuple-element.178), channel_id=1, source_target_pairs={{0,16},{16,32},{32,48},{48,0},{1,17},{17,33},{33,49},{49,1},{2,18}... | collective-permute-start | bytes 1916936 | tf_op jit(solution)/shard_map/ppermute | solution.py:531
  523.7 30.7 %collective-permute-start.21 = (bf16[4,2,24,1664]{3,2,1,0:T(8,128)(2,1)}, bf16[4,2,24,1664]{3,2,1,0:T(8,128)(2,1)}, u32[]{:S(2)}, u32[]{:S(2)}) collective-permute-start(bf16[4,2,24,1664]{3,2,1,0:T(8,128)(2,1)} %get-tuple-element.179), channel_id=1, source_target_pairs={{0,32},{16,48},{32,0},{48,16},{1,33},{17,49},{33,1},{49,17},{2,34}... | collective-permute-start | bytes 1916936 | tf_op jit(solution)/shard_map/ppermute | solution.py:531
  526.4 28.0 %collective-permute-start.22 = (bf16[4,2,24,1664]{3,2,1,0:T(8,128)(2,1)}, bf16[4,2,24,1664]{3,2,1,0:T(8,128)(2,1)}, u32[]{:S(2)}, u32[]{:S(2)}) collective-permute-start(bf16[4,2,24,1664]{3,2,1,0:T(8,128)(2,1)} %get-tuple-element.180), channel_id=1, source_target_pairs={{0,48},{16,0},{32,16},{48,32},{1,49},{17,1},{33,17},{49,33},{2,50}... | collective-permute-start | bytes 1916936 | tf_op jit(solution)/shard_map/ppermute | solution.py:531
  530.3 27.9 %all-to-all-start.7 = ((bf16[4,4,2,24,640]{4,3,2,1,0:T(8,128)(2,1)}), bf16[4,4,2,24,640]{4,3,2,1,0:T(8,128)(2,1)S(1)}, u32[]{:S(2)}, u32[]{:S(2)}) async-start(bf16[4,4,2,24,640]{4,3,2,1,0:T(8,128)(2,1)} %add_convert_fusion), calls=%async_computation.8 | async-start | bytes 1966080 | tf_op jit(solution)/shard_map/all_to_all | solution.py:775
  558.4 11.5 %collective-permute-start.28 = (bf16[2,24,640]{2,1,0:T(8,128)(2,1)S(1)}, bf16[2,24,640]{2,1,0:T(8,128)(2,1)S(1)}, u32[]{:S(2)}, u32[]{:S(2)}) collective-permute-start(bf16[2,24,640]{2,1,0:T(8,128)(2,1)S(1)} %get-tuple-element.284), channel_id=1, source_target_pairs={{0,16},{16,32},{32,48},{48,0},{1,17},{17,33},{33,49},{49,1},{2,18}... | collective-permute-start | bytes 184328 | tf_op jit(solution)/shard_map/ppermute | solution.py:83
  560.0 11.5 %collective-permute-start.30 = (bf16[2,24,640]{2,1,0:T(8,128)(2,1)S(1)}, bf16[2,24,640]{2,1,0:T(8,128)(2,1)S(1)}, u32[]{:S(2)}, u32[]{:S(2)}) collective-permute-start(bf16[2,24,640]{2,1,0:T(8,128)(2,1)S(1)} %get-tuple-element.285), channel_id=1, source_target_pairs={{0,48},{16,0},{32,16},{48,32},{1,49},{17,1},{33,17},{49,33},{2,50}... | collective-permute-start | bytes 184328 | tf_op jit(solution)/shard_map/ppermute | solution.py:83
  561.7 15.6 %copy-start.23 = (bf16[512,1536]{1,0:T(8,128)(2,1)S(1)}, bf16[512,1536]{1,0:T(8,128)(2,1)}, u32[]{:S(2)}) copy-start(bf16[512,1536]{1,0:T(8,128)(2,1)} %param.15) | copy-start | bytes 4718596
  561.7 15.6 %copy-start.50 = (f32[1536]{0:T(1024)S(1)}, f32[1536]{0:T(1024)}, u32[]{:S(2)}) copy-start(f32[1536]{0:T(1024)} %copy-done.49) | copy-start | bytes 18436
  561.7 9.7 %collective-permute-start.29 = (bf16[2,24,640]{2,1,0:T(8,128)(2,1)S(1)}, bf16[2,24,640]{2,1,0:T(8,128)(2,1)S(1)}, u32[]{:S(2)}, u32[]{:S(2)}) collective-permute-start(bf16[2,24,640]{2,1,0:T(8,128)(2,1)S(1)} %get-tuple-element.286), channel_id=1, source_target_pairs={{0,32},{16,48},{32,0},{48,16},{1,33},{17,49},{33,1},{49,17},{2,34}... | collective-permute-start | bytes 184328 | tf_op jit(solution)/shard_map/ppermute | solution.py:83
  565.3 9.5 %collective-permute-start.25 = (bf16[2,24,1664]{2,1,0:T(8,128)(2,1)S(1)}, bf16[2,24,1664]{2,1,0:T(8,128)(2,1)S(1)}, u32[]{:S(2)}, u32[]{:S(2)}) collective-permute-start(bf16[2,24,1664]{2,1,0:T(8,128)(2,1)S(1)} %get-tuple-element.281), channel_id=1, source_target_pairs={{0,2},{2,4},{4,6},{6,0},{1,3},{3,5},{5,7},{7,1},{8,10},{10,12},{12... | collective-permute-start | bytes 479240 | tf_op jit(solution)/shard_map/ppermute | solution.py:83
  569.3 5.8 collective-permute-start.27
  570.0 7.3 %collective-permute-start.26 = (bf16[2,24,1664]{2,1,0:T(8,128)(2,1)S(1)}, bf16[2,24,1664]{2,1,0:T(8,128)(2,1)S(1)}, u32[]{:S(2)}, u32[]{:S(2)}) collective-permute-start(bf16[2,24,1664]{2,1,0:T(8,128)(2,1)S(1)} %get-tuple-element.283), channel_id=1, source_target_pairs={{0,4},{2,6},{4,0},{6,2},{1,5},{3,7},{5,1},{7,3},{8,12},{10,14},{12... | collective-permute-start | bytes 479240 | tf_op jit(solution)/shard_map/ppermute | solution.py:83
  580.3 7.8 %collective-permute-start.31 = (bf16[24,2304]{1,0:T(8,128)(2,1)S(1)}, bf16[24,2304]{1,0:T(8,128)(2,1)S(1)}, u32[]{:S(2)}, u32[]{:S(2)}) collective-permute-start(bf16[24,2304]{1,0:T(8,128)(2,1)S(1)} %dynamic-slice_bitcast_fusion.3), channel_id=1, source_target_pairs={{0,64},{64,0},{1,65},{65,1},{2,66},{66,2},{3,67},{67,3},{4,68},{68... | collective-permute-start | bytes 331784 | tf_op jit(solution)/shard_map/ppermute | solution.py:83
  590.8 4.0 collective-permute-start.32
  (42 other events, 221.1 us)
Sparse Core Ops, SparseCore 0:
  94.9 90.5 all-gather.2
  360.9 99.0 reduce-scatter.1

commit v8 on v7

--- a/solution.py
+++ b/solution.py
@@ -497,6 +497,30 @@
     )(jnp.full((1,), lax.axis_index("c"), jnp.int32), *arrays)
 
 
+def token_grads_kernel(tokens_ref, gain_ref, mine_ref, other_ref, later_ref, out_ref):
+    resid = tokens_ref[...].astype(F32)
+    scale = rms_scale(resid)
+    gained = both(mine_ref[...], other_ref[...]) * gain_ref[...]
+    middle = jnp.mean(resid * gained, axis=-1, keepdims=True)
+    out_ref[...] = later_ref[...] + (scale * gained - resid * scale * scale * scale * middle)
+
+
+def token_grads(tokens, gain_row, mine, other, later):
+    rows, width = tokens.shape
+    block = pl.BlockSpec((128, width), lambda b: (b, 0))
+    return pl.pallas_call(
+        token_grads_kernel,
+        grid=(rows // 128,),
+        in_specs=[block, pl.BlockSpec((1, width), lambda b: (0, 0)), block, block, block],
+        out_specs=block,
+        out_shape=jax.ShapeDtypeStruct((rows, width), F32),
+        compiler_params=pltpu.CompilerParams(vmem_limit_bytes=24 << 20),
+        cost_estimate=pl.CostEstimate(
+            flops=12 * rows * width, bytes_accessed=14 * rows * width, transcendentals=rows
+        ),
+    )(tokens, gain_row, mine, other, later)
+
+
 def turned_sum_kernel(left_ref, right_ref, out_ref):
     out_ref[...] = both(left_ref[...], right_ref[...]).T
 
@@ -796,8 +820,7 @@
         feat_width * (summed[0, at + 2] + summed[0, at + 10])
     )
     own_gain_one = own_kv[:, 2 * k_width + EXPERTS] + own_kv[:, 2 * k_width + EXPERTS + 8]
-    d_hidden_one, _ = norm_back(resid_in, scale_one, gain_one, both(part, other))
-    grad_tokens = d_hidden + d_hidden_one
+    grad_tokens = token_grads(tokens, gain_one, part, other, d_hidden)
     own_gain_one = own_gain_one + swap(own_gain_one, "t")
     return (
         output,

time: 613 us -> 619 us (level)
    ppermute x3, waiting for transfers between devices: 12.6 us -> 21.9 us  [send_blocks(): lax.ppermute(blocks[r], axis, [(i, (i + r) % 4) for i in range(4)])]
  transfers between devices with their start and end apart: 42 -> 42, of which waited for: 22 -> 23; matrix products, arithmetic and copies ran while one was open for 11% -> 11% of each run, Pallas kernels for 8% -> 9%
where the time goes in v8:
time: 619 us; the launch traced here: 610 us
  waiting for transfers between devices  291 us (47%)
  Pallas kernels  83.5 us (13%)
  starting transfers between devices  82.7 us (13%)
  other arithmetic  38.2 us (6%)
  blocking collectives  37.4 us (6%)
  local copies, waits for them, and re-layouts  29.5 us (5%)
  matrix products  28.5 us (5%)
  between operations  19.3 us (3%)
    ppermute x14, waiting for transfers between devices, swap(): return lax.ppermute(value, axis, [(0, 1), (1, 0)])  138 us
    all_to_all x3, waiting for transfers between devices, exchange_slots(): lax.all_to_all(rows.reshape(EXPERTS, -1, width), ('h', 'x', 'c'), 0, 0, t...  54.8 us
    all_to_all x1, blocking collectives, exchange_slots(): lax.all_to_all(rows.reshape(EXPERTS, -1, width), ('h', 'x', 'c'), 0, 0, t...  37.4 us
    dot_general x16, matrix products, dot(): lax.dot_general(left, right, (((left_dim,), (right_dim,)), ((), ())), pre...  28.5 us
    reduce_scatter x1, waiting for transfers between devices, local(): grad_experts = lax.psum_scatter(grad_parts, 'y', scatter_dimension=0)  25.3 us
    ppermute x3, waiting for transfers between devices, send_blocks(): lax.ppermute(blocks[r], axis, [(i, (i + r) % 4) for i in range(4)])  21.9 us
    pallas_call x1, Pallas kernels, run_experts_back(): pl.pallas_call(experts_back_kernel, in_specs=[whole, column, column] + we...  17.1 us
    pallas_call x2, Pallas kernels, attend_back(): pl.pallas_call(bwd_kernel, grid=(count,), in_specs=[pl.BlockSpec(memory_s...  13.9 us
  transfers between devices with their start and end apart: 42, of which 23 were waited for; matrix products, arithmetic and copies ran while one was open for 11% of the time, Pallas kernels for 9%

profile of v8, /device:TPU:0, one launch (start us, length us, event | category | flops | bytes accessed | tf_op | source)
XLA Modules:
  0.0 609.6 jit_solution(6677311000021286503)
XLA Ops:
  11.4 7.9 %all-to-all-start = ((bf16[8,24,2176]{2,1,0:T(8,128)(2,1)}), bf16[8,24,2176]{2,1,0:T(8,128)(2,1)S(1)}, u32[]{:S(2)}, u32[]{:S(2)}) async-start(bf16[8,24,2176]{2,1,0:T(8,128)(2,1)} %broadcast_in_dim.148), calls=%async_computation | async-start | bytes 1671168 | tf_op jit(solution)/shard_map/all_to_all | solution.py:56
  20.7 13.5 %all-to-all-done = bf16[8,24,2176]{2,1,0:T(8,128)(2,1)S(1)} async-done(((bf16[8,24,2176]{2,1,0:T(8,128)(2,1)}), bf16[8,24,2176]{2,1,0:T(8,128)(2,1)S(1)}, u32[]{:S(2)}, u32[]{:S(2)}) %all-to-all-start) | async-done | bytes 835616 | tf_op jit(solution)/shard_map/all_to_all | solution.py:56
  35.3 4.3 all-to-all-start.1
  40.4 13.4 %all-to-all-done.1 = bf16[4,8,24,640]{3,2,1,0:T(8,128)(2,1)S(1)} async-done(((bf16[4,8,24,640]{3,2,1,0:T(8,128)(2,1)}), bf16[4,8,24,640]{3,2,1,0:T(8,128)(2,1)S(1)}, u32[]{:S(2)}, u32[]{:S(2)}) %all-to-all-start.1) | async-done | bytes 983072 | tf_op jit(solution)/shard_map/all_to_all | solution.py:61
  53.8 2.7 broadcast_in_dim.150
  58.0 4.5 all-to-all-start.2
  63.9 1.8 fusion.27
  65.7 2.1 collective-permute-start.3
  67.8 3.2 collective-permute-start.2
  71.0 2.1 collective-permute-start.1
  73.1 12.5 %collective-permute-done.4 = bf16[3,384,512]{2,1,0:T(8,128)(2,1)} collective-permute-done((bf16[3,384,512]{2,1,0:T(8,128)(2,1)}, bf16[3,384,512]{2,1,0:T(8,128)(2,1)}, u32[]{:S(2)}, u32[]{:S(2)}) %collective-permute-start.4) | collective-permute-done | bytes 1179680 | tf_op jit(solution)/shard_map/ppermute | solution.py:47
  85.6 6.7 %all-to-all-done.2 = bf16[4,8,24,1536]{3,2,1,0:T(8,128)(2,1)} async-done(((bf16[4,8,24,1536]{3,2,1,0:T(8,128)(2,1)}), bf16[4,8,24,1536]{3,2,1,0:T(8,128)(2,1)}, u32[]{:S(2)}, u32[]{:S(2)}) %all-to-all-start.2) | async-done | bytes 2359328 | tf_op jit(solution)/shard_map/all_to_all | solution.py:605
  92.3 3.2 pad_maximum_fusion.1
  100.6 2.9 select_bitcast_fusion.1
  106.5 4.7 shard_map.246
  113.4 5.1 shard_map.247
  118.5 13.5 %collective-permute-done.6 = bf16[256,1536]{1,0:T(8,128)(2,1)S(1)} collective-permute-done((bf16[256,1536]{1,0:T(8,128)(2,1)S(1)}, bf16[256,1536]{1,0:T(8,128)(2,1)S(1)}, u32[]{:S(2)}, u32[]{:S(2)}) %collective-permute-start.6) | collective-permute-done | bytes 786464 | tf_op jit(solution)/shard_map/ppermute | solution.py:47
  132.0 1.7 convolution_convert_fusion.4
  136.4 16.6 %collective-permute-done.7 = bf16[256,1536]{1,0:T(8,128)(2,1)} collective-permute-done((bf16[256,1536]{1,0:T(8,128)(2,1)}, bf16[256,1536]{1,0:T(8,128)(2,1)}, u32[]{:S(2)}, u32[]{:S(2)}) %collective-permute-start.7) | collective-permute-done | bytes 786464 | tf_op jit(solution)/shard_map/ppermute | solution.py:47
  157.6 2.8 convolution_convert_fusion.1
  160.4 3.9 all-to-all-start.3
  166.7 29.6 %all-to-all-done.3 = bf16[16,48,1536]{2,1,0:T(8,128)(2,1)S(1)} async-done(((bf16[16,48,1536]{2,1,0:T(8,128)(2,1)}), bf16[16,48,1536]{2,1,0:T(8,128)(2,1)S(1)}, u32[]{:S(2)}, u32[]{:S(2)}) %all-to-all-start.3) | async-done | bytes 2359328 | tf_op jit(solution)/shard_map/all_to_all | solution.py:96
  196.2 12.1 %shard_map.248 = (f32[768,1024]{1,0:T(8,128)S(1)}, f32[768,1024]{1,0:T(8,128)S(1)}, bf16[768,1024]{1,0:T(8,128)(2,1)S(1)}, bf16[768,1536]{1,0:T(8,128)(2,1)S(1)}) custom-call(bf16[768,1536]{1,0:T(8,128)(2,1)S(1)} %bitcast.135, bf16[4,2,3,384,512]{4,3,2,1,0:T(8,128)(2,1)} %bitcast.140, bf16[4,2,3,384,512]{4,3,2,1,0:T(8,128)(2,1)} %bitcast.141, ...), custom_call_target="tpu_custom_call" | custom-call | flops 7247757312 | bytes 20000000 | tf_op jit(solution)/shard_map/pallas_call | solution.py:388
  210.0 37.4 %all_to_all.40 = bf16[16,48,1536]{2,1,0:T(8,128)(2,1)S(1)} all-to-all(bf16[16,48,1536]{2,1,0:T(8,128)(2,1)S(1)} %bitcast.137), channel_id=1, replica_groups=mesh['h'=2,'x'=4,'c'=2,'y'=4,'t'=2] {'h','x','c'}, dimensions={0} | all-to-all | bytes 4718592 | tf_op jit(solution)/shard_map/all_to_all | solution.py:96
  250.2 35.1 %collective-permute-done.8 = bf16[512,1536]{1,0:T(8,128)(2,1)S(1)} collective-permute-done((bf16[512,1536]{1,0:T(8,128)(2,1)S(1)}, bf16[512,1536]{1,0:T(8,128)(2,1)S(1)}, u32[]{:S(2)}, u32[]{:S(2)}) %collective-permute-start.8) | collective-permute-done | bytes 1572896 | tf_op jit(solution)/shard_map/ppermute | solution.py:47
  285.3 2.0 fusion
  288.9 2.8 convolution_convert_fusion
  291.7 4.5 all-to-all-start.5
  296.2 3.8 select_reduce_fusion.1
  301.0 20.2 %collective-permute-done.9 = f32[2,512]{1,0:T(2,128)S(1)} collective-permute-done((f32[2,512]{1,0:T(2,128)S(1)}, f32[2,512]{1,0:T(2,128)S(1)}, u32[]{:S(2)}, u32[]{:S(2)}) %collective-permute-start.9) | collective-permute-done | bytes 4128 | tf_op jit(solution)/shard_map/ppermute | solution.py:47
  321.2 7.1 %all-to-all-done.5 = bf16[16,48,1536]{2,1,0:T(8,128)(2,1)} async-done(((bf16[16,48,1536]{2,1,0:T(8,128)(2,1)}), bf16[16,48,1536]{2,1,0:T(8,128)(2,1)}, u32[]{:S(2)}, u32[]{:S(2)}) %all-to-all-start.5) | async-done | bytes 2359328 | tf_op jit(solution)/shard_map/all_to_all | solution.py:96
  328.2 17.1 %shard_map.249 = (bf16[768,1024]{1,0:T(8,128)(2,1)}, bf16[768,1024]{1,0:T(8,128)(2,1)}, bf16[768,1536]{1,0:T(8,128)(2,1)}) custom-call(bf16[768,1536]{1,0:T(8,128)(2,1)} %bitcast.50.d_ref, f32[768,1024]{1,0:T(8,128)} %copy-done.4, f32[768,1024]{1,0:T(8,128)} %copy-done.5, bf16[4,2,3,384,512]{4,3,2,1,0:T(8,128)(2,1)} %bitcast.143, ...), custom_call_target="tpu_custom_call" | custom-call | flops 7247757312 | bytes 20000000 | tf_op jit(solution)/shard_map/pallas_call | solution.py:408
  345.4 5.5 all-to-all-start.6
  351.0 13.9 %shard_map.250 = bf16[4,2,3,384,512]{4,3,2,1,0:T(8,128)(2,1)} custom-call(bf16[768,1536]{1,0:T(8,128)(2,1)} %bitcast.136, bf16[768,1536]{1,0:T(8,128)(2,1)} %bitcast.50.d_ref, bf16[768,1024]{1,0:T(8,128)(2,1)} %get-tuple-element.129.dg_ref, bf16[768,1024]{1,0:T(8,128)(2,1)} %get-tuple-element.130.du_ref, bf16[768,1024]{1,0:T(8,128)(2,1)} %copy-done.10), custom_call_target="tpu_custom_call" | custom-call | flops 7247757312 | bytes 20000000 | tf_op jit(solution)/shard_map/pallas_call | solution.py:422
  364.9 18.1 %all-to-all-done.6 = bf16[16,48,1536]{2,1,0:T(8,128)(2,1)} async-done(((bf16[16,48,1536]{2,1,0:T(8,128)(2,1)}), bf16[16,48,1536]{2,1,0:T(8,128)(2,1)}, u32[]{:S(2)}, u32[]{:S(2)}) %all-to-all-start.6) | async-done | bytes 2359328 | tf_op jit(solution)/shard_map/all_to_all | solution.py:96
  383.0 3.4 convolution_convert_fusion.2
  391.8 31.1 %collective-permute-done.10 = bf16[512,1536]{1,0:T(8,128)(2,1)S(1)} collective-permute-done((bf16[512,1536]{1,0:T(8,128)(2,1)S(1)}, bf16[512,1536]{1,0:T(8,128)(2,1)S(1)}, u32[]{:S(2)}, u32[]{:S(2)}) %collective-permute-start.10) | collective-permute-done | bytes 1572896 | tf_op jit(solution)/shard_map/ppermute | solution.py:47
  424.8 3.3 fusion.67
  428.1 2.3 fusion.18.d_ref
  430.4 7.0 %shard_map.251 = (bf16[384,512]{1,0:T(8,128)(2,1)}, bf16[2,128,512]{2,1,0:T(8,128)(2,1)}, bf16[2,128,512]{2,1,0:T(8,128)(2,1)}, bf16[2,128,512]{2,1,0:T(8,128)(2,1)}, bf16[2,128,512]{2,1,0:T(8,128)(2,1)}) custom-call(s32[1]{0:T(128)} %bitcast.y_ref, bf16[768,512]{1,0:T(8,128)(2,1)} %copy-done.13, bf16[768,512]{1,0:T(8,128)(2,1)} %fusion.18.d_ref, ...), custom_call_target="tpu_custom_call" | custom-call | flops 149999992832 | bytes 6000000 | tf_op jit(solution)/shard_map/pallas_call | solution.py:273
  437.4 25.3 %reduce-scatter.2.cloned.1.call-done = bf16[1,2,3,384,512]{4,3,2,1,0:T(8,128)(2,1)} async-done(((bf16[4,2,3,384,512]{4,3,2,1,0:T(8,128)(2,1)}), bf16[1,2,3,384,512]{4,3,2,1,0:T(8,128)(2,1)}) %reduce-scatter.2.cloned.1.call-update) | async-done | bytes 2359312 | tf_op jit(solution)/shard_map/reduce_scatter | solution.py:707
  468.9 1.8 collective-permute-start.14
  470.7 6.9 %shard_map.252 = (bf16[384,512]{1,0:T(8,128)(2,1)}, bf16[2,128,512]{2,1,0:T(8,128)(2,1)}, bf16[2,128,512]{2,1,0:T(8,128)(2,1)}, bf16[2,128,512]{2,1,0:T(8,128)(2,1)}, bf16[2,128,512]{2,1,0:T(8,128)(2,1)}) custom-call(s32[1]{0:T(128)} %bitcast.y_ref, bf16[768,512]{1,0:T(8,128)(2,1)} %copy-done.13, bf16[768,512]{1,0:T(8,128)(2,1)} %fusion.18.d_ref, ...), custom_call_target="tpu_custom_call" | custom-call | flops 149999992832 | bytes 6000000 | tf_op jit(solution)/shard_map/pallas_call | solution.py:273
  478.7 4.1 collective-permute-done.13
  482.8 5.9 collective-permute-done.14
  495.7 8.4 %shard_map.253 = (bf16[4,4,2,24,1664]{4,3,2,1,0:T(8,128)(2,1)}, bf16[4,4,2,24,1664]{4,3,2,1,0:T(8,128)(2,1)}) custom-call(s32[1]{0:T(128)} %bitcast.55.core_ref, bf16[512,1536]{1,0:T(8,128)(2,1)} %copy-done.30, bf16[512,1536]{1,0:T(8,128)(2,1)} %copy-done.6, bf16[512,1536]{1,0:T(8,128)(2,1)} %copy-done.25, f32[8,1536]{1,0:T(8,128)} %maximum_maximum_fusion.refs_3_, ...), custom_call_target="tpu_custom_call" | custom-call | flops 20000000000 | bytes 10000000 | tf_op jit(solution)/shard_map/pallas_call | solution.py:484
  504.1 6.9 %collective-permute-done.17 = bf16[2,128,512]{2,1,0:T(8,128)(2,1)S(1)} collective-permute-done((bf16[2,128,512]{2,1,0:T(8,128)(2,1)}, bf16[2,128,512]{2,1,0:T(8,128)(2,1)S(1)}, u32[]{:S(2)}, u32[]{:S(2)}) %collective-permute-start.17) | collective-permute-done | bytes 262176 | tf_op jit(solution)/shard_map/ppermute | solution.py:731
  512.5 3.3 fusion.6
  517.3 2.4 shard_map.254
  519.7 3.7 fusion.44
  524.4 1.8 collective-permute-done.23
  527.3 6.0 all-to-all-start.7
  534.7 2.7 collective-permute-start.21
  539.9 2.8 convert_add_fusion.1
  543.8 7.4 %collective-permute-done.20 = bf16[4,2,24,1664]{3,2,1,0:T(8,128)(2,1)} collective-permute-done((bf16[4,2,24,1664]{3,2,1,0:T(8,128)(2,1)}, bf16[4,2,24,1664]{3,2,1,0:T(8,128)(2,1)}, u32[]{:S(2)}, u32[]{:S(2)}) %collective-permute-start.20) | collective-permute-done | bytes 639008 | tf_op jit(solution)/shard_map/ppermute | solution.py:555
  551.2 14.6 %collective-permute-done.21 = bf16[4,2,24,1664]{3,2,1,0:T(8,128)(2,1)} collective-permute-done((bf16[4,2,24,1664]{3,2,1,0:T(8,128)(2,1)}, bf16[4,2,24,1664]{3,2,1,0:T(8,128)(2,1)}, u32[]{:S(2)}, u32[]{:S(2)}) %collective-permute-start.21) | collective-permute-done | bytes 639008 | tf_op jit(solution)/shard_map/ppermute | solution.py:555
  568.7 1.8 collective-permute-start.30
  572.0 2.0 add_convert_fusion.3
  574.0 2.8 collective-permute-start.25
  577.5 1.9 collective-permute-start.26
  579.4 2.4 collective-permute-done.25
  582.9 2.2 collective-permute-done.26
  585.2 2.9 collective-permute-start.31
  589.3 4.8 shard_map.256
  (250 shorter events, 80.5 us)
Async XLA Ops:
  7.2 12.3 %copy-start.35 = (bf16[1,384,512]{2,1,0:T(8,128)(2,1)S(1)}, bf16[1,384,512]{2,1,0:T(8,128)(2,1)}, u32[]{:S(2)}) copy-start(bf16[1,384,512]{2,1,0:T(8,128)(2,1)} %param.28) | copy-start | bytes 1179652
  7.2 12.3 %copy-start.36 = (bf16[1,384,512]{2,1,0:T(8,128)(2,1)S(1)}, bf16[1,384,512]{2,1,0:T(8,128)(2,1)}, u32[]{:S(2)}) copy-start(bf16[1,384,512]{2,1,0:T(8,128)(2,1)} %param.27) | copy-start | bytes 1179652
  11.4 22.8 %all-to-all-start = ((bf16[8,24,2176]{2,1,0:T(8,128)(2,1)}), bf16[8,24,2176]{2,1,0:T(8,128)(2,1)S(1)}, u32[]{:S(2)}, u32[]{:S(2)}) async-start(bf16[8,24,2176]{2,1,0:T(8,128)(2,1)} %broadcast_in_dim.148), calls=%async_computation | async-start | bytes 1671168 | tf_op jit(solution)/shard_map/all_to_all | solution.py:56
  35.3 18.5 %all-to-all-start.1 = ((bf16[4,8,24,640]{3,2,1,0:T(8,128)(2,1)}), bf16[4,8,24,640]{3,2,1,0:T(8,128)(2,1)S(1)}, u32[]{:S(2)}, u32[]{:S(2)}) async-start(bf16[4,8,24,640]{3,2,1,0:T(8,128)(2,1)} %broadcast_in_dim.149), calls=%async_computation.1 | async-start | bytes 1966080 | tf_op jit(solution)/shard_map/all_to_all | solution.py:61
  39.6 16.9 %copy-start = (bf16[512,1536]{1,0:T(8,128)(2,1)S(1)}, bf16[512,1536]{1,0:T(8,128)(2,1)}, u32[]{:S(2)}) copy-start(bf16[512,1536]{1,0:T(8,128)(2,1)} %tokens_ref.1) | copy-start | bytes 4718596
  56.5 6.1 collective-permute-start
  56.9 28.8 %collective-permute-start.4 = (bf16[3,384,512]{2,1,0:T(8,128)(2,1)}, bf16[3,384,512]{2,1,0:T(8,128)(2,1)}, u32[]{:S(2)}, u32[]{:S(2)}) collective-permute-start(bf16[3,384,512]{2,1,0:T(8,128)(2,1)} %pad_maximum_fusion.3), channel_id=1, source_target_pairs={{0,1},{1,0},{2,3},{3,2},{4,5},{5,4},{6,7},{7,6},{8,9},{9,8},{10,11... | collective-permute-start | bytes 3538952 | tf_op jit(solution)/shard_map/ppermute | solution.py:47
  58.0 34.4 %all-to-all-start.2 = ((bf16[4,8,24,1536]{3,2,1,0:T(8,128)(2,1)}), bf16[4,8,24,1536]{3,2,1,0:T(8,128)(2,1)}, u32[]{:S(2)}, u32[]{:S(2)}) async-start(bf16[4,8,24,1536]{3,2,1,0:T(8,128)(2,1)} %broadcast_in_dim.150), calls=%async_computation.2 | async-start | bytes 4718592 | tf_op jit(solution)/shard_map/all_to_all | solution.py:605
  62.5 133.8 %all-gather.3.cloned.1.call-start = ((), (), s32[]{:S(2)}) async-start(), calls=%async_computation.10 | async-start | bytes 11796480 | tf_op jit(solution)/shard_map/all_gather | solution.py:631
  63.9 40.4 %copy-start.6 = (bf16[512,1536]{1,0:T(8,128)(2,1)}, bf16[512,1536]{1,0:T(8,128)(2,1)S(1)}, u32[]{:S(2)}) copy-start(bf16[512,1536]{1,0:T(8,128)(2,1)S(1)} %fusion.3.refs_1_.refs_0_) | copy-start | bytes 4718596
  65.7 29.8 %collective-permute-start.3 = (bf16[2,256,512]{2,1,0:T(8,128)(2,1)}, bf16[2,256,512]{2,1,0:T(8,128)(2,1)}, u32[]{:S(2)}, u32[]{:S(2)}) collective-permute-start(bf16[2,256,512]{2,1,0:T(8,128)(2,1)} %bitcast.13.kv0), channel_id=1, source_target_pairs={{0,6},{1,7},{8,14},{9,15},{16,22},{17,23},{24,30},{25,31},{32,38},... | collective-permute-start | bytes 1572872 | tf_op jit(solution)/shard_map/ppermute | solution.py:619
  67.8 27.8 %collective-permute-start.2 = (bf16[2,256,512]{2,1,0:T(8,128)(2,1)}, bf16[2,256,512]{2,1,0:T(8,128)(2,1)}, u32[]{:S(2)}, u32[]{:S(2)}) collective-permute-start(bf16[2,256,512]{2,1,0:T(8,128)(2,1)} %bitcast.13.kv0), channel_id=1, source_target_pairs={{0,4},{2,6},{1,5},{3,7},{8,12},{10,14},{9,13},{11,15},{16,20},{18,... | collective-permute-start | bytes 1572872 | tf_op jit(solution)/shard_map/ppermute | solution.py:619
  71.0 24.6 %collective-permute-start.1 = (bf16[2,256,512]{2,1,0:T(8,128)(2,1)}, bf16[2,256,512]{2,1,0:T(8,128)(2,1)}, u32[]{:S(2)}, u32[]{:S(2)}) collective-permute-start(bf16[2,256,512]{2,1,0:T(8,128)(2,1)} %bitcast.13.kv0), channel_id=1, source_target_pairs={{0,2},{2,4},{4,6},{1,3},{3,5},{5,7},{8,10},{10,12},{12,14},{9,11},... | collective-permute-start | bytes 1572872 | tf_op jit(solution)/shard_map/ppermute | solution.py:619
  95.6 5.0 collective-permute-start.5
  99.0 151.2 %copy-start.9 = (s32[1,512]{1,0:T(1,128)}, s32[1,512]{1,0:T(1,128)S(1)}, u32[]{:S(2)}) copy-start(s32[1,512]{1,0:T(1,128)S(1)} %get-tuple-element.264.seg_q) | copy-start | bytes 6148
  104.3 27.7 %copy-start.27 = (bf16[2,4,2,96,1536]{4,3,2,1,0:T(8,128)(2,1)}, bf16[2,4,2,96,1536]{4,3,2,1,0:T(8,128)(2,1)S(1)}, u32[]{:S(2)}) copy-start(bf16[2,4,2,96,1536]{4,3,2,1,0:T(8,128)(2,1)S(1)} %copy.66) | copy-start | bytes 14155780
  112.1 19.9 %collective-permute-start.6 = (bf16[256,1536]{1,0:T(8,128)(2,1)S(1)}, bf16[256,1536]{1,0:T(8,128)(2,1)S(1)}, u32[]{:S(2)}, u32[]{:S(2)}) collective-permute-start(bf16[256,1536]{1,0:T(8,128)(2,1)S(1)} %convolution_convert_fusion.5), channel_id=1, source_target_pairs={{0,1},{1,0},{2,3},{3,2},{4,5},{5,4},{6,7},{7,6},{8,9},{9,8},{10,11... | collective-permute-start | bytes 2359304 | tf_op jit(solution)/shard_map/ppermute | solution.py:47
  118.5 15.3 %copy-start.12 = (bf16[768,256]{1,0:T(8,128)(2,1)}, bf16[768,256]{1,0:T(8,128)(2,1)S(1)}, u32[]{:S(2)}) copy-start(bf16[768,256]{1,0:T(8,128)(2,1)S(1)} %get-tuple-element.117.o_1.refs_5_) | copy-start | bytes 1179652
  118.5 15.3 %copy-start.15 = (f32[4,8,256]{2,1,0:T(8,128)}, f32[4,8,256]{2,1,0:T(8,128)S(1)}, u32[]{:S(2)}) copy-start(f32[4,8,256]{2,1,0:T(8,128)S(1)} %get-tuple-element.135.lse_1) | copy-start | bytes 98308
  133.7 19.3 %collective-permute-start.7 = (bf16[256,1536]{1,0:T(8,128)(2,1)}, bf16[256,1536]{1,0:T(8,128)(2,1)}, u32[]{:S(2)}, u32[]{:S(2)}) collective-permute-start(bf16[256,1536]{1,0:T(8,128)(2,1)} %convolution_convert_fusion.4), channel_id=1, source_target_pairs={{0,1},{1,0},{2,3},{3,2},{4,5},{5,4},{6,7},{7,6},{8,9},{9,8},{10,11... | collective-permute-start | bytes 2359304 | tf_op jit(solution)/shard_map/ppermute | solution.py:47
  160.4 35.9 %all-to-all-start.3 = ((bf16[16,48,1536]{2,1,0:T(8,128)(2,1)}), bf16[16,48,1536]{2,1,0:T(8,128)(2,1)S(1)}, u32[]{:S(2)}, u32[]{:S(2)}) async-start(bf16[16,48,1536]{2,1,0:T(8,128)(2,1)} %bitcast.162), calls=%async_computation.3 | async-start | bytes 4718592 | tf_op jit(solution)/shard_map/all_to_all | solution.py:96
  210.0 37.4 %copy-start.4 = (f32[768,1024]{1,0:T(8,128)}, f32[768,1024]{1,0:T(8,128)S(1)}, u32[]{:S(2)}) copy-start(f32[768,1024]{1,0:T(8,128)S(1)} %get-tuple-element.124.g_ref) | copy-start | bytes 9437188
  210.0 37.4 %copy-start.10 = (bf16[768,1024]{1,0:T(8,128)(2,1)}, bf16[768,1024]{1,0:T(8,128)(2,1)S(1)}, u32[]{:S(2)}) copy-start(bf16[768,1024]{1,0:T(8,128)(2,1)S(1)} %get-tuple-element.131.inner_ref) | copy-start | bytes 4718596
  210.0 37.4 %copy-start.32 = (bf16[512,768]{1,0:T(8,128)(2,1)S(1)}, bf16[512,768]{1,0:T(8,128)(2,1)}, u32[]{:S(2)}) copy-start(bf16[512,768]{1,0:T(8,128)(2,1)} %add_convert_fusion.2) | copy-start | bytes 2359300
  247.4 37.9 %copy-start.17 = (f32[512,1536]{1,0:T(8,128)S(1)}, f32[512,1536]{1,0:T(8,128)}, u32[]{:S(2)}) copy-start(f32[512,1536]{1,0:T(8,128)} %copy-done.16) | copy-start | bytes 9437188
  247.4 37.9 %copy-start.20 = (bf16[512,1536]{1,0:T(8,128)(2,1)S(1)}, bf16[512,1536]{1,0:T(8,128)(2,1)}, u32[]{:S(2)}) copy-start(bf16[512,1536]{1,0:T(8,128)(2,1)} %param.16) | copy-start | bytes 4718596
  248.8 36.5 %collective-permute-start.8 = (bf16[512,1536]{1,0:T(8,128)(2,1)S(1)}, bf16[512,1536]{1,0:T(8,128)(2,1)S(1)}, u32[]{:S(2)}, u32[]{:S(2)}) collective-permute-start(bf16[512,1536]{1,0:T(8,128)(2,1)S(1)} %convolution_convert_fusion.3), channel_id=1, source_target_pairs={{0,1},{1,0},{2,3},{3,2},{4,5},{5,4},{6,7},{7,6},{8,9},{9,8},{10,11... | collective-permute-start | bytes 4718600 | tf_op jit(solution)/shard_map/ppermute | solution.py:47
  291.7 36.5 %all-to-all-start.5 = ((bf16[16,48,1536]{2,1,0:T(8,128)(2,1)}), bf16[16,48,1536]{2,1,0:T(8,128)(2,1)}, u32[]{:S(2)}, u32[]{:S(2)}) async-start(bf16[16,48,1536]{2,1,0:T(8,128)(2,1)} %bitcast.161), calls=%async_computation.5 | async-start | bytes 4718592 | tf_op jit(solution)/shard_map/all_to_all | solution.py:96
  300.0 21.2 %collective-permute-start.9 = (f32[2,512]{1,0:T(2,128)S(1)}, f32[2,512]{1,0:T(2,128)S(1)}, u32[]{:S(2)}, u32[]{:S(2)}) collective-permute-start(f32[2,512]{1,0:T(2,128)S(1)} %pad_maximum_fusion.6), channel_id=1, source_target_pairs={{0,1},{1,0},{2,3},{3,2},{4,5},{5,4},{6,7},{7,6},{8,9},{9,8},{10,11... | collective-permute-start | bytes 12296 | tf_op jit(solution)/shard_map/ppermute | solution.py:47
  345.4 37.6 %all-to-all-start.6 = ((bf16[16,48,1536]{2,1,0:T(8,128)(2,1)}), bf16[16,48,1536]{2,1,0:T(8,128)(2,1)}, u32[]{:S(2)}, u32[]{:S(2)}) async-start(bf16[16,48,1536]{2,1,0:T(8,128)(2,1)} %bitcast.160), calls=%async_computation.6 | async-start | bytes 4718592 | tf_op jit(solution)/shard_map/all_to_all | solution.py:96
  350.9 111.8 %reduce-scatter.2.cloned.1.call-start = ((), (), s32[]{:S(2)}) async-start(), calls=%async_computation.9 | async-start | bytes 11796480 | tf_op jit(solution)/shard_map/reduce_scatter | solution.py:707
  386.4 36.4 %collective-permute-start.10 = (bf16[512,1536]{1,0:T(8,128)(2,1)S(1)}, bf16[512,1536]{1,0:T(8,128)(2,1)S(1)}, u32[]{:S(2)}, u32[]{:S(2)}) collective-permute-start(bf16[512,1536]{1,0:T(8,128)(2,1)S(1)} %convolution_convert_fusion.2), channel_id=1, source_target_pairs={{0,1},{1,0},{2,3},{3,2},{4,5},{5,4},{6,7},{7,6},{8,9},{9,8},{10,11... | collective-permute-start | bytes 4718600 | tf_op jit(solution)/shard_map/ppermute | solution.py:47
  391.7 33.0 %copy-start.21 = (bf16[512,1536]{1,0:T(8,128)(2,1)S(1)}, bf16[512,1536]{1,0:T(8,128)(2,1)}, u32[]{:S(2)}) copy-start(bf16[512,1536]{1,0:T(8,128)(2,1)} %param.16) | copy-start | bytes 4718596
  464.1 14.6 %collective-permute-start.11 = (bf16[2,128,512]{2,1,0:T(8,128)(2,1)}, bf16[2,128,512]{2,1,0:T(8,128)(2,1)}, u32[]{:S(2)}, u32[]{:S(2)}) collective-permute-start(bf16[2,128,512]{2,1,0:T(8,128)(2,1)} %get-tuple-element.147), channel_id=1, source_target_pairs={{2,0},{4,2},{6,4},{3,1},{5,3},{7,5},{10,8},{12,10},{14,12},{11,9},... | collective-permute-start | bytes 786440 | tf_op jit(solution)/shard_map/ppermute | solution.py:731
  465.4 13.3 %collective-permute-start.12 = (bf16[2,128,512]{2,1,0:T(8,128)(2,1)}, bf16[2,128,512]{2,1,0:T(8,128)(2,1)}, u32[]{:S(2)}, u32[]{:S(2)}) collective-permute-start(bf16[2,128,512]{2,1,0:T(8,128)(2,1)} %get-tuple-element.148), channel_id=1, source_target_pairs={{4,0},{6,2},{5,1},{7,3},{12,8},{14,10},{13,9},{15,11},{20,16},{22,... | collective-permute-start | bytes 786440 | tf_op jit(solution)/shard_map/ppermute | solution.py:731
  466.7 16.2 %collective-permute-start.13 = (bf16[2,128,512]{2,1,0:T(8,128)(2,1)}, bf16[2,128,512]{2,1,0:T(8,128)(2,1)}, u32[]{:S(2)}, u32[]{:S(2)}) collective-permute-start(bf16[2,128,512]{2,1,0:T(8,128)(2,1)} %get-tuple-element.149), channel_id=1, source_target_pairs={{6,0},{7,1},{14,8},{15,9},{22,16},{23,17},{30,24},{31,25},{38,32},... | collective-permute-start | bytes 786440 | tf_op jit(solution)/shard_map/ppermute | solution.py:731
  468.9 19.9 %collective-permute-start.14 = (bf16[2,384,512]{2,1,0:T(8,128)(2,1)}, bf16[2,384,512]{2,1,0:T(8,128)(2,1)}, u32[]{:S(2)}, u32[]{:S(2)}) collective-permute-start(bf16[2,384,512]{2,1,0:T(8,128)(2,1)} %slice.138), channel_id=1, source_target_pairs={{0,1},{1,0},{2,3},{3,2},{4,5},{5,4},{6,7},{7,6},{8,9},{9,8},{10,11... | collective-permute-start | bytes 2359304 | tf_op jit(solution)/shard_map/ppermute | solution.py:47
  470.7 18.1 %copy-start.41 = (bf16[16,512]{1,0:T(8,128)(2,1)S(1)}, bf16[16,512]{1,0:T(8,128)(2,1)}, u32[]{:S(2)}) copy-start(bf16[16,512]{1,0:T(8,128)(2,1)} %copy-done.40) | copy-start | bytes 49156
  470.7 24.3 %copy-start.42 = (f32[1,1536]{1,0:T(1,128)S(1)}, f32[1,1536]{1,0:T(1,128)}, u32[]{:S(2)}) copy-start(f32[1,1536]{1,0:T(1,128)} %broadcast_in_dim.170) | copy-start | bytes 18436
  470.7 24.3 %copy-start.48 = (f32[8]{0:T(128)S(1)}, f32[8]{0:T(128)}, u32[]{:S(2)}) copy-start(f32[8]{0:T(128)} %pad.11.clone) | copy-start | bytes 100
  470.7 24.3 %copy-start.49 = (f32[8]{0:T(128)S(1)}, f32[8]{0:T(128)}, u32[]{:S(2)}) copy-start(f32[8]{0:T(128)} %pad.10.clone) | copy-start | bytes 100
  470.7 24.3 %copy-start.50 = (f32[8]{0:T(128)S(1)}, f32[8]{0:T(128)}, u32[]{:S(2)}) copy-start(f32[8]{0:T(128)} %pad.9.clone) | copy-start | bytes 100
  489.4 14.6 %collective-permute-start.15 = (bf16[2,128,512]{2,1,0:T(8,128)(2,1)}, bf16[2,128,512]{2,1,0:T(8,128)(2,1)S(1)}, u32[]{:S(2)}, u32[]{:S(2)}) collective-permute-start(bf16[2,128,512]{2,1,0:T(8,128)(2,1)} %get-tuple-element.152), channel_id=1, source_target_pairs={{2,0},{4,2},{6,4},{3,1},{5,3},{7,5},{10,8},{12,10},{14,12},{11,9},... | collective-permute-start | bytes 786440 | tf_op jit(solution)/shard_map/ppermute | solution.py:731
  490.7 13.3 %collective-permute-start.16 = (bf16[2,128,512]{2,1,0:T(8,128)(2,1)}, bf16[2,128,512]{2,1,0:T(8,128)(2,1)S(1)}, u32[]{:S(2)}, u32[]{:S(2)}) collective-permute-start(bf16[2,128,512]{2,1,0:T(8,128)(2,1)} %get-tuple-element.153), channel_id=1, source_target_pairs={{4,0},{6,2},{5,1},{7,3},{12,8},{14,10},{13,9},{15,11},{20,16},{22,... | collective-permute-start | bytes 786440 | tf_op jit(solution)/shard_map/ppermute | solution.py:731
  492.0 18.9 %collective-permute-start.17 = (bf16[2,128,512]{2,1,0:T(8,128)(2,1)}, bf16[2,128,512]{2,1,0:T(8,128)(2,1)S(1)}, u32[]{:S(2)}, u32[]{:S(2)}) collective-permute-start(bf16[2,128,512]{2,1,0:T(8,128)(2,1)} %get-tuple-element.154), channel_id=1, source_target_pairs={{6,0},{7,1},{14,8},{15,9},{22,16},{23,17},{30,24},{31,25},{38,32},... | collective-permute-start | bytes 786440 | tf_op jit(solution)/shard_map/ppermute | solution.py:731
  493.3 17.6 %collective-permute-start.18 = (bf16[384,512]{1,0:T(8,128)(2,1)S(1)}, bf16[384,512]{1,0:T(8,128)(2,1)S(1)}, u32[]{:S(2)}, u32[]{:S(2)}) collective-permute-start(bf16[384,512]{1,0:T(8,128)(2,1)S(1)} %slice_bitcast_fusion.3), channel_id=1, source_target_pairs={{0,1},{1,0},{2,3},{3,2},{4,5},{5,4},{6,7},{7,6},{8,9},{9,8},{10,11... | collective-permute-start | bytes 1179656 | tf_op jit(solution)/shard_map/ppermute | solution.py:47
  495.7 15.3 %copy-start.38 = (bf16[2,128,512]{2,1,0:T(8,128)(2,1)S(1)}, bf16[2,128,512]{2,1,0:T(8,128)(2,1)}, u32[]{:S(2)}) copy-start(bf16[2,128,512]{2,1,0:T(8,128)(2,1)} %get-tuple-element.165) | copy-start | bytes 786436
  495.7 16.5 %copy-start.39 = (bf16[2,128,512]{2,1,0:T(8,128)(2,1)S(1)}, bf16[2,128,512]{2,1,0:T(8,128)(2,1)}, u32[]{:S(2)}) copy-start(bf16[2,128,512]{2,1,0:T(8,128)(2,1)} %get-tuple-element.169) | copy-start | bytes 786436
  511.0 8.7 %collective-permute-start.19 = (bf16[4,4,2,24,1664]{4,3,2,1,0:T(8,128)(2,1)}, bf16[4,4,2,24,1664]{4,3,2,1,0:T(8,128)(2,1)}, u32[]{:S(2)}, u32[]{:S(2)}) collective-permute-start(bf16[4,4,2,24,1664]{4,3,2,1,0:T(8,128)(2,1)} %get-tuple-element.176), channel_id=1, source_target_pairs={{0,8},{8,0},{1,9},{9,1},{2,10},{10,2},{3,11},{11,3},{4,12},{12,4},... | collective-permute-start | bytes 7667720 | tf_op jit(solution)/shard_map/ppermute | solution.py:47
  523.3 2.8 collective-permute-start.23
  523.9 41.9 %collective-permute-start.24 = (bf16[512,1536]{1,0:T(8,128)(2,1)S(1)}, bf16[512,1536]{1,0:T(8,128)(2,1)}, u32[]{:S(2)}, u32[]{:S(2)}) collective-permute-start(bf16[512,1536]{1,0:T(8,128)(2,1)S(1)} %get-tuple-element.184.mine_ref), channel_id=1, source_target_pairs={{0,1},{1,0},{2,3},{3,2},{4,5},{5,4},{6,7},{7,6},{8,9},{9,8},{10,11... | collective-permute-start | bytes 4718600 | tf_op jit(solution)/shard_map/ppermute | solution.py:47
  527.3 38.4 %all-to-all-start.7 = ((bf16[4,4,2,24,640]{4,3,2,1,0:T(8,128)(2,1)}), bf16[4,4,2,24,640]{4,3,2,1,0:T(8,128)(2,1)}, u32[]{:S(2)}, u32[]{:S(2)}) async-start(bf16[4,4,2,24,640]{4,3,2,1,0:T(8,128)(2,1)} %add_convert_fusion), calls=%async_computation.8 | async-start | bytes 1966080 | tf_op jit(solution)/shard_map/all_to_all | solution.py:799
  533.3 17.9 %collective-permute-start.20 = (bf16[4,2,24,1664]{3,2,1,0:T(8,128)(2,1)}, bf16[4,2,24,1664]{3,2,1,0:T(8,128)(2,1)}, u32[]{:S(2)}, u32[]{:S(2)}) collective-permute-start(bf16[4,2,24,1664]{3,2,1,0:T(8,128)(2,1)} %get-tuple-element.178), channel_id=1, source_target_pairs={{0,16},{16,32},{32,48},{48,0},{1,17},{17,33},{33,49},{49,1},{2,18}... | collective-permute-start | bytes 1916936 | tf_op jit(solution)/shard_map/ppermute | solution.py:555
  534.7 31.0 %collective-permute-start.21 = (bf16[4,2,24,1664]{3,2,1,0:T(8,128)(2,1)}, bf16[4,2,24,1664]{3,2,1,0:T(8,128)(2,1)}, u32[]{:S(2)}, u32[]{:S(2)}) collective-permute-start(bf16[4,2,24,1664]{3,2,1,0:T(8,128)(2,1)} %get-tuple-element.179), channel_id=1, source_target_pairs={{0,32},{16,48},{32,0},{48,16},{1,33},{17,49},{33,1},{49,17},{2,34}... | collective-permute-start | bytes 1916936 | tf_op jit(solution)/shard_map/ppermute | solution.py:555
  537.4 28.4 %collective-permute-start.22 = (bf16[4,2,24,1664]{3,2,1,0:T(8,128)(2,1)}, bf16[4,2,24,1664]{3,2,1,0:T(8,128)(2,1)}, u32[]{:S(2)}, u32[]{:S(2)}) collective-permute-start(bf16[4,2,24,1664]{3,2,1,0:T(8,128)(2,1)} %get-tuple-element.180), channel_id=1, source_target_pairs={{0,48},{16,0},{32,16},{48,32},{1,49},{17,1},{33,17},{49,33},{2,50}... | collective-permute-start | bytes 1916936 | tf_op jit(solution)/shard_map/ppermute | solution.py:555
  567.2 10.3 %collective-permute-start.28 = (bf16[2,24,640]{2,1,0:T(8,128)(2,1)S(1)}, bf16[2,24,640]{2,1,0:T(8,128)(2,1)S(1)}, u32[]{:S(2)}, u32[]{:S(2)}) collective-permute-start(bf16[2,24,640]{2,1,0:T(8,128)(2,1)S(1)} %get-tuple-element.284), channel_id=1, source_target_pairs={{0,16},{16,32},{32,48},{48,0},{1,17},{17,33},{33,49},{49,1},{2,18}... | collective-permute-start | bytes 184328 | tf_op jit(solution)/shard_map/ppermute | solution.py:83
  568.7 10.7 %collective-permute-start.30 = (bf16[2,24,640]{2,1,0:T(8,128)(2,1)S(1)}, bf16[2,24,640]{2,1,0:T(8,128)(2,1)S(1)}, u32[]{:S(2)}, u32[]{:S(2)}) collective-permute-start(bf16[2,24,640]{2,1,0:T(8,128)(2,1)S(1)} %get-tuple-element.285), channel_id=1, source_target_pairs={{0,48},{16,0},{32,16},{48,32},{1,49},{17,1},{33,17},{49,33},{2,50}... | collective-permute-start | bytes 184328 | tf_op jit(solution)/shard_map/ppermute | solution.py:83
  570.5 8.9 %collective-permute-start.29 = (bf16[2,24,640]{2,1,0:T(8,128)(2,1)S(1)}, bf16[2,24,640]{2,1,0:T(8,128)(2,1)S(1)}, u32[]{:S(2)}, u32[]{:S(2)}) collective-permute-start(bf16[2,24,640]{2,1,0:T(8,128)(2,1)S(1)} %get-tuple-element.286), channel_id=1, source_target_pairs={{0,32},{16,48},{32,0},{48,16},{1,33},{17,49},{33,1},{49,17},{2,34}... | collective-permute-start | bytes 184328 | tf_op jit(solution)/shard_map/ppermute | solution.py:83
  573.9 14.1 %copy-start.24 = (f32[2,384,512]{2,1,0:T(8,128)S(1)}, f32[2,384,512]{2,1,0:T(8,128)}, u32[]{:S(2)}) copy-start(f32[2,384,512]{2,1,0:T(8,128)} %convert_add_fusion.1) | copy-start | bytes 4718596
  574.0 7.8 %collective-permute-start.25 = (bf16[2,24,1664]{2,1,0:T(8,128)(2,1)S(1)}, bf16[2,24,1664]{2,1,0:T(8,128)(2,1)S(1)}, u32[]{:S(2)}, u32[]{:S(2)}) collective-permute-start(bf16[2,24,1664]{2,1,0:T(8,128)(2,1)S(1)} %get-tuple-element.281), channel_id=1, source_target_pairs={{0,2},{2,4},{4,6},{6,0},{1,3},{3,5},{5,7},{7,1},{8,10},{10,12},{12... | collective-permute-start | bytes 479240 | tf_op jit(solution)/shard_map/ppermute | solution.py:83
  576.8 6.0 collective-permute-start.27
  577.5 7.5 %collective-permute-start.26 = (bf16[2,24,1664]{2,1,0:T(8,128)(2,1)S(1)}, bf16[2,24,1664]{2,1,0:T(8,128)(2,1)S(1)}, u32[]{:S(2)}, u32[]{:S(2)}) collective-permute-start(bf16[2,24,1664]{2,1,0:T(8,128)(2,1)S(1)} %get-tuple-element.283), channel_id=1, source_target_pairs={{0,4},{2,6},{4,0},{6,2},{1,5},{3,7},{5,1},{7,3},{8,12},{10,14},{12... | collective-permute-start | bytes 479240 | tf_op jit(solution)/shard_map/ppermute | solution.py:83
  585.2 9.0 %collective-permute-start.31 = (bf16[24,2304]{1,0:T(8,128)(2,1)S(1)}, bf16[24,2304]{1,0:T(8,128)(2,1)S(1)}, u32[]{:S(2)}, u32[]{:S(2)}) collective-permute-start(bf16[24,2304]{1,0:T(8,128)(2,1)S(1)} %dynamic-slice_bitcast_fusion.3), channel_id=1, source_target_pairs={{0,64},{64,0},{1,65},{65,1},{2,66},{66,2},{3,67},{67,3},{4,68},{68... | collective-permute-start | bytes 331784 | tf_op jit(solution)/shard_map/ppermute | solution.py:83
  596.8 3.8 collective-permute-start.32
  (33 other events, 125.1 us)
Sparse Core Ops, SparseCore 0:
  95.7 90.2 all-gather.2
  365.0 97.6 reduce-scatter.1

commit v9 on v8

--- a/solution.py
+++ b/solution.py
@@ -514,7 +514,7 @@
         in_specs=[block, pl.BlockSpec((1, width), lambda b: (0, 0)), block, block, block],
         out_specs=block,
         out_shape=jax.ShapeDtypeStruct((rows, width), F32),
-        compiler_params=pltpu.CompilerParams(vmem_limit_bytes=24 << 20),
+        compiler_params=pltpu.CompilerParams(vmem_limit_bytes=60 << 20),
         cost_estimate=pl.CostEstimate(
             flops=12 * rows * width, bytes_accessed=14 * rows * width, transcendentals=rows
         ),

time: 619 us -> 617 us (level)
  transfers between devices with their start and end apart: 42 -> 42, of which waited for: 23 -> 23; matrix products, arithmetic and copies ran while one was open for 11% -> 10% of each run, Pallas kernels for 9% -> 9%
where the time goes in v9:
time: 617 us; the launch traced here: 607 us
  waiting for transfers between devices  294 us (48%)
  Pallas kernels  84 us (14%)
  starting transfers between devices  80.4 us (13%)
  blocking collectives  37.4 us (6%)
  other arithmetic  35.4 us (6%)
  local copies, waits for them, and re-layouts  29.7 us (5%)
  matrix products  27.5 us (4%)
  between operations  19.4 us (3%)
    ppermute x14, waiting for transfers between devices, swap(): return lax.ppermute(value, axis, [(0, 1), (1, 0)])  140 us
    all_to_all x3, waiting for transfers between devices, exchange_slots(): lax.all_to_all(rows.reshape(EXPERTS, -1, width), ('h', 'x', 'c'), 0, 0, t...  54.7 us
    all_to_all x1, blocking collectives, exchange_slots(): lax.all_to_all(rows.reshape(EXPERTS, -1, width), ('h', 'x', 'c'), 0, 0, t...  37.4 us
    dot_general x16, matrix products, dot(): lax.dot_general(left, right, (((left_dim,), (right_dim,)), ((), ())), pre...  27.5 us
    reduce_scatter x1, waiting for transfers between devices, local(): grad_experts = lax.psum_scatter(grad_parts, 'y', scatter_dimension=0)  26.2 us
    ppermute x3, waiting for transfers between devices, send_blocks(): lax.ppermute(blocks[r], axis, [(i, (i + r) % 4) for i in range(4)])  23.1 us
    pallas_call x1, Pallas kernels, run_experts_back(): pl.pallas_call(experts_back_kernel, in_specs=[whole, column, column] + we...  17.1 us
    pallas_call x2, Pallas kernels, attend_back(): pl.pallas_call(bwd_kernel, grid=(count,), in_specs=[pl.BlockSpec(memory_s...  13.9 us
  transfers between devices with their start and end apart: 42, of which 23 were waited for; matrix products, arithmetic and copies ran while one was open for 10% of the time, Pallas kernels for 9%

profile of v9, /device:TPU:0, one launch (start us, length us, event | category | flops | bytes accessed | tf_op | source)
XLA Modules:
  0.0 607.3 jit_solution(14723373326160771884)
XLA Ops:
  11.4 7.9 %all-to-all-start = ((bf16[8,24,2176]{2,1,0:T(8,128)(2,1)}), bf16[8,24,2176]{2,1,0:T(8,128)(2,1)S(1)}, u32[]{:S(2)}, u32[]{:S(2)}) async-start(bf16[8,24,2176]{2,1,0:T(8,128)(2,1)} %broadcast_in_dim.148), calls=%async_computation | async-start | bytes 1671168 | tf_op jit(solution)/shard_map/all_to_all | solution.py:56
  20.7 13.6 %all-to-all-done = bf16[8,24,2176]{2,1,0:T(8,128)(2,1)S(1)} async-done(((bf16[8,24,2176]{2,1,0:T(8,128)(2,1)}), bf16[8,24,2176]{2,1,0:T(8,128)(2,1)S(1)}, u32[]{:S(2)}, u32[]{:S(2)}) %all-to-all-start) | async-done | bytes 835616 | tf_op jit(solution)/shard_map/all_to_all | solution.py:56
  35.5 4.3 all-to-all-start.1
  41.0 13.0 %all-to-all-done.1 = bf16[4,8,24,640]{3,2,1,0:T(8,128)(2,1)S(1)} async-done(((bf16[4,8,24,640]{3,2,1,0:T(8,128)(2,1)}), bf16[4,8,24,640]{3,2,1,0:T(8,128)(2,1)S(1)}, u32[]{:S(2)}, u32[]{:S(2)}) %all-to-all-start.1) | async-done | bytes 983072 | tf_op jit(solution)/shard_map/all_to_all | solution.py:61
  54.0 1.6 broadcast_in_dim.150
  57.1 4.5 all-to-all-start.2
  67.5 2.4 collective-permute-start.2
  69.9 2.1 collective-permute-start.1
  72.0 12.8 %collective-permute-done.4 = bf16[3,384,512]{2,1,0:T(8,128)(2,1)} collective-permute-done((bf16[3,384,512]{2,1,0:T(8,128)(2,1)}, bf16[3,384,512]{2,1,0:T(8,128)(2,1)}, u32[]{:S(2)}, u32[]{:S(2)}) %collective-permute-start.4) | collective-permute-done | bytes 1179680 | tf_op jit(solution)/shard_map/ppermute | solution.py:47
  84.8 6.7 %all-to-all-done.2 = bf16[4,8,24,1536]{3,2,1,0:T(8,128)(2,1)} async-done(((bf16[4,8,24,1536]{3,2,1,0:T(8,128)(2,1)}), bf16[4,8,24,1536]{3,2,1,0:T(8,128)(2,1)}, u32[]{:S(2)}, u32[]{:S(2)}) %all-to-all-start.2) | async-done | bytes 2359328 | tf_op jit(solution)/shard_map/all_to_all | solution.py:605
  91.5 3.2 pad_maximum_fusion.1
  97.4 2.3 collective-permute-done.5
  99.7 2.7 select_bitcast_fusion.1
  105.5 4.2 shard_map.246
  111.8 4.7 shard_map.247
  116.6 13.9 %collective-permute-done.6 = bf16[256,1536]{1,0:T(8,128)(2,1)S(1)} collective-permute-done((bf16[256,1536]{1,0:T(8,128)(2,1)S(1)}, bf16[256,1536]{1,0:T(8,128)(2,1)S(1)}, u32[]{:S(2)}, u32[]{:S(2)}) %collective-permute-start.6) | collective-permute-done | bytes 786464 | tf_op jit(solution)/shard_map/ppermute | solution.py:47
  132.5 17.7 %collective-permute-done.7 = bf16[256,1536]{1,0:T(8,128)(2,1)S(1)} collective-permute-done((bf16[256,1536]{1,0:T(8,128)(2,1)S(1)}, bf16[256,1536]{1,0:T(8,128)(2,1)S(1)}, u32[]{:S(2)}, u32[]{:S(2)}) %collective-permute-start.7) | collective-permute-done | bytes 786464 | tf_op jit(solution)/shard_map/ppermute | solution.py:47
  153.4 2.8 convolution_convert_fusion.1
  156.2 3.9 all-to-all-start.3
  162.5 29.6 %all-to-all-done.3 = bf16[16,48,1536]{2,1,0:T(8,128)(2,1)S(1)} async-done(((bf16[16,48,1536]{2,1,0:T(8,128)(2,1)}), bf16[16,48,1536]{2,1,0:T(8,128)(2,1)S(1)}, u32[]{:S(2)}, u32[]{:S(2)}) %all-to-all-start.3) | async-done | bytes 2359328 | tf_op jit(solution)/shard_map/all_to_all | solution.py:96
  192.1 12.1 %shard_map.248 = (f32[768,1024]{1,0:T(8,128)S(1)}, f32[768,1024]{1,0:T(8,128)S(1)}, bf16[768,1024]{1,0:T(8,128)(2,1)S(1)}, bf16[768,1536]{1,0:T(8,128)(2,1)S(1)}) custom-call(bf16[768,1536]{1,0:T(8,128)(2,1)S(1)} %bitcast.135, bf16[4,2,3,384,512]{4,3,2,1,0:T(8,128)(2,1)} %bitcast.147, bf16[4,2,3,384,512]{4,3,2,1,0:T(8,128)(2,1)} %bitcast.148, ...), custom_call_target="tpu_custom_call" | custom-call | flops 7247757312 | bytes 20000000 | tf_op jit(solution)/shard_map/pallas_call | solution.py:388
  204.2 1.6 copy-done.2
  205.8 37.4 %all_to_all.40 = bf16[16,48,1536]{2,1,0:T(8,128)(2,1)S(1)} all-to-all(bf16[16,48,1536]{2,1,0:T(8,128)(2,1)S(1)} %bitcast.137), channel_id=1, replica_groups=mesh['h'=2,'x'=4,'c'=2,'y'=4,'t'=2] {'h','x','c'}, dimensions={0} | all-to-all | bytes 4718592 | tf_op jit(solution)/shard_map/all_to_all | solution.py:96
  246.1 35.1 %collective-permute-done.8 = bf16[512,1536]{1,0:T(8,128)(2,1)S(1)} collective-permute-done((bf16[512,1536]{1,0:T(8,128)(2,1)S(1)}, bf16[512,1536]{1,0:T(8,128)(2,1)S(1)}, u32[]{:S(2)}, u32[]{:S(2)}) %collective-permute-start.8) | collective-permute-done | bytes 1572896 | tf_op jit(solution)/shard_map/ppermute | solution.py:47
  281.1 1.9 fusion
  284.7 2.8 convolution_convert_fusion
  287.5 4.5 all-to-all-start.5
  292.0 3.8 select_reduce_fusion.1
  296.8 20.2 %collective-permute-done.9 = f32[2,512]{1,0:T(2,128)S(1)} collective-permute-done((f32[2,512]{1,0:T(2,128)S(1)}, f32[2,512]{1,0:T(2,128)S(1)}, u32[]{:S(2)}, u32[]{:S(2)}) %collective-permute-start.9) | collective-permute-done | bytes 4128 | tf_op jit(solution)/shard_map/ppermute | solution.py:47
  317.0 7.0 %all-to-all-done.5 = bf16[16,48,1536]{2,1,0:T(8,128)(2,1)} async-done(((bf16[16,48,1536]{2,1,0:T(8,128)(2,1)}), bf16[16,48,1536]{2,1,0:T(8,128)(2,1)}, u32[]{:S(2)}, u32[]{:S(2)}) %all-to-all-start.5) | async-done | bytes 2359328 | tf_op jit(solution)/shard_map/all_to_all | solution.py:96
  324.0 17.1 %shard_map.249 = (bf16[768,1024]{1,0:T(8,128)(2,1)}, bf16[768,1024]{1,0:T(8,128)(2,1)}, bf16[768,1536]{1,0:T(8,128)(2,1)}) custom-call(bf16[768,1536]{1,0:T(8,128)(2,1)} %bitcast.50.d_ref, f32[768,1024]{1,0:T(8,128)} %copy-done.1, f32[768,1024]{1,0:T(8,128)} %copy-done.2, bf16[4,2,3,384,512]{4,3,2,1,0:T(8,128)(2,1)} %bitcast.150, ...), custom_call_target="tpu_custom_call" | custom-call | flops 7247757312 | bytes 20000000 | tf_op jit(solution)/shard_map/pallas_call | solution.py:408
  341.2 5.5 all-to-all-start.6
  346.8 13.9 %shard_map.250 = bf16[4,2,3,384,512]{4,3,2,1,0:T(8,128)(2,1)} custom-call(bf16[768,1536]{1,0:T(8,128)(2,1)} %bitcast.136, bf16[768,1536]{1,0:T(8,128)(2,1)} %bitcast.50.d_ref, bf16[768,1024]{1,0:T(8,128)(2,1)} %get-tuple-element.129.dg_ref, bf16[768,1024]{1,0:T(8,128)(2,1)} %get-tuple-element.130.du_ref, bf16[768,1024]{1,0:T(8,128)(2,1)} %copy-done.7), custom_call_target="tpu_custom_call" | custom-call | flops 7247757312 | bytes 20000000 | tf_op jit(solution)/shard_map/pallas_call | solution.py:422
  360.7 18.1 %all-to-all-done.6 = bf16[16,48,1536]{2,1,0:T(8,128)(2,1)} async-done(((bf16[16,48,1536]{2,1,0:T(8,128)(2,1)}), bf16[16,48,1536]{2,1,0:T(8,128)(2,1)}, u32[]{:S(2)}, u32[]{:S(2)}) %all-to-all-start.6) | async-done | bytes 2359328 | tf_op jit(solution)/shard_map/all_to_all | solution.py:96
  378.8 4.1 convolution_convert_fusion.2
  388.1 31.1 %collective-permute-done.10 = bf16[512,1536]{1,0:T(8,128)(2,1)S(1)} collective-permute-done((bf16[512,1536]{1,0:T(8,128)(2,1)S(1)}, bf16[512,1536]{1,0:T(8,128)(2,1)S(1)}, u32[]{:S(2)}, u32[]{:S(2)}) %collective-permute-start.10) | collective-permute-done | bytes 1572896 | tf_op jit(solution)/shard_map/ppermute | solution.py:47
  421.2 3.4 fusion.67
  424.5 2.3 fusion.18.d_ref
  426.9 6.9 %shard_map.251 = (bf16[384,512]{1,0:T(8,128)(2,1)}, bf16[2,128,512]{2,1,0:T(8,128)(2,1)}, bf16[2,128,512]{2,1,0:T(8,128)(2,1)}, bf16[2,128,512]{2,1,0:T(8,128)(2,1)}, bf16[2,128,512]{2,1,0:T(8,128)(2,1)}) custom-call(s32[1]{0:T(128)} %bitcast.y_ref, bf16[768,512]{1,0:T(8,128)(2,1)} %copy-done.15, bf16[768,512]{1,0:T(8,128)(2,1)} %fusion.18.d_ref, ...), custom_call_target="tpu_custom_call" | custom-call | flops 149999992832 | bytes 6000000 | tf_op jit(solution)/shard_map/pallas_call | solution.py:273
  433.8 26.2 %reduce-scatter.2.cloned.1.call-done = bf16[1,2,3,384,512]{4,3,2,1,0:T(8,128)(2,1)} async-done(((bf16[4,2,3,384,512]{4,3,2,1,0:T(8,128)(2,1)}), bf16[1,2,3,384,512]{4,3,2,1,0:T(8,128)(2,1)}) %reduce-scatter.2.cloned.1.call-update) | async-done | bytes 2359312 | tf_op jit(solution)/shard_map/reduce_scatter | solution.py:707
  466.2 1.8 collective-permute-start.14
  468.0 7.0 %shard_map.252 = (bf16[384,512]{1,0:T(8,128)(2,1)}, bf16[2,128,512]{2,1,0:T(8,128)(2,1)}, bf16[2,128,512]{2,1,0:T(8,128)(2,1)}, bf16[2,128,512]{2,1,0:T(8,128)(2,1)}, bf16[2,128,512]{2,1,0:T(8,128)(2,1)}) custom-call(s32[1]{0:T(128)} %bitcast.y_ref, bf16[768,512]{1,0:T(8,128)(2,1)} %copy-done.15, bf16[768,512]{1,0:T(8,128)(2,1)} %fusion.18.d_ref, ...), custom_call_target="tpu_custom_call" | custom-call | flops 149999992832 | bytes 6000000 | tf_op jit(solution)/shard_map/pallas_call | solution.py:273
  476.0 4.1 collective-permute-done.13
  480.1 5.9 collective-permute-done.14
  490.6 1.6 collective-permute-start.18
  492.9 8.4 %shard_map.253 = (bf16[4,4,2,24,1664]{4,3,2,1,0:T(8,128)(2,1)}, bf16[4,4,2,24,1664]{4,3,2,1,0:T(8,128)(2,1)}) custom-call(s32[1]{0:T(128)} %bitcast.55.core_ref, bf16[512,1536]{1,0:T(8,128)(2,1)} %copy-done.36, bf16[512,1536]{1,0:T(8,128)(2,1)} %copy-done.3, bf16[512,1536]{1,0:T(8,128)(2,1)} %copy-done.29, f32[8,1536]{1,0:T(8,128)} %maximum_maximum_fusion.refs_3_, ...), custom_call_target="tpu_custom_call" | custom-call | flops 20000000000 | bytes 10000000 | tf_op jit(solution)/shard_map/pallas_call | solution.py:484
  501.4 6.3 %collective-permute-done.17 = bf16[2,128,512]{2,1,0:T(8,128)(2,1)S(1)} collective-permute-done((bf16[2,128,512]{2,1,0:T(8,128)(2,1)}, bf16[2,128,512]{2,1,0:T(8,128)(2,1)S(1)}, u32[]{:S(2)}, u32[]{:S(2)}) %collective-permute-start.17) | collective-permute-done | bytes 262176 | tf_op jit(solution)/shard_map/ppermute | solution.py:731
  509.1 3.3 fusion.6
  513.9 2.4 shard_map.254
  516.4 3.7 fusion.44
  521.3 1.5 collective-permute-done.23
  524.0 5.7 all-to-all-start.7
  531.2 2.7 collective-permute-start.21
  536.4 1.6 convert_add_fusion.1
  539.1 8.5 %collective-permute-done.20 = bf16[4,2,24,1664]{3,2,1,0:T(8,128)(2,1)} collective-permute-done((bf16[4,2,24,1664]{3,2,1,0:T(8,128)(2,1)}, bf16[4,2,24,1664]{3,2,1,0:T(8,128)(2,1)}, u32[]{:S(2)}, u32[]{:S(2)}) %collective-permute-start.20) | collective-permute-done | bytes 639008 | tf_op jit(solution)/shard_map/ppermute | solution.py:555
  547.6 14.6 %collective-permute-done.21 = bf16[4,2,24,1664]{3,2,1,0:T(8,128)(2,1)} collective-permute-done((bf16[4,2,24,1664]{3,2,1,0:T(8,128)(2,1)}, bf16[4,2,24,1664]{3,2,1,0:T(8,128)(2,1)}, u32[]{:S(2)}, u32[]{:S(2)}) %collective-permute-start.21) | collective-permute-done | bytes 639008 | tf_op jit(solution)/shard_map/ppermute | solution.py:555
  565.1 1.8 collective-permute-start.30
  568.4 2.0 add_convert_fusion.3
  570.5 2.8 collective-permute-start.25
  573.9 1.9 collective-permute-start.26
  575.9 2.5 collective-permute-done.25
  579.3 2.2 collective-permute-done.26
  581.6 2.9 collective-permute-start.31
  585.8 6.1 %shard_map.256 = f32[512,1536]{1,0:T(8,128)} custom-call(bf16[512,1536]{1,0:T(8,128)(2,1)} %tokens_ref.1, f32[1,1536]{1,0:T(1,128)} %get-tuple-element.295.gain_ref, bf16[512,1536]{1,0:T(8,128)(2,1)} %copy-done.30, bf16[512,1536]{1,0:T(8,128)(2,1)} %collective-permute-done.24.other_ref, f32[512,1536]{1,0:T(8,128)} %get-tuple-element.266.later_ref), custom_call_target="tpu_custom_call" | custom-call | flops 9437184 | bytes 11010048 | tf_op jit(solution)/shard_map/pallas_call | solution.py:511
  (262 shorter events, 78.0 us)
Async XLA Ops:
  11.4 22.8 %all-to-all-start = ((bf16[8,24,2176]{2,1,0:T(8,128)(2,1)}), bf16[8,24,2176]{2,1,0:T(8,128)(2,1)S(1)}, u32[]{:S(2)}, u32[]{:S(2)}) async-start(bf16[8,24,2176]{2,1,0:T(8,128)(2,1)} %broadcast_in_dim.148), calls=%async_computation | async-start | bytes 1671168 | tf_op jit(solution)/shard_map/all_to_all | solution.py:56
  35.5 18.5 %all-to-all-start.1 = ((bf16[4,8,24,640]{3,2,1,0:T(8,128)(2,1)}), bf16[4,8,24,640]{3,2,1,0:T(8,128)(2,1)S(1)}, u32[]{:S(2)}, u32[]{:S(2)}) async-start(bf16[4,8,24,640]{3,2,1,0:T(8,128)(2,1)} %broadcast_in_dim.149), calls=%async_computation.1 | async-start | bytes 1966080 | tf_op jit(solution)/shard_map/all_to_all | solution.py:61
  39.8 15.8 %copy-start.20 = (bf16[512,1536]{1,0:T(8,128)(2,1)S(1)}, bf16[512,1536]{1,0:T(8,128)(2,1)}, u32[]{:S(2)}) copy-start(bf16[512,1536]{1,0:T(8,128)(2,1)} %tokens_ref.1) | copy-start | bytes 4718596
  55.6 6.1 collective-permute-start
  56.0 28.8 %collective-permute-start.4 = (bf16[3,384,512]{2,1,0:T(8,128)(2,1)}, bf16[3,384,512]{2,1,0:T(8,128)(2,1)}, u32[]{:S(2)}, u32[]{:S(2)}) collective-permute-start(bf16[3,384,512]{2,1,0:T(8,128)(2,1)} %pad_maximum_fusion.3), channel_id=1, source_target_pairs={{0,1},{1,0},{2,3},{3,2},{4,5},{5,4},{6,7},{7,6},{8,9},{9,8},{10,11... | collective-permute-start | bytes 3538952 | tf_op jit(solution)/shard_map/ppermute | solution.py:47
  57.1 34.4 %all-to-all-start.2 = ((bf16[4,8,24,1536]{3,2,1,0:T(8,128)(2,1)}), bf16[4,8,24,1536]{3,2,1,0:T(8,128)(2,1)}, u32[]{:S(2)}, u32[]{:S(2)}) async-start(bf16[4,8,24,1536]{3,2,1,0:T(8,128)(2,1)} %broadcast_in_dim.150), calls=%async_computation.2 | async-start | bytes 4718592 | tf_op jit(solution)/shard_map/all_to_all | solution.py:605
  61.6 130.5 %all-gather.3.cloned.1.call-start = ((), (), s32[]{:S(2)}) async-start(), calls=%async_computation.10 | async-start | bytes 11796480 | tf_op jit(solution)/shard_map/all_gather | solution.py:631
  65.1 38.2 %copy-start.3 = (bf16[512,1536]{1,0:T(8,128)(2,1)}, bf16[512,1536]{1,0:T(8,128)(2,1)S(1)}, u32[]{:S(2)}) copy-start(bf16[512,1536]{1,0:T(8,128)(2,1)S(1)} %fusion.3.refs_1_.refs_0_) | copy-start | bytes 4718596
  66.2 45.6 %copy-start.8 = (bf16[512,512]{1,0:T(8,128)(2,1)}, bf16[512,512]{1,0:T(8,128)(2,1)S(1)}, u32[]{:S(2)}) copy-start(bf16[512,512]{1,0:T(8,128)(2,1)S(1)} %fusion.27) | copy-start | bytes 1572868
  66.2 28.5 %collective-permute-start.3 = (bf16[2,256,512]{2,1,0:T(8,128)(2,1)S(1)}, bf16[2,256,512]{2,1,0:T(8,128)(2,1)S(1)}, u32[]{:S(2)}, u32[]{:S(2)}) collective-permute-start(bf16[2,256,512]{2,1,0:T(8,128)(2,1)S(1)} %bitcast.140), channel_id=1, source_target_pairs={{0,6},{1,7},{8,14},{9,15},{16,22},{17,23},{24,30},{25,31},{32,38},... | collective-permute-start | bytes 1572872 | tf_op jit(solution)/shard_map/ppermute | solution.py:619
  67.5 27.2 %collective-permute-start.2 = (bf16[2,256,512]{2,1,0:T(8,128)(2,1)S(1)}, bf16[2,256,512]{2,1,0:T(8,128)(2,1)S(1)}, u32[]{:S(2)}, u32[]{:S(2)}) collective-permute-start(bf16[2,256,512]{2,1,0:T(8,128)(2,1)S(1)} %bitcast.141), channel_id=1, source_target_pairs={{0,4},{2,6},{1,5},{3,7},{8,12},{10,14},{9,13},{11,15},{16,20},{18,... | collective-permute-start | bytes 1572872 | tf_op jit(solution)/shard_map/ppermute | solution.py:619
  69.9 24.8 %collective-permute-start.1 = (bf16[2,256,512]{2,1,0:T(8,128)(2,1)S(1)}, bf16[2,256,512]{2,1,0:T(8,128)(2,1)}, u32[]{:S(2)}, u32[]{:S(2)}) collective-permute-start(bf16[2,256,512]{2,1,0:T(8,128)(2,1)S(1)} %bitcast.142), channel_id=1, source_target_pairs={{0,2},{2,4},{4,6},{1,3},{3,5},{5,7},{8,10},{10,12},{12,14},{9,11},... | collective-permute-start | bytes 1572872 | tf_op jit(solution)/shard_map/ppermute | solution.py:619
  94.8 5.0 collective-permute-start.5
  96.7 15.1 %copy-start.5 = (s32[2048,1]{1,0:T(8,128)}, s32[2048,1]{1,0:T(8,128)S(1)}, u32[]{:S(2)}) copy-start(s32[2048,1]{1,0:T(8,128)S(1)} %copy.67.seg_k) | copy-start | bytes 24580
  97.4 148.6 %copy-start.6 = (s32[1,512]{1,0:T(1,128)}, s32[1,512]{1,0:T(1,128)S(1)}, u32[]{:S(2)}) copy-start(s32[1,512]{1,0:T(1,128)S(1)} %get-tuple-element.264.seg_q) | copy-start | bytes 6148
  103.3 27.1 %copy-start.32 = (bf16[2,4,2,96,1536]{4,3,2,1,0:T(8,128)(2,1)}, bf16[2,4,2,96,1536]{4,3,2,1,0:T(8,128)(2,1)S(1)}, u32[]{:S(2)}) copy-start(bf16[2,4,2,96,1536]{4,3,2,1,0:T(8,128)(2,1)S(1)} %copy.66) | copy-start | bytes 14155780
  110.6 19.9 %collective-permute-start.6 = (bf16[256,1536]{1,0:T(8,128)(2,1)S(1)}, bf16[256,1536]{1,0:T(8,128)(2,1)S(1)}, u32[]{:S(2)}, u32[]{:S(2)}) collective-permute-start(bf16[256,1536]{1,0:T(8,128)(2,1)S(1)} %convolution_convert_fusion.5), channel_id=1, source_target_pairs={{0,1},{1,0},{2,3},{3,2},{4,5},{5,4},{6,7},{7,6},{8,9},{9,8},{10,11... | collective-permute-start | bytes 2359304 | tf_op jit(solution)/shard_map/ppermute | solution.py:47
  116.6 14.7 %copy-start.14 = (bf16[768,256]{1,0:T(8,128)(2,1)}, bf16[768,256]{1,0:T(8,128)(2,1)S(1)}, u32[]{:S(2)}) copy-start(bf16[768,256]{1,0:T(8,128)(2,1)S(1)} %get-tuple-element.117.o_1.refs_5_) | copy-start | bytes 1179652
  116.6 14.7 %copy-start.17 = (f32[4,8,256]{2,1,0:T(8,128)}, f32[4,8,256]{2,1,0:T(8,128)S(1)}, u32[]{:S(2)}) copy-start(f32[4,8,256]{2,1,0:T(8,128)S(1)} %get-tuple-element.135.lse_1) | copy-start | bytes 98308
  131.3 18.9 %collective-permute-start.7 = (bf16[256,1536]{1,0:T(8,128)(2,1)S(1)}, bf16[256,1536]{1,0:T(8,128)(2,1)S(1)}, u32[]{:S(2)}, u32[]{:S(2)}) collective-permute-start(bf16[256,1536]{1,0:T(8,128)(2,1)S(1)} %convolution_convert_fusion.4), channel_id=1, source_target_pairs={{0,1},{1,0},{2,3},{3,2},{4,5},{5,4},{6,7},{7,6},{8,9},{9,8},{10,11... | collective-permute-start | bytes 2359304 | tf_op jit(solution)/shard_map/ppermute | solution.py:47
  132.5 17.9 %copy-start.21 = (bf16[512,1536]{1,0:T(8,128)(2,1)S(1)}, bf16[512,1536]{1,0:T(8,128)(2,1)}, u32[]{:S(2)}) copy-start(bf16[512,1536]{1,0:T(8,128)(2,1)} %tokens_ref.1) | copy-start | bytes 4718596
  156.2 35.9 %all-to-all-start.3 = ((bf16[16,48,1536]{2,1,0:T(8,128)(2,1)}), bf16[16,48,1536]{2,1,0:T(8,128)(2,1)S(1)}, u32[]{:S(2)}, u32[]{:S(2)}) async-start(bf16[16,48,1536]{2,1,0:T(8,128)(2,1)} %bitcast.169), calls=%async_computation.3 | async-start | bytes 4718592 | tf_op jit(solution)/shard_map/all_to_all | solution.py:96
  205.8 37.4 %copy-start.1 = (f32[768,1024]{1,0:T(8,128)}, f32[768,1024]{1,0:T(8,128)S(1)}, u32[]{:S(2)}) copy-start(f32[768,1024]{1,0:T(8,128)S(1)} %get-tuple-element.124.g_ref) | copy-start | bytes 9437188
  205.8 37.4 %copy-start.7 = (bf16[768,1024]{1,0:T(8,128)(2,1)}, bf16[768,1024]{1,0:T(8,128)(2,1)S(1)}, u32[]{:S(2)}) copy-start(bf16[768,1024]{1,0:T(8,128)(2,1)S(1)} %get-tuple-element.131.inner_ref) | copy-start | bytes 4718596
  205.8 37.4 %copy-start.40 = (bf16[512,768]{1,0:T(8,128)(2,1)S(1)}, bf16[512,768]{1,0:T(8,128)(2,1)}, u32[]{:S(2)}) copy-start(bf16[512,768]{1,0:T(8,128)(2,1)} %add_convert_fusion.2) | copy-start | bytes 2359300
  243.2 37.9 %copy-start.19 = (f32[512,1536]{1,0:T(8,128)S(1)}, f32[512,1536]{1,0:T(8,128)}, u32[]{:S(2)}) copy-start(f32[512,1536]{1,0:T(8,128)} %copy-done.18) | copy-start | bytes 9437188
  243.2 37.9 %copy-start.25 = (bf16[512,1536]{1,0:T(8,128)(2,1)S(1)}, bf16[512,1536]{1,0:T(8,128)(2,1)}, u32[]{:S(2)}) copy-start(bf16[512,1536]{1,0:T(8,128)(2,1)} %param.16) | copy-start | bytes 4718596
  244.6 36.5 %collective-permute-start.8 = (bf16[512,1536]{1,0:T(8,128)(2,1)S(1)}, bf16[512,1536]{1,0:T(8,128)(2,1)S(1)}, u32[]{:S(2)}, u32[]{:S(2)}) collective-permute-start(bf16[512,1536]{1,0:T(8,128)(2,1)S(1)} %convolution_convert_fusion.3), channel_id=1, source_target_pairs={{0,1},{1,0},{2,3},{3,2},{4,5},{5,4},{6,7},{7,6},{8,9},{9,8},{10,11... | collective-permute-start | bytes 4718600 | tf_op jit(solution)/shard_map/ppermute | solution.py:47
  287.5 36.5 %all-to-all-start.5 = ((bf16[16,48,1536]{2,1,0:T(8,128)(2,1)}), bf16[16,48,1536]{2,1,0:T(8,128)(2,1)}, u32[]{:S(2)}, u32[]{:S(2)}) async-start(bf16[16,48,1536]{2,1,0:T(8,128)(2,1)} %bitcast.168), calls=%async_computation.5 | async-start | bytes 4718592 | tf_op jit(solution)/shard_map/all_to_all | solution.py:96
  295.8 21.2 %collective-permute-start.9 = (f32[2,512]{1,0:T(2,128)S(1)}, f32[2,512]{1,0:T(2,128)S(1)}, u32[]{:S(2)}, u32[]{:S(2)}) collective-permute-start(f32[2,512]{1,0:T(2,128)S(1)} %pad_maximum_fusion.6), channel_id=1, source_target_pairs={{0,1},{1,0},{2,3},{3,2},{4,5},{5,4},{6,7},{7,6},{8,9},{9,8},{10,11... | collective-permute-start | bytes 12296 | tf_op jit(solution)/shard_map/ppermute | solution.py:47
  341.2 37.6 %all-to-all-start.6 = ((bf16[16,48,1536]{2,1,0:T(8,128)(2,1)}), bf16[16,48,1536]{2,1,0:T(8,128)(2,1)}, u32[]{:S(2)}, u32[]{:S(2)}) async-start(bf16[16,48,1536]{2,1,0:T(8,128)(2,1)} %bitcast.167), calls=%async_computation.6 | async-start | bytes 4718592 | tf_op jit(solution)/shard_map/all_to_all | solution.py:96
  346.7 113.3 %reduce-scatter.2.cloned.1.call-start = ((), (), s32[]{:S(2)}) async-start(), calls=%async_computation.9 | async-start | bytes 11796480 | tf_op jit(solution)/shard_map/reduce_scatter | solution.py:707
  382.9 36.3 %collective-permute-start.10 = (bf16[512,1536]{1,0:T(8,128)(2,1)S(1)}, bf16[512,1536]{1,0:T(8,128)(2,1)S(1)}, u32[]{:S(2)}, u32[]{:S(2)}) collective-permute-start(bf16[512,1536]{1,0:T(8,128)(2,1)S(1)} %convolution_convert_fusion.2), channel_id=1, source_target_pairs={{0,1},{1,0},{2,3},{3,2},{4,5},{5,4},{6,7},{7,6},{8,9},{9,8},{10,11... | collective-permute-start | bytes 4718600 | tf_op jit(solution)/shard_map/ppermute | solution.py:47
  388.1 32.9 %copy-start.26 = (bf16[512,1536]{1,0:T(8,128)(2,1)S(1)}, bf16[512,1536]{1,0:T(8,128)(2,1)}, u32[]{:S(2)}) copy-start(bf16[512,1536]{1,0:T(8,128)(2,1)} %param.16) | copy-start | bytes 4718596
  461.3 14.7 %collective-permute-start.11 = (bf16[2,128,512]{2,1,0:T(8,128)(2,1)}, bf16[2,128,512]{2,1,0:T(8,128)(2,1)}, u32[]{:S(2)}, u32[]{:S(2)}) collective-permute-start(bf16[2,128,512]{2,1,0:T(8,128)(2,1)} %get-tuple-element.147), channel_id=1, source_target_pairs={{2,0},{4,2},{6,4},{3,1},{5,3},{7,5},{10,8},{12,10},{14,12},{11,9},... | collective-permute-start | bytes 786440 | tf_op jit(solution)/shard_map/ppermute | solution.py:731
  462.6 13.4 %collective-permute-start.12 = (bf16[2,128,512]{2,1,0:T(8,128)(2,1)}, bf16[2,128,512]{2,1,0:T(8,128)(2,1)}, u32[]{:S(2)}, u32[]{:S(2)}) collective-permute-start(bf16[2,128,512]{2,1,0:T(8,128)(2,1)} %get-tuple-element.148), channel_id=1, source_target_pairs={{4,0},{6,2},{5,1},{7,3},{12,8},{14,10},{13,9},{15,11},{20,16},{22,... | collective-permute-start | bytes 786440 | tf_op jit(solution)/shard_map/ppermute | solution.py:731
  463.9 16.1 %collective-permute-start.13 = (bf16[2,128,512]{2,1,0:T(8,128)(2,1)}, bf16[2,128,512]{2,1,0:T(8,128)(2,1)}, u32[]{:S(2)}, u32[]{:S(2)}) collective-permute-start(bf16[2,128,512]{2,1,0:T(8,128)(2,1)} %get-tuple-element.149), channel_id=1, source_target_pairs={{6,0},{7,1},{14,8},{15,9},{22,16},{23,17},{30,24},{31,25},{38,32},... | collective-permute-start | bytes 786440 | tf_op jit(solution)/shard_map/ppermute | solution.py:731
  466.2 19.8 %collective-permute-start.14 = (bf16[2,384,512]{2,1,0:T(8,128)(2,1)}, bf16[2,384,512]{2,1,0:T(8,128)(2,1)}, u32[]{:S(2)}, u32[]{:S(2)}) collective-permute-start(bf16[2,384,512]{2,1,0:T(8,128)(2,1)} %slice.138), channel_id=1, source_target_pairs={{0,1},{1,0},{2,3},{3,2},{4,5},{5,4},{6,7},{7,6},{8,9},{9,8},{10,11... | collective-permute-start | bytes 2359304 | tf_op jit(solution)/shard_map/ppermute | solution.py:47
  467.9 18.1 %copy-start.47 = (bf16[16,512]{1,0:T(8,128)(2,1)S(1)}, bf16[16,512]{1,0:T(8,128)(2,1)}, u32[]{:S(2)}) copy-start(bf16[16,512]{1,0:T(8,128)(2,1)} %copy-done.46) | copy-start | bytes 49156
  467.9 24.3 %copy-start.48 = (f32[1,1536]{1,0:T(1,128)S(1)}, f32[1,1536]{1,0:T(1,128)}, u32[]{:S(2)}) copy-start(f32[1,1536]{1,0:T(1,128)} %broadcast_in_dim.170) | copy-start | bytes 18436
  467.9 24.3 %copy-start.54 = (f32[8]{0:T(128)S(1)}, f32[8]{0:T(128)}, u32[]{:S(2)}) copy-start(f32[8]{0:T(128)} %pad.11.clone) | copy-start | bytes 100
  467.9 24.3 %copy-start.55 = (f32[8]{0:T(128)S(1)}, f32[8]{0:T(128)}, u32[]{:S(2)}) copy-start(f32[8]{0:T(128)} %pad.10.clone) | copy-start | bytes 100
  467.9 24.3 %copy-start.56 = (f32[8]{0:T(128)S(1)}, f32[8]{0:T(128)}, u32[]{:S(2)}) copy-start(f32[8]{0:T(128)} %pad.9.clone) | copy-start | bytes 100
  486.7 14.7 %collective-permute-start.15 = (bf16[2,128,512]{2,1,0:T(8,128)(2,1)}, bf16[2,128,512]{2,1,0:T(8,128)(2,1)S(1)}, u32[]{:S(2)}, u32[]{:S(2)}) collective-permute-start(bf16[2,128,512]{2,1,0:T(8,128)(2,1)} %get-tuple-element.152), channel_id=1, source_target_pairs={{2,0},{4,2},{6,4},{3,1},{5,3},{7,5},{10,8},{12,10},{14,12},{11,9},... | collective-permute-start | bytes 786440 | tf_op jit(solution)/shard_map/ppermute | solution.py:731
  488.0 13.4 %collective-permute-start.16 = (bf16[2,128,512]{2,1,0:T(8,128)(2,1)}, bf16[2,128,512]{2,1,0:T(8,128)(2,1)S(1)}, u32[]{:S(2)}, u32[]{:S(2)}) collective-permute-start(bf16[2,128,512]{2,1,0:T(8,128)(2,1)} %get-tuple-element.153), channel_id=1, source_target_pairs={{4,0},{6,2},{5,1},{7,3},{12,8},{14,10},{13,9},{15,11},{20,16},{22,... | collective-permute-start | bytes 786440 | tf_op jit(solution)/shard_map/ppermute | solution.py:731
  489.3 18.4 %collective-permute-start.17 = (bf16[2,128,512]{2,1,0:T(8,128)(2,1)}, bf16[2,128,512]{2,1,0:T(8,128)(2,1)S(1)}, u32[]{:S(2)}, u32[]{:S(2)}) collective-permute-start(bf16[2,128,512]{2,1,0:T(8,128)(2,1)} %get-tuple-element.154), channel_id=1, source_target_pairs={{6,0},{7,1},{14,8},{15,9},{22,16},{23,17},{30,24},{31,25},{38,32},... | collective-permute-start | bytes 786440 | tf_op jit(solution)/shard_map/ppermute | solution.py:731
  490.6 17.1 %collective-permute-start.18 = (bf16[384,512]{1,0:T(8,128)(2,1)S(1)}, bf16[384,512]{1,0:T(8,128)(2,1)S(1)}, u32[]{:S(2)}, u32[]{:S(2)}) collective-permute-start(bf16[384,512]{1,0:T(8,128)(2,1)S(1)} %slice_bitcast_fusion.3), channel_id=1, source_target_pairs={{0,1},{1,0},{2,3},{3,2},{4,5},{5,4},{6,7},{7,6},{8,9},{9,8},{10,11... | collective-permute-start | bytes 1179656 | tf_op jit(solution)/shard_map/ppermute | solution.py:47
  492.9 14.7 %copy-start.44 = (bf16[2,128,512]{2,1,0:T(8,128)(2,1)S(1)}, bf16[2,128,512]{2,1,0:T(8,128)(2,1)}, u32[]{:S(2)}) copy-start(bf16[2,128,512]{2,1,0:T(8,128)(2,1)} %get-tuple-element.165) | copy-start | bytes 786436
  492.9 16.0 %copy-start.45 = (bf16[2,128,512]{2,1,0:T(8,128)(2,1)S(1)}, bf16[2,128,512]{2,1,0:T(8,128)(2,1)}, u32[]{:S(2)}) copy-start(bf16[2,128,512]{2,1,0:T(8,128)(2,1)} %get-tuple-element.169) | copy-start | bytes 786436
  507.6 8.7 %collective-permute-start.19 = (bf16[4,4,2,24,1664]{4,3,2,1,0:T(8,128)(2,1)}, bf16[4,4,2,24,1664]{4,3,2,1,0:T(8,128)(2,1)}, u32[]{:S(2)}, u32[]{:S(2)}) collective-permute-start(bf16[4,4,2,24,1664]{4,3,2,1,0:T(8,128)(2,1)} %get-tuple-element.176), channel_id=1, source_target_pairs={{0,8},{8,0},{1,9},{9,1},{2,10},{10,2},{3,11},{11,3},{4,12},{12,4},... | collective-permute-start | bytes 7667720 | tf_op jit(solution)/shard_map/ppermute | solution.py:47
  520.1 2.7 collective-permute-start.23
  520.6 41.6 %collective-permute-start.24 = (bf16[512,1536]{1,0:T(8,128)(2,1)S(1)}, bf16[512,1536]{1,0:T(8,128)(2,1)}, u32[]{:S(2)}, u32[]{:S(2)}) collective-permute-start(bf16[512,1536]{1,0:T(8,128)(2,1)S(1)} %get-tuple-element.184.mine_ref), channel_id=1, source_target_pairs={{0,1},{1,0},{2,3},{3,2},{4,5},{5,4},{6,7},{7,6},{8,9},{9,8},{10,11... | collective-permute-start | bytes 4718600 | tf_op jit(solution)/shard_map/ppermute | solution.py:47
  524.0 38.2 %all-to-all-start.7 = ((bf16[4,4,2,24,640]{4,3,2,1,0:T(8,128)(2,1)}), bf16[4,4,2,24,640]{4,3,2,1,0:T(8,128)(2,1)}, u32[]{:S(2)}, u32[]{:S(2)}) async-start(bf16[4,4,2,24,640]{4,3,2,1,0:T(8,128)(2,1)} %add_convert_fusion), calls=%async_computation.8 | async-start | bytes 1966080 | tf_op jit(solution)/shard_map/all_to_all | solution.py:799
  529.7 17.9 %collective-permute-start.20 = (bf16[4,2,24,1664]{3,2,1,0:T(8,128)(2,1)}, bf16[4,2,24,1664]{3,2,1,0:T(8,128)(2,1)}, u32[]{:S(2)}, u32[]{:S(2)}) collective-permute-start(bf16[4,2,24,1664]{3,2,1,0:T(8,128)(2,1)} %get-tuple-element.178), channel_id=1, source_target_pairs={{0,16},{16,32},{32,48},{48,0},{1,17},{17,33},{33,49},{49,1},{2,18}... | collective-permute-start | bytes 1916936 | tf_op jit(solution)/shard_map/ppermute | solution.py:555
  531.2 31.0 %collective-permute-start.21 = (bf16[4,2,24,1664]{3,2,1,0:T(8,128)(2,1)}, bf16[4,2,24,1664]{3,2,1,0:T(8,128)(2,1)}, u32[]{:S(2)}, u32[]{:S(2)}) collective-permute-start(bf16[4,2,24,1664]{3,2,1,0:T(8,128)(2,1)} %get-tuple-element.179), channel_id=1, source_target_pairs={{0,32},{16,48},{32,0},{48,16},{1,33},{17,49},{33,1},{49,17},{2,34}... | collective-permute-start | bytes 1916936 | tf_op jit(solution)/shard_map/ppermute | solution.py:555
  533.9 28.4 %collective-permute-start.22 = (bf16[4,2,24,1664]{3,2,1,0:T(8,128)(2,1)}, bf16[4,2,24,1664]{3,2,1,0:T(8,128)(2,1)}, u32[]{:S(2)}, u32[]{:S(2)}) collective-permute-start(bf16[4,2,24,1664]{3,2,1,0:T(8,128)(2,1)} %get-tuple-element.180), channel_id=1, source_target_pairs={{0,48},{16,0},{32,16},{48,32},{1,49},{17,1},{33,17},{49,33},{2,50}... | collective-permute-start | bytes 1916936 | tf_op jit(solution)/shard_map/ppermute | solution.py:555
  563.7 10.3 %collective-permute-start.28 = (bf16[2,24,640]{2,1,0:T(8,128)(2,1)S(1)}, bf16[2,24,640]{2,1,0:T(8,128)(2,1)S(1)}, u32[]{:S(2)}, u32[]{:S(2)}) collective-permute-start(bf16[2,24,640]{2,1,0:T(8,128)(2,1)S(1)} %get-tuple-element.284), channel_id=1, source_target_pairs={{0,16},{16,32},{32,48},{48,0},{1,17},{17,33},{33,49},{49,1},{2,18}... | collective-permute-start | bytes 184328 | tf_op jit(solution)/shard_map/ppermute | solution.py:83
  565.1 10.7 %collective-permute-start.30 = (bf16[2,24,640]{2,1,0:T(8,128)(2,1)S(1)}, bf16[2,24,640]{2,1,0:T(8,128)(2,1)S(1)}, u32[]{:S(2)}, u32[]{:S(2)}) collective-permute-start(bf16[2,24,640]{2,1,0:T(8,128)(2,1)S(1)} %get-tuple-element.285), channel_id=1, source_target_pairs={{0,48},{16,0},{32,16},{48,32},{1,49},{17,1},{33,17},{49,33},{2,50}... | collective-permute-start | bytes 184328 | tf_op jit(solution)/shard_map/ppermute | solution.py:83
  567.0 8.9 %collective-permute-start.29 = (bf16[2,24,640]{2,1,0:T(8,128)(2,1)S(1)}, bf16[2,24,640]{2,1,0:T(8,128)(2,1)S(1)}, u32[]{:S(2)}, u32[]{:S(2)}) collective-permute-start(bf16[2,24,640]{2,1,0:T(8,128)(2,1)S(1)} %get-tuple-element.286), channel_id=1, source_target_pairs={{0,32},{16,48},{32,0},{48,16},{1,33},{17,49},{33,1},{49,17},{2,34}... | collective-permute-start | bytes 184328 | tf_op jit(solution)/shard_map/ppermute | solution.py:83
  570.5 7.9 %collective-permute-start.25 = (bf16[2,24,1664]{2,1,0:T(8,128)(2,1)S(1)}, bf16[2,24,1664]{2,1,0:T(8,128)(2,1)S(1)}, u32[]{:S(2)}, u32[]{:S(2)}) collective-permute-start(bf16[2,24,1664]{2,1,0:T(8,128)(2,1)S(1)} %get-tuple-element.281), channel_id=1, source_target_pairs={{0,2},{2,4},{4,6},{6,0},{1,3},{3,5},{5,7},{7,1},{8,10},{10,12},{12... | collective-permute-start | bytes 479240 | tf_op jit(solution)/shard_map/ppermute | solution.py:83
  573.3 6.0 collective-permute-start.27
  573.9 7.5 %collective-permute-start.26 = (bf16[2,24,1664]{2,1,0:T(8,128)(2,1)S(1)}, bf16[2,24,1664]{2,1,0:T(8,128)(2,1)S(1)}, u32[]{:S(2)}, u32[]{:S(2)}) collective-permute-start(bf16[2,24,1664]{2,1,0:T(8,128)(2,1)S(1)} %get-tuple-element.283), channel_id=1, source_target_pairs={{0,4},{2,6},{4,0},{6,2},{1,5},{3,7},{5,1},{7,3},{8,12},{10,14},{12... | collective-permute-start | bytes 479240 | tf_op jit(solution)/shard_map/ppermute | solution.py:83
  581.6 10.3 %collective-permute-start.31 = (bf16[24,2304]{1,0:T(8,128)(2,1)S(1)}, bf16[24,2304]{1,0:T(8,128)(2,1)S(1)}, u32[]{:S(2)}, u32[]{:S(2)}) collective-permute-start(bf16[24,2304]{1,0:T(8,128)(2,1)S(1)} %dynamic-slice_bitcast_fusion.3), channel_id=1, source_target_pairs={{0,64},{64,0},{1,65},{65,1},{2,66},{66,2},{3,67},{67,3},{4,68},{68... | collective-permute-start | bytes 331784 | tf_op jit(solution)/shard_map/ppermute | solution.py:83
  594.6 3.8 collective-permute-start.32
  (39 other events, 152.6 us)
Sparse Core Ops, SparseCore 0:
  94.9 90.5 all-gather.2
  360.8 99.1 reduce-scatter.1
